TPU v7x, 32 devices: a whole 2x2x4 slice. The times are simulated.
32 devices in a mesh: phi: 16 (over z, y, core), row: 2 (over x).
Axes of the slice: x: 2, y: 2, z: 4, core: 2. Of those that a mesh axis runs over, the one named last changes fastest.
Arguments:
- density: float32 [2, 512, 512], P(None, 'phi', 'row'), may hold values from 0.6 to 1.8
- momentum: float32 [2, 2, 512, 512], P(None, None, 'phi', 'row'), may hold values from -1 to 1
- magnetic: float32 [2, 2, 512, 512], P(None, None, 'phi', 'row'), may hold values from -1 to 1
- rotation: float32 [512], P('row'), may hold values from 1 to 4
- shifts: int32 [512], P('row'), may hold values from 8 to 56, as said below
Outputs:
- density_out: float32 [2, 512, 512], P(None, 'phi', 'row')
- momentum_out: float32 [2, 2, 512, 512], P(None, None, 'phi', 'row')
- magnetic_out: float32 [2, 2, 512, 512], P(None, None, 'phi', 'row')
Inputs may be any that keep to these rules, and one draw needn't show every extreme that they name: shifts[r] = 8 + floor((47) d^2 / 511^2) + j_r with d = 511 - r and j_r either 0 or 1, except that row 0 shifts by exactly 56 and the last row by exactly 8.
All inputs are finite; a program needn't handle non-finite values.
Results may differ from a plain program's by a relative error of at most 0.0003.
Values sent between devices are 32-bit elements; how exact they have to be, the bound alone decides.
No kernel may reach another device: no remote copies, remote signals or barrier semaphores. Data moves between devices by JAX's collectives and lax.ppermute only.
A program may use at most 64 MiB of HBM per device.

v0:
```python
import jax
import jax.numpy as jnp
from jax import lax
from jax.sharding import PartitionSpec as P

STEPS = 2
SMIN = 8
SMAX = 56


time_step = 0.08
sound_sq = 1.0


def padded(cells, sides, width):
    for axis, dim in sides:
        count = lax.axis_size(axis)
        head = lax.slice_in_dim(cells, 0, width, axis=dim)
        tail = lax.slice_in_dim(cells, cells.shape[dim] - width, cells.shape[dim], axis=dim)
        cells = jnp.concatenate(
            [
                lax.ppermute(tail, axis, [(i, (i + 1) % count) for i in range(count)]),
                cells,
                lax.ppermute(head, axis, [((i + 1) % count, i) for i in range(count)]),
            ],
            axis=dim,
        )
    return cells


def from_partner(x, axis, stride):
    return lax.ppermute(x, axis, [(i, i ^ 1 << stride) for i in range(lax.axis_size(axis))])


def passed_along(block, axis, distance):
    devices = range(lax.axis_size(axis))
    route = [((i - distance) % len(devices), i) for i in devices]
    return lax.ppermute(block, axis, route)


def window(values, begin_at, end_at, along_axis):
    return lax.slice_in_dim(values, begin_at, values.shape[along_axis] + end_at, 1, along_axis)


def minmod(lower_jump, upper_jump):
    return (
        0.5
        * (jnp.sign(lower_jump) + jnp.sign(upper_jump))
        * jnp.minimum(jnp.abs(lower_jump), jnp.abs(upper_jump))
    )


def physical(fields, normal):
    density, mom_phi, mom_rad, mag_phi, mag_rad = (
        fields[0],
        fields[1],
        fields[2],
        fields[3],
        fields[4],
    )
    vel_phi = mom_phi / density
    vel_rad = mom_rad / density
    magnetic_sq = mag_phi * mag_phi + mag_rad * mag_rad
    pressure = sound_sq * density + 0.5 * magnetic_sq
    nothing = jnp.zeros_like(density)
    if normal == 0:
        fluxes = jnp.stack(
            [
                mom_phi,
                mom_phi * vel_phi + pressure - mag_phi * mag_phi,
                mom_rad * vel_phi - mag_phi * mag_rad,
                nothing,
                mag_rad * vel_phi - mag_phi * vel_rad,
            ]
        )
        normal_vel = vel_phi
    else:
        fluxes = jnp.stack(
            [
                mom_rad,
                mom_phi * vel_rad - mag_phi * mag_rad,
                mom_rad * vel_rad + pressure - mag_rad * mag_rad,
                mag_phi * vel_rad - mag_rad * vel_phi,
                nothing,
            ]
        )
        normal_vel = vel_rad
    speeds = jnp.abs(normal_vel) + jnp.sqrt(sound_sq + magnetic_sq / density)
    return (fluxes, speeds)


def interfaces(fields, along_axis, normal):
    differences = window(fields, 1, 0, along_axis) - window(fields, 0, -1, along_axis)
    slopes = minmod(window(differences, 0, -1, along_axis), window(differences, 1, 0, along_axis))
    centres = window(fields, 1, -1, along_axis)
    left_state = window(centres + 0.5 * slopes, 0, -1, along_axis)
    right_state = window(centres - 0.5 * slopes, 1, 0, along_axis)
    left_flux, left_speed = physical(left_state, normal)
    right_flux, right_speed = physical(right_state, normal)
    wave_bound = jnp.maximum(left_speed, right_speed)
    return 0.5 * (left_flux + right_flux) - 0.5 * wave_bound * (right_state - left_state)


def tendency(along_phi, along_rad, rotation):
    phi_flux = interfaces(along_phi, 2, 0)
    rad_flux = interfaces(along_rad, 3, 1)
    centre = window(along_phi, 2, -2, 2)
    change = -(window(phi_flux, 1, 0, 2) - window(phi_flux, 0, -1, 2)) - (
        window(rad_flux, 1, 0, 3) - window(rad_flux, 0, -1, 3)
    )
    spin_rate = rotation[None, None, :]
    nothing = jnp.zeros_like(centre[0])
    source = jnp.stack(
        [
            nothing,
            -0.5 * spin_rate * centre[2],
            2.0 * spin_rate * centre[1],
            -1.5 * spin_rate * centre[4],
            nothing,
        ]
    )
    return change + source


def azimuth_ghosts(fields):
    return padded(fields, (("phi", 2),), 2)


def radial_ghosts(fields):
    lowest = lax.axis_index("row") == 0
    sending = jnp.where(lowest, fields[..., -2:], fields[..., :2])
    partner = from_partner(sending, "row", 0)
    inner_copy = jnp.broadcast_to(fields[..., :1], partner.shape)
    outer_copy = jnp.broadcast_to(fields[..., -1:], partner.shape)
    inner_ghost = jnp.where(lowest, inner_copy, partner)
    outer_ghost = jnp.where(lowest, partner, outer_copy)
    return jnp.concatenate([inner_ghost, fields, outer_ghost], axis=3)


def evaluate(fields, rotation):
    along_phi = azimuth_ghosts(fields)
    along_rad = radial_ghosts(fields)
    return tendency(along_phi, along_rad, rotation)


def fargo_local(fields, shifts, ghost_cells):
    own_cells = fields.shape[2]
    reach_cells = SMAX + ghost_cells
    blocks_needed = (reach_cells + own_cells - 1) // own_cells
    kept_cells = reach_cells - (blocks_needed - 1) * own_cells
    pieces = []
    for distance in range(blocks_needed, 0, -1):
        sender = fields[:, :, own_cells - kept_cells :] if distance == blocks_needed else fields
        pieces.append(passed_along(sender, "phi", distance))
    pieces.append(fields)
    joined = jnp.concatenate(pieces, axis=2)
    out_cells = own_cells + 2 * ghost_cells
    current = joined
    bit_count = max((SMAX - SMIN).bit_length(), 1)
    padding = jnp.zeros(
        (fields.shape[0], fields.shape[1], 2**bit_count, fields.shape[3]), fields.dtype
    )
    current = jnp.concatenate([current, padding], axis=2)
    remaining = SMAX - shifts
    for bit_number in range(bit_count):
        step_cells = 2**bit_number
        chosen = remaining >> bit_number & 1 == 1
        current = jnp.where(
            chosen[None, None, None, :], current[:, :, step_cells:], current[:, :, :-step_cells]
        )
    return current[:, :, :out_cells]


def body(density, momentum, magnetic, rotation, shifts):
    fields = jnp.concatenate([density[None], momentum, magnetic], axis=0)
    for step_number in range(STEPS):
        first_section = fields + time_step * evaluate(fields, rotation)
        second_section = 0.75 * fields + 0.25 * (
            first_section + time_step * evaluate(first_section, rotation)
        )
        third_section = fields / 3.0 + 2.0 / 3.0 * (
            second_section + time_step * evaluate(second_section, rotation)
        )
        ghost_cells = 0
        shifted = fargo_local(third_section, shifts, ghost_cells)
        fields = shifted
    return (fields[0], fields[1:3], fields[3:5])


def solution(mesh):
    placed = (
        P(None, "phi", "row"),
        P(None, None, "phi", "row"),
        P(None, None, "phi", "row"),
        P("row"),
        P("row"),
    )
    return jax.shard_map(
        body,
        mesh=mesh,
        in_specs=placed,
        out_specs=(P(None, "phi", "row"), P(None, None, "phi", "row"), P(None, None, "phi", "row")),
        check_vma=False,
    )
```

profile of v0, /device:TPU:1, one launch (start us, length us, event | category | flops | bytes accessed | tf_op | source)
XLA Modules:
  0.0 93.5 jit_solution(11204290081159260210)
XLA Ops:
  0.7 1.1 %pad_maximum_fusion.12 = f32[5,2,32,256]{3,2,1,0:T(8,128)S(1)} fusion(f32[2,2,32,256]{3,2,1,0:T(8,128)} %param.7, f32[2,2,32,256]{3,2,1,0:T(8,128)} %param.6, f32[1,2,32,256]{3,2,1,0:T(8,128)} %bitcast.27), kind=kLoop, calls=%fused_computation.160 | loop fusion | flops 163840 | bytes 655360 | tf_op jit(solution)/shard_map/concatenate | solution.py:175
  1.9 2.1 %collective-permute-start.2 = (f32[5,2,32,2]{3,2,1,0:T(8,128)S(1)}, f32[5,2,32,2]{3,2,1,0:T(8,128)S(1)}, u32[]{:S(2)}, u32[]{:S(2)}) collective-permute-start(f32[5,2,32,2]{3,2,1,0:T(8,128)S(1)} %slice_select_fusion.17), channel_id=1, source_target_pairs={{0,1},{1,0},{2,3},{3,2},{4,5},{5,4},{6,7},{7,6},{8,9},{9,8},{10,11... | collective-permute-start | bytes 7688 | tf_op jit(solution)/shard_map/ppermute | solution.py:32
  4.0 1.0 %collective-permute-start.1 = (f32[5,2,2,256]{3,2,1,0:T(2,128)S(1)}, f32[5,2,2,256]{3,2,1,0:T(2,128)S(1)}, u32[]{:S(2)}, u32[]{:S(2)}) collective-permute-start(f32[5,2,2,256]{3,2,1,0:T(2,128)S(1)} %get-tuple-element.112), channel_id=1, source_target_pairs={{2,0},{4,2},{6,4},{8,6},{10,8},{12,10},{14,12},{16,14},{18,16},{20... | collective-permute-start | bytes 61448 | tf_op jit(solution)/shard_map/ppermute | solution.py:24
  5.0 1.2 %collective-permute-start = (f32[5,2,2,256]{3,2,1,0:T(2,128)S(1)}, f32[5,2,2,256]{3,2,1,0:T(2,128)S(1)}, u32[]{:S(2)}, u32[]{:S(2)}) collective-permute-start(f32[5,2,2,256]{3,2,1,0:T(2,128)S(1)} %get-tuple-element.111), channel_id=1, source_target_pairs={{0,2},{2,4},{4,6},{6,8},{8,10},{10,12},{12,14},{14,16},{16,18},{18... | collective-permute-start | bytes 61448 | tf_op jit(solution)/shard_map/ppermute | solution.py:22
  6.6 1.3 %collective-permute-done.2 = f32[5,2,32,2]{3,2,1,0:T(8,128)S(1)} collective-permute-done((f32[5,2,32,2]{3,2,1,0:T(8,128)S(1)}, f32[5,2,32,2]{3,2,1,0:T(8,128)S(1)}, u32[]{:S(2)}, u32[]{:S(2)}) %collective-permute-start.2) | collective-permute-done | bytes 2592 | tf_op jit(solution)/shard_map/ppermute | solution.py:32
  11.6 1.2 %collective-permute-start.5 = (f32[5,2,32,2]{3,2,1,0:T(8,128)S(1)}, f32[5,2,32,2]{3,2,1,0:T(8,128)S(1)}, u32[]{:S(2)}, u32[]{:S(2)}) collective-permute-start(f32[5,2,32,2]{3,2,1,0:T(8,128)S(1)} %slice_select_fusion.16), channel_id=1, source_target_pairs={{0,1},{1,0},{2,3},{3,2},{4,5},{5,4},{6,7},{7,6},{8,9},{9,8},{10,11... | collective-permute-start | bytes 7688 | tf_op jit(solution)/shard_map/ppermute | solution.py:32
  12.8 4.0 %collective-permute-start.4 = (f32[5,2,2,256]{3,2,1,0:T(2,128)S(1)}, f32[5,2,2,256]{3,2,1,0:T(2,128)S(1)}, u32[]{:S(2)}, u32[]{:S(2)}) collective-permute-start(f32[5,2,2,256]{3,2,1,0:T(2,128)S(1)} %get-tuple-element.110), channel_id=1, source_target_pairs={{2,0},{4,2},{6,4},{8,6},{10,8},{12,10},{14,12},{16,14},{18,16},{20... | collective-permute-start | bytes 61448 | tf_op jit(solution)/shard_map/ppermute | solution.py:24
  20.6 1.3 %collective-permute-start.8 = (f32[5,2,32,2]{3,2,1,0:T(8,128)S(1)}, f32[5,2,32,2]{3,2,1,0:T(8,128)S(1)}, u32[]{:S(2)}, u32[]{:S(2)}) collective-permute-start(f32[5,2,32,2]{3,2,1,0:T(8,128)S(1)} %slice_select_fusion.15), channel_id=1, source_target_pairs={{0,1},{1,0},{2,3},{3,2},{4,5},{5,4},{6,7},{7,6},{8,9},{9,8},{10,11... | collective-permute-start | bytes 7688 | tf_op jit(solution)/shard_map/ppermute | solution.py:32
  21.9 4.8 %collective-permute-start.7 = (f32[5,2,2,256]{3,2,1,0:T(2,128)S(1)}, f32[5,2,2,256]{3,2,1,0:T(2,128)S(1)}, u32[]{:S(2)}, u32[]{:S(2)}) collective-permute-start(f32[5,2,2,256]{3,2,1,0:T(2,128)S(1)} %get-tuple-element.108), channel_id=1, source_target_pairs={{2,0},{4,2},{6,4},{8,6},{10,8},{12,10},{14,12},{16,14},{18,16},{20... | collective-permute-start | bytes 61448 | tf_op jit(solution)/shard_map/ppermute | solution.py:24
  30.1 2.1 %collective-permute-start.10 = (f32[5,2,32,256]{3,2,1,0:T(8,128)S(1)}, f32[5,2,32,256]{3,2,1,0:T(8,128)S(1)}, u32[]{:S(2)}, u32[]{:S(2)}) collective-permute-start(f32[5,2,32,256]{3,2,1,0:T(8,128)S(1)} %fusion.48), channel_id=1, source_target_pairs={{30,0},{0,2},{2,4},{4,6},{6,8},{8,10},{10,12},{12,14},{14,16},{16,... | collective-permute-start | bytes 983048 | tf_op jit(solution)/shard_map/ppermute | solution.py:38
  32.2 1.5 %collective-permute-start.9 = (f32[5,2,24,256]{3,2,1,0:T(8,128)S(1)}, f32[5,2,24,256]{3,2,1,0:T(8,128)S(1)}, u32[]{:S(2)}, u32[]{:S(2)}) collective-permute-start(f32[5,2,24,256]{3,2,1,0:T(8,128)S(1)} %slice.1519), channel_id=1, source_target_pairs={{28,0},{30,2},{0,4},{2,6},{4,8},{6,10},{8,12},{10,14},{12,16},{14,... | collective-permute-start | bytes 737288 | tf_op jit(solution)/shard_map/ppermute | solution.py:38
  33.7 14.3 %collective-permute-done.9 = f32[5,2,24,256]{3,2,1,0:T(8,128)S(1)} collective-permute-done((f32[5,2,24,256]{3,2,1,0:T(8,128)S(1)}, f32[5,2,24,256]{3,2,1,0:T(8,128)S(1)}, u32[]{:S(2)}, u32[]{:S(2)}) %collective-permute-start.9) | collective-permute-done | bytes 245792 | tf_op jit(solution)/shard_map/ppermute | solution.py:38
  49.6 0.9 collective-permute-start.13
  50.6 1.7 %collective-permute-start.11 = (f32[5,2,2,256]{3,2,1,0:T(2,128)S(1)}, f32[5,2,2,256]{3,2,1,0:T(2,128)S(1)}, u32[]{:S(2)}, u32[]{:S(2)}) collective-permute-start(f32[5,2,2,256]{3,2,1,0:T(2,128)S(1)} %get-tuple-element.57), channel_id=1, source_target_pairs={{0,2},{2,4},{4,6},{6,8},{8,10},{10,12},{12,14},{14,16},{16,18},{18... | collective-permute-start | bytes 61448 | tf_op jit(solution)/shard_map/ppermute | solution.py:22
  52.4 1.7 %collective-permute-done.13 = f32[5,2,32,2]{3,2,1,0:T(8,128)S(1)} collective-permute-done((f32[5,2,32,2]{3,2,1,0:T(8,128)S(1)}, f32[5,2,32,2]{3,2,1,0:T(8,128)S(1)}, u32[]{:S(2)}, u32[]{:S(2)}) %collective-permute-start.13) | collective-permute-done | bytes 2592 | tf_op jit(solution)/shard_map/ppermute | solution.py:32
  57.8 0.9 collective-permute-start.16
  59.0 1.5 %collective-permute-start.14 = (f32[5,2,2,256]{3,2,1,0:T(2,128)S(1)}, f32[5,2,2,256]{3,2,1,0:T(2,128)S(1)}, u32[]{:S(2)}, u32[]{:S(2)}) collective-permute-start(f32[5,2,2,256]{3,2,1,0:T(2,128)S(1)} %get-tuple-element.105), channel_id=1, source_target_pairs={{0,2},{2,4},{4,6},{6,8},{8,10},{10,12},{12,14},{14,16},{16,18},{18... | collective-permute-start | bytes 61448 | tf_op jit(solution)/shard_map/ppermute | solution.py:22
  60.5 2.9 %collective-permute-done.16 = f32[5,2,32,2]{3,2,1,0:T(8,128)S(1)} collective-permute-done((f32[5,2,32,2]{3,2,1,0:T(8,128)S(1)}, f32[5,2,32,2]{3,2,1,0:T(8,128)S(1)}, u32[]{:S(2)}, u32[]{:S(2)}) %collective-permute-start.16) | collective-permute-done | bytes 2592 | tf_op jit(solution)/shard_map/ppermute | solution.py:32
  67.2 1.2 %collective-permute-start.19 = (f32[5,2,32,2]{3,2,1,0:T(8,128)S(1)}, f32[5,2,32,2]{3,2,1,0:T(8,128)S(1)}, u32[]{:S(2)}, u32[]{:S(2)}) collective-permute-start(f32[5,2,32,2]{3,2,1,0:T(8,128)S(1)} %slice_select_fusion.12), channel_id=1, source_target_pairs={{0,1},{1,0},{2,3},{3,2},{4,5},{5,4},{6,7},{7,6},{8,9},{9,8},{10,11... | collective-permute-start | bytes 7688 | tf_op jit(solution)/shard_map/ppermute | solution.py:32
  68.5 1.1 %collective-permute-start.18 = (f32[5,2,2,256]{3,2,1,0:T(2,128)S(1)}, f32[5,2,2,256]{3,2,1,0:T(2,128)S(1)}, u32[]{:S(2)}, u32[]{:S(2)}) collective-permute-start(f32[5,2,2,256]{3,2,1,0:T(2,128)S(1)} %get-tuple-element.104), channel_id=1, source_target_pairs={{2,0},{4,2},{6,4},{8,6},{10,8},{12,10},{14,12},{16,14},{18,16},{20... | collective-permute-start | bytes 61448 | tf_op jit(solution)/shard_map/ppermute | solution.py:24
  69.5 0.7 collective-permute-start.17
  70.2 1.7 %collective-permute-done.19 = f32[5,2,32,2]{3,2,1,0:T(8,128)S(1)} collective-permute-done((f32[5,2,32,2]{3,2,1,0:T(8,128)S(1)}, f32[5,2,32,2]{3,2,1,0:T(8,128)S(1)}, u32[]{:S(2)}, u32[]{:S(2)}) %collective-permute-start.19) | collective-permute-done | bytes 2592 | tf_op jit(solution)/shard_map/ppermute | solution.py:32
  75.4 15.7 %collective-permute-done.20 = f32[5,2,24,256]{3,2,1,0:T(8,128)S(1)} collective-permute-done((f32[5,2,24,256]{3,2,1,0:T(8,128)S(1)}, f32[5,2,24,256]{3,2,1,0:T(8,128)S(1)}, u32[]{:S(2)}, u32[]{:S(2)}) %collective-permute-start.20) | collective-permute-done | bytes 245792 | tf_op jit(solution)/shard_map/ppermute | solution.py:38
  92.8 0.7 fusion.62
  (268 shorter events, 24.6 us)
Async XLA Ops:
  0.6 5.9 %copy-start.1 = (f32[2,2,32,256]{3,2,1,0:T(8,128)S(1)}, f32[2,2,32,256]{3,2,1,0:T(8,128)}, u32[]{:S(2)}) copy-start(f32[2,2,32,256]{3,2,1,0:T(8,128)} %param.7) | copy-start | bytes 393220
  0.7 7.4 %copy-start.2 = (f32[2,32,256]{2,1,0:T(8,128)S(1)}, f32[2,32,256]{2,1,0:T(8,128)}, u32[]{:S(2)}) copy-start(f32[2,32,256]{2,1,0:T(8,128)} %param.5) | copy-start | bytes 196612
  1.9 6.0 %collective-permute-start.2 = (f32[5,2,32,2]{3,2,1,0:T(8,128)S(1)}, f32[5,2,32,2]{3,2,1,0:T(8,128)S(1)}, u32[]{:S(2)}, u32[]{:S(2)}) collective-permute-start(f32[5,2,32,2]{3,2,1,0:T(8,128)S(1)} %slice_select_fusion.17), channel_id=1, source_target_pairs={{0,1},{1,0},{2,3},{3,2},{4,5},{5,4},{6,7},{7,6},{8,9},{9,8},{10,11... | collective-permute-start | bytes 7688 | tf_op jit(solution)/shard_map/ppermute | solution.py:32
  4.0 6.0 %collective-permute-start.1 = (f32[5,2,2,256]{3,2,1,0:T(2,128)S(1)}, f32[5,2,2,256]{3,2,1,0:T(2,128)S(1)}, u32[]{:S(2)}, u32[]{:S(2)}) collective-permute-start(f32[5,2,2,256]{3,2,1,0:T(2,128)S(1)} %get-tuple-element.112), channel_id=1, source_target_pairs={{2,0},{4,2},{6,4},{8,6},{10,8},{12,10},{14,12},{16,14},{18,16},{20... | collective-permute-start | bytes 61448 | tf_op jit(solution)/shard_map/ppermute | solution.py:24
  5.0 5.0 %collective-permute-start = (f32[5,2,2,256]{3,2,1,0:T(2,128)S(1)}, f32[5,2,2,256]{3,2,1,0:T(2,128)S(1)}, u32[]{:S(2)}, u32[]{:S(2)}) collective-permute-start(f32[5,2,2,256]{3,2,1,0:T(2,128)S(1)} %get-tuple-element.111), channel_id=1, source_target_pairs={{0,2},{2,4},{4,6},{6,8},{8,10},{10,12},{12,14},{14,16},{16,18},{18... | collective-permute-start | bytes 61448 | tf_op jit(solution)/shard_map/ppermute | solution.py:22
  11.6 5.2 %collective-permute-start.5 = (f32[5,2,32,2]{3,2,1,0:T(8,128)S(1)}, f32[5,2,32,2]{3,2,1,0:T(8,128)S(1)}, u32[]{:S(2)}, u32[]{:S(2)}) collective-permute-start(f32[5,2,32,2]{3,2,1,0:T(8,128)S(1)} %slice_select_fusion.16), channel_id=1, source_target_pairs={{0,1},{1,0},{2,3},{3,2},{4,5},{5,4},{6,7},{7,6},{8,9},{9,8},{10,11... | collective-permute-start | bytes 7688 | tf_op jit(solution)/shard_map/ppermute | solution.py:32
  12.8 6.1 %collective-permute-start.4 = (f32[5,2,2,256]{3,2,1,0:T(2,128)S(1)}, f32[5,2,2,256]{3,2,1,0:T(2,128)S(1)}, u32[]{:S(2)}, u32[]{:S(2)}) collective-permute-start(f32[5,2,2,256]{3,2,1,0:T(2,128)S(1)} %get-tuple-element.110), channel_id=1, source_target_pairs={{2,0},{4,2},{6,4},{8,6},{10,8},{12,10},{14,12},{16,14},{18,16},{20... | collective-permute-start | bytes 61448 | tf_op jit(solution)/shard_map/ppermute | solution.py:24
  16.8 2.1 %collective-permute-start.3 = (f32[5,2,2,256]{3,2,1,0:T(2,128)S(1)}, f32[5,2,2,256]{3,2,1,0:T(2,128)S(1)}, u32[]{:S(2)}, u32[]{:S(2)}) collective-permute-start(f32[5,2,2,256]{3,2,1,0:T(2,128)S(1)} %get-tuple-element.109), channel_id=1, source_target_pairs={{0,2},{2,4},{4,6},{6,8},{8,10},{10,12},{12,14},{14,16},{16,18},{18... | collective-permute-start | bytes 61448 | tf_op jit(solution)/shard_map/ppermute | solution.py:22
  20.6 6.1 %collective-permute-start.8 = (f32[5,2,32,2]{3,2,1,0:T(8,128)S(1)}, f32[5,2,32,2]{3,2,1,0:T(8,128)S(1)}, u32[]{:S(2)}, u32[]{:S(2)}) collective-permute-start(f32[5,2,32,2]{3,2,1,0:T(8,128)S(1)} %slice_select_fusion.15), channel_id=1, source_target_pairs={{0,1},{1,0},{2,3},{3,2},{4,5},{5,4},{6,7},{7,6},{8,9},{9,8},{10,11... | collective-permute-start | bytes 7688 | tf_op jit(solution)/shard_map/ppermute | solution.py:32
  21.9 6.9 %collective-permute-start.7 = (f32[5,2,2,256]{3,2,1,0:T(2,128)S(1)}, f32[5,2,2,256]{3,2,1,0:T(2,128)S(1)}, u32[]{:S(2)}, u32[]{:S(2)}) collective-permute-start(f32[5,2,2,256]{3,2,1,0:T(2,128)S(1)} %get-tuple-element.108), channel_id=1, source_target_pairs={{2,0},{4,2},{6,4},{8,6},{10,8},{12,10},{14,12},{16,14},{18,16},{20... | collective-permute-start | bytes 61448 | tf_op jit(solution)/shard_map/ppermute | solution.py:24
  26.7 2.1 %collective-permute-start.6 = (f32[5,2,2,256]{3,2,1,0:T(2,128)S(1)}, f32[5,2,2,256]{3,2,1,0:T(2,128)S(1)}, u32[]{:S(2)}, u32[]{:S(2)}) collective-permute-start(f32[5,2,2,256]{3,2,1,0:T(2,128)S(1)} %get-tuple-element.107), channel_id=1, source_target_pairs={{0,2},{2,4},{4,6},{6,8},{8,10},{10,12},{12,14},{14,16},{16,18},{18... | collective-permute-start | bytes 61448 | tf_op jit(solution)/shard_map/ppermute | solution.py:22
  30.1 18.0 %collective-permute-start.10 = (f32[5,2,32,256]{3,2,1,0:T(8,128)S(1)}, f32[5,2,32,256]{3,2,1,0:T(8,128)S(1)}, u32[]{:S(2)}, u32[]{:S(2)}) collective-permute-start(f32[5,2,32,256]{3,2,1,0:T(8,128)S(1)} %fusion.48), channel_id=1, source_target_pairs={{30,0},{0,2},{2,4},{4,6},{6,8},{8,10},{10,12},{12,14},{14,16},{16,... | collective-permute-start | bytes 983048 | tf_op jit(solution)/shard_map/ppermute | solution.py:38
  32.2 15.9 %collective-permute-start.9 = (f32[5,2,24,256]{3,2,1,0:T(8,128)S(1)}, f32[5,2,24,256]{3,2,1,0:T(8,128)S(1)}, u32[]{:S(2)}, u32[]{:S(2)}) collective-permute-start(f32[5,2,24,256]{3,2,1,0:T(8,128)S(1)} %slice.1519), channel_id=1, source_target_pairs={{28,0},{30,2},{0,4},{2,6},{4,8},{6,10},{8,12},{10,14},{12,16},{14,... | collective-permute-start | bytes 737288 | tf_op jit(solution)/shard_map/ppermute | solution.py:38
  49.6 4.5 %collective-permute-start.13 = (f32[5,2,32,2]{3,2,1,0:T(8,128)S(1)}, f32[5,2,32,2]{3,2,1,0:T(8,128)S(1)}, u32[]{:S(2)}, u32[]{:S(2)}) collective-permute-start(f32[5,2,32,2]{3,2,1,0:T(8,128)S(1)} %slice_select_fusion.14), channel_id=1, source_target_pairs={{0,1},{1,0},{2,3},{3,2},{4,5},{5,4},{6,7},{7,6},{8,9},{9,8},{10,11... | collective-permute-start | bytes 7688 | tf_op jit(solution)/shard_map/ppermute | solution.py:32
  50.6 5.6 %collective-permute-start.12 = (f32[5,2,2,256]{3,2,1,0:T(2,128)S(1)}, f32[5,2,2,256]{3,2,1,0:T(2,128)S(1)}, u32[]{:S(2)}, u32[]{:S(2)}) collective-permute-start(f32[5,2,2,256]{3,2,1,0:T(2,128)S(1)} %get-tuple-element.58), channel_id=1, source_target_pairs={{2,0},{4,2},{6,4},{8,6},{10,8},{12,10},{14,12},{16,14},{18,16},{20... | collective-permute-start | bytes 61448 | tf_op jit(solution)/shard_map/ppermute | solution.py:24
  50.6 5.6 %collective-permute-start.11 = (f32[5,2,2,256]{3,2,1,0:T(2,128)S(1)}, f32[5,2,2,256]{3,2,1,0:T(2,128)S(1)}, u32[]{:S(2)}, u32[]{:S(2)}) collective-permute-start(f32[5,2,2,256]{3,2,1,0:T(2,128)S(1)} %get-tuple-element.57), channel_id=1, source_target_pairs={{0,2},{2,4},{4,6},{6,8},{8,10},{10,12},{12,14},{14,16},{16,18},{18... | collective-permute-start | bytes 61448 | tf_op jit(solution)/shard_map/ppermute | solution.py:22
  57.8 5.6 %collective-permute-start.16 = (f32[5,2,32,2]{3,2,1,0:T(8,128)S(1)}, f32[5,2,32,2]{3,2,1,0:T(8,128)S(1)}, u32[]{:S(2)}, u32[]{:S(2)}) collective-permute-start(f32[5,2,32,2]{3,2,1,0:T(8,128)S(1)} %slice_select_fusion.13), channel_id=1, source_target_pairs={{0,1},{1,0},{2,3},{3,2},{4,5},{5,4},{6,7},{7,6},{8,9},{9,8},{10,11... | collective-permute-start | bytes 7688 | tf_op jit(solution)/shard_map/ppermute | solution.py:32
  58.8 6.8 %collective-permute-start.15 = (f32[5,2,2,256]{3,2,1,0:T(2,128)S(1)}, f32[5,2,2,256]{3,2,1,0:T(2,128)S(1)}, u32[]{:S(2)}, u32[]{:S(2)}) collective-permute-start(f32[5,2,2,256]{3,2,1,0:T(2,128)S(1)} %get-tuple-element.106), channel_id=1, source_target_pairs={{2,0},{4,2},{6,4},{8,6},{10,8},{12,10},{14,12},{16,14},{18,16},{20... | collective-permute-start | bytes 61448 | tf_op jit(solution)/shard_map/ppermute | solution.py:24
  59.0 6.5 %collective-permute-start.14 = (f32[5,2,2,256]{3,2,1,0:T(2,128)S(1)}, f32[5,2,2,256]{3,2,1,0:T(2,128)S(1)}, u32[]{:S(2)}, u32[]{:S(2)}) collective-permute-start(f32[5,2,2,256]{3,2,1,0:T(2,128)S(1)} %get-tuple-element.105), channel_id=1, source_target_pairs={{0,2},{2,4},{4,6},{6,8},{8,10},{10,12},{12,14},{14,16},{16,18},{18... | collective-permute-start | bytes 61448 | tf_op jit(solution)/shard_map/ppermute | solution.py:22
  67.2 4.7 %collective-permute-start.19 = (f32[5,2,32,2]{3,2,1,0:T(8,128)S(1)}, f32[5,2,32,2]{3,2,1,0:T(8,128)S(1)}, u32[]{:S(2)}, u32[]{:S(2)}) collective-permute-start(f32[5,2,32,2]{3,2,1,0:T(8,128)S(1)} %slice_select_fusion.12), channel_id=1, source_target_pairs={{0,1},{1,0},{2,3},{3,2},{4,5},{5,4},{6,7},{7,6},{8,9},{9,8},{10,11... | collective-permute-start | bytes 7688 | tf_op jit(solution)/shard_map/ppermute | solution.py:32
  68.5 5.5 %collective-permute-start.18 = (f32[5,2,2,256]{3,2,1,0:T(2,128)S(1)}, f32[5,2,2,256]{3,2,1,0:T(2,128)S(1)}, u32[]{:S(2)}, u32[]{:S(2)}) collective-permute-start(f32[5,2,2,256]{3,2,1,0:T(2,128)S(1)} %get-tuple-element.104), channel_id=1, source_target_pairs={{2,0},{4,2},{6,4},{8,6},{10,8},{12,10},{14,12},{16,14},{18,16},{20... | collective-permute-start | bytes 61448 | tf_op jit(solution)/shard_map/ppermute | solution.py:24
  69.5 4.5 %collective-permute-start.17 = (f32[5,2,2,256]{3,2,1,0:T(2,128)S(1)}, f32[5,2,2,256]{3,2,1,0:T(2,128)S(1)}, u32[]{:S(2)}, u32[]{:S(2)}) collective-permute-start(f32[5,2,2,256]{3,2,1,0:T(2,128)S(1)} %get-tuple-element.103), channel_id=1, source_target_pairs={{0,2},{2,4},{4,6},{6,8},{8,10},{10,12},{12,14},{14,16},{16,18},{18... | collective-permute-start | bytes 61448 | tf_op jit(solution)/shard_map/ppermute | solution.py:22
  75.2 15.8 %collective-permute-start.21 = (f32[5,2,32,256]{3,2,1,0:T(8,128)S(1)}, f32[5,2,32,256]{3,2,1,0:T(8,128)S(1)}, u32[]{:S(2)}, u32[]{:S(2)}) collective-permute-start(f32[5,2,32,256]{3,2,1,0:T(8,128)S(1)} %fusion.29), channel_id=1, source_target_pairs={{30,0},{0,2},{2,4},{4,6},{6,8},{8,10},{10,12},{12,14},{14,16},{16,... | collective-permute-start | bytes 983048 | tf_op jit(solution)/shard_map/ppermute | solution.py:38
  75.3 15.7 %collective-permute-start.20 = (f32[5,2,24,256]{3,2,1,0:T(8,128)S(1)}, f32[5,2,24,256]{3,2,1,0:T(8,128)S(1)}, u32[]{:S(2)}, u32[]{:S(2)}) collective-permute-start(f32[5,2,24,256]{3,2,1,0:T(8,128)S(1)} %slice.1674), channel_id=1, source_target_pairs={{28,0},{30,2},{0,4},{2,6},{4,8},{6,10},{8,12},{10,14},{12,16},{14,... | collective-permute-start | bytes 737288 | tf_op jit(solution)/shard_map/ppermute | solution.py:38
  (3 other events, 15.6 us)
where the time goes:
time: 93.7 us; the launch traced here: 93.5 us
  waiting for transfers between devices  37.7 us (40%)
  starting transfers between devices  27.7 us (30%)
  other arithmetic  22.6 us (24%)
  local copies, waits for them, and re-layouts  3.26 us (3%)
  between operations  2.31 us (2%)
    ppermute x4, waiting for transfers between devices, passed_along(): return lax.ppermute(block, axis, route)  30 us
    ppermute x6, starting transfers between devices, padded(): lax.ppermute(head, axis, [((i + 1) % count, i) for i in range(count)])  11.2 us
    ppermute x6, starting transfers between devices, from_partner(): lax.ppermute(x, axis, [(i, i ^ 1 << stride) for i in range(lax.axis_size(...  7.68 us
    ppermute x6, waiting for transfers between devices, from_partner(): lax.ppermute(x, axis, [(i, i ^ 1 << stride) for i in range(lax.axis_size(...  7.67 us
    ppermute x6, starting transfers between devices, padded(): lax.ppermute(tail, axis, [(i, (i + 1) % count) for i in range(count)])  5.09 us
    sub x12, other arithmetic, interfaces(): right_state = window(centres - 0.5 * slopes, 1, 0, along_axis)  4.77 us
    unnamed x77, other arithmetic  4.44 us
    ppermute x4, starting transfers between devices, passed_along(): return lax.ppermute(block, axis, route)  3.66 us
  transfers between devices with their start and end apart: 22, of which 6 were waited for; matrix products, arithmetic and copies ran while one was open for 13% of the time, Pallas kernels for 0%

commit v1 on v0

v1 whole, which is shorter than its diff:
```python
import functools

import jax
import jax.numpy as jnp
from jax import lax
from jax.experimental import pallas as pl
from jax.experimental.pallas import tpu as pltpu
from jax.sharding import PartitionSpec as P

STEPS = 2
SMIN = 8
SMAX = 56
STAGES = 3
REACH = 2 * STAGES
LANES = 128
SUB = 8
HALF = LANES // 2
SLOTS = 2 * SUB
CHUNK = 4
VMEM_LIMIT = 32 * 1024 * 1024

time_step = 0.08
sound_sq = 1.0


def shift_bound(first_row, rows):
    d = rows - 1 - first_row
    return min(SMIN + (SMAX - SMIN - 1) * d * d // ((rows - 1) * (rows - 1)) + 1, SMAX)


def minmod(lower, upper):
    return jnp.maximum(jnp.minimum(lower, 0.0), jnp.minimum(upper, jnp.maximum(lower, 0.0)))


def physical(state):
    rho, mn, mt, bn, bt = state
    inverse = 1.0 / rho
    vn = mn * inverse
    vt = mt * inverse
    bn_sq = bn * bn
    bt_sq = bt * bt
    flux_n = mn * vn + (sound_sq * rho + 0.5 * (bt_sq - bn_sq))
    flux_t = mt * vn - bn * bt
    flux_b = bt * vn - bn * vt
    inside = sound_sq + (bn_sq + bt_sq) * inverse
    speed = jnp.abs(vn) + inside * lax.rsqrt(inside)
    return (mn, flux_n, flux_t, None, flux_b), speed


def face_twice(left, right):
    left_flux, left_speed = physical(left)
    right_flux, right_speed = physical(right)
    bound = jnp.maximum(left_speed, right_speed)
    out = []
    for k in range(5):
        jump = bound * (right[k] - left[k])
        if left_flux[k] is None:
            out.append(-jump)
        else:
            out.append((left_flux[k] + right_flux[k]) - jump)
    return out


def swapped(five):
    return [five[0], five[2], five[1], five[4], five[3]]


def run_stage(start, src, dst, spin, lo, hi, keep, weight, edges):
    half_dt = 0.5 * time_step
    low_mask, high_mask, first, last = edges
    for f in range(5):
        row = lambda i: pl.ds(i * SUB, SUB)
        inner = src[f, row(first), :]
        outer = src[f, row(last), :]
        for k in (1, 2):
            src[f, row(first - k), :] = jnp.where(low_mask, inner, src[f, row(first - k), :])
            src[f, row(last + k), :] = jnp.where(high_mask, outer, src[f, row(last + k), :])

    def load(ref, f, i):
        if isinstance(i, int):
            return ref[f, i * SUB : (i + 1) * SUB, :]
        return ref[f, pl.ds(pl.multiple_of(i * SUB, SUB), SUB), :]

    def radial_states(rows):
        halves = [[0.5 * x for x in r] for r in rows]
        jumps = [[b - a for a, b in zip(p, q)] for p, q in zip(halves[:-1], halves[1:])]
        slopes = [[minmod(a, b) for a, b in zip(p, q)] for p, q in zip(jumps[:-1], jumps[1:])]
        upper = [[x + s for x, s in zip(r, sl)] for r, sl in zip(rows[1:-1], slopes)]
        lower = [[x - s for x, s in zip(r, sl)] for r, sl in zip(rows[1:-1], slopes)]
        return lower, upper

    def radial_faces(rows):
        lower, upper = radial_states(rows)
        return [
            swapped(face_twice(swapped(u), swapped(l))) for u, l in zip(upper[:-1], lower[1:])
        ]

    def azimuth_change(fields):
        right_of = lambda x: pltpu.roll(x, LANES - 1, 1)
        left_of = lambda x: pltpu.roll(x, 1, 1)
        lower = []
        upper = []
        for x in fields:
            half = 0.5 * x
            jump = right_of(half) - half
            slope = minmod(left_of(jump), jump)
            upper.append(x + slope)
            lower.append(right_of(x - slope))
        faces = face_twice(upper, lower)
        return [x - left_of(x) for x in faces]

    def work(i0, count, before):
        rows = [[load(src, f, i0 + k) for f in range(5)] for k in range(-1, count + 2)]
        faces = [before] + radial_faces(rows)
        for k in range(count):
            fields = rows[k + 1]
            change = azimuth_change(fields)
            i = i0 + k
            turn = load(spin, 0, i)
            source = [
                None,
                (-0.5 * turn) * fields[2],
                (2.0 * turn) * fields[1],
                (-1.5 * turn) * fields[4],
                None,
            ]
            for f in range(5):
                new = fields[f] - half_dt * (change[f] + (faces[k + 1][f] - faces[k][f]))
                if source[f] is not None:
                    new = new + source[f]
                if weight != 1.0:
                    new = weight * new + keep * load(start, f, i)
                if isinstance(i, int):
                    dst[f, i * SUB : (i + 1) * SUB, :] = new
                else:
                    dst[f, pl.ds(pl.multiple_of(i * SUB, SUB), SUB), :] = new
        return faces[-1]

    before = radial_faces([[load(src, f, lo + k) for f in range(5)] for k in range(-2, 2)])[0]
    if CHUNK >= hi - lo:
        work(lo, hi - lo, before)
    else:

        def step(c, carried):
            return tuple(work(lo + c * CHUNK, CHUNK, list(carried)))

        lax.fori_loop(0, (hi - lo) // CHUNK, step, tuple(before))


def step_kernel(
    plan, place, own, near, far, side, corner, spin_rows, shift_rows, out, far_out, edge_out, cells, a, b, c, spin, extra
):
    n, radius, own_cells, total, row_count, spare = plan
    row = place[0]
    lane = lax.broadcasted_iota(jnp.int32, (SUB, LANES), 1)
    sublane = lax.broadcasted_iota(jnp.int32, (SUB, LANES), 0)

    def bound_of(slot):
        d = (total - 1) - (row * radius + n * slot)
        smooth = lax.div((SMAX - SMIN - 1) * d * d, jnp.int32((total - 1) * (total - 1)))
        return jnp.minimum(SMIN + smooth + 1, SMAX)

    bounds = [bound_of(k) for k in range(SLOTS)]
    tall = n + 2 * SUB
    front = lax.broadcasted_iota(jnp.int32, (tall, LANES), 1) < HALF
    narrow = lax.broadcasted_iota(jnp.int32, (n, LANES), 1) < HALF

    for f in range(5):
        for part in range(radius // LANES):
            columns = slice(part * LANES, (part + 1) * LANES)
            if part == 0:
                top = far[f, 0:own_cells, :]
            else:
                rest = far[f, 0:SUB, :]
                top = jnp.concatenate(
                    [
                        jnp.zeros((own_cells - 2 * SUB, LANES), jnp.float32),
                        pltpu.roll(rest, SUB - spare, 0),
                        far[f, own_cells : own_cells + SUB, :],
                    ],
                    axis=0,
                )
            block = jnp.concatenate(
                [top, near[f, :, columns], own[f, :, columns], jnp.zeros((own_cells, LANES), jnp.float32)], axis=0
            )
            cells[f, SUB + part * LANES : SUB + (part + 1) * LANES, :] = block.T
        beside = jnp.where(
            lane < 2 * own_cells, pltpu.roll(corner[f], own_cells, 1), pltpu.roll(side[f], 2 * own_cells, 1)
        )
        cells[f, 0:SUB, :] = pltpu.roll(beside, SUB - REACH, 0)
        cells[f, SUB + radius : 2 * SUB + radius, :] = beside

    for j in range(SUB):
        low, high = j, SUB + j
        at = [slice(SUB - REACH + n * k, SUB - REACH + n * k + tall) for k in (low, high)]
        turn_low = (LANES - (2 * own_cells - REACH)) + bounds[low]
        turn_high = (HALF - (2 * own_cells - REACH)) + bounds[high]
        for f in range(5):
            a[f, pl.ds(j, tall, stride=SUB), :] = jnp.where(
                front, pltpu.roll(cells[f, at[0], :], turn_low, 1), pltpu.roll(cells[f, at[1], :], turn_high, 1)
            )
        spin[0, pl.ds(j, tall, stride=SUB), :] = jnp.where(front, spin_rows[at[0], :], spin_rows[at[1], :])
        extra[pl.ds(j, n, stride=SUB), :] = jnp.where(
            narrow,
            bounds[low] - shift_rows[n * low : n * low + n, :],
            bounds[high] - shift_rows[n * high : n * high + n, :],
        )

    first, last = REACH, REACH + n - 1
    edges = (
        (sublane == 0) & (lane < HALF) & (row == 0),
        (sublane == SUB - 1) & (lane >= HALF) & (row == row_count - 1),
        first,
        last,
    )
    run_stage(a, a, b, spin, 2, n + 10, 0.0, 1.0, edges)
    run_stage(a, b, c, spin, 4, n + 8, 0.75, 0.25, edges)
    run_stage(a, c, b, spin, 6, n + 6, 1.0 / 3.0, 2.0 / 3.0, edges)

    for i in range(n):
        more = extra[i * SUB : (i + 1) * SUB, :]
        picks = [((more >> bit) & 1) == 1 for bit in range(3)]
        for f in range(5):
            x = pltpu.roll(b[f, (REACH + i) * SUB : (REACH + i + 1) * SUB, :], LANES - REACH, 1)
            for bit in range(3):
                x = jnp.where(picks[bit], pltpu.roll(x, LANES - (1 << bit), 1), x)
            a[f, i * SUB : (i + 1) * SUB, :] = x
    for f in range(5):
        block = jnp.concatenate([a[f, pl.ds(j, n, stride=SUB), :] for j in range(SUB)], axis=0)
        turned = block.T
        low, high = turned[0:own_cells], turned[HALF : HALF + own_cells]
        out[f, :, 0:LANES] = low
        out[f, :, LANES : 2 * LANES] = high
        if far_out is not None:
            far_out[f, 0:own_cells, :] = low
            far_out[f, 0:SUB, :] = jnp.where(
                sublane < spare, pltpu.roll(high[own_cells - 2 * SUB : own_cells - SUB], spare, 0), low[0:SUB]
            )
            far_out[f, own_cells : own_cells + SUB, :] = high[own_cells - SUB : own_cells]
            final_rows = pltpu.roll(pltpu.roll(block[LANES - SUB : LANES], REACH, 0), HALF, 1)
            edge_out[f] = jnp.where(row == 0, final_rows, block[0:SUB])


def step_call(plan, operands, more):
    n, radius, own_cells, total, row_count, spare = plan
    shape = lambda *s: jax.ShapeDtypeStruct(s, jnp.float32)
    out_shape = [shape(5, own_cells, radius)]
    if more:
        out_shape += [shape(5, own_cells + SUB, LANES), shape(5, SUB, LANES)]

    def kernel(*refs):
        ins, rest = refs[:8], refs[8:]
        if more:
            outs, scratch = rest[:3], rest[3:]
        else:
            outs, scratch = (rest[0], None, None), rest[1:]
        step_kernel(plan, *ins, *outs, *scratch)

    stage = pltpu.VMEM((5, (n + 2 * SUB) * SUB, LANES), jnp.float32)
    vmem = pl.BlockSpec(memory_space=pltpu.VMEM)
    return pl.pallas_call(
        kernel,
        out_shape=out_shape,
        in_specs=[pl.BlockSpec(memory_space=pltpu.SMEM)] + [vmem] * 7,
        out_specs=[vmem] * len(out_shape),
        scratch_shapes=[
            pltpu.VMEM((5, radius + 3 * SUB, LANES), jnp.float32),
            stage,
            stage,
            stage,
            pltpu.VMEM((1, (n + 2 * SUB) * SUB, LANES), jnp.float32),
            pltpu.VMEM((n * SUB, LANES), jnp.int32),
        ],
        compiler_params=pltpu.CompilerParams(vmem_limit_bytes=VMEM_LIMIT),
        cost_estimate=pl.CostEstimate(flops=20_000_000, bytes_accessed=600_000, transcendentals=0),
        name="disc_step",
    )(*operands)


def body(density, momentum, magnetic, rotation, shifts):
    phi_count = lax.axis_size("phi")
    row_count = lax.axis_size("row")
    levels, own_cells, radius = density.shape
    total = radius * row_count
    n = radius // SLOTS
    need = [max(shift_bound(part * LANES, total) + REACH - own_cells, 0) for part in range(radius // LANES)]
    spare = own_cells - need[0]
    assert row_count == 2 and radius == 2 * LANES and own_cells == HALF // 2
    assert 0 < need[0] < own_cells and need[1] <= SUB + spare and spare <= SUB
    plan = (n, radius, own_cells, total, row_count, spare)

    row = lax.axis_index("row")
    place = jnp.reshape(row, (1,)).astype(jnp.int32)
    here = lambda p, r: (p % phi_count) * row_count + r
    everyone = [(p, r) for p in range(phi_count) for r in range(row_count)]
    both = ("phi", "row")
    send_near = lambda x: lax.ppermute(x, "phi", [(p, (p + 1) % phi_count) for p in range(phi_count)])
    send_far = lambda x: lax.ppermute(x, both, [(here(p, 0), here(p + 2, 0)) for p in range(phi_count)])
    send_side = lambda x: lax.ppermute(x, "row", [(0, 1), (1, 0)])
    send_corner = lambda x: lax.ppermute(x, both, [(here(p, r), here(p + 1, 1 - r)) for p, r in everyone])

    edge_spin = jnp.where(row == 0, rotation[radius - REACH :], rotation[:REACH])
    beside_spin = lax.ppermute(edge_spin, "row", [(0, 1), (1, 0)])
    gap = jnp.zeros((SUB - REACH,), rotation.dtype)
    spins = jnp.concatenate([gap, beside_spin, rotation, beside_spin, gap, jnp.zeros((SUB,), rotation.dtype)])
    spin_rows = jnp.broadcast_to((time_step * spins)[:, None], (radius + 3 * SUB, LANES))
    shift_rows = jnp.broadcast_to(shifts[:, None], (radius, LANES))

    states = []
    for level in range(levels):
        fields = jnp.concatenate([density[level][None], momentum[:, level], magnetic[:, level]], axis=0)
        far = jnp.concatenate(
            [
                fields[:, own_cells - SUB - spare : own_cells - SUB, LANES:],
                fields[:, spare:, :LANES],
                fields[:, own_cells - SUB :, LANES:],
            ],
            axis=1,
        )
        edge = jnp.where(row == 0, fields[..., radius - REACH :], fields[..., :REACH])
        edge = jnp.swapaxes(edge, 1, 2)
        edge = jnp.pad(edge, ((0, 0), (0, SUB - REACH), (0, LANES - own_cells)))
        states.append((fields, far, edge))

    for step in range(STEPS):
        moved = [(own, send_near(own), send_far(far), send_side(edge), send_corner(edge)) for own, far, edge in states]
        more = step < STEPS - 1
        states = []
        for own, near, far, side, corner in moved:
            states.append(step_call(plan, (place, own, near, far, side, corner, spin_rows, shift_rows), more))
    fields = jnp.stack([s[0] for s in states], axis=1)
    return (fields[0], fields[1:3], fields[3:5])


def solution(mesh):
    placed = (
        P(None, "phi", "row"),
        P(None, None, "phi", "row"),
        P(None, None, "phi", "row"),
        P("row"),
        P("row"),
    )
    return jax.shard_map(
        body,
        mesh=mesh,
        in_specs=placed,
        out_specs=(P(None, "phi", "row"), P(None, None, "phi", "row"), P(None, None, "phi", "row")),
        check_vma=False,
    )
```

time: 93.7 us -> 90 us (0.961)
  the two profiles are of different devices: /device:TPU:1 before, /device:TPU:0 now
where the time goes in v1:
time: 90 us; the launch traced here: 89.2 us
  Pallas kernels  45.7 us (51%)
  starting transfers between devices  23.2 us (26%)
  waiting for transfers between devices  13.7 us (15%)
  local copies, waits for them, and re-layouts  4.71 us (5%)
  between operations  0.99 us (1%)
    pallas_call x4, Pallas kernels, step_call(): pl.pallas_call(kernel, out_shape=out_shape, in_specs=[pl.BlockSpec(memory...  45.7 us
    ppermute x4, starting transfers between devices, body(): lax.ppermute(x, both, [(here(p, 0), here(p + 2, 0)) for p in range(phi_co...  13.7 us
    ppermute x4, waiting for transfers between devices, body(): lax.ppermute(x, both, [(here(p, r), here(p + 1, 1 - r)) for p, r in every...  6.81 us
    ppermute x4, starting transfers between devices, body(): lax.ppermute(x, 'phi', [(p, (p + 1) % phi_count) for p in range(phi_count)])  6.25 us
    ppermute x4, waiting for transfers between devices, body(): send_side = lambda x: lax.ppermute(x, 'row', [(0, 1), (1, 0)])  3.78 us
    ppermute x1, waiting for transfers between devices, body(): beside_spin = lax.ppermute(edge_spin, 'row', [(0, 1), (1, 0)])  3.11 us
    ppermute x4, starting transfers between devices, body(): send_side = lambda x: lax.ppermute(x, 'row', [(0, 1), (1, 0)])  3.09 us
    unnamed x12, local copies, waits for them, and re-layouts  2.52 us
  transfers between devices with their start and end apart: 17, of which 3 were waited for; matrix products, arithmetic and copies ran while one was open for 1% of the time, Pallas kernels for 40%

profile of v1, /device:TPU:0, one launch (start us, length us, event | category | flops | bytes accessed | tf_op | source)
XLA Modules:
  0.0 89.2 jit_solution(5301632358319157519)
XLA Ops:
  0.6 0.8 fusion.2
  1.5 0.1 copy-done
  1.6 0.9 slice_bitcast_fusion.2
  2.8 3.0 %collective-permute-start.2 = (f32[5,8,128]{2,1,0:T(8,128)S(1)}, f32[5,8,128]{2,1,0:T(8,128)S(1)}, u32[]{:S(2)}, u32[]{:S(2)}) collective-permute-start(f32[5,8,128]{2,1,0:T(8,128)S(1)} %pad.7), channel_id=1, source_target_pairs={{0,1},{1,0},{2,3},{3,2},{4,5},{5,4},{6,7},{7,6},{8,9},{9,8},{10,11... | collective-permute-start | bytes 61448 | tf_op jit(solution)/shard_map/ppermute | solution.py:299
  5.8 1.6 %collective-permute-start = (f32[5,32,256]{2,1,0:T(8,128)S(1)}, f32[5,32,256]{2,1,0:T(8,128)S(1)}, u32[]{:S(2)}, u32[]{:S(2)}) collective-permute-start(f32[5,32,256]{2,1,0:T(8,128)S(1)} %pad_maximum_fusion.refs_1_), channel_id=1, source_target_pairs={{0,2},{2,4},{4,6},{6,8},{8,10},{10,12},{12,14},{14,16},{16,18},{18... | collective-permute-start | bytes 491528 | tf_op jit(solution)/shard_map/ppermute | solution.py:297
  7.5 3.4 %collective-permute-start.1 = (f32[5,40,128]{2,1,0:T(8,128)S(1)}, f32[5,40,128]{2,1,0:T(8,128)S(1)}, u32[]{:S(2)}, u32[]{:S(2)}) collective-permute-start(f32[5,40,128]{2,1,0:T(8,128)S(1)} %pad_maximum_fusion.4), channel_id=1, source_target_pairs={{0,4},{2,6},{4,8},{6,10},{8,12},{10,14},{12,16},{14,18},{16,20},{1... | collective-permute-start | bytes 307208 | tf_op jit(solution)/shard_map/ppermute | solution.py:298
  11.3 0.1 copy.39
  11.4 3.1 %collective-permute-done.4 = f32[6]{0:T(128)S(1)} collective-permute-done((f32[6]{0:T(128)S(1)}, f32[6]{0:T(128)S(1)}, u32[]{:S(2)}, u32[]{:S(2)}) %collective-permute-start.4) | collective-permute-done | bytes 56 | tf_op jit(solution)/shard_map/ppermute | solution.py:303
  14.6 0.2 collective-permute-start.12
  14.8 2.9 %collective-permute-start.9 = (f32[5,32,256]{2,1,0:T(8,128)S(1)}, f32[5,32,256]{2,1,0:T(8,128)S(1)}, u32[]{:S(2)}, u32[]{:S(2)}) collective-permute-start(f32[5,32,256]{2,1,0:T(8,128)S(1)} %pad_maximum_fusion.1.refs_1_), channel_id=1, source_target_pairs={{0,2},{2,4},{4,6},{6,8},{8,10},{10,12},{12,14},{14,16},{16,18},{18... | collective-permute-start | bytes 491528 | tf_op jit(solution)/shard_map/ppermute | solution.py:297
  17.8 3.4 %collective-permute-start.10 = (f32[5,40,128]{2,1,0:T(8,128)S(1)}, f32[5,40,128]{2,1,0:T(8,128)S(1)}, u32[]{:S(2)}, u32[]{:S(2)}) collective-permute-start(f32[5,40,128]{2,1,0:T(8,128)S(1)} %pad_maximum_fusion.5), channel_id=1, source_target_pairs={{0,4},{2,6},{4,8},{6,10},{8,12},{10,14},{12,16},{14,18},{16,20},{1... | collective-permute-start | bytes 307208 | tf_op jit(solution)/shard_map/ppermute | solution.py:298
  21.3 0.7 copy-done.2
  22.1 12.7 %disc_step.4 = (f32[5,32,256]{2,1,0:T(8,128)S(1)}, f32[5,40,128]{2,1,0:T(8,128)S(1)}, f32[5,8,128]{2,1,0:T(8,128)S(1)}) custom-call(s32[1]{0:T(128)} %bitcast.refs_0_, f32[5,32,256]{2,1,0:T(8,128)S(1)} %pad_maximum_fusion.refs_1_, f32[5,32,256]{2,1,0:T(8,128)S(1)} %collective-permute-done.refs_2_, f32[5,40,128]{2,1,0:T(8,128)S(1)} %collective-permute-done.1.refs_3_, ...), custom_call_target="tpu_custom_call" | custom-call | flops 20000000 | bytes 600000 | tf_op jit(solution)/shard_map/disc_step/pallas_call | solution.py:261
  34.9 12.7 %disc_step.6 = (f32[5,32,256]{2,1,0:T(8,128)S(1)}, f32[5,40,128]{2,1,0:T(8,128)S(1)}, f32[5,8,128]{2,1,0:T(8,128)S(1)}) custom-call(s32[1]{0:T(128)} %bitcast.refs_0_, f32[5,32,256]{2,1,0:T(8,128)S(1)} %pad_maximum_fusion.1.refs_1_, f32[5,32,256]{2,1,0:T(8,128)S(1)} %collective-permute-done.9.refs_2_, f32[5,40,128]{2,1,0:T(8,128)S(1)} %collective-permute-done.10.refs_3_, ...), custom_call_target="tpu_custom_call" | custom-call | flops 20000000 | bytes 600000 | tf_op jit(solution)/shard_map/disc_step/pallas_call | solution.py:261
  47.6 1.7 %collective-permute-start.13 = (f32[5,32,256]{2,1,0:T(8,128)S(1)}, f32[5,32,256]{2,1,0:T(8,128)S(1)}, u32[]{:S(2)}, u32[]{:S(2)}) collective-permute-start(f32[5,32,256]{2,1,0:T(8,128)S(1)} %get-tuple-element.12.refs_1_), channel_id=1, source_target_pairs={{0,2},{2,4},{4,6},{6,8},{8,10},{10,12},{12,14},{14,16},{16,18},{18... | collective-permute-start | bytes 491528 | tf_op jit(solution)/shard_map/ppermute | solution.py:297
  49.2 3.4 %collective-permute-start.6 = (f32[5,40,128]{2,1,0:T(8,128)S(1)}, f32[5,40,128]{2,1,0:T(8,128)S(1)}, u32[]{:S(2)}, u32[]{:S(2)}) collective-permute-start(f32[5,40,128]{2,1,0:T(8,128)S(1)} %get-tuple-element.10), channel_id=1, source_target_pairs={{0,4},{2,6},{4,8},{6,10},{8,12},{10,14},{12,16},{14,18},{16,20},{1... | collective-permute-start | bytes 307208 | tf_op jit(solution)/shard_map/ppermute | solution.py:298
  52.6 3.4 %collective-permute-start.14 = (f32[5,40,128]{2,1,0:T(8,128)S(1)}, f32[5,40,128]{2,1,0:T(8,128)S(1)}, u32[]{:S(2)}, u32[]{:S(2)}) collective-permute-start(f32[5,40,128]{2,1,0:T(8,128)S(1)} %get-tuple-element.13), channel_id=1, source_target_pairs={{0,4},{2,6},{4,8},{6,10},{8,12},{10,14},{12,16},{14,18},{16,20},{1... | collective-permute-start | bytes 307208 | tf_op jit(solution)/shard_map/ppermute | solution.py:298
  56.2 3.8 %collective-permute-done.7.refs_4_ = f32[5,8,128]{2,1,0:T(8,128)S(1)} collective-permute-done((f32[5,8,128]{2,1,0:T(8,128)S(1)}, f32[5,8,128]{2,1,0:T(8,128)S(1)}, u32[]{:S(2)}, u32[]{:S(2)}) %collective-permute-start.7) | collective-permute-done | bytes 20512 | tf_op jit(solution)/shard_map/ppermute | solution.py:299
  59.9 6.8 %collective-permute-done.8.refs_5_ = f32[5,8,128]{2,1,0:T(8,128)S(1)} collective-permute-done((f32[5,8,128]{2,1,0:T(8,128)S(1)}, f32[5,8,128]{2,1,0:T(8,128)S(1)}, u32[]{:S(2)}, u32[]{:S(2)}) %collective-permute-start.8) | collective-permute-done | bytes 20512 | tf_op jit(solution)/shard_map/ppermute | solution.py:300
  66.8 10.2 %disc_step.5 = f32[5,32,256]{2,1,0:T(8,128)S(1)} custom-call(s32[1]{0:T(128)} %bitcast.refs_0_, f32[5,32,256]{2,1,0:T(8,128)S(1)} %get-tuple-element.9.refs_1_, f32[5,32,256]{2,1,0:T(8,128)S(1)} %collective-permute-done.5.refs_2_, f32[5,40,128]{2,1,0:T(8,128)S(1)} %collective-permute-done.6.refs_3_, f32[5,8,128]{2,1,0:T(8,128)S(1)} %collective-permute-done.7.refs_4_, ...), custom_call_target="tpu_custom_call" | custom-call | flops 20000000 | bytes 600000 | tf_op jit(solution)/shard_map/disc_step/pallas_call | solution.py:261
  77.0 10.2 %disc_step.7 = f32[5,32,256]{2,1,0:T(8,128)S(1)} custom-call(s32[1]{0:T(128)} %bitcast.refs_0_, f32[5,32,256]{2,1,0:T(8,128)S(1)} %get-tuple-element.12.refs_1_, f32[5,32,256]{2,1,0:T(8,128)S(1)} %collective-permute-done.13.refs_2_, f32[5,40,128]{2,1,0:T(8,128)S(1)} %collective-permute-done.14.refs_3_, f32[5,8,128]{2,1,0:T(8,128)S(1)} %collective-permute-done.15.refs_4_, ...), custom_call_target="tpu_custom_call" | custom-call | flops 20000000 | bytes 600000 | tf_op jit(solution)/shard_map/disc_step/pallas_call | solution.py:261
  87.2 0.6 maximum_bitcast_fusion
  87.9 0.7 copy.30
  88.5 0.7 copy.31
  (53 shorter events, 1.2 us)
Async XLA Ops:
  0.6 0.9 %copy-start = (f32[2,2,32,256]{3,2,1,0:T(8,128)S(1)}, f32[2,2,32,256]{3,2,1,0:T(8,128)}, u32[]{:S(2)}) copy-start(f32[2,2,32,256]{3,2,1,0:T(8,128)} %param.7) | copy-start | bytes 393220
  2.8 11.8 %collective-permute-start.2 = (f32[5,8,128]{2,1,0:T(8,128)S(1)}, f32[5,8,128]{2,1,0:T(8,128)S(1)}, u32[]{:S(2)}, u32[]{:S(2)}) collective-permute-start(f32[5,8,128]{2,1,0:T(8,128)S(1)} %pad.7), channel_id=1, source_target_pairs={{0,1},{1,0},{2,3},{3,2},{4,5},{5,4},{6,7},{7,6},{8,9},{9,8},{10,11... | collective-permute-start | bytes 61448 | tf_op jit(solution)/shard_map/ppermute | solution.py:299
  5.8 9.0 %collective-permute-start.3 = (f32[5,8,128]{2,1,0:T(8,128)S(1)}, f32[5,8,128]{2,1,0:T(8,128)S(1)}, u32[]{:S(2)}, u32[]{:S(2)}) collective-permute-start(f32[5,8,128]{2,1,0:T(8,128)S(1)} %pad.7), channel_id=1, source_target_pairs={{0,3},{1,2},{2,5},{3,4},{4,7},{5,6},{6,9},{7,8},{8,11},{9,10},{10,... | collective-permute-start | bytes 61448 | tf_op jit(solution)/shard_map/ppermute | solution.py:300
  5.8 15.4 %collective-permute-start = (f32[5,32,256]{2,1,0:T(8,128)S(1)}, f32[5,32,256]{2,1,0:T(8,128)S(1)}, u32[]{:S(2)}, u32[]{:S(2)}) collective-permute-start(f32[5,32,256]{2,1,0:T(8,128)S(1)} %pad_maximum_fusion.refs_1_), channel_id=1, source_target_pairs={{0,2},{2,4},{4,6},{6,8},{8,10},{10,12},{12,14},{14,16},{16,18},{18... | collective-permute-start | bytes 491528 | tf_op jit(solution)/shard_map/ppermute | solution.py:297
  7.5 3.5 %copy-start.1 = (f32[256]{0:T(256)S(1)}, f32[256]{0:T(256)}, u32[]{:S(2)}) copy-start(f32[256]{0:T(256)} %param.8) | copy-start | bytes 3076
  7.5 10.3 %collective-permute-start.1 = (f32[5,40,128]{2,1,0:T(8,128)S(1)}, f32[5,40,128]{2,1,0:T(8,128)S(1)}, u32[]{:S(2)}, u32[]{:S(2)}) collective-permute-start(f32[5,40,128]{2,1,0:T(8,128)S(1)} %pad_maximum_fusion.4), channel_id=1, source_target_pairs={{0,4},{2,6},{4,8},{6,10},{8,12},{10,14},{12,16},{14,18},{16,20},{1... | collective-permute-start | bytes 307208 | tf_op jit(solution)/shard_map/ppermute | solution.py:298
  11.0 3.5 %collective-permute-start.4 = (f32[6]{0:T(128)S(1)}, f32[6]{0:T(128)S(1)}, u32[]{:S(2)}, u32[]{:S(2)}) collective-permute-start(f32[6]{0:T(128)S(1)} %broadcast_select_fusion), channel_id=1, source_target_pairs={{0,1},{1,0},{2,3},{3,2},{4,5},{5,4},{6,7},{7,6},{8,9},{9,8},{10,11... | collective-permute-start | bytes 80 | tf_op jit(solution)/shard_map/ppermute | solution.py:303
  14.6 20.3 %collective-permute-start.11 = (f32[5,8,128]{2,1,0:T(8,128)S(1)}, f32[5,8,128]{2,1,0:T(8,128)S(1)}, u32[]{:S(2)}, u32[]{:S(2)}) collective-permute-start(f32[5,8,128]{2,1,0:T(8,128)S(1)} %pad.8), channel_id=1, source_target_pairs={{0,1},{1,0},{2,3},{3,2},{4,5},{5,4},{6,7},{7,6},{8,9},{9,8},{10,11... | collective-permute-start | bytes 61448 | tf_op jit(solution)/shard_map/ppermute | solution.py:299
  14.6 20.2 %collective-permute-start.12 = (f32[5,8,128]{2,1,0:T(8,128)S(1)}, f32[5,8,128]{2,1,0:T(8,128)S(1)}, u32[]{:S(2)}, u32[]{:S(2)}) collective-permute-start(f32[5,8,128]{2,1,0:T(8,128)S(1)} %pad.8), channel_id=1, source_target_pairs={{0,3},{1,2},{2,5},{3,4},{4,7},{5,6},{6,9},{7,8},{8,11},{9,10},{10,... | collective-permute-start | bytes 61448 | tf_op jit(solution)/shard_map/ppermute | solution.py:300
  14.8 20.0 %collective-permute-start.9 = (f32[5,32,256]{2,1,0:T(8,128)S(1)}, f32[5,32,256]{2,1,0:T(8,128)S(1)}, u32[]{:S(2)}, u32[]{:S(2)}) collective-permute-start(f32[5,32,256]{2,1,0:T(8,128)S(1)} %pad_maximum_fusion.1.refs_1_), channel_id=1, source_target_pairs={{0,2},{2,4},{4,6},{6,8},{8,10},{10,12},{12,14},{14,16},{16,18},{18... | collective-permute-start | bytes 491528 | tf_op jit(solution)/shard_map/ppermute | solution.py:297
  17.8 17.1 %collective-permute-start.10 = (f32[5,40,128]{2,1,0:T(8,128)S(1)}, f32[5,40,128]{2,1,0:T(8,128)S(1)}, u32[]{:S(2)}, u32[]{:S(2)}) collective-permute-start(f32[5,40,128]{2,1,0:T(8,128)S(1)} %pad_maximum_fusion.5), channel_id=1, source_target_pairs={{0,4},{2,6},{4,8},{6,10},{8,12},{10,14},{12,16},{14,18},{16,20},{1... | collective-permute-start | bytes 307208 | tf_op jit(solution)/shard_map/ppermute | solution.py:298
  21.3 0.7 copy-start.2
  34.8 32.0 %collective-permute-start.5 = (f32[5,32,256]{2,1,0:T(8,128)S(1)}, f32[5,32,256]{2,1,0:T(8,128)S(1)}, u32[]{:S(2)}, u32[]{:S(2)}) collective-permute-start(f32[5,32,256]{2,1,0:T(8,128)S(1)} %get-tuple-element.9.refs_1_), channel_id=1, source_target_pairs={{0,2},{2,4},{4,6},{6,8},{8,10},{10,12},{12,14},{14,16},{16,18},{18... | collective-permute-start | bytes 491528 | tf_op jit(solution)/shard_map/ppermute | solution.py:297
  47.6 29.4 %collective-permute-start.13 = (f32[5,32,256]{2,1,0:T(8,128)S(1)}, f32[5,32,256]{2,1,0:T(8,128)S(1)}, u32[]{:S(2)}, u32[]{:S(2)}) collective-permute-start(f32[5,32,256]{2,1,0:T(8,128)S(1)} %get-tuple-element.12.refs_1_), channel_id=1, source_target_pairs={{0,2},{2,4},{4,6},{6,8},{8,10},{10,12},{12,14},{14,16},{16,18},{18... | collective-permute-start | bytes 491528 | tf_op jit(solution)/shard_map/ppermute | solution.py:297
  49.2 17.5 %collective-permute-start.6 = (f32[5,40,128]{2,1,0:T(8,128)S(1)}, f32[5,40,128]{2,1,0:T(8,128)S(1)}, u32[]{:S(2)}, u32[]{:S(2)}) collective-permute-start(f32[5,40,128]{2,1,0:T(8,128)S(1)} %get-tuple-element.10), channel_id=1, source_target_pairs={{0,4},{2,6},{4,8},{6,10},{8,12},{10,14},{12,16},{14,18},{16,20},{1... | collective-permute-start | bytes 307208 | tf_op jit(solution)/shard_map/ppermute | solution.py:298
  52.6 24.3 %collective-permute-start.14 = (f32[5,40,128]{2,1,0:T(8,128)S(1)}, f32[5,40,128]{2,1,0:T(8,128)S(1)}, u32[]{:S(2)}, u32[]{:S(2)}) collective-permute-start(f32[5,40,128]{2,1,0:T(8,128)S(1)} %get-tuple-element.13), channel_id=1, source_target_pairs={{0,4},{2,6},{4,8},{6,10},{8,12},{10,14},{12,16},{14,18},{16,20},{1... | collective-permute-start | bytes 307208 | tf_op jit(solution)/shard_map/ppermute | solution.py:298
  56.1 3.8 %collective-permute-start.7 = (f32[5,8,128]{2,1,0:T(8,128)S(1)}, f32[5,8,128]{2,1,0:T(8,128)S(1)}, u32[]{:S(2)}, u32[]{:S(2)}) collective-permute-start(f32[5,8,128]{2,1,0:T(8,128)S(1)} %get-tuple-element.11), channel_id=1, source_target_pairs={{0,1},{1,0},{2,3},{3,2},{4,5},{5,4},{6,7},{7,6},{8,9},{9,8},{10,11... | collective-permute-start | bytes 61448 | tf_op jit(solution)/shard_map/ppermute | solution.py:299
  59.9 6.8 %collective-permute-start.8 = (f32[5,8,128]{2,1,0:T(8,128)S(1)}, f32[5,8,128]{2,1,0:T(8,128)S(1)}, u32[]{:S(2)}, u32[]{:S(2)}) collective-permute-start(f32[5,8,128]{2,1,0:T(8,128)S(1)} %get-tuple-element.11), channel_id=1, source_target_pairs={{0,3},{1,2},{2,5},{3,4},{4,7},{5,6},{6,9},{7,8},{8,11},{9,10},{10,... | collective-permute-start | bytes 61448 | tf_op jit(solution)/shard_map/ppermute | solution.py:300
  66.7 10.2 %collective-permute-start.15 = (f32[5,8,128]{2,1,0:T(8,128)S(1)}, f32[5,8,128]{2,1,0:T(8,128)S(1)}, u32[]{:S(2)}, u32[]{:S(2)}) collective-permute-start(f32[5,8,128]{2,1,0:T(8,128)S(1)} %get-tuple-element.14), channel_id=1, source_target_pairs={{0,1},{1,0},{2,3},{3,2},{4,5},{5,4},{6,7},{7,6},{8,9},{9,8},{10,11... | collective-permute-start | bytes 61448 | tf_op jit(solution)/shard_map/ppermute | solution.py:299
  66.7 10.2 %collective-permute-start.16 = (f32[5,8,128]{2,1,0:T(8,128)S(1)}, f32[5,8,128]{2,1,0:T(8,128)S(1)}, u32[]{:S(2)}, u32[]{:S(2)}) collective-permute-start(f32[5,8,128]{2,1,0:T(8,128)S(1)} %get-tuple-element.14), channel_id=1, source_target_pairs={{0,3},{1,2},{2,5},{3,4},{4,7},{5,6},{6,9},{7,8},{8,11},{9,10},{10,... | collective-permute-start | bytes 61448 | tf_op jit(solution)/shard_map/ppermute | solution.py:300

commit v2 on v1

v2 whole, which is shorter than its diff:
```python
import jax
import jax.numpy as jnp
from jax import lax
from jax.experimental import pallas as pl
from jax.experimental.pallas import tpu as pltpu
from jax.sharding import PartitionSpec as P

STEPS = 2
SMIN = 8
SMAX = 56
STAGES = 3
REACH = 2 * STAGES
FIELDS = 5
LANES = 128
SUB = 8
HALF = LANES // 2
SLOTS = 2 * SUB
EXTRA = 2 * SUB
TALL = 32
BITS = 3
UNROLL = 64
VMEM_LIMIT = 32 * 1024 * 1024

time_step = 0.08
sound_sq = 1.0


def shift_bound(first_row, rows):
    d = rows - 1 - first_row
    return min(SMIN + (SMAX - SMIN - 1) * d * d // ((rows - 1) * (rows - 1)) + 1, SMAX)


def minmod(lower, upper):
    return jnp.maximum(jnp.minimum(lower, 0.0), jnp.minimum(upper, jnp.maximum(lower, 0.0)))


def physical(state):
    rho, mn, mt, bn, bt = state
    inverse = pltpu.reciprocal(rho, approx=True)
    vn = mn * inverse
    vt = mt * inverse
    bn_sq = bn * bn
    bt_sq = bt * bt
    flux_n = mn * vn + (sound_sq * rho + 0.5 * (bt_sq - bn_sq))
    flux_t = mt * vn - bn * bt
    flux_b = bt * vn - bn * vt
    inside = sound_sq + (bn_sq + bt_sq) * inverse
    speed = jnp.abs(vn) + inside * lax.rsqrt(inside)
    return (mn, flux_n, flux_t, None, flux_b), speed


def face_twice(left, right):
    left_flux, left_speed = physical(left)
    right_flux, right_speed = physical(right)
    bound = jnp.maximum(left_speed, right_speed)
    out = []
    for k in range(FIELDS):
        jump = bound * (right[k] - left[k])
        if left_flux[k] is None:
            out.append(-jump)
        else:
            out.append((left_flux[k] + right_flux[k]) - jump)
    return out


def swapped(five):
    return [five[0], five[2], five[1], five[4], five[3]]


def run_stage(start, src, dst, spin, lo, hi, keep, weight, edges):
    half_dt = 0.5 * time_step
    low_mask, high_mask, first, last = edges
    for f in range(FIELDS):
        row = lambda i: pl.ds(i * SUB, SUB)
        inner = src[f, row(first), :]
        outer = src[f, row(last), :]
        for k in (1, 2):
            src[f, row(first - k), :] = jnp.where(low_mask, inner, src[f, row(first - k), :])
            src[f, row(last + k), :] = jnp.where(high_mask, outer, src[f, row(last + k), :])

    def at(i):
        if isinstance(i, int):
            return pl.ds(i * SUB, SUB)
        return pl.ds(pl.multiple_of(i * SUB, SUB), SUB)

    def radial_faces(rows):
        halves = [[0.5 * x for x in r] for r in rows]
        jumps = [[b - a for a, b in zip(p, q)] for p, q in zip(halves[:-1], halves[1:])]
        slopes = [[minmod(a, b) for a, b in zip(p, q)] for p, q in zip(jumps[:-1], jumps[1:])]
        upper = [[x + s for x, s in zip(r, sl)] for r, sl in zip(rows[1:-1], slopes)]
        lower = [[x - s for x, s in zip(r, sl)] for r, sl in zip(rows[1:-1], slopes)]
        return [swapped(face_twice(swapped(u), swapped(l))) for u, l in zip(upper[:-1], lower[1:])]

    def azimuth_change(fields):
        right_of = lambda x: pltpu.roll(x, LANES - 1, 1)
        left_of = lambda x: pltpu.roll(x, 1, 1)
        lower = []
        upper = []
        for x in fields:
            half = 0.5 * x
            slope = minmod(half - left_of(half), right_of(half) - half)
            upper.append(x + slope)
            lower.append(right_of(x - slope))
        faces = face_twice(upper, lower)
        return [x - left_of(x) for x in faces]

    def work(i0, count, before):
        rows = [[src[f, at(i0 + k), :] for f in range(FIELDS)] for k in range(-1, count + 2)]
        faces = [before] + radial_faces(rows)
        for k in range(count):
            fields = rows[k + 1]
            change = azimuth_change(fields)
            i = i0 + k
            turn = spin[at(i), :]
            source = [
                None,
                (-0.5 * turn) * fields[2],
                (2.0 * turn) * fields[1],
                (-1.5 * turn) * fields[4],
                None,
            ]
            for f in range(FIELDS):
                new = fields[f] - half_dt * (change[f] + (faces[k + 1][f] - faces[k][f]))
                if source[f] is not None:
                    new = new + source[f]
                if weight != 1.0:
                    new = weight * new + keep * start[f, at(i), :]
                dst[f, at(i), :] = new
        return faces[-1]

    before = radial_faces([[src[f, at(lo + k), :] for f in range(FIELDS)] for k in range(-2, 2)])[0]
    if UNROLL >= hi - lo:
        work(lo, hi - lo, before)
    else:

        def step(c, carried):
            return tuple(work(lo + c * UNROLL, UNROLL, list(carried)))

        lax.fori_loop(0, (hi - lo) // UNROLL, step, tuple(before))


def spread(block, first, width):
    block = pltpu.roll(block, (LANES - first) % LANES, 1)
    lane = lax.broadcasted_iota(jnp.int32, block.shape, 1)
    while width < LANES:
        block = jnp.where(lane < width, block, pltpu.roll(block, width, 1))
        width *= 2
    return block


def pack_kernel(spare, place, density, momentum, magnetic, rotation, shifts, *outs):
    levels, own_cells, radius = density.shape
    nears, fars, edge, spin_rows, shift_rows = outs[:levels], outs[levels : 2 * levels], *outs[2 * levels :]
    on_low = place[0] == 0
    parts = radius // LANES
    for part in range(parts):
        rows = slice(part * LANES, (part + 1) * LANES)
        spin_rows[rows, :] = jnp.broadcast_to(rotation[part : part + 1, :], (LANES, LANES)).T * time_step
        shift_rows[rows, :] = jnp.broadcast_to(shifts[part : part + 1, :].astype(jnp.float32), (LANES, LANES)).T
    wide = lambda ref: jnp.broadcast_to(
        jnp.where(on_low, ref[parts - 1 : parts, :], ref[0:1, :]).astype(jnp.float32), (own_cells, LANES)
    )
    for level in range(levels):
        fields = [density[level], momentum[0, level], momentum[1, level], magnetic[0, level], magnetic[1, level]]
        for f, x in enumerate(fields):
            nears[level][f * own_cells : (f + 1) * own_cells, :] = x
            pack_far(fars[level], f, x[:, 0:LANES], x[:, LANES : 2 * LANES], spare)
        ends = [jnp.where(on_low, x[:, radius - LANES :], x[:, 0:LANES]) for x in fields]
        last = [ends[4], wide(rotation) * time_step, wide(shifts), jnp.zeros((own_cells, LANES), jnp.float32)]
        for side, group in enumerate((ends[:4], last)):
            turned = jnp.concatenate(group, axis=0).T
            edge[level * EXTRA : (level + 1) * EXTRA, side * LANES : (side + 1) * LANES] = jnp.where(
                on_low, turned[LANES - EXTRA :], turned[0:EXTRA]
            )


def pack_far(far, f, low, high, spare):
    own_cells = low.shape[0]
    base = f * (own_cells + SUB)
    sublane = lax.broadcasted_iota(jnp.int32, (SUB, LANES), 0)
    moved = pltpu.roll(high[own_cells - 2 * SUB : own_cells - SUB], spare, 0)
    far[base : base + SUB, :] = jnp.where(sublane < spare, moved, low[0:SUB])
    far[base + SUB : base + own_cells, :] = low[SUB:]
    far[base + own_cells : base + own_cells + SUB, :] = high[own_cells - SUB :]


def step_kernel(plan, refs, write, scratch):
    n, radius, own_cells, total, row_count, spare, moved = plan
    place, own, own_edge, near, near_edge, far, side, spin_rows, shift_rows = refs
    cells, a, b, c, spin, extra, packed = scratch
    row = place[0]
    on_low = row == 0
    lane = lax.broadcasted_iota(jnp.int32, (SUB, LANES), 1)
    sublane = lax.broadcasted_iota(jnp.int32, (SUB, LANES), 0)
    base = jnp.where(on_low, 0, -moved)
    own_at = pl.multiple_of(EXTRA - base, SUB)
    edge_at = pl.multiple_of(jnp.where(on_low, EXTRA + radius, moved), SUB)

    def bound_of(slot):
        d = (total - 1) - (row * radius + base + n * slot)
        smooth = lax.div((SMAX - SMIN - 1) * d * d, jnp.int32((total - 1) * (total - 1)))
        return jnp.minimum(SMIN + smooth + 1, SMAX)

    bounds = [bound_of(k) for k in range(SLOTS)]

    edge_lane = lax.broadcasted_iota(jnp.int32, (EXTRA, LANES), 1)
    for f in range(FIELDS):
        rows = slice(f * own_cells, (f + 1) * own_cells)
        start = f * (own_cells + SUB)
        for part in range(radius // LANES):
            columns = slice(part * LANES, (part + 1) * LANES)
            if part == 0:
                top = far[start : start + own_cells, :]
            else:
                top = jnp.concatenate(
                    [
                        jnp.zeros((own_cells - 2 * SUB, LANES), jnp.float32),
                        pltpu.roll(far[start : start + SUB, :], SUB - spare, 0),
                        far[start + own_cells : start + own_cells + SUB, :],
                    ],
                    axis=0,
                )
            block = jnp.concatenate(
                [top, near[rows, columns], own[rows, columns], jnp.zeros((own_cells, LANES), jnp.float32)], axis=0
            )
            cells[f, pl.ds(own_at + part * LANES, LANES), :] = block.T
        columns = slice(f // 4 * LANES, (f // 4 + 1) * LANES)
        lanes_at = f % 4 * own_cells
        cells[f, pl.ds(edge_at, EXTRA), :] = jnp.where(
            edge_lane < 2 * own_cells,
            pltpu.roll(near_edge[:, columns], (LANES + own_cells - lanes_at) % LANES, 1),
            pltpu.roll(own_edge[:, columns], (LANES + 2 * own_cells - lanes_at) % LANES, 1),
        )
    more = side[0:EXTRA, LANES : 2 * LANES]
    packed[0, pl.ds(own_at, radius), :] = spin_rows[...]
    packed[0, pl.ds(edge_at, EXTRA), :] = spread(more, own_cells, own_cells)
    packed[1, pl.ds(own_at, radius), :] = shift_rows[...]
    packed[1, pl.ds(edge_at, EXTRA), :] = spread(more, 2 * own_cells, own_cells)

    front = lax.broadcasted_iota(jnp.int32, (TALL, LANES), 1) < HALF
    for j in range(SUB):
        low, high = j, SUB + j
        at = [slice(EXTRA - REACH + n * k, EXTRA - REACH + n * k + TALL) for k in (low, high)]
        turn_low = (LANES - (2 * own_cells - REACH)) + bounds[low]
        turn_high = (HALF - (2 * own_cells - REACH)) + bounds[high]
        for f in range(FIELDS):
            a[f, pl.ds(j, TALL, stride=SUB), :] = jnp.where(
                front, pltpu.roll(cells[f, at[0], :], turn_low, 1), pltpu.roll(cells[f, at[1], :], turn_high, 1)
            )
        spin[pl.ds(j, TALL, stride=SUB), :] = jnp.where(front, packed[0, at[0], :], packed[0, at[1], :])
        behind = jnp.where(front, bounds[low], bounds[high]) - jnp.where(
            front, packed[1, at[0], :], packed[1, at[1], :]
        ).astype(jnp.int32)
        extra[pl.ds(j, TALL, stride=SUB), :] = behind

    first, last = REACH, REACH + n - 1
    edges = (
        (sublane == 0) & (lane < HALF) & on_low,
        (sublane == SUB - 1) & (lane >= HALF) & (row == row_count - 1),
        first,
        last,
    )
    run_stage(a, a, b, spin, 2, n + 10, 0.0, 1.0, edges)
    run_stage(a, b, c, spin, 4, n + 8, 0.75, 0.25, edges)
    run_stage(a, c, b, spin, 6, n + 6, 1.0 / 3.0, 2.0 / 3.0, edges)

    even = (lane // own_cells) % 2 == 0
    for i in range(n):
        rows = slice((REACH + i) * SUB, (REACH + i + 1) * SUB)
        behind = extra[rows, :]
        picks = [((behind >> bit) & 1) == 1 for bit in range(BITS)]
        turned = []
        for f in range(FIELDS):
            x = b[f, rows, :]
            for bit in range(BITS):
                x = jnp.where(picks[bit], pltpu.roll(x, LANES - (1 << bit), 1), x)
            turned.append(pltpu.roll(x, (LANES - REACH + f % 2 * own_cells) % LANES, 1))
        here = slice(i * SUB, (i + 1) * SUB)
        a[0, here, :] = jnp.where(even, turned[0], turned[1])
        a[1, here, :] = jnp.where(even, turned[2], turned[3])
        a[2, here, :] = turned[4]
    narrow = lax.broadcasted_iota(jnp.int32, (n, LANES), 1) < HALF
    for j in range(SUB):
        one, two, three = [a[g, pl.ds(j, n, stride=SUB), :] for g in range(3)]
        low = slice(EXTRA + n * j, EXTRA + n * (j + 1))
        high = slice(EXTRA + n * (SUB + j), EXTRA + n * (SUB + j + 1))
        packed[0, low, :] = jnp.where(narrow, one, pltpu.roll(two, HALF, 1))
        packed[0, high, :] = jnp.where(narrow, pltpu.roll(one, HALF, 1), two)
        packed[1, low, :] = three
        packed[1, high, :] = pltpu.roll(three, HALF, 1)
    for part in range(radius // LANES):
        rows = pl.ds(own_at + part * LANES, LANES)
        turned = packed[0, rows, :].T
        fourth = packed[1, rows, :].T
        write.fields(part, [turned[f * own_cells : (f + 1) * own_cells] for f in range(4)] + [fourth[0:own_cells]])
    write.rest(packed[0, pl.ds(edge_at, EXTRA), :], packed[1, pl.ds(edge_at, EXTRA), :])


class ToMessage:
    def __init__(self, near, far, spare):
        self.near, self.far, self.spare = near, far, spare
        self.low = None

    def fields(self, part, five):
        own_cells = five[0].shape[0]
        columns = slice(part * LANES, (part + 1) * LANES)
        for f, x in enumerate(five):
            self.near[f * own_cells : (f + 1) * own_cells, columns] = x
        if part == 0:
            self.low = five
        else:
            for f, (low, high) in enumerate(zip(self.low, five)):
                pack_far(self.far, f, low, high, self.spare)

    def rest(self, first, second):
        tail = self.near.shape[0] - EXTRA
        self.near[tail:, 0:LANES] = first
        self.near[tail:, LANES : 2 * LANES] = second


class ToResult:
    def __init__(self, density, momentum, magnetic):
        self.outs = (density, momentum, magnetic)

    def fields(self, part, five):
        columns = slice(part * LANES, (part + 1) * LANES)
        density, momentum, magnetic = self.outs
        density[0, :, columns] = five[0]
        for k in range(2):
            momentum[k, 0, :, columns] = five[1 + k]
            magnetic[k, 0, :, columns] = five[3 + k]

    def rest(self, first, second):
        pass


def step_scratch(n, radius):
    tall = EXTRA + SLOTS * n + 2 * SUB
    stage = pltpu.VMEM((FIELDS, TALL * SUB, LANES), jnp.float32)
    return [
        pltpu.VMEM((FIELDS, tall, LANES), jnp.float32),
        stage,
        stage,
        stage,
        pltpu.VMEM((TALL * SUB, LANES), jnp.float32),
        pltpu.VMEM((TALL * SUB, LANES), jnp.int32),
        pltpu.VMEM((2, tall, LANES), jnp.float32),
    ]


vmem = pl.BlockSpec(memory_space=pltpu.VMEM)
smem = pl.BlockSpec(memory_space=pltpu.SMEM)
f32 = lambda *s: jax.ShapeDtypeStruct(s, jnp.float32)
params = pltpu.CompilerParams(vmem_limit_bytes=VMEM_LIMIT)
cost = pl.CostEstimate(flops=20_000_000, bytes_accessed=600_000, transcendentals=0)


def first_step(plan, level, operands):
    n, radius, own_cells, total, row_count, spare, moved = plan
    edge_rows = slice(level * EXTRA, (level + 1) * EXTRA)

    def kernel(place, own, near, far, side, corner, spin_rows, shift_rows, near_out, far_out, *scratch):
        refs = (place, own, side.at[edge_rows], near, corner.at[edge_rows], far, side, spin_rows, shift_rows)
        step_kernel(plan, refs, ToMessage(near_out, far_out, spare), scratch)

    return pl.pallas_call(
        kernel,
        out_shape=[f32(FIELDS * own_cells + EXTRA, radius), f32(FIELDS * (own_cells + SUB), LANES)],
        in_specs=[smem] + [vmem] * 7,
        out_specs=[vmem] * 2,
        scratch_shapes=step_scratch(n, radius),
        compiler_params=params,
        cost_estimate=cost,
        name="first_step",
    )(*operands)


def last_step(plan, level, operands, results, levels):
    n, radius, own_cells, total, row_count, spare, moved = plan
    tail = slice(FIELDS * own_cells, FIELDS * own_cells + EXTRA)
    count = len(results)

    def kernel(place, own, near, far, side, spin_rows, shift_rows, *rest):
        outs, scratch = rest[count : count + 3], rest[count + 3 :]
        refs = (place, own, own.at[tail], near, near.at[tail], far, side, spin_rows, shift_rows)
        step_kernel(plan, refs, ToResult(*outs), scratch)

    pair = pl.BlockSpec((2, 1, own_cells, radius), lambda i: (0, level, 0, 0))
    return pl.pallas_call(
        kernel,
        grid=(1,),
        out_shape=[f32(levels, own_cells, radius), f32(2, levels, own_cells, radius), f32(2, levels, own_cells, radius)],
        in_specs=[smem] + [vmem] * 6 + [pl.BlockSpec(memory_space=pl.ANY)] * count,
        out_specs=[pl.BlockSpec((1, own_cells, radius), lambda i: (level, 0, 0)), pair, pair],
        scratch_shapes=step_scratch(n, radius),
        input_output_aliases={len(operands) + k: k for k in range(count)},
        compiler_params=params,
        cost_estimate=cost,
        name="last_step",
    )(*operands, *results)


def body(density, momentum, magnetic, rotation, shifts):
    phi_count = lax.axis_size("phi")
    row_count = lax.axis_size("row")
    levels, own_cells, radius = density.shape
    total = radius * row_count
    parts = radius // LANES
    n = radius // SLOTS
    need = [max(shift_bound(part * LANES, total) + REACH - own_cells, 0) for part in range(parts)]
    spare = own_cells - need[0]
    assert row_count == 2 and radius == 2 * LANES and own_cells == HALF // 2
    assert 0 < need[0] < own_cells and need[1] <= SUB + spare and spare <= SUB

    row = lax.axis_index("row")
    place = jnp.reshape(row, (1,)).astype(jnp.int32)
    here = lambda p, r: (p % phi_count) * row_count + r
    everyone = [(p, r) for p in range(phi_count) for r in range(row_count)]
    both = ("phi", "row")
    send_near = lambda x: lax.ppermute(x, "phi", [(p, (p + 1) % phi_count) for p in range(phi_count)])
    send_far = lambda x: lax.ppermute(x, both, [(here(p, 0), here(p + 2, 0)) for p in range(phi_count)])
    send_side = lambda x: lax.ppermute(x, "row", [(0, 1), (1, 0)])
    send_corner = lambda x: lax.ppermute(x, both, [(here(p, r), here(p + 1, 1 - r)) for p, r in everyone])

    message = f32(FIELDS * own_cells, radius)
    far_message = f32(FIELDS * (own_cells + SUB), LANES)
    packed = pl.pallas_call(
        lambda *refs: pack_kernel(spare, *refs),
        out_shape=[message] * levels
        + [far_message] * levels
        + [f32(levels * EXTRA, 2 * LANES), f32(radius, LANES), f32(radius, LANES)],
        in_specs=[smem] + [vmem] * 5,
        out_specs=[vmem] * (2 * levels + 3),
        compiler_params=params,
        name="pack",
    )(place, density, momentum, magnetic, rotation.reshape(parts, LANES), shifts.reshape(parts, LANES))
    owns, fars, (edge, spin_rows, shift_rows) = packed[:levels], packed[levels : 2 * levels], packed[2 * levels :]

    side = send_side(edge)
    corner = send_corner(edge)
    plan = (n + 1, radius, own_cells, total, row_count, spare, EXTRA)
    moved = [(send_near(own), send_far(far)) for own, far in zip(owns, fars)]
    states = []
    for level in range(levels):
        near, far = moved[level]
        states.append(first_step(plan, level, (place, owns[level], near, far, side, corner, spin_rows, shift_rows)))
    plan = (n, radius, own_cells, total, row_count, spare, 0)
    moved = [(send_near(own), send_far(far)) for own, far in states]
    results = ()
    for level in range(levels):
        near, far = moved[level]
        operands = (place, states[level][0], near, far, side, spin_rows, shift_rows)
        results = last_step(plan, level, operands, results, levels)
    return tuple(results)


def solution(mesh):
    placed = (
        P(None, "phi", "row"),
        P(None, None, "phi", "row"),
        P(None, None, "phi", "row"),
        P("row"),
        P("row"),
    )
    return jax.shard_map(
        body,
        mesh=mesh,
        in_specs=placed,
        out_specs=(P(None, "phi", "row"), P(None, None, "phi", "row"), P(None, None, "phi", "row")),
        check_vma=False,
    )
```

time: 90 us -> 189 us (2.10)
  Pallas kernels: 45.7 us -> 154 us
  starting transfers between devices: 23.2 us -> 16.3 us
    pallas_call x4 -> x5, Pallas kernels: 45.7 us -> 154 us  [the longest x2 79.1 us: first_step(): pl.pallas_call(kernel, out_shape=[f32(FIELDS * own_cells + EXTRA, radius)...]
    ppermute x4, waiting for transfers between devices: 0.01 us -> 3.85 us  [body(): lax.ppermute(x, both, [(here(p, 0), here(p + 2, 0)) for p in range(phi_co...]
    ppermute x1 -> x0, waiting for transfers between devices: 3.11 us -> none  [body(): beside_spin = lax.ppermute(edge_spin, 'row', [(0, 1), (1, 0)])]
    ppermute x4 -> x1, starting transfers between devices: 3.09 us -> 0.01 us  [body(): send_side = lambda x: lax.ppermute(x, 'row', [(0, 1), (1, 0)])]
    ppermute x4, starting transfers between devices: 6.25 us -> 3.43 us  [body(): lax.ppermute(x, 'phi', [(p, (p + 1) % phi_count) for p in range(phi_count)])]
    ppermute x4 -> x1, waiting for transfers between devices: 6.81 us -> 6.94 us  [body(): lax.ppermute(x, both, [(here(p, r), here(p + 1, 1 - r)) for p, r in every...]
    ppermute x4 -> x1, waiting for transfers between devices: 3.78 us -> 3.91 us  [body(): send_side = lambda x: lax.ppermute(x, 'row', [(0, 1), (1, 0)])]
  transfers between devices with their start and end apart: 17 -> 10, of which waited for: 3 -> 3; matrix products, arithmetic and copies ran while one was open for 1% -> 0% of each run, Pallas kernels for 40% -> 62%
where the time goes in v2:
time: 189 us
  Pallas kernels  154 us (81%)
  starting transfers between devices  16.3 us (9%)
  waiting for transfers between devices  14.7 us (8%)
  local copies, waits for them, and re-layouts  3.33 us (2%)
    pallas_call x2, Pallas kernels, first_step(): pl.pallas_call(kernel, out_shape=[f32(FIELDS * own_cells + EXTRA, radius)...  79.1 us
    pallas_call x2, Pallas kernels, last_step(): pl.pallas_call(kernel, grid=(1,), out_shape=[f32(levels, own_cells, radiu...  74.3 us
    ppermute x4, starting transfers between devices, body(): lax.ppermute(x, both, [(here(p, 0), here(p + 2, 0)) for p in range(phi_co...  12.8 us
    ppermute x1, waiting for transfers between devices, body(): lax.ppermute(x, both, [(here(p, r), here(p + 1, 1 - r)) for p, r in every...  6.94 us
    ppermute x1, waiting for transfers between devices, body(): send_side = lambda x: lax.ppermute(x, 'row', [(0, 1), (1, 0)])  3.91 us
    ppermute x4, waiting for transfers between devices, body(): lax.ppermute(x, both, [(here(p, 0), here(p + 2, 0)) for p in range(phi_co...  3.85 us
  transfers between devices with their start and end apart: 10, of which 3 were waited for; matrix products, arithmetic and copies ran while one was open for 0% of the time, Pallas kernels for 62%

profile of v2, /device:TPU:0, one launch (start us, length us, event | category | flops | bytes accessed | tf_op | source)
XLA Modules:
  0.0 188.6 jit_solution(17614393727856273552)
XLA Ops:
  0.7 0.7 copy-done.4
  1.3 0.0 copy-done.3
  1.3 0.9 copy-done
  2.2 0.9 copy-done.1
  3.1 0.8 copy-done.2
  4.0 0.2 pack.1
  4.2 0.5 collective-permute-start.6
  4.7 2.6 %collective-permute-start = (f32[160,256]{1,0:T(8,128)S(1)}, f32[160,256]{1,0:T(8,128)S(1)}, u32[]{:S(2)}, u32[]{:S(2)}) collective-permute-start(f32[160,256]{1,0:T(8,128)S(1)} %get-tuple-element.17.own), channel_id=1, source_target_pairs={{0,2},{2,4},{4,6},{6,8},{8,10},{10,12},{12,14},{14,16},{16,18},{18... | collective-permute-start | bytes 491528 | tf_op jit(solution)/shard_map/ppermute | solution.py:420
  7.3 3.4 %collective-permute-start.7 = (f32[200,128]{1,0:T(8,128)S(1)}, f32[200,128]{1,0:T(8,128)S(1)}, u32[]{:S(2)}, u32[]{:S(2)}) collective-permute-start(f32[200,128]{1,0:T(8,128)S(1)} %get-tuple-element.25), channel_id=1, source_target_pairs={{0,4},{2,6},{4,8},{6,10},{8,12},{10,14},{12,16},{14,18},{16,20},{1... | collective-permute-start | bytes 307208 | tf_op jit(solution)/shard_map/ppermute | solution.py:421
  10.7 3.4 %collective-permute-start.1 = (f32[200,128]{1,0:T(8,128)S(1)}, f32[200,128]{1,0:T(8,128)S(1)}, u32[]{:S(2)}, u32[]{:S(2)}) collective-permute-start(f32[200,128]{1,0:T(8,128)S(1)} %get-tuple-element.18), channel_id=1, source_target_pairs={{0,4},{2,6},{4,8},{6,10},{8,12},{10,14},{12,16},{14,18},{16,20},{1... | collective-permute-start | bytes 307208 | tf_op jit(solution)/shard_map/ppermute | solution.py:421
  14.2 0.1 collective-permute-start.3
  14.2 6.9 %collective-permute-done.3.corner = f32[32,256]{1,0:T(8,128)S(1)} collective-permute-done((f32[32,256]{1,0:T(8,128)S(1)}, f32[32,256]{1,0:T(8,128)S(1)}, u32[]{:S(2)}, u32[]{:S(2)}) %collective-permute-start.3) | collective-permute-done | bytes 32800 | tf_op jit(solution)/shard_map/ppermute | solution.py:423
  21.2 0.0 collective-permute-start.2
  21.2 3.9 %collective-permute-done.2.side = f32[32,256]{1,0:T(8,128)S(1)} collective-permute-done((f32[32,256]{1,0:T(8,128)S(1)}, f32[32,256]{1,0:T(8,128)S(1)}, u32[]{:S(2)}, u32[]{:S(2)}) %collective-permute-start.2) | collective-permute-done | bytes 32800 | tf_op jit(solution)/shard_map/ppermute | solution.py:422
  25.1 0.0 collective-permute-done.7.far
  25.1 39.5 %first_step.3 = (f32[176,256]{1,0:T(8,128)S(1)}, f32[200,128]{1,0:T(8,128)S(1)}) custom-call(s32[1]{0:T(128)} %bitcast.refs_0_.place, f32[160,256]{1,0:T(8,128)S(1)} %get-tuple-element.24.own, f32[160,256]{1,0:T(8,128)S(1)} %collective-permute-done.6.near, f32[200,128]{1,0:T(8,128)S(1)} %collective-permute-done.7.far, ...), custom_call_target="tpu_custom_call" | custom-call | flops 20000000 | bytes 600000 | tf_op jit(solution)/shard_map/first_step/pallas_call | solution.py:366
  64.6 0.2 collective-permute-start.8
  64.9 39.5 %first_step.2 = (f32[176,256]{1,0:T(8,128)S(1)}, f32[200,128]{1,0:T(8,128)S(1)}) custom-call(s32[1]{0:T(128)} %bitcast.refs_0_.place, f32[160,256]{1,0:T(8,128)S(1)} %get-tuple-element.17.own, f32[160,256]{1,0:T(8,128)S(1)} %collective-permute-done.near, f32[200,128]{1,0:T(8,128)S(1)} %collective-permute-done.1.far, ...), custom_call_target="tpu_custom_call" | custom-call | flops 20000000 | bytes 600000 | tf_op jit(solution)/shard_map/first_step/pallas_call | solution.py:366
  104.4 0.1 collective-permute-start.4
  104.5 3.2 %collective-permute-start.9 = (f32[200,128]{1,0:T(8,128)S(1)}, f32[200,128]{1,0:T(8,128)S(1)}, u32[]{:S(2)}, u32[]{:S(2)}) collective-permute-start(f32[200,128]{1,0:T(8,128)S(1)} %get-tuple-element.27), channel_id=1, source_target_pairs={{0,4},{2,6},{4,8},{6,10},{8,12},{10,14},{12,16},{14,18},{16,20},{1... | collective-permute-start | bytes 307208 | tf_op jit(solution)/shard_map/ppermute | solution.py:421
  107.7 2.7 %collective-permute-start.5 = (f32[200,128]{1,0:T(8,128)S(1)}, f32[200,128]{1,0:T(8,128)S(1)}, u32[]{:S(2)}, u32[]{:S(2)}) collective-permute-start(f32[200,128]{1,0:T(8,128)S(1)} %get-tuple-element.23), channel_id=1, source_target_pairs={{0,4},{2,6},{4,8},{6,10},{8,12},{10,14},{12,16},{14,18},{16,20},{1... | collective-permute-start | bytes 307208 | tf_op jit(solution)/shard_map/ppermute | solution.py:421
  110.5 3.8 %collective-permute-done.9.far = f32[200,128]{1,0:T(8,128)S(1)} collective-permute-done((f32[200,128]{1,0:T(8,128)S(1)}, f32[200,128]{1,0:T(8,128)S(1)}, u32[]{:S(2)}, u32[]{:S(2)}) %collective-permute-start.9) | collective-permute-done | bytes 102432 | tf_op jit(solution)/shard_map/ppermute | solution.py:421
  114.3 37.1 %last_step.2 = (f32[2,32,256]{2,1,0:T(8,128)}, f32[2,2,32,256]{3,2,1,0:T(8,128)}, f32[2,2,32,256]{3,2,1,0:T(8,128)}) custom-call(s32[1]{0:T(128)} %bitcast.refs_0_.place, f32[176,256]{1,0:T(8,128)S(1)} %get-tuple-element.26.own, f32[176,256]{1,0:T(8,128)S(1)} %collective-permute-done.8.near, f32[200,128]{1,0:T(8,128)S(1)} %collective-permute-done.9.far, ...), custom_call_target="tpu_custom_call" | custom-call | flops 20000000 | bytes 600000 | tf_op jit(solution)/shard_map/last_step/pallas_call | solution.py:389
  151.5 37.1 %last_step.3 = (f32[2,32,256]{2,1,0:T(8,128)}, f32[2,2,32,256]{3,2,1,0:T(8,128)}, f32[2,2,32,256]{3,2,1,0:T(8,128)}) custom-call(s32[1]{0:T(128)} %bitcast.refs_0_.place, f32[176,256]{1,0:T(8,128)S(1)} %get-tuple-element.22.own, f32[176,256]{1,0:T(8,128)S(1)} %collective-permute-done.4.near, ...), custom_call_target="tpu_custom_call", output_to_operand_aliasing={{0}: (7, {}), {1}: (8, {}), {2}: (9, {})} | custom-call | flops 20000000 | bytes 600000 | tf_op jit(solution)/shard_map/last_step/pallas_call | solution.py:389
  (11 shorter events, 0.0 us)
Async XLA Ops:
  0.6 0.7 copy-start.4
  0.6 0.7 copy-start.3
  1.3 0.9 copy-start
  2.2 0.9 copy-start.1
  3.1 0.8 copy-start.2
  4.2 20.9 %collective-permute-start.6 = (f32[160,256]{1,0:T(8,128)S(1)}, f32[160,256]{1,0:T(8,128)S(1)}, u32[]{:S(2)}, u32[]{:S(2)}) collective-permute-start(f32[160,256]{1,0:T(8,128)S(1)} %get-tuple-element.24.own), channel_id=1, source_target_pairs={{0,2},{2,4},{4,6},{6,8},{8,10},{10,12},{12,14},{14,16},{16,18},{18... | collective-permute-start | bytes 491528 | tf_op jit(solution)/shard_map/ppermute | solution.py:420
  4.7 60.2 %collective-permute-start = (f32[160,256]{1,0:T(8,128)S(1)}, f32[160,256]{1,0:T(8,128)S(1)}, u32[]{:S(2)}, u32[]{:S(2)}) collective-permute-start(f32[160,256]{1,0:T(8,128)S(1)} %get-tuple-element.17.own), channel_id=1, source_target_pairs={{0,2},{2,4},{4,6},{6,8},{8,10},{10,12},{12,14},{14,16},{16,18},{18... | collective-permute-start | bytes 491528 | tf_op jit(solution)/shard_map/ppermute | solution.py:420
  7.3 17.8 %collective-permute-start.7 = (f32[200,128]{1,0:T(8,128)S(1)}, f32[200,128]{1,0:T(8,128)S(1)}, u32[]{:S(2)}, u32[]{:S(2)}) collective-permute-start(f32[200,128]{1,0:T(8,128)S(1)} %get-tuple-element.25), channel_id=1, source_target_pairs={{0,4},{2,6},{4,8},{6,10},{8,12},{10,14},{12,16},{14,18},{16,20},{1... | collective-permute-start | bytes 307208 | tf_op jit(solution)/shard_map/ppermute | solution.py:421
  10.7 54.1 %collective-permute-start.1 = (f32[200,128]{1,0:T(8,128)S(1)}, f32[200,128]{1,0:T(8,128)S(1)}, u32[]{:S(2)}, u32[]{:S(2)}) collective-permute-start(f32[200,128]{1,0:T(8,128)S(1)} %get-tuple-element.18), channel_id=1, source_target_pairs={{0,4},{2,6},{4,8},{6,10},{8,12},{10,14},{12,16},{14,18},{16,20},{1... | collective-permute-start | bytes 307208 | tf_op jit(solution)/shard_map/ppermute | solution.py:421
  14.2 7.0 %collective-permute-start.3 = (f32[32,256]{1,0:T(8,128)S(1)}, f32[32,256]{1,0:T(8,128)S(1)}, u32[]{:S(2)}, u32[]{:S(2)}) collective-permute-start(f32[32,256]{1,0:T(8,128)S(1)} %get-tuple-element.19), channel_id=1, source_target_pairs={{0,3},{1,2},{2,5},{3,4},{4,7},{5,6},{6,9},{7,8},{8,11},{9,10},{10,... | collective-permute-start | bytes 98312 | tf_op jit(solution)/shard_map/ppermute | solution.py:423
  21.2 3.9 %collective-permute-start.2 = (f32[32,256]{1,0:T(8,128)S(1)}, f32[32,256]{1,0:T(8,128)S(1)}, u32[]{:S(2)}, u32[]{:S(2)}) collective-permute-start(f32[32,256]{1,0:T(8,128)S(1)} %get-tuple-element.19), channel_id=1, source_target_pairs={{0,1},{1,0},{2,3},{3,2},{4,5},{5,4},{6,7},{7,6},{8,9},{9,8},{10,11... | collective-permute-start | bytes 98312 | tf_op jit(solution)/shard_map/ppermute | solution.py:422
  64.6 49.7 %collective-permute-start.8 = (f32[176,256]{1,0:T(8,128)S(1)}, f32[176,256]{1,0:T(8,128)S(1)}, u32[]{:S(2)}, u32[]{:S(2)}) collective-permute-start(f32[176,256]{1,0:T(8,128)S(1)} %get-tuple-element.26.own), channel_id=1, source_target_pairs={{0,2},{2,4},{4,6},{6,8},{8,10},{10,12},{12,14},{14,16},{16,18},{18... | collective-permute-start | bytes 540680 | tf_op jit(solution)/shard_map/ppermute | solution.py:420
  104.4 47.0 %collective-permute-start.4 = (f32[176,256]{1,0:T(8,128)S(1)}, f32[176,256]{1,0:T(8,128)S(1)}, u32[]{:S(2)}, u32[]{:S(2)}) collective-permute-start(f32[176,256]{1,0:T(8,128)S(1)} %get-tuple-element.22.own), channel_id=1, source_target_pairs={{0,2},{2,4},{4,6},{6,8},{8,10},{10,12},{12,14},{14,16},{16,18},{18... | collective-permute-start | bytes 540680 | tf_op jit(solution)/shard_map/ppermute | solution.py:420
  104.5 9.8 %collective-permute-start.9 = (f32[200,128]{1,0:T(8,128)S(1)}, f32[200,128]{1,0:T(8,128)S(1)}, u32[]{:S(2)}, u32[]{:S(2)}) collective-permute-start(f32[200,128]{1,0:T(8,128)S(1)} %get-tuple-element.27), channel_id=1, source_target_pairs={{0,4},{2,6},{4,8},{6,10},{8,12},{10,14},{12,16},{14,18},{16,20},{1... | collective-permute-start | bytes 307208 | tf_op jit(solution)/shard_map/ppermute | solution.py:421
  107.7 43.8 %collective-permute-start.5 = (f32[200,128]{1,0:T(8,128)S(1)}, f32[200,128]{1,0:T(8,128)S(1)}, u32[]{:S(2)}, u32[]{:S(2)}) collective-permute-start(f32[200,128]{1,0:T(8,128)S(1)} %get-tuple-element.23), channel_id=1, source_target_pairs={{0,4},{2,6},{4,8},{6,10},{8,12},{10,14},{12,16},{14,18},{16,20},{1... | collective-permute-start | bytes 307208 | tf_op jit(solution)/shard_map/ppermute | solution.py:421

commit v3 on v2

v3 whole, which is shorter than its diff:
```python
import jax
import jax.numpy as jnp
from jax import lax
from jax.experimental import pallas as pl
from jax.experimental.pallas import tpu as pltpu
from jax.sharding import PartitionSpec as P

STEPS = 2
SMIN = 8
SMAX = 56
STAGES = 3
REACH = 2 * STAGES
FIELDS = 5
LANES = 128
SUB = 8
HALF = LANES // 2
SLOTS = 2 * SUB
EXTRA = 2 * SUB
TALL = 32
ROWS = 4
VMEM_LIMIT = 32 * 1024 * 1024

time_step = 0.08
sound_sq = 1.0


def shift_bound(first_row, rows):
    d = rows - 1 - first_row
    return min(SMIN + (SMAX - SMIN - 1) * d * d // ((rows - 1) * (rows - 1)) + 1, SMAX)


def minmod(lower, upper):
    return jnp.maximum(jnp.minimum(lower, 0.0), jnp.minimum(upper, jnp.maximum(lower, 0.0)))


def physical(state):
    rho, mn, mt, bn, bt = state
    inverse = pltpu.reciprocal(rho, approx=True)
    vn = mn * inverse
    vt = mt * inverse
    bn_sq = bn * bn
    bt_sq = bt * bt
    flux_n = mn * vn + (sound_sq * rho + 0.5 * (bt_sq - bn_sq))
    flux_t = mt * vn - bn * bt
    flux_b = bt * vn - bn * vt
    inside = sound_sq + (bn_sq + bt_sq) * inverse
    speed = jnp.abs(vn) + inside * lax.rsqrt(inside)
    return (mn, flux_n, flux_t, None, flux_b), speed


def face_twice(left, right):
    left_flux, left_speed = physical(left)
    right_flux, right_speed = physical(right)
    bound = jnp.maximum(left_speed, right_speed)
    out = []
    for k in range(FIELDS):
        jump = bound * (right[k] - left[k])
        if left_flux[k] is None:
            out.append(-jump)
        else:
            out.append((left_flux[k] + right_flux[k]) - jump)
    return out


def swapped(five):
    return [five[0], five[2], five[1], five[4], five[3]]


def radial_faces(rows):
    halves = [[0.5 * x for x in r] for r in rows]
    jumps = [[b - a for a, b in zip(p, q)] for p, q in zip(halves[:-1], halves[1:])]
    slopes = [[minmod(a, b) for a, b in zip(p, q)] for p, q in zip(jumps[:-1], jumps[1:])]
    upper = [[x + s for x, s in zip(r, sl)] for r, sl in zip(rows[1:-1], slopes)]
    lower = [[x - s for x, s in zip(r, sl)] for r, sl in zip(rows[1:-1], slopes)]
    return [swapped(face_twice(swapped(u), swapped(l))) for u, l in zip(upper[:-1], lower[1:])]


def azimuth_change(fields):
    right_of = lambda x: pltpu.roll(x, LANES - 1, 1)
    left_of = lambda x: pltpu.roll(x, 1, 1)
    lower = []
    upper = []
    for x in fields:
        half = 0.5 * x
        slope = minmod(half - left_of(half), right_of(half) - half)
        upper.append(x + slope)
        lower.append(right_of(x - slope))
    return [x - left_of(x) for x in face_twice(upper, lower)]


def tile(i):
    return pl.ds(pl.multiple_of(i * SUB, SUB), SUB)


def run_stages(n, levels, stages, edges):
    half_dt = 0.5 * time_step
    low_mask, high_mask = edges
    first, last = REACH, REACH + n - 1
    spin_at = levels * FIELDS

    def work(stage, i0, count, before):
        src, dst = stage, (stage & 1) + 1
        later = stage > 0
        weight = jnp.where(later, jnp.where(stage == 1, 0.25, 2.0 / 3.0), 1.0)
        keep = jnp.where(later, jnp.where(stage == 1, 0.75, 1.0 / 3.0), 0.0)
        load = lambda level, k: [stages[src, level * FIELDS + f, tile(i0 + k), :] for f in range(FIELDS)]
        rows = [[load(level, k) for k in range(-1, count + 2)] for level in range(levels)]
        turns = [stages[0, spin_at, tile(i0 + k), :] for k in range(count)]
        after = []
        for level in range(levels):
            faces = [before[level * FIELDS : (level + 1) * FIELDS]] + radial_faces(rows[level])
            for k in range(count):
                fields = rows[level][k + 1]
                change = azimuth_change(fields)
                turn = turns[k]
                source = [
                    None,
                    (-0.5 * turn) * fields[2],
                    (2.0 * turn) * fields[1],
                    (-1.5 * turn) * fields[4],
                    None,
                ]
                for f in range(FIELDS):
                    new = fields[f] - half_dt * (change[f] + (faces[k + 1][f] - faces[k][f]))
                    if source[f] is not None:
                        new = new + source[f]
                    at = level * FIELDS + f
                    stages[dst, at, tile(i0 + k), :] = weight * new + keep * stages[0, at, tile(i0 + k), :]
            after += faces[-1]
        return after

    def run(stage, _):
        for at in range(levels * FIELDS):
            inner = stages[stage, at, tile(first), :]
            outer = stages[stage, at, tile(last), :]
            for k in (1, 2):
                stages[stage, at, tile(first - k), :] = jnp.where(low_mask, inner, stages[stage, at, tile(first - k), :])
                stages[stage, at, tile(last + k), :] = jnp.where(high_mask, outer, stages[stage, at, tile(last + k), :])
        lo = 2 * stage + 2
        count = n + 2 * REACH - 4 - 4 * stage
        before = []
        for level in range(levels):
            rows = [[stages[stage, level * FIELDS + f, tile(lo + k), :] for f in range(FIELDS)] for k in range(-2, 2)]
            before += radial_faces(rows)[0]
        turns = lax.div(count + ROWS - 1, ROWS)
        lax.fori_loop(0, turns, lambda c, carried: tuple(work(stage, lo + c * ROWS, ROWS, list(carried))), tuple(before))
        return 0

    lax.fori_loop(0, STAGES, run, 0)


def spread(block, first, width):
    block = pltpu.roll(block, (LANES - first) % LANES, 1)
    lane = lax.broadcasted_iota(jnp.int32, block.shape, 1)
    while width < LANES:
        block = jnp.where(lane < width, block, pltpu.roll(block, width, 1))
        width *= 2
    return block


def pack_far(far, near, levels, own_cells, spare):
    sublane = lax.broadcasted_iota(jnp.int32, (SUB, LANES), 0)

    def one(k, _):
        level, f = lax.div(k, FIELDS), lax.rem(k, FIELDS)
        start = pl.multiple_of(f * own_cells, SUB)
        base = pl.multiple_of(f * (own_cells + SUB), SUB)
        low = near[level, pl.ds(start, own_cells), 0:LANES]
        high = near[level, pl.ds(start + own_cells - 2 * SUB, 2 * SUB), LANES : 2 * LANES]
        moved = pltpu.roll(high[0:SUB], spare, 0)
        far[level, pl.ds(base, SUB), :] = jnp.where(sublane < spare, moved, low[0:SUB])
        far[level, pl.ds(base + SUB, own_cells - SUB), :] = low[SUB:]
        far[level, pl.ds(base + own_cells, SUB), :] = high[SUB:]
        return 0

    lax.fori_loop(0, levels * FIELDS, one, 0)


def pack_kernel(spare, place, density, momentum, magnetic, rotation, shifts, near, far, edge, spin_rows, shift_rows, arrived):
    levels, own_cells, radius = density.shape
    on_low = place[0] == 0
    parts = radius // LANES
    copies = []
    for level in range(levels):
        sources = [density.at[level]] + [x.at[k, level] for x in (momentum, magnetic) for k in range(2)]
        for f, x in enumerate(sources):
            at = near.at[level, pl.ds(f * own_cells, own_cells), :]
            copies.append(pltpu.make_async_copy(x, at, arrived.at[level * FIELDS + f]))
    for copy in copies:
        copy.start()
    for part in range(parts):
        rows = slice(part * LANES, (part + 1) * LANES)
        spin_rows[rows, :] = jnp.broadcast_to(rotation[part : part + 1, :], (LANES, LANES)).T * time_step
        shift_rows[rows, :] = jnp.broadcast_to(shifts[part : part + 1, :].astype(jnp.float32), (LANES, LANES)).T
    wide = lambda ref: jnp.broadcast_to(
        jnp.where(on_low, ref[parts - 1 : parts, :], ref[0:1, :]).astype(jnp.float32), (own_cells, LANES)
    )
    for copy in copies:
        copy.wait()
    pack_far(far, near, levels, own_cells, spare)
    turn = wide(rotation) * time_step
    shift = wide(shifts)
    zero = jnp.zeros((own_cells, LANES), jnp.float32)

    def ends(level, _):
        rows = near[level, 0 : FIELDS * own_cells, :]
        block = jnp.where(on_low, rows[:, radius - LANES :], rows[:, 0:LANES])
        split = 4 * own_cells
        for side, group in enumerate((block[0:split], jnp.concatenate([block[split:], turn, shift, zero], axis=0))):
            turned = group.T
            edge[level, :, side * LANES : (side + 1) * LANES] = jnp.where(on_low, turned[LANES - EXTRA :], turned[0:EXTRA])
        return 0

    lax.fori_loop(0, levels, ends, 0)


def step_kernel(plan, refs, write, scratch):
    n, levels, radius, own_cells, total, row_count, spare, moved = plan
    place, own, own_edge, near, near_edge, far, side, spin_rows, shift_rows = refs
    cells, stages, packed = scratch
    row = place[0]
    on_low = row == 0
    lane = lax.broadcasted_iota(jnp.int32, (SUB, LANES), 1)
    sublane = lax.broadcasted_iota(jnp.int32, (SUB, LANES), 0)
    base = jnp.where(on_low, 0, -moved)
    own_at = pl.multiple_of(EXTRA - base, SUB)
    edge_at = pl.multiple_of(jnp.where(on_low, EXTRA + radius, moved), SUB)
    bounds = []
    for k in range(SLOTS):
        known = [shift_bound(r * radius - (moved if r else 0) + n * k, total) for r in range(row_count)]
        bounds.append(jnp.where(on_low, known[0], known[1]))

    edge_lane = lax.broadcasted_iota(jnp.int32, (EXTRA, LANES), 1)
    parts = radius // LANES

    def gather(k, _):
        level, f = lax.div(k, FIELDS), lax.rem(k, FIELDS)
        rows = pl.ds(pl.multiple_of(f * own_cells, SUB), own_cells)
        start = pl.multiple_of(f * (own_cells + SUB), SUB)
        for part in range(parts):
            columns = slice(part * LANES, (part + 1) * LANES)
            if part == 0:
                top = far[level, pl.ds(start, own_cells), :]
            else:
                top = jnp.concatenate(
                    [
                        jnp.zeros((own_cells - 2 * SUB, LANES), jnp.float32),
                        pltpu.roll(far[level, pl.ds(start, SUB), :], SUB - spare, 0),
                        far[level, pl.ds(start + own_cells, SUB), :],
                    ],
                    axis=0,
                )
            fill = jnp.zeros((own_cells, LANES), jnp.float32)
            block = jnp.concatenate([top, near[level, rows, columns], own[level, rows, columns], fill], axis=0)
            cells[k, pl.ds(own_at + part * LANES, LANES), :] = block.T
        columns = pl.ds(pl.multiple_of(lax.div(f, 4) * LANES, LANES), LANES)
        lanes_at = lax.rem(f, 4) * own_cells
        cells[k, pl.ds(edge_at, EXTRA), :] = jnp.where(
            edge_lane < 2 * own_cells,
            pltpu.roll(near_edge[level, :, columns], lax.rem(LANES + own_cells - lanes_at, LANES), 1),
            pltpu.roll(own_edge[level, :, columns], lax.rem(LANES + 2 * own_cells - lanes_at, LANES), 1),
        )
        return 0

    lax.fori_loop(0, levels * FIELDS, gather, 0)
    spin_at = levels * FIELDS
    more = side[0, :, LANES : 2 * LANES]
    cells[spin_at, pl.ds(own_at, radius), :] = spin_rows[...]
    cells[spin_at, pl.ds(edge_at, EXTRA), :] = spread(more, own_cells, own_cells)
    cells[spin_at + 1, pl.ds(own_at, radius), :] = shift_rows[...]
    cells[spin_at + 1, pl.ds(edge_at, EXTRA), :] = spread(more, 2 * own_cells, own_cells)

    front = lax.broadcasted_iota(jnp.int32, (TALL, LANES), 1) < HALF

    def deal(k, _):
        for j in range(SUB):
            low, high = j, SUB + j
            at = [slice(EXTRA - REACH + n * b, EXTRA - REACH + n * b + TALL) for b in (low, high)]
            turn_low = (LANES - (2 * own_cells - REACH)) + bounds[low]
            turn_high = (HALF - (2 * own_cells - REACH)) + bounds[high]
            stages[0, k, pl.ds(j, TALL, stride=SUB), :] = jnp.where(
                front, pltpu.roll(cells[k, at[0], :], turn_low, 1), pltpu.roll(cells[k, at[1], :], turn_high, 1)
            )
        return 0

    lax.fori_loop(0, levels * FIELDS + 2, deal, 0)

    edges = (
        (sublane == 0) & (lane < HALF) & on_low,
        (sublane == SUB - 1) & (lane >= HALF) & (row == row_count - 1),
    )
    run_stages(n, levels, stages, edges)

    bound = jnp.zeros((SUB, LANES), jnp.int32)
    for j in range(SUB):
        bound = jnp.where(sublane == j, jnp.where(lane < HALF, bounds[j], bounds[SUB + j]), bound)
    even = (lane & own_cells) == 0

    def shift(i, _):
        rows = tile(REACH + i)
        source = (lane + (REACH + bound)) - stages[0, spin_at + 1, rows, :].astype(jnp.int32)
        picks = [source & (LANES - 1), (source - own_cells) & (LANES - 1)]
        for level in range(levels):
            turned = [
                jnp.take_along_axis(
                    stages[1, level * FIELDS + f, rows, :], picks[f % 2], axis=1, mode="promise_in_bounds"
                )
                for f in range(FIELDS)
            ]
            stages[2, level * FIELDS, tile(i), :] = jnp.where(even, turned[0], turned[1])
            stages[2, level * FIELDS + 1, tile(i), :] = jnp.where(even, turned[2], turned[3])
            stages[2, level * FIELDS + 2, tile(i), :] = turned[4]
        return 0

    lax.fori_loop(0, n, shift, 0)
    narrow = lax.broadcasted_iota(jnp.int32, (n, LANES), 1) < HALF

    def finish(level, _):
        for j in range(SUB):
            one, two, three = [stages[2, level * FIELDS + g, pl.ds(j, n, stride=SUB), :] for g in range(3)]
            low = slice(EXTRA + n * j, EXTRA + n * (j + 1))
            high = slice(EXTRA + n * (SUB + j), EXTRA + n * (SUB + j + 1))
            packed[0, low, :] = jnp.where(narrow, one, pltpu.roll(two, HALF, 1))
            packed[0, high, :] = jnp.where(narrow, pltpu.roll(one, HALF, 1), two)
            packed[1, low, :] = three
            packed[1, high, :] = pltpu.roll(three, HALF, 1)
        for part in range(parts):
            rows = pl.ds(own_at + part * LANES, LANES)
            write.fields(level, slice(part * LANES, (part + 1) * LANES), packed[0, rows, :].T, packed[1, rows, :].T)
        write.edge(level, packed[0, pl.ds(edge_at, EXTRA), :], packed[1, pl.ds(edge_at, EXTRA), :])
        return 0

    lax.fori_loop(0, levels, finish, 0)
    write.end()


class ToMessage:
    def __init__(self, near, far, own_cells, spare):
        self.near, self.far, self.own_cells, self.spare = near, far, own_cells, spare

    def fields(self, level, columns, four, fifth):
        split = 4 * self.own_cells
        self.near[level, 0:split, columns] = four
        self.near[level, split : split + self.own_cells, columns] = fifth[0 : self.own_cells]

    def edge(self, level, first, second):
        tail = FIELDS * self.own_cells
        self.near[level, tail : tail + EXTRA, 0:LANES] = first
        self.near[level, tail : tail + EXTRA, LANES : 2 * LANES] = second

    def end(self):
        pack_far(self.far, self.near, self.near.shape[0], self.own_cells, self.spare)


class ToResult:
    def __init__(self, density, momentum, magnetic):
        self.outs = (density, momentum, magnetic)

    def fields(self, level, columns, four, fifth):
        density, momentum, magnetic = self.outs
        cells = density.shape[1]
        density[level, :, columns] = four[0:cells]
        momentum[0, level, :, columns] = four[cells : 2 * cells]
        momentum[1, level, :, columns] = four[2 * cells : 3 * cells]
        magnetic[0, level, :, columns] = four[3 * cells : 4 * cells]
        magnetic[1, level, :, columns] = fifth[0:cells]

    def edge(self, level, first, second):
        pass

    def end(self):
        pass


def step_scratch(n, levels):
    tall = EXTRA + SLOTS * n + 2 * SUB
    count = levels * FIELDS + 2
    return [
        pltpu.VMEM((count, tall, LANES), jnp.float32),
        pltpu.VMEM((STAGES, count, TALL * SUB, LANES), jnp.float32),
        pltpu.VMEM((2, tall, LANES), jnp.float32),
    ]


vmem = pl.BlockSpec(memory_space=pltpu.VMEM)
smem = pl.BlockSpec(memory_space=pltpu.SMEM)
f32 = lambda *s: jax.ShapeDtypeStruct(s, jnp.float32)
params = pltpu.CompilerParams(vmem_limit_bytes=VMEM_LIMIT)
cost = pl.CostEstimate(flops=20_000_000, bytes_accessed=600_000, transcendentals=0)


def first_step(plan, operands):
    n, levels, radius, own_cells, total, row_count, spare, moved = plan

    def kernel(place, own, near, far, side, corner, spin_rows, shift_rows, near_out, far_out, *scratch):
        refs = (place, own, side, near, corner, far, side, spin_rows, shift_rows)
        step_kernel(plan, refs, ToMessage(near_out, far_out, own_cells, spare), scratch)

    return pl.pallas_call(
        kernel,
        out_shape=[f32(levels, FIELDS * own_cells + EXTRA, radius), f32(levels, FIELDS * (own_cells + SUB), LANES)],
        in_specs=[smem] + [vmem] * 7,
        out_specs=[vmem] * 2,
        scratch_shapes=step_scratch(n, levels),
        compiler_params=params,
        cost_estimate=cost,
        name="first_step",
    )(*operands)


def last_step(plan, operands):
    n, levels, radius, own_cells, total, row_count, spare, moved = plan
    tail = pl.ds(FIELDS * own_cells, EXTRA)

    def kernel(place, own, near, far, side, spin_rows, shift_rows, density, momentum, magnetic, *scratch):
        edge_of = lambda ref: ref.at[:, tail, :]
        refs = (place, own, edge_of(own), near, edge_of(near), far, side, spin_rows, shift_rows)
        step_kernel(plan, refs, ToResult(density, momentum, magnetic), scratch)

    return pl.pallas_call(
        kernel,
        out_shape=[f32(levels, own_cells, radius), f32(2, levels, own_cells, radius), f32(2, levels, own_cells, radius)],
        in_specs=[smem] + [vmem] * 6,
        out_specs=[vmem] * 3,
        scratch_shapes=step_scratch(n, levels),
        compiler_params=params,
        cost_estimate=cost,
        name="last_step",
    )(*operands)


def body(density, momentum, magnetic, rotation, shifts):
    phi_count = lax.axis_size("phi")
    row_count = lax.axis_size("row")
    levels, own_cells, radius = density.shape
    total = radius * row_count
    parts = radius // LANES
    n = radius // SLOTS
    need = [max(shift_bound(part * LANES, total) + REACH - own_cells, 0) for part in range(parts)]
    spare = own_cells - need[0]
    assert row_count == 2 and radius == 2 * LANES and own_cells == HALF // 2
    assert 0 < need[0] < own_cells and need[1] <= SUB + spare and spare <= SUB

    row = lax.axis_index("row")
    place = jnp.reshape(row, (1,)).astype(jnp.int32)
    here = lambda p, r: (p % phi_count) * row_count + r
    everyone = [(p, r) for p in range(phi_count) for r in range(row_count)]
    both = ("phi", "row")
    send_near = lambda x: lax.ppermute(x, "phi", [(p, (p + 1) % phi_count) for p in range(phi_count)])
    send_far = lambda x: lax.ppermute(x, both, [(here(p, 0), here(p + 2, 0)) for p in range(phi_count)])
    send_side = lambda x: lax.ppermute(x, "row", [(0, 1), (1, 0)])
    send_corner = lambda x: lax.ppermute(x, both, [(here(p, r), here(p + 1, 1 - r)) for p, r in everyone])

    own, far, edge, spin_rows, shift_rows = pl.pallas_call(
        lambda *refs: pack_kernel(spare, *refs),
        out_shape=[
            f32(levels, FIELDS * own_cells, radius),
            f32(levels, FIELDS * (own_cells + SUB), LANES),
            f32(levels, EXTRA, 2 * LANES),
            f32(radius, LANES),
            f32(radius, LANES),
        ],
        in_specs=[smem] + [pl.BlockSpec(memory_space=pl.ANY)] * 3 + [vmem] * 2,
        out_specs=[vmem] * 5,
        scratch_shapes=[pltpu.SemaphoreType.DMA((levels * FIELDS,))],
        compiler_params=params,
        name="pack",
    )(place, density, momentum, magnetic, rotation.reshape(parts, LANES), shifts.reshape(parts, LANES))

    side = send_side(edge)
    corner = send_corner(edge)
    plan = (n + 1, levels, radius, own_cells, total, row_count, spare, EXTRA)
    own, far = first_step(plan, (place, own, send_near(own), send_far(far), side, corner, spin_rows, shift_rows))
    plan = (n, levels, radius, own_cells, total, row_count, spare, 0)
    return tuple(last_step(plan, (place, own, send_near(own), send_far(far), side, spin_rows, shift_rows)))


def solution(mesh):
    placed = (
        P(None, "phi", "row"),
        P(None, None, "phi", "row"),
        P(None, None, "phi", "row"),
        P("row"),
        P("row"),
    )
    return jax.shard_map(
        body,
        mesh=mesh,
        in_specs=placed,
        out_specs=(P(None, "phi", "row"), P(None, None, "phi", "row"), P(None, None, "phi", "row")),
        check_vma=False,
    )
```

time: 189 us -> 65.8 us (0.35)
  Pallas kernels: 154 us -> 33.9 us
  starting transfers between devices: 16.3 us -> 10.4 us
  waiting for transfers between devices: 14.7 us -> 17 us
    pallas_call x5 -> x3, Pallas kernels: 154 us -> 33.9 us  [the longest x1 17.3 us: first_step(): pl.pallas_call(kernel, out_shape=[f32(levels, FIELDS * own_cells + EXTRA,...]
    ppermute x4 -> x2, waiting for transfers between devices: 3.85 us -> 12.7 us  [body(): lax.ppermute(x, both, [(here(p, 0), here(p + 2, 0)) for p in range(phi_co...]
    ppermute x4 -> x2, starting transfers between devices: 12.8 us -> 6.34 us  [body(): lax.ppermute(x, both, [(here(p, 0), here(p + 2, 0)) for p in range(phi_co...]
    ppermute x1, waiting for transfers between devices: 3.91 us -> 0.01 us  [body(): send_side = lambda x: lax.ppermute(x, 'row', [(0, 1), (1, 0)])]
    ppermute x1, starting transfers between devices: 0.01 us -> 2.95 us  [body(): send_side = lambda x: lax.ppermute(x, 'row', [(0, 1), (1, 0)])]
    ppermute x1, waiting for transfers between devices: 6.94 us -> 4.36 us  [body(): lax.ppermute(x, both, [(here(p, r), here(p + 1, 1 - r)) for p, r in every...]
    ppermute x4 -> x2, starting transfers between devices: 3.43 us -> 1.06 us  [body(): lax.ppermute(x, 'phi', [(p, (p + 1) % phi_count) for p in range(phi_count)])]
  transfers between devices with their start and end apart: 10 -> 6, of which waited for: 3 -> 3; matrix products, arithmetic and copies ran while one was open for 0% -> 0% of each run, Pallas kernels for 62% -> 0%
where the time goes in v3:
time: 65.8 us; the launch traced here: 65.4 us
  Pallas kernels  33.9 us (52%)
  waiting for transfers between devices  17 us (26%)
  starting transfers between devices  10.4 us (16%)
  local copies, waits for them, and re-layouts  3.33 us (5%)
  between operations  0.7 us (1%)
    pallas_call x1, Pallas kernels, first_step(): pl.pallas_call(kernel, out_shape=[f32(levels, FIELDS * own_cells + EXTRA,...  17.3 us
    pallas_call x1, Pallas kernels, last_step(): pl.pallas_call(kernel, out_shape=[f32(levels, own_cells, radius), f32(2,...  15.6 us
    ppermute x2, waiting for transfers between devices, body(): lax.ppermute(x, both, [(here(p, 0), here(p + 2, 0)) for p in range(phi_co...  12.7 us
    ppermute x2, starting transfers between devices, body(): lax.ppermute(x, both, [(here(p, 0), here(p + 2, 0)) for p in range(phi_co...  6.34 us
    ppermute x1, waiting for transfers between devices, body(): lax.ppermute(x, both, [(here(p, r), here(p + 1, 1 - r)) for p, r in every...  4.36 us
    unnamed x10, local copies, waits for them, and re-layouts  3.33 us
    ppermute x1, starting transfers between devices, body(): send_side = lambda x: lax.ppermute(x, 'row', [(0, 1), (1, 0)])  2.95 us
  transfers between devices with their start and end apart: 6, of which 3 were waited for; matrix products, arithmetic and copies ran while one was open for 0% of the time, Pallas kernels for 0%

profile of v3, /device:TPU:0, one launch (start us, length us, event | category | flops | bytes accessed | tf_op | source)
XLA Modules:
  0.0 65.4 jit_solution(18004985986387914953)
XLA Ops:
  0.6 0.0 copy-start.4
  0.6 0.0 copy-start.3
  0.7 0.7 %copy-done.4 = s32[256]{0:T(256)S(1)} copy-done((s32[256]{0:T(256)S(1)}, s32[256]{0:T(256)}, u32[]{:S(2)}) %copy-start.4) | copy-done | bytes 1048
  1.3 0.0 copy-done.3
  1.3 0.0 copy-start
  1.3 0.9 %copy-done = f32[2,2,32,256]{3,2,1,0:T(8,128)S(1)} copy-done((f32[2,2,32,256]{3,2,1,0:T(8,128)S(1)}, f32[2,2,32,256]{3,2,1,0:T(8,128)}, u32[]{:S(2)}) %copy-start) | copy-done | bytes 131096
  2.2 0.9 %copy-done.1 = f32[2,2,32,256]{3,2,1,0:T(8,128)S(1)} copy-done((f32[2,2,32,256]{3,2,1,0:T(8,128)S(1)}, f32[2,2,32,256]{3,2,1,0:T(8,128)}, u32[]{:S(2)}) %copy-start.1) | copy-done | bytes 131096
  3.1 0.0 copy-start.2
  3.1 0.8 %copy-done.2 = f32[2,32,256]{2,1,0:T(8,128)S(1)} copy-done((f32[2,32,256]{2,1,0:T(8,128)S(1)}, f32[2,32,256]{2,1,0:T(8,128)}, u32[]{:S(2)}) %copy-start.2) | copy-done | bytes 65560
  4.0 1.0 %pack.1 = (f32[2,160,256]{2,1,0:T(8,128)S(1)}, f32[2,200,128]{2,1,0:T(8,128)S(1)}, f32[2,16,256]{2,1,0:T(8,128)S(1)}, f32[256,128]{1,0:T(8,128)S(1)}, f32[256,128]{1,0:T(8,128)S(1)}) custom-call(s32[1]{0:T(128)} %bitcast.refs_0_.place, f32[2,32,256]{2,1,0:T(8,128)S(1)} %copy-done.2, f32[2,2,32,256]{3,2,1,0:T(8,128)S(1)} %copy-done, ...), custom_call_target="tpu_custom_call" | custom-call | tf_op jit(solution)/shard_map/pack/pallas_call | solution.py:454
  5.0 0.5 collective-permute-start
  5.5 4.4 %collective-permute-start.1 = (f32[2,200,128]{2,1,0:T(8,128)S(1)}, f32[2,200,128]{2,1,0:T(8,128)S(1)}, u32[]{:S(2)}, u32[]{:S(2)}) collective-permute-start(f32[2,200,128]{2,1,0:T(8,128)S(1)} %get-tuple-element.11), channel_id=1, source_target_pairs={{0,4},{2,6},{4,8},{6,10},{8,12},{10,14},{12,16},{14,18},{16,20},{1... | collective-permute-start | bytes 614408 | tf_op jit(solution)/shard_map/ppermute | solution.py:450
  9.9 0.1 collective-permute-start.3
  10.0 2.9 %collective-permute-start.2 = (f32[2,16,256]{2,1,0:T(8,128)S(1)}, f32[2,16,256]{2,1,0:T(8,128)S(1)}, u32[]{:S(2)}, u32[]{:S(2)}) collective-permute-start(f32[2,16,256]{2,1,0:T(8,128)S(1)} %get-tuple-element.12), channel_id=1, source_target_pairs={{0,1},{1,0},{2,3},{3,2},{4,5},{5,4},{6,7},{7,6},{8,9},{9,8},{10,11... | collective-permute-start | bytes 98312 | tf_op jit(solution)/shard_map/ppermute | solution.py:451
  12.9 4.4 %collective-permute-done.3.corner = f32[2,16,256]{2,1,0:T(8,128)S(1)} collective-permute-done((f32[2,16,256]{2,1,0:T(8,128)S(1)}, f32[2,16,256]{2,1,0:T(8,128)S(1)}, u32[]{:S(2)}, u32[]{:S(2)}) %collective-permute-start.3) | collective-permute-done | bytes 32800 | tf_op jit(solution)/shard_map/ppermute | solution.py:452
  17.3 0.0 collective-permute-done.2.side
  17.3 2.0 %collective-permute-done.1.far = f32[2,200,128]{2,1,0:T(8,128)S(1)} collective-permute-done((f32[2,200,128]{2,1,0:T(8,128)S(1)}, f32[2,200,128]{2,1,0:T(8,128)S(1)}, u32[]{:S(2)}, u32[]{:S(2)}) %collective-permute-start.1) | collective-permute-done | bytes 204832 | tf_op jit(solution)/shard_map/ppermute | solution.py:450
  19.3 0.0 collective-permute-done.near
  19.3 17.3 %first_step.1 = (f32[2,176,256]{2,1,0:T(8,128)S(1)}, f32[2,200,128]{2,1,0:T(8,128)S(1)}) custom-call(s32[1]{0:T(128)} %bitcast.refs_0_.place, f32[2,160,256]{2,1,0:T(8,128)S(1)} %get-tuple-element.10.own, f32[2,160,256]{2,1,0:T(8,128)S(1)} %collective-permute-done.near, f32[2,200,128]{2,1,0:T(8,128)S(1)} %collective-permute-done.1.far, ...), custom_call_target="tpu_custom_call" | custom-call | flops 20000000 | bytes 600000 | tf_op jit(solution)/shard_map/first_step/pallas_call | solution.py:399
  36.6 0.6 collective-permute-start.4
  37.2 1.9 %collective-permute-start.5 = (f32[2,200,128]{2,1,0:T(8,128)S(1)}, f32[2,200,128]{2,1,0:T(8,128)S(1)}, u32[]{:S(2)}, u32[]{:S(2)}) collective-permute-start(f32[2,200,128]{2,1,0:T(8,128)S(1)} %get-tuple-element.16), channel_id=1, source_target_pairs={{0,4},{2,6},{4,8},{6,10},{8,12},{10,14},{12,16},{14,18},{16,20},{1... | collective-permute-start | bytes 614408 | tf_op jit(solution)/shard_map/ppermute | solution.py:450
  39.1 10.7 %collective-permute-done.5.far = f32[2,200,128]{2,1,0:T(8,128)S(1)} collective-permute-done((f32[2,200,128]{2,1,0:T(8,128)S(1)}, f32[2,200,128]{2,1,0:T(8,128)S(1)}, u32[]{:S(2)}, u32[]{:S(2)}) %collective-permute-start.5) | collective-permute-done | bytes 204832 | tf_op jit(solution)/shard_map/ppermute | solution.py:450
  49.8 0.0 collective-permute-done.4.near
  49.8 15.6 %last_step.1 = (f32[2,32,256]{2,1,0:T(8,128)}, f32[2,2,32,256]{3,2,1,0:T(8,128)}, f32[2,2,32,256]{3,2,1,0:T(8,128)}) custom-call(s32[1]{0:T(128)} %bitcast.refs_0_.place, f32[2,176,256]{2,1,0:T(8,128)S(1)} %get-tuple-element.15.own, f32[2,176,256]{2,1,0:T(8,128)S(1)} %collective-permute-done.4.near, f32[2,200,128]{2,1,0:T(8,128)S(1)} %collective-permute-done.5.far, ...), custom_call_target="tpu_custom_call" | custom-call | flops 20000000 | bytes 600000 | tf_op jit(solution)/shard_map/last_step/pallas_call | solution.py:420
  (1 shorter events, 0.0 us)
Async XLA Ops:
  0.6 0.7 %copy-start.4 = (s32[256]{0:T(256)S(1)}, s32[256]{0:T(256)}, u32[]{:S(2)}) copy-start(s32[256]{0:T(256)} %param.9) | copy-start | bytes 3076
  0.6 0.7 %copy-start.3 = (f32[256]{0:T(256)S(1)}, f32[256]{0:T(256)}, u32[]{:S(2)}) copy-start(f32[256]{0:T(256)} %param.8) | copy-start | bytes 3076
  1.3 0.9 %copy-start = (f32[2,2,32,256]{3,2,1,0:T(8,128)S(1)}, f32[2,2,32,256]{3,2,1,0:T(8,128)}, u32[]{:S(2)}) copy-start(f32[2,2,32,256]{3,2,1,0:T(8,128)} %refs_2_.1) | copy-start | bytes 393220
  2.2 0.9 %copy-start.1 = (f32[2,2,32,256]{3,2,1,0:T(8,128)S(1)}, f32[2,2,32,256]{3,2,1,0:T(8,128)}, u32[]{:S(2)}) copy-start(f32[2,2,32,256]{3,2,1,0:T(8,128)} %refs_3_.1) | copy-start | bytes 393220
  3.1 0.8 %copy-start.2 = (f32[2,32,256]{2,1,0:T(8,128)S(1)}, f32[2,32,256]{2,1,0:T(8,128)}, u32[]{:S(2)}) copy-start(f32[2,32,256]{2,1,0:T(8,128)} %refs_1_.1) | copy-start | bytes 196612
  5.0 14.3 %collective-permute-start = (f32[2,160,256]{2,1,0:T(8,128)S(1)}, f32[2,160,256]{2,1,0:T(8,128)S(1)}, u32[]{:S(2)}, u32[]{:S(2)}) collective-permute-start(f32[2,160,256]{2,1,0:T(8,128)S(1)} %get-tuple-element.10.own), channel_id=1, source_target_pairs={{0,2},{2,4},{4,6},{6,8},{8,10},{10,12},{12,14},{14,16},{16,18},{18... | collective-permute-start | bytes 983048 | tf_op jit(solution)/shard_map/ppermute | solution.py:449
  5.5 13.8 %collective-permute-start.1 = (f32[2,200,128]{2,1,0:T(8,128)S(1)}, f32[2,200,128]{2,1,0:T(8,128)S(1)}, u32[]{:S(2)}, u32[]{:S(2)}) collective-permute-start(f32[2,200,128]{2,1,0:T(8,128)S(1)} %get-tuple-element.11), channel_id=1, source_target_pairs={{0,4},{2,6},{4,8},{6,10},{8,12},{10,14},{12,16},{14,18},{16,20},{1... | collective-permute-start | bytes 614408 | tf_op jit(solution)/shard_map/ppermute | solution.py:450
  9.9 7.4 %collective-permute-start.3 = (f32[2,16,256]{2,1,0:T(8,128)S(1)}, f32[2,16,256]{2,1,0:T(8,128)S(1)}, u32[]{:S(2)}, u32[]{:S(2)}) collective-permute-start(f32[2,16,256]{2,1,0:T(8,128)S(1)} %get-tuple-element.12), channel_id=1, source_target_pairs={{0,3},{1,2},{2,5},{3,4},{4,7},{5,6},{6,9},{7,8},{8,11},{9,10},{10,... | collective-permute-start | bytes 98312 | tf_op jit(solution)/shard_map/ppermute | solution.py:452
  10.0 7.3 %collective-permute-start.2 = (f32[2,16,256]{2,1,0:T(8,128)S(1)}, f32[2,16,256]{2,1,0:T(8,128)S(1)}, u32[]{:S(2)}, u32[]{:S(2)}) collective-permute-start(f32[2,16,256]{2,1,0:T(8,128)S(1)} %get-tuple-element.12), channel_id=1, source_target_pairs={{0,1},{1,0},{2,3},{3,2},{4,5},{5,4},{6,7},{7,6},{8,9},{9,8},{10,11... | collective-permute-start | bytes 98312 | tf_op jit(solution)/shard_map/ppermute | solution.py:451
  36.6 13.2 %collective-permute-start.4 = (f32[2,176,256]{2,1,0:T(8,128)S(1)}, f32[2,176,256]{2,1,0:T(8,128)S(1)}, u32[]{:S(2)}, u32[]{:S(2)}) collective-permute-start(f32[2,176,256]{2,1,0:T(8,128)S(1)} %get-tuple-element.15.own), channel_id=1, source_target_pairs={{0,2},{2,4},{4,6},{6,8},{8,10},{10,12},{12,14},{14,16},{16,18},{18... | collective-permute-start | bytes 1081352 | tf_op jit(solution)/shard_map/ppermute | solution.py:449
  37.2 12.6 %collective-permute-start.5 = (f32[2,200,128]{2,1,0:T(8,128)S(1)}, f32[2,200,128]{2,1,0:T(8,128)S(1)}, u32[]{:S(2)}, u32[]{:S(2)}) collective-permute-start(f32[2,200,128]{2,1,0:T(8,128)S(1)} %get-tuple-element.16), channel_id=1, source_target_pairs={{0,4},{2,6},{4,8},{6,10},{8,12},{10,14},{12,16},{14,18},{16,20},{1... | collective-permute-start | bytes 614408 | tf_op jit(solution)/shard_map/ppermute | solution.py:450

commit v4 on v3

v4 whole, which is shorter than its diff:
```python
import jax
import jax.numpy as jnp
from jax import lax
from jax.experimental import pallas as pl
from jax.experimental.pallas import tpu as pltpu
from jax.sharding import PartitionSpec as P

STEPS = 2
SMIN = 8
SMAX = 56
STAGES = 3
REACH = 2 * STAGES
FIELDS = 5
LANES = 128
SUB = 8
HALF = LANES // 2
SLOTS = 2 * SUB
EXTRA = 2 * SUB
TALL = 32
ROWS = 4
VMEM_LIMIT = 32 * 1024 * 1024

time_step = 0.08


def shift_bound(first_row, rows):
    d = rows - 1 - first_row
    return min(SMIN + (SMAX - SMIN - 1) * d * d // ((rows - 1) * (rows - 1)) + 1, SMAX)


def minmod(lower, upper):
    return jnp.maximum(jnp.minimum(lower, 0.0), jnp.minimum(upper, jnp.maximum(lower, 0.0)))


def physical(state):
    rho, mn, mt, bn, bt = state
    inverse = pltpu.reciprocal(rho, approx=True)
    vn = mn * inverse
    vt = mt * inverse
    bn_sq = bn * bn
    bt_sq = bt * bt
    ram = mn * vn + rho
    tension = bt_sq - bn_sq
    flux_t = mt * vn - bn * bt
    flux_b = bt * vn - bn * vt
    inside = (bn_sq + bt_sq) * inverse + 1.0
    speed = jnp.abs(vn) + inside * lax.rsqrt(inside)
    return ram, tension, flux_t, flux_b, speed


def face_twice(left, right):
    left_ram, left_tension, left_t, left_b, left_speed = physical(left)
    right_ram, right_tension, right_t, right_b, right_speed = physical(right)
    bound = jnp.maximum(left_speed, right_speed)
    jumps = [bound * (l - r) for l, r in zip(left, right)]
    return [
        (left[1] + right[1]) + jumps[0],
        ((left_ram + right_ram) + 0.5 * (left_tension + right_tension)) + jumps[1],
        (left_t + right_t) + jumps[2],
        jumps[3],
        (left_b + right_b) + jumps[4],
    ]


def swapped(five):
    return [five[0], five[2], five[1], five[4], five[3]]


def radial_faces(rows):
    halves = [[0.5 * x for x in r] for r in rows]
    jumps = [[b - a for a, b in zip(p, q)] for p, q in zip(halves[:-1], halves[1:])]
    slopes = [[minmod(a, b) for a, b in zip(p, q)] for p, q in zip(jumps[:-1], jumps[1:])]
    upper = [[x + s for x, s in zip(r, sl)] for r, sl in zip(rows[1:-1], slopes)]
    lower = [[x - s for x, s in zip(r, sl)] for r, sl in zip(rows[1:-1], slopes)]
    return [swapped(face_twice(swapped(u), swapped(l))) for u, l in zip(upper[:-1], lower[1:])]


def azimuth_change(fields):
    right_of = lambda x: pltpu.roll(x, LANES - 1, 1)
    left_of = lambda x: pltpu.roll(x, 1, 1)
    lower = []
    upper = []
    for x in fields:
        half = 0.5 * x
        jump = right_of(half) - half
        slope = minmod(left_of(jump), jump)
        upper.append(x + slope)
        lower.append(right_of(x - slope))
    return [x - left_of(x) for x in face_twice(upper, lower)]


def tile(i):
    return pl.ds(pl.multiple_of(i * SUB, SUB), SUB)


def run_stages(n, stages, spin, edges):
    half_dt = 0.5 * time_step
    low_mask, high_mask = edges
    first, last = REACH, REACH + n - 1

    def work(stage, i0, count, before):
        src, dst = stage, (stage & 1) + 1
        weight = jnp.where(stage == 0, 1.0, jnp.where(stage == 1, 0.25, 2.0 / 3.0))
        keep = jnp.where(stage == 0, 0.0, jnp.where(stage == 1, 0.75, 1.0 / 3.0))
        rows = [[stages[src, f, tile(i0 + k), :] for f in range(FIELDS)] for k in range(-1, count + 2)]
        starts = [[stages[0, f, tile(i0 + k), :] for f in range(FIELDS)] for k in range(count)]
        turns = [spin[tile(i0 + k), :] for k in range(count)]
        faces = [before] + radial_faces(rows)
        for k in range(count):
            fields = rows[k + 1]
            change = azimuth_change(fields)
            turn = turns[k]
            source = [
                None,
                (-0.5 * turn) * fields[2],
                (2.0 * turn) * fields[1],
                (-1.5 * turn) * fields[4],
                None,
            ]
            for f in range(FIELDS):
                new = fields[f] - half_dt * (change[f] + (faces[k + 1][f] - faces[k][f]))
                if source[f] is not None:
                    new = new + source[f]
                stages[dst, f, tile(i0 + k), :] = weight * new + keep * starts[k][f]
        return faces[-1]

    def run(stage, _):
        for f in range(FIELDS):
            inner = stages[stage, f, tile(first), :]
            outer = stages[stage, f, tile(last), :]
            for k in (1, 2):
                stages[stage, f, tile(first - k), :] = jnp.where(low_mask, inner, stages[stage, f, tile(first - k), :])
                stages[stage, f, tile(last + k), :] = jnp.where(high_mask, outer, stages[stage, f, tile(last + k), :])
        lo = 2 * stage + 2
        count = n + 2 * REACH - 4 - 4 * stage
        before = radial_faces([[stages[stage, f, tile(lo + k), :] for f in range(FIELDS)] for k in range(-2, 2)])[0]
        turns = lax.div(count + ROWS - 1, ROWS)
        lax.fori_loop(0, turns, lambda c, carried: tuple(work(stage, lo + c * ROWS, ROWS, list(carried))), tuple(before))
        return 0

    lax.fori_loop(0, STAGES, run, 0)


def spread(block, first, width):
    block = pltpu.roll(block, (LANES - first) % LANES, 1)
    lane = lax.broadcasted_iota(jnp.int32, block.shape, 1)
    while width < LANES:
        block = jnp.where(lane < width, block, pltpu.roll(block, width, 1))
        width *= 2
    return block


def pack_far(far, near, own_cells, spare):
    sublane = lax.broadcasted_iota(jnp.int32, (SUB, LANES), 0)

    def one(f, _):
        start = pl.multiple_of(f * own_cells, SUB)
        base = pl.multiple_of(f * (own_cells + SUB), SUB)
        low = near[pl.ds(start, own_cells), 0:LANES]
        high = near[pl.ds(start + own_cells - 2 * SUB, 2 * SUB), LANES : 2 * LANES]
        moved = pltpu.roll(high[0:SUB], spare, 0)
        far[pl.ds(base, SUB), :] = jnp.where(sublane < spare, moved, low[0:SUB])
        far[pl.ds(base + SUB, own_cells - SUB), :] = low[SUB:]
        far[pl.ds(base + own_cells, SUB), :] = high[SUB:]
        return 0

    lax.fori_loop(0, FIELDS, one, 0)


def pack_kernel(spare, levels, place, density, momentum, magnetic, rotation, shifts, *rest):
    nears, fars, rest = rest[:levels], rest[levels : 2 * levels], rest[2 * levels :]
    edge, spin_rows, shift_rows, spin_in, shift_in, arrived = rest
    own_cells, radius = density.shape[1:]
    on_low = place[0] == 0
    parts = radius // LANES
    copies = [
        pltpu.make_async_copy(rotation, spin_in, arrived.at[levels * FIELDS]),
        pltpu.make_async_copy(shifts, shift_in, arrived.at[levels * FIELDS + 1]),
    ]
    for level in range(levels):
        sources = [density.at[level]] + [x.at[k, level] for x in (momentum, magnetic) for k in range(2)]
        for f, x in enumerate(sources):
            at = nears[level].at[pl.ds(f * own_cells, own_cells), :]
            copies.append(pltpu.make_async_copy(x, at, arrived.at[level * FIELDS + f]))
    for copy in copies:
        copy.start()
    for copy in copies[:2]:
        copy.wait()
    for part in range(parts):
        rows = slice(part * LANES, (part + 1) * LANES)
        spin_rows[rows, :] = jnp.broadcast_to(spin_in[part : part + 1, :], (LANES, LANES)).T * time_step
        shift_rows[rows, :] = jnp.broadcast_to(shift_in[part : part + 1, :].astype(jnp.float32), (LANES, LANES)).T
    wide = lambda ref: jnp.broadcast_to(
        jnp.where(on_low, ref[parts - 1 : parts, :], ref[0:1, :]).astype(jnp.float32), (own_cells, LANES)
    )
    turn = wide(spin_in) * time_step
    shift = wide(shift_in)
    zero = jnp.zeros((own_cells, LANES), jnp.float32)
    for copy in copies[2:]:
        copy.wait()
    for level in range(levels):
        near = nears[level]
        pack_far(fars[level], near, own_cells, spare)
        block = jnp.where(on_low, near[:, radius - LANES :], near[:, 0:LANES])
        split = 4 * own_cells
        for side, group in enumerate((block[0:split], jnp.concatenate([block[split:], turn, shift, zero], axis=0))):
            turned = group.T
            edge[level, :, side * LANES : (side + 1) * LANES] = jnp.where(on_low, turned[LANES - EXTRA :], turned[0:EXTRA])


class Blocks:
    def __init__(self, row, n, radius, total, moved):
        self.on_low = row == 0
        self.n = n
        self.own_at = pl.multiple_of(jnp.where(self.on_low, EXTRA, EXTRA + moved), SUB)
        self.edge_at = pl.multiple_of(jnp.where(self.on_low, EXTRA + radius, moved), SUB)
        bounds = [[shift_bound(r * radius - (moved if r else 0) + n * k, total) for k in range(SLOTS)] for r in range(2)]
        self.bounds = [jnp.where(self.on_low, a, b) for a, b in zip(*bounds)]

    def rows_of(self, k):
        start = EXTRA - REACH + self.n * k
        return slice(start, start + TALL)


def table_kernel(plans, place, side, spin_rows, shift_rows, *rest):
    outs, held = rest[:-1], rest[-1]
    lane = lax.broadcasted_iota(jnp.int32, (SUB, LANES), 1)
    sublane = lax.broadcasted_iota(jnp.int32, (SUB, LANES), 0)
    front = lax.broadcasted_iota(jnp.int32, (TALL, LANES), 1) < HALF
    more = side[0, :, LANES : 2 * LANES]
    for which, (n, radius, own_cells, total, spare, moved) in enumerate(plans):
        spin, pick = outs[2 * which : 2 * which + 2]
        blocks = Blocks(place[0], n, radius, total, moved)
        held[0, pl.ds(blocks.own_at, radius), :] = spin_rows[...]
        held[0, pl.ds(blocks.edge_at, EXTRA), :] = spread(more, own_cells, own_cells)
        held[1, pl.ds(blocks.own_at, radius), :] = shift_rows[...]
        held[1, pl.ds(blocks.edge_at, EXTRA), :] = spread(more, 2 * own_cells, own_cells)
        bound = jnp.zeros((SUB, LANES), jnp.int32)
        for j in range(SUB):
            low, high = blocks.rows_of(j), blocks.rows_of(SUB + j)
            spin[pl.ds(j, TALL, stride=SUB), :] = jnp.where(front, held[0, low, :], held[0, high, :])
            pick[pl.ds(j, TALL, stride=SUB), :] = jnp.where(front, held[1, low, :], held[1, high, :]).astype(jnp.int32)
            bound = jnp.where(sublane == j, jnp.where(lane < HALF, blocks.bounds[j], blocks.bounds[SUB + j]), bound)

        def one(i, _):
            pick[tile(i), :] = (lane + (REACH + bound)) - pick[tile(i), :]
            return 0

        lax.fori_loop(0, TALL, one, 0)


def step_kernel(plan, refs, write, scratch):
    n, radius, own_cells, total, spare, moved = plan
    place, own, own_edge, near, near_edge, far, spin, pick = refs
    cells, stages, packed = scratch
    row = place[0]
    lane = lax.broadcasted_iota(jnp.int32, (SUB, LANES), 1)
    sublane = lax.broadcasted_iota(jnp.int32, (SUB, LANES), 0)
    blocks = Blocks(row, n, radius, total, moved)

    edge_lane = lax.broadcasted_iota(jnp.int32, (EXTRA, LANES), 1)
    parts = radius // LANES

    def gather(f, _):
        rows = pl.ds(pl.multiple_of(f * own_cells, SUB), own_cells)
        start = pl.multiple_of(f * (own_cells + SUB), SUB)
        for part in range(parts):
            columns = slice(part * LANES, (part + 1) * LANES)
            if part == 0:
                top = far[pl.ds(start, own_cells), :]
            else:
                top = jnp.concatenate(
                    [
                        jnp.zeros((own_cells - 2 * SUB, LANES), jnp.float32),
                        pltpu.roll(far[pl.ds(start, SUB), :], SUB - spare, 0),
                        far[pl.ds(start + own_cells, SUB), :],
                    ],
                    axis=0,
                )
            fill = jnp.zeros((own_cells, LANES), jnp.float32)
            block = jnp.concatenate([top, near[rows, columns], own[rows, columns], fill], axis=0)
            cells[f, pl.ds(blocks.own_at + part * LANES, LANES), :] = block.T
        columns = pl.ds(pl.multiple_of(lax.div(f, 4) * LANES, LANES), LANES)
        lanes_at = lax.rem(f, 4) * own_cells
        cells[f, pl.ds(blocks.edge_at, EXTRA), :] = jnp.where(
            edge_lane < 2 * own_cells,
            pltpu.roll(near_edge[:, columns], lax.rem(LANES + own_cells - lanes_at, LANES), 1),
            pltpu.roll(own_edge[:, columns], lax.rem(LANES + 2 * own_cells - lanes_at, LANES), 1),
        )
        return 0

    lax.fori_loop(0, FIELDS, gather, 0)

    front = lax.broadcasted_iota(jnp.int32, (TALL, LANES), 1) < HALF

    def deal(f, _):
        for j in range(SUB):
            low, high = j, SUB + j
            turn_low = (LANES - (2 * own_cells - REACH)) + blocks.bounds[low]
            turn_high = (HALF - (2 * own_cells - REACH)) + blocks.bounds[high]
            stages[0, f, pl.ds(j, TALL, stride=SUB), :] = jnp.where(
                front,
                pltpu.roll(cells[f, blocks.rows_of(low), :], turn_low, 1),
                pltpu.roll(cells[f, blocks.rows_of(high), :], turn_high, 1),
            )
        return 0

    lax.fori_loop(0, FIELDS, deal, 0)

    edges = (
        (sublane == 0) & (lane < HALF) & (row == 0),
        (sublane == SUB - 1) & (lane >= HALF) & (row == total // radius - 1),
    )
    run_stages(n, stages, spin, edges)

    even = (lane & own_cells) == 0

    def shift(i, _):
        rows = tile(REACH + i)
        source = pick[rows, :]
        picks = [source & (LANES - 1), (source - own_cells) & (LANES - 1)]
        turned = [
            jnp.take_along_axis(stages[1, f, rows, :], picks[f % 2], axis=1, mode="promise_in_bounds")
            for f in range(FIELDS)
        ]
        stages[2, 0, tile(i), :] = jnp.where(even, turned[0], turned[1])
        stages[2, 1, tile(i), :] = jnp.where(even, turned[2], turned[3])
        stages[2, 2, tile(i), :] = turned[4]
        return 0

    lax.fori_loop(0, n, shift, 0)
    narrow = lax.broadcasted_iota(jnp.int32, (n, LANES), 1) < HALF
    for j in range(SUB):
        one, two, three = [stages[2, g, pl.ds(j, n, stride=SUB), :] for g in range(3)]
        low = slice(EXTRA + n * j, EXTRA + n * (j + 1))
        high = slice(EXTRA + n * (SUB + j), EXTRA + n * (SUB + j + 1))
        packed[0, low, :] = jnp.where(narrow, one, pltpu.roll(two, HALF, 1))
        packed[0, high, :] = jnp.where(narrow, pltpu.roll(one, HALF, 1), two)
        packed[1, low, :] = three
        packed[1, high, :] = pltpu.roll(three, HALF, 1)
    for part in range(parts):
        rows = pl.ds(blocks.own_at + part * LANES, LANES)
        write.fields(slice(part * LANES, (part + 1) * LANES), packed[0, rows, :].T, packed[1, rows, :].T)
    write.edge(packed[0, pl.ds(blocks.edge_at, EXTRA), :], packed[1, pl.ds(blocks.edge_at, EXTRA), :])
    write.end()


class ToMessage:
    def __init__(self, near, far, own_cells, spare):
        self.near, self.far, self.own_cells, self.spare = near, far, own_cells, spare

    def fields(self, columns, four, fifth):
        split = 4 * self.own_cells
        self.near[0:split, columns] = four
        self.near[split : split + self.own_cells, columns] = fifth[0 : self.own_cells]

    def edge(self, first, second):
        tail = FIELDS * self.own_cells
        self.near[tail : tail + EXTRA, 0:LANES] = first
        self.near[tail : tail + EXTRA, LANES : 2 * LANES] = second

    def end(self):
        pack_far(self.far, self.near, self.own_cells, self.spare)


class ToResult:
    def __init__(self, density, momentum, magnetic):
        self.outs = (density, momentum, magnetic)

    def fields(self, columns, four, fifth):
        density, momentum, magnetic = self.outs
        cells = density.shape[1]
        density[0, :, columns] = four[0:cells]
        momentum[0, 0, :, columns] = four[cells : 2 * cells]
        momentum[1, 0, :, columns] = four[2 * cells : 3 * cells]
        magnetic[0, 0, :, columns] = four[3 * cells : 4 * cells]
        magnetic[1, 0, :, columns] = fifth[0:cells]

    def edge(self, first, second):
        pass

    def end(self):
        pass


def tall_of(n):
    return EXTRA + SLOTS * n + 2 * SUB


def step_scratch(n):
    return [
        pltpu.VMEM((FIELDS, tall_of(n), LANES), jnp.float32),
        pltpu.VMEM((STAGES, FIELDS, TALL * SUB, LANES), jnp.float32),
        pltpu.VMEM((2, tall_of(n), LANES), jnp.float32),
    ]


vmem = pl.BlockSpec(memory_space=pltpu.VMEM)
smem = pl.BlockSpec(memory_space=pltpu.SMEM)
f32 = lambda *s: jax.ShapeDtypeStruct(s, jnp.float32)
params = pltpu.CompilerParams(vmem_limit_bytes=VMEM_LIMIT)
cost = pl.CostEstimate(flops=20_000_000, bytes_accessed=600_000, transcendentals=0)


def first_step(plan, level, operands):
    n, radius, own_cells, total, spare, moved = plan

    def kernel(place, own, near, far, side, corner, spin, pick, near_out, far_out, *scratch):
        refs = (place, own, side.at[level], near, corner.at[level], far, spin, pick)
        step_kernel(plan, refs, ToMessage(near_out, far_out, own_cells, spare), scratch)

    return pl.pallas_call(
        kernel,
        out_shape=[f32(FIELDS * own_cells + EXTRA, radius), f32(FIELDS * (own_cells + SUB), LANES)],
        in_specs=[smem] + [vmem] * 7,
        out_specs=[vmem] * 2,
        scratch_shapes=step_scratch(n),
        compiler_params=params,
        cost_estimate=cost,
        name="first_step",
    )(*operands)


def last_step(plan, level, operands, results, levels):
    n, radius, own_cells, total, spare, moved = plan
    tail = pl.ds(FIELDS * own_cells, EXTRA)
    count = len(results)

    def kernel(place, own, near, far, spin, pick, *rest):
        outs, scratch = rest[count : count + 3], rest[count + 3 :]
        refs = (place, own, own.at[tail, :], near, near.at[tail, :], far, spin, pick)
        step_kernel(plan, refs, ToResult(*outs), scratch)

    pair = pl.BlockSpec((2, 1, own_cells, radius), lambda i: (0, level, 0, 0))
    return pl.pallas_call(
        kernel,
        grid=(1,),
        out_shape=[f32(levels, own_cells, radius), f32(2, levels, own_cells, radius), f32(2, levels, own_cells, radius)],
        in_specs=[smem] + [vmem] * 5 + [pl.BlockSpec(memory_space=pl.ANY)] * count,
        out_specs=[pl.BlockSpec((1, own_cells, radius), lambda i: (level, 0, 0)), pair, pair],
        scratch_shapes=step_scratch(n),
        input_output_aliases={len(operands) + k: k for k in range(count)},
        compiler_params=params,
        cost_estimate=cost,
        name="last_step",
    )(*operands, *results)


def body(density, momentum, magnetic, rotation, shifts):
    phi_count = lax.axis_size("phi")
    row_count = lax.axis_size("row")
    levels, own_cells, radius = density.shape
    total = radius * row_count
    parts = radius // LANES
    n = radius // SLOTS
    need = [max(shift_bound(part * LANES, total) + REACH - own_cells, 0) for part in range(parts)]
    spare = own_cells - need[0]
    assert row_count == 2 and radius == 2 * LANES and own_cells == HALF // 2
    assert 0 < need[0] < own_cells and need[1] <= SUB + spare and spare <= SUB

    row = lax.axis_index("row")
    place = jnp.reshape(row, (1,)).astype(jnp.int32)
    here = lambda p, r: (p % phi_count) * row_count + r
    everyone = [(p, r) for p in range(phi_count) for r in range(row_count)]
    both = ("phi", "row")
    send_near = lambda x: lax.ppermute(x, "phi", [(p, (p + 1) % phi_count) for p in range(phi_count)])
    send_far = lambda x: lax.ppermute(x, both, [(here(p, 0), here(p + 2, 0)) for p in range(phi_count)])
    send_side = lambda x: lax.ppermute(x, "row", [(0, 1), (1, 0)])
    send_corner = lambda x: lax.ppermute(x, both, [(here(p, r), here(p + 1, 1 - r)) for p, r in everyone])

    near_message = f32(FIELDS * own_cells, radius)
    far_message = f32(FIELDS * (own_cells + SUB), LANES)
    packed = pl.pallas_call(
        lambda *refs: pack_kernel(spare, levels, *refs),
        out_shape=[near_message] * levels
        + [far_message] * levels
        + [f32(levels, EXTRA, 2 * LANES), f32(radius, LANES), f32(radius, LANES)],
        in_specs=[smem] + [pl.BlockSpec(memory_space=pltpu.HBM)] * 5,
        out_specs=[vmem] * (2 * levels + 3),
        scratch_shapes=[
            pltpu.VMEM((parts, LANES), jnp.float32),
            pltpu.VMEM((parts, LANES), jnp.int32),
            pltpu.SemaphoreType.DMA((levels * FIELDS + 2,)),
        ],
        compiler_params=params,
        name="pack",
    )(place, density, momentum, magnetic, rotation.reshape(parts, LANES), shifts.reshape(parts, LANES))
    owns, fars, (edge, spin_rows, shift_rows) = packed[:levels], packed[levels : 2 * levels], packed[2 * levels :]

    side = send_side(edge)
    corner = send_corner(edge)
    wide = (n + 1, radius, own_cells, total, spare, EXTRA)
    plain = (n, radius, own_cells, total, spare, 0)
    i32 = jax.ShapeDtypeStruct((TALL * SUB, LANES), jnp.int32)
    tables = pl.pallas_call(
        lambda *refs: table_kernel((wide, plain), *refs),
        out_shape=[f32(TALL * SUB, LANES), i32] * 2,
        in_specs=[smem] + [vmem] * 3,
        out_specs=[vmem] * 4,
        scratch_shapes=[pltpu.VMEM((2, tall_of(n + 1), LANES), jnp.float32)],
        compiler_params=params,
        name="tables",
    )(place, side, spin_rows, shift_rows)
    moved = [(send_near(own), send_far(far)) for own, far in zip(owns, fars)]
    states = []
    for level in range(levels):
        near, far = moved[level]
        states.append(first_step(wide, level, (place, owns[level], near, far, side, corner, *tables[:2])))
    moved = [(send_near(own), send_far(far)) for own, far in states]
    results = ()
    for level in range(levels):
        near, far = moved[level]
        results = last_step(plain, level, (place, states[level][0], near, far, *tables[2:]), results, levels)
    return tuple(results)


def solution(mesh):
    placed = (
        P(None, "phi", "row"),
        P(None, None, "phi", "row"),
        P(None, None, "phi", "row"),
        P("row"),
        P("row"),
    )
    return jax.shard_map(
        body,
        mesh=mesh,
        in_specs=placed,
        out_specs=(P(None, "phi", "row"), P(None, None, "phi", "row"), P(None, None, "phi", "row")),
        check_vma=False,
    )
```

time: 65.8 us -> 72.4 us (1.10)
  starting transfers between devices: 10.4 us -> 15.9 us
  Pallas kernels: 33.9 us -> 37.8 us
  waiting for transfers between devices: 17 us -> 14.3 us
    ppermute x2 -> x4, waiting for transfers between devices: 12.7 us -> 4.06 us  [body(): lax.ppermute(x, both, [(here(p, 0), here(p + 2, 0)) for p in range(phi_co...]
    ppermute x2 -> x4, starting transfers between devices: 6.34 us -> 12.6 us  [body(): lax.ppermute(x, both, [(here(p, 0), here(p + 2, 0)) for p in range(phi_co...]
    pallas_call x3 -> x6, Pallas kernels: 33.9 us -> 37.8 us  [the longest x2 18.8 us: first_step(): pl.pallas_call(kernel, out_shape=[f32(FIELDS * own_cells + EXTRA, radius)...]
    ppermute x1, waiting for transfers between devices: 0.01 us -> 3.9 us  [body(): send_side = lambda x: lax.ppermute(x, 'row', [(0, 1), (1, 0)])]
    ppermute x1, starting transfers between devices: 2.95 us -> 0.07 us  [body(): send_side = lambda x: lax.ppermute(x, 'row', [(0, 1), (1, 0)])]
    ppermute x2 -> x4, starting transfers between devices: 1.06 us -> 3.25 us  [body(): lax.ppermute(x, 'phi', [(p, (p + 1) % phi_count) for p in range(phi_count)])]
    ppermute x1, waiting for transfers between devices: 4.36 us -> 6.29 us  [body(): lax.ppermute(x, both, [(here(p, r), here(p + 1, 1 - r)) for p, r in every...]
  transfers between devices with their start and end apart: 6 -> 10, of which waited for: 3 -> 3; matrix products, arithmetic and copies ran while one was open for 0% -> 0% of each run, Pallas kernels for 0% -> 39%
where the time goes in v4:
time: 72.4 us; the launch traced here: 72.1 us
  Pallas kernels  37.8 us (52%)
  starting transfers between devices  15.9 us (22%)
  waiting for transfers between devices  14.3 us (20%)
  local copies, waits for them, and re-layouts  3.33 us (5%)
  between operations  0.76 us (1%)
    pallas_call x2, Pallas kernels, first_step(): pl.pallas_call(kernel, out_shape=[f32(FIELDS * own_cells + EXTRA, radius)...  18.8 us
    pallas_call x2, Pallas kernels, last_step(): pl.pallas_call(kernel, grid=(1,), out_shape=[f32(levels, own_cells, radiu...  17.5 us
    ppermute x4, starting transfers between devices, body(): lax.ppermute(x, both, [(here(p, 0), here(p + 2, 0)) for p in range(phi_co...  12.6 us
    ppermute x1, waiting for transfers between devices, body(): lax.ppermute(x, both, [(here(p, r), here(p + 1, 1 - r)) for p, r in every...  6.29 us
    ppermute x4, waiting for transfers between devices, body(): lax.ppermute(x, both, [(here(p, 0), here(p + 2, 0)) for p in range(phi_co...  4.06 us
    ppermute x1, waiting for transfers between devices, body(): send_side = lambda x: lax.ppermute(x, 'row', [(0, 1), (1, 0)])  3.9 us
    unnamed x10, local copies, waits for them, and re-layouts  3.33 us
    ppermute x4, starting transfers between devices, body(): lax.ppermute(x, 'phi', [(p, (p + 1) % phi_count) for p in range(phi_count)])  3.25 us
  transfers between devices with their start and end apart: 10, of which 3 were waited for; matrix products, arithmetic and copies ran while one was open for 0% of the time, Pallas kernels for 39%

profile of v4, /device:TPU:0, one launch (start us, length us, event | category | flops | bytes accessed | tf_op | source)
XLA Modules:
  0.0 72.1 jit_solution(10704418390186172295)
XLA Ops:
  0.7 0.7 copy-done.4
  1.3 0.0 copy-done.3
  1.3 0.9 %copy-done = f32[2,2,32,256]{3,2,1,0:T(8,128)S(1)} copy-done((f32[2,2,32,256]{3,2,1,0:T(8,128)S(1)}, f32[2,2,32,256]{3,2,1,0:T(8,128)}, u32[]{:S(2)}) %copy-start) | copy-done | bytes 131096
  2.2 0.9 %copy-done.1 = f32[2,2,32,256]{3,2,1,0:T(8,128)S(1)} copy-done((f32[2,2,32,256]{3,2,1,0:T(8,128)S(1)}, f32[2,2,32,256]{3,2,1,0:T(8,128)}, u32[]{:S(2)}) %copy-start.1) | copy-done | bytes 131096
  3.1 0.8 %copy-done.2 = f32[2,32,256]{2,1,0:T(8,128)S(1)} copy-done((f32[2,32,256]{2,1,0:T(8,128)S(1)}, f32[2,32,256]{2,1,0:T(8,128)}, u32[]{:S(2)}) %copy-start.2) | copy-done | bytes 65560
  4.0 0.9 %pack.1 = (f32[160,256]{1,0:T(8,128)S(1)}, f32[160,256]{1,0:T(8,128)S(1)}, f32[200,128]{1,0:T(8,128)S(1)}, f32[200,128]{1,0:T(8,128)S(1)}, f32[2,16,256]{2,1,0:T...) custom-call(s32[1]{0:T(128)} %bitcast.refs_0_.place, f32[2,32,256]{2,1,0:T(8,128)S(1)} %copy-done.2, ...), custom_call_target="tpu_custom_call" | custom-call | tf_op jit(solution)/shard_map/pack/pallas_call | solution.py:473
  4.9 0.5 collective-permute-start.6
  5.4 2.6 %collective-permute-start = (f32[160,256]{1,0:T(8,128)S(1)}, f32[160,256]{1,0:T(8,128)S(1)}, u32[]{:S(2)}, u32[]{:S(2)}) collective-permute-start(f32[160,256]{1,0:T(8,128)S(1)} %get-tuple-element.21.own), channel_id=1, source_target_pairs={{0,2},{2,4},{4,6},{6,8},{8,10},{10,12},{12,14},{14,16},{16,18},{18... | collective-permute-start | bytes 491528 | tf_op jit(solution)/shard_map/ppermute | solution.py:466
  8.1 3.4 %collective-permute-start.7 = (f32[200,128]{1,0:T(8,128)S(1)}, f32[200,128]{1,0:T(8,128)S(1)}, u32[]{:S(2)}, u32[]{:S(2)}) collective-permute-start(f32[200,128]{1,0:T(8,128)S(1)} %get-tuple-element.33), channel_id=1, source_target_pairs={{0,4},{2,6},{4,8},{6,10},{8,12},{10,14},{12,16},{14,18},{16,20},{1... | collective-permute-start | bytes 307208 | tf_op jit(solution)/shard_map/ppermute | solution.py:467
  11.5 3.4 %collective-permute-start.1 = (f32[200,128]{1,0:T(8,128)S(1)}, f32[200,128]{1,0:T(8,128)S(1)}, u32[]{:S(2)}, u32[]{:S(2)}) collective-permute-start(f32[200,128]{1,0:T(8,128)S(1)} %get-tuple-element.22), channel_id=1, source_target_pairs={{0,4},{2,6},{4,8},{6,10},{8,12},{10,14},{12,16},{14,18},{16,20},{1... | collective-permute-start | bytes 307208 | tf_op jit(solution)/shard_map/ppermute | solution.py:467
  14.9 0.1 collective-permute-start.2
  15.0 3.9 %collective-permute-done.2.refs_1_.side = f32[2,16,256]{2,1,0:T(8,128)S(1)} collective-permute-done((f32[2,16,256]{2,1,0:T(8,128)S(1)}, f32[2,16,256]{2,1,0:T(8,128)S(1)}, u32[]{:S(2)}, u32[]{:S(2)}) %collective-permute-start.2) | collective-permute-done | bytes 32800 | tf_op jit(solution)/shard_map/ppermute | solution.py:468
  18.9 0.0 collective-permute-start.3
  18.9 0.6 tables.1
  19.5 6.3 %collective-permute-done.3.corner = f32[2,16,256]{2,1,0:T(8,128)S(1)} collective-permute-done((f32[2,16,256]{2,1,0:T(8,128)S(1)}, f32[2,16,256]{2,1,0:T(8,128)S(1)}, u32[]{:S(2)}, u32[]{:S(2)}) %collective-permute-start.3) | collective-permute-done | bytes 32800 | tf_op jit(solution)/shard_map/ppermute | solution.py:469
  25.8 9.4 %first_step.3 = (f32[176,256]{1,0:T(8,128)S(1)}, f32[200,128]{1,0:T(8,128)S(1)}) custom-call(s32[1]{0:T(128)} %bitcast.refs_0_.place, f32[160,256]{1,0:T(8,128)S(1)} %get-tuple-element.32.own, f32[160,256]{1,0:T(8,128)S(1)} %collective-permute-done.6.near, f32[200,128]{1,0:T(8,128)S(1)} %collective-permute-done.7.far, ...), custom_call_target="tpu_custom_call" | custom-call | flops 20000000 | bytes 600000 | tf_op jit(solution)/shard_map/first_step/pallas_call | solution.py:412
  35.2 0.1 collective-permute-start.8
  35.3 9.4 %first_step.2 = (f32[176,256]{1,0:T(8,128)S(1)}, f32[200,128]{1,0:T(8,128)S(1)}) custom-call(s32[1]{0:T(128)} %bitcast.refs_0_.place, f32[160,256]{1,0:T(8,128)S(1)} %get-tuple-element.21.own, f32[160,256]{1,0:T(8,128)S(1)} %collective-permute-done.near, f32[200,128]{1,0:T(8,128)S(1)} %collective-permute-done.1.far, ...), custom_call_target="tpu_custom_call" | custom-call | flops 20000000 | bytes 600000 | tf_op jit(solution)/shard_map/first_step/pallas_call | solution.py:412
  44.7 0.1 collective-permute-start.4
  44.8 3.2 %collective-permute-start.9 = (f32[200,128]{1,0:T(8,128)S(1)}, f32[200,128]{1,0:T(8,128)S(1)}, u32[]{:S(2)}, u32[]{:S(2)}) collective-permute-start(f32[200,128]{1,0:T(8,128)S(1)} %get-tuple-element.35), channel_id=1, source_target_pairs={{0,4},{2,6},{4,8},{6,10},{8,12},{10,14},{12,16},{14,18},{16,20},{1... | collective-permute-start | bytes 307208 | tf_op jit(solution)/shard_map/ppermute | solution.py:467
  48.0 2.5 %collective-permute-start.5 = (f32[200,128]{1,0:T(8,128)S(1)}, f32[200,128]{1,0:T(8,128)S(1)}, u32[]{:S(2)}, u32[]{:S(2)}) collective-permute-start(f32[200,128]{1,0:T(8,128)S(1)} %get-tuple-element.29), channel_id=1, source_target_pairs={{0,4},{2,6},{4,8},{6,10},{8,12},{10,14},{12,16},{14,18},{16,20},{1... | collective-permute-start | bytes 307208 | tf_op jit(solution)/shard_map/ppermute | solution.py:467
  50.5 4.1 %collective-permute-done.9.far = f32[200,128]{1,0:T(8,128)S(1)} collective-permute-done((f32[200,128]{1,0:T(8,128)S(1)}, f32[200,128]{1,0:T(8,128)S(1)}, u32[]{:S(2)}, u32[]{:S(2)}) %collective-permute-start.9) | collective-permute-done | bytes 102432 | tf_op jit(solution)/shard_map/ppermute | solution.py:467
  54.6 8.8 %last_step.2 = (f32[2,32,256]{2,1,0:T(8,128)}, f32[2,2,32,256]{3,2,1,0:T(8,128)}, f32[2,2,32,256]{3,2,1,0:T(8,128)}) custom-call(s32[1]{0:T(128)} %bitcast.refs_0_.place, f32[176,256]{1,0:T(8,128)S(1)} %get-tuple-element.34.own, f32[176,256]{1,0:T(8,128)S(1)} %collective-permute-done.8.near, f32[200,128]{1,0:T(8,128)S(1)} %collective-permute-done.9.far, ...), custom_call_target="tpu_custom_call" | custom-call | flops 20000000 | bytes 600000 | tf_op jit(solution)/shard_map/last_step/pallas_call | solution.py:435
  63.3 8.8 %last_step.3 = (f32[2,32,256]{2,1,0:T(8,128)}, f32[2,2,32,256]{3,2,1,0:T(8,128)}, f32[2,2,32,256]{3,2,1,0:T(8,128)}) custom-call(s32[1]{0:T(128)} %bitcast.refs_0_.place, f32[176,256]{1,0:T(8,128)S(1)} %get-tuple-element.28.own, f32[176,256]{1,0:T(8,128)S(1)} %collective-permute-done.4.near, ...), custom_call_target="tpu_custom_call", output_to_operand_aliasing={{0}: (6, {}), {1}: (7, {}), {2}: (8, {})} | custom-call | flops 20000000 | bytes 600000 | tf_op jit(solution)/shard_map/last_step/pallas_call | solution.py:435
  (12 shorter events, 0.0 us)
Async XLA Ops:
  0.6 0.7 copy-start.4
  0.6 0.7 copy-start.3
  1.3 0.9 %copy-start = (f32[2,2,32,256]{3,2,1,0:T(8,128)S(1)}, f32[2,2,32,256]{3,2,1,0:T(8,128)}, u32[]{:S(2)}) copy-start(f32[2,2,32,256]{3,2,1,0:T(8,128)} %refs_2_.1) | copy-start | bytes 393220
  2.2 0.9 %copy-start.1 = (f32[2,2,32,256]{3,2,1,0:T(8,128)S(1)}, f32[2,2,32,256]{3,2,1,0:T(8,128)}, u32[]{:S(2)}) copy-start(f32[2,2,32,256]{3,2,1,0:T(8,128)} %refs_3_.1) | copy-start | bytes 393220
  3.1 0.8 %copy-start.2 = (f32[2,32,256]{2,1,0:T(8,128)S(1)}, f32[2,32,256]{2,1,0:T(8,128)}, u32[]{:S(2)}) copy-start(f32[2,32,256]{2,1,0:T(8,128)} %refs_1_.1) | copy-start | bytes 196612
  4.9 20.9 %collective-permute-start.6 = (f32[160,256]{1,0:T(8,128)S(1)}, f32[160,256]{1,0:T(8,128)S(1)}, u32[]{:S(2)}, u32[]{:S(2)}) collective-permute-start(f32[160,256]{1,0:T(8,128)S(1)} %get-tuple-element.32.own), channel_id=1, source_target_pairs={{0,2},{2,4},{4,6},{6,8},{8,10},{10,12},{12,14},{14,16},{16,18},{18... | collective-permute-start | bytes 491528 | tf_op jit(solution)/shard_map/ppermute | solution.py:466
  5.4 29.9 %collective-permute-start = (f32[160,256]{1,0:T(8,128)S(1)}, f32[160,256]{1,0:T(8,128)S(1)}, u32[]{:S(2)}, u32[]{:S(2)}) collective-permute-start(f32[160,256]{1,0:T(8,128)S(1)} %get-tuple-element.21.own), channel_id=1, source_target_pairs={{0,2},{2,4},{4,6},{6,8},{8,10},{10,12},{12,14},{14,16},{16,18},{18... | collective-permute-start | bytes 491528 | tf_op jit(solution)/shard_map/ppermute | solution.py:466
  8.1 17.8 %collective-permute-start.7 = (f32[200,128]{1,0:T(8,128)S(1)}, f32[200,128]{1,0:T(8,128)S(1)}, u32[]{:S(2)}, u32[]{:S(2)}) collective-permute-start(f32[200,128]{1,0:T(8,128)S(1)} %get-tuple-element.33), channel_id=1, source_target_pairs={{0,4},{2,6},{4,8},{6,10},{8,12},{10,14},{12,16},{14,18},{16,20},{1... | collective-permute-start | bytes 307208 | tf_op jit(solution)/shard_map/ppermute | solution.py:467
  11.5 23.8 %collective-permute-start.1 = (f32[200,128]{1,0:T(8,128)S(1)}, f32[200,128]{1,0:T(8,128)S(1)}, u32[]{:S(2)}, u32[]{:S(2)}) collective-permute-start(f32[200,128]{1,0:T(8,128)S(1)} %get-tuple-element.22), channel_id=1, source_target_pairs={{0,4},{2,6},{4,8},{6,10},{8,12},{10,14},{12,16},{14,18},{16,20},{1... | collective-permute-start | bytes 307208 | tf_op jit(solution)/shard_map/ppermute | solution.py:467
  14.9 4.0 %collective-permute-start.2 = (f32[2,16,256]{2,1,0:T(8,128)S(1)}, f32[2,16,256]{2,1,0:T(8,128)S(1)}, u32[]{:S(2)}, u32[]{:S(2)}) collective-permute-start(f32[2,16,256]{2,1,0:T(8,128)S(1)} %get-tuple-element.23), channel_id=1, source_target_pairs={{0,1},{1,0},{2,3},{3,2},{4,5},{5,4},{6,7},{7,6},{8,9},{9,8},{10,11... | collective-permute-start | bytes 98312 | tf_op jit(solution)/shard_map/ppermute | solution.py:468
  18.9 6.9 %collective-permute-start.3 = (f32[2,16,256]{2,1,0:T(8,128)S(1)}, f32[2,16,256]{2,1,0:T(8,128)S(1)}, u32[]{:S(2)}, u32[]{:S(2)}) collective-permute-start(f32[2,16,256]{2,1,0:T(8,128)S(1)} %get-tuple-element.23), channel_id=1, source_target_pairs={{0,3},{1,2},{2,5},{3,4},{4,7},{5,6},{6,9},{7,8},{8,11},{9,10},{10,... | collective-permute-start | bytes 98312 | tf_op jit(solution)/shard_map/ppermute | solution.py:469
  35.2 19.3 %collective-permute-start.8 = (f32[176,256]{1,0:T(8,128)S(1)}, f32[176,256]{1,0:T(8,128)S(1)}, u32[]{:S(2)}, u32[]{:S(2)}) collective-permute-start(f32[176,256]{1,0:T(8,128)S(1)} %get-tuple-element.34.own), channel_id=1, source_target_pairs={{0,2},{2,4},{4,6},{6,8},{8,10},{10,12},{12,14},{14,16},{16,18},{18... | collective-permute-start | bytes 540680 | tf_op jit(solution)/shard_map/ppermute | solution.py:466
  44.7 18.6 %collective-permute-start.4 = (f32[176,256]{1,0:T(8,128)S(1)}, f32[176,256]{1,0:T(8,128)S(1)}, u32[]{:S(2)}, u32[]{:S(2)}) collective-permute-start(f32[176,256]{1,0:T(8,128)S(1)} %get-tuple-element.28.own), channel_id=1, source_target_pairs={{0,2},{2,4},{4,6},{6,8},{8,10},{10,12},{12,14},{14,16},{16,18},{18... | collective-permute-start | bytes 540680 | tf_op jit(solution)/shard_map/ppermute | solution.py:466
  44.8 9.8 %collective-permute-start.9 = (f32[200,128]{1,0:T(8,128)S(1)}, f32[200,128]{1,0:T(8,128)S(1)}, u32[]{:S(2)}, u32[]{:S(2)}) collective-permute-start(f32[200,128]{1,0:T(8,128)S(1)} %get-tuple-element.35), channel_id=1, source_target_pairs={{0,4},{2,6},{4,8},{6,10},{8,12},{10,14},{12,16},{14,18},{16,20},{1... | collective-permute-start | bytes 307208 | tf_op jit(solution)/shard_map/ppermute | solution.py:467
  48.0 15.3 %collective-permute-start.5 = (f32[200,128]{1,0:T(8,128)S(1)}, f32[200,128]{1,0:T(8,128)S(1)}, u32[]{:S(2)}, u32[]{:S(2)}) collective-permute-start(f32[200,128]{1,0:T(8,128)S(1)} %get-tuple-element.29), channel_id=1, source_target_pairs={{0,4},{2,6},{4,8},{6,10},{8,12},{10,14},{12,16},{14,18},{16,20},{1... | collective-permute-start | bytes 307208 | tf_op jit(solution)/shard_map/ppermute | solution.py:467

commit v5 on v4

--- a/solution.py
+++ b/solution.py
@@ -19,6 +19,7 @@
 TALL = 32
 ROWS = 4
 VMEM_LIMIT = 32 * 1024 * 1024
+PACK_LIMIT = 60 * 1024 * 1024
 
 time_step = 0.08
 
@@ -315,20 +316,22 @@
 
     even = (lane & own_cells) == 0
 
-    def shift(i, _):
-        rows = tile(REACH + i)
-        source = pick[rows, :]
-        picks = [source & (LANES - 1), (source - own_cells) & (LANES - 1)]
-        turned = [
-            jnp.take_along_axis(stages[1, f, rows, :], picks[f % 2], axis=1, mode="promise_in_bounds")
-            for f in range(FIELDS)
-        ]
-        stages[2, 0, tile(i), :] = jnp.where(even, turned[0], turned[1])
-        stages[2, 1, tile(i), :] = jnp.where(even, turned[2], turned[3])
-        stages[2, 2, tile(i), :] = turned[4]
+    def shift(turn, _):
+        for k in range(ROWS):
+            i = turn * ROWS + k
+            rows = tile(REACH + i)
+            source = pick[rows, :]
+            picks = [source & (LANES - 1), (source - own_cells) & (LANES - 1)]
+            turned = [
+                jnp.take_along_axis(stages[1, f, rows, :], picks[f % 2], axis=1, mode="promise_in_bounds")
+                for f in range(FIELDS)
+            ]
+            stages[2, 0, tile(i), :] = jnp.where(even, turned[0], turned[1])
+            stages[2, 1, tile(i), :] = jnp.where(even, turned[2], turned[3])
+            stages[2, 2, tile(i), :] = turned[4]
         return 0
 
-    lax.fori_loop(0, n, shift, 0)
+    lax.fori_loop(0, (n + ROWS - 1) // ROWS, shift, 0)
     narrow = lax.broadcasted_iota(jnp.int32, (n, LANES), 1) < HALF
     for j in range(SUB):
         one, two, three = [stages[2, g, pl.ds(j, n, stride=SUB), :] for g in range(3)]
@@ -399,7 +402,7 @@
 smem = pl.BlockSpec(memory_space=pltpu.SMEM)
 f32 = lambda *s: jax.ShapeDtypeStruct(s, jnp.float32)
 params = pltpu.CompilerParams(vmem_limit_bytes=VMEM_LIMIT)
-cost = pl.CostEstimate(flops=20_000_000, bytes_accessed=600_000, transcendentals=0)
+cost = pl.CostEstimate(flops=9_000_000_000, bytes_accessed=29_000_000, transcendentals=0)
 
 
 def first_step(plan, level, operands):
@@ -482,7 +485,7 @@
             pltpu.VMEM((parts, LANES), jnp.int32),
             pltpu.SemaphoreType.DMA((levels * FIELDS + 2,)),
         ],
-        compiler_params=params,
+        compiler_params=pltpu.CompilerParams(vmem_limit_bytes=PACK_LIMIT),
         name="pack",
     )(place, density, momentum, magnetic, rotation.reshape(parts, LANES), shifts.reshape(parts, LANES))
     owns, fars, (edge, spin_rows, shift_rows) = packed[:levels], packed[levels : 2 * levels], packed[2 * levels :]

time: 72.4 us -> 59.7 us (0.82)
  waiting for transfers between devices: 14.3 us -> 1.05 us
  starting transfers between devices: 15.9 us -> 19.8 us
  Pallas kernels: 37.8 us -> 35.6 us
  local copies, waits for them, and re-layouts: 3.33 us -> 2.05 us
    ppermute x1, waiting for transfers between devices: 6.29 us -> 0.01 us  [body(): lax.ppermute(x, both, [(here(p, r), here(p + 1, 1 - r)) for p, r in every...]
    ppermute x4, waiting for transfers between devices: 4.06 us -> 0.01 us  [body(): lax.ppermute(x, both, [(here(p, 0), here(p + 2, 0)) for p in range(phi_co...]
    ppermute x1, waiting for transfers between devices: 3.9 us -> 1.03 us  [body(): send_side = lambda x: lax.ppermute(x, 'row', [(0, 1), (1, 0)])]
    ppermute x1, starting transfers between devices: 0.01 us -> 2.67 us  [body(): lax.ppermute(x, both, [(here(p, r), here(p + 1, 1 - r)) for p, r in every...]
    ppermute x4, starting transfers between devices: 12.6 us -> 14.7 us  [body(): lax.ppermute(x, both, [(here(p, 0), here(p + 2, 0)) for p in range(phi_co...]
    pallas_call x2, Pallas kernels: 17.5 us -> 15.8 us  [last_step(): pl.pallas_call(kernel, grid=(1,), out_shape=[f32(levels, own_cells, radiu...]
    pallas_call x2, Pallas kernels: 18.8 us -> 17.1 us  [first_step(): pl.pallas_call(kernel, out_shape=[f32(FIELDS * own_cells + EXTRA, radius)...]
    unnamed x10 -> x8, local copies, waits for them, and re-layouts: 3.33 us -> 2.05 us
  transfers between devices with their start and end apart: 10 -> 10, of which waited for: 3 -> 1; matrix products, arithmetic and copies ran while one was open for 0% -> 0% of each run, Pallas kernels for 39% -> 43%
where the time goes in v5:
time: 59.7 us; the launch traced here: 59.3 us
  Pallas kernels  35.6 us (60%)
  starting transfers between devices  19.8 us (33%)
  local copies, waits for them, and re-layouts  2.05 us (3%)
  waiting for transfers between devices  1.05 us (2%)
  between operations  0.79 us (1%)
    pallas_call x2, Pallas kernels, first_step(): pl.pallas_call(kernel, out_shape=[f32(FIELDS * own_cells + EXTRA, radius)...  17.1 us
    pallas_call x2, Pallas kernels, last_step(): pl.pallas_call(kernel, grid=(1,), out_shape=[f32(levels, own_cells, radiu...  15.8 us
    ppermute x4, starting transfers between devices, body(): lax.ppermute(x, both, [(here(p, 0), here(p + 2, 0)) for p in range(phi_co...  14.7 us
    ppermute x1, starting transfers between devices, body(): lax.ppermute(x, both, [(here(p, r), here(p + 1, 1 - r)) for p, r in every...  2.67 us
    ppermute x4, starting transfers between devices, body(): lax.ppermute(x, 'phi', [(p, (p + 1) % phi_count) for p in range(phi_count)])  2.39 us
    pallas_call x1, Pallas kernels, body(): pl.pallas_call(lambda *refs: pack_kernel(spare, levels, *refs), out_shape...  2.07 us
    unnamed x8, local copies, waits for them, and re-layouts  2.05 us
  transfers between devices with their start and end apart: 10, of which 1 were waited for; matrix products, arithmetic and copies ran while one was open for 0% of the time, Pallas kernels for 43%

profile of v5, /device:TPU:0, one launch (start us, length us, event | category | flops | bytes accessed | tf_op | source)
XLA Modules:
  0.0 59.3 jit_solution(2505030649298222614)
XLA Ops:
  0.6 2.1 %pack.1 = (f32[160,256]{1,0:T(8,128)}, f32[160,256]{1,0:T(8,128)}, f32[200,128]{1,0:T(8,128)}, f32[200,128]{1,0:T(8,128)}, f32[2,16,256]{2,1,0:T(8,128)}, /*index=5*/f32[256,128]{1,0:T(8,128)}, f32[256,128]{1,0:T(8,128)}) custom-call(s32[1]{0:T(128)} %bitcast.refs_0_.place, f32[2,32,256]{2,1,0:T(8,128)} %refs_1_.1, f32[2,2,32,256]{3,2,1,0:T(8,128)} %refs_2_.1, ...), custom_call_target="tpu_custom_call" | custom-call | tf_op jit(solution)/shard_map/pack/pallas_call | solution.py:476
  2.7 0.5 collective-permute-start.6
  3.2 4.4 %collective-permute-start.7 = (f32[200,128]{1,0:T(8,128)}, f32[200,128]{1,0:T(8,128)S(1)}, u32[]{:S(2)}, u32[]{:S(2)}) collective-permute-start(f32[200,128]{1,0:T(8,128)} %get-tuple-element.33), channel_id=1, source_target_pairs={{0,4},{2,6},{4,8},{6,10},{8,12},{10,14},{12,16},{14,18},{16,20},{1... | collective-permute-start | bytes 307208 | tf_op jit(solution)/shard_map/ppermute | solution.py:470
  7.7 0.1 collective-permute-start.2
  7.7 2.7 %collective-permute-start.3 = (f32[2,16,256]{2,1,0:T(8,128)}, f32[2,16,256]{2,1,0:T(8,128)S(1)}, u32[]{:S(2)}, u32[]{:S(2)}) collective-permute-start(f32[2,16,256]{2,1,0:T(8,128)} %get-tuple-element.23), channel_id=1, source_target_pairs={{0,3},{1,2},{2,5},{3,4},{4,7},{5,6},{6,9},{7,8},{8,11},{9,10},{10,... | collective-permute-start | bytes 98312 | tf_op jit(solution)/shard_map/ppermute | solution.py:472
  10.4 0.4 collective-permute-start
  10.8 1.0 %collective-permute-done.2.refs_1_.side = f32[2,16,256]{2,1,0:T(8,128)S(1)} collective-permute-done((f32[2,16,256]{2,1,0:T(8,128)}, f32[2,16,256]{2,1,0:T(8,128)S(1)}, u32[]{:S(2)}, u32[]{:S(2)}) %collective-permute-start.2) | collective-permute-done | bytes 32800 | tf_op jit(solution)/shard_map/ppermute | solution.py:471
  11.9 3.4 %collective-permute-start.1 = (f32[200,128]{1,0:T(8,128)}, f32[200,128]{1,0:T(8,128)S(1)}, u32[]{:S(2)}, u32[]{:S(2)}) collective-permute-start(f32[200,128]{1,0:T(8,128)} %get-tuple-element.22), channel_id=1, source_target_pairs={{0,4},{2,6},{4,8},{6,10},{8,12},{10,14},{12,16},{14,18},{16,20},{1... | collective-permute-start | bytes 307208 | tf_op jit(solution)/shard_map/ppermute | solution.py:470
  15.3 0.0 copy-start
  15.3 0.9 %copy-done = f32[256,128]{1,0:T(8,128)S(1)} copy-done((f32[256,128]{1,0:T(8,128)S(1)}, f32[256,128]{1,0:T(8,128)}, u32[]{:S(2)}) %copy-start) | copy-done | bytes 131096
  16.2 0.9 %copy-done.1 = f32[256,128]{1,0:T(8,128)S(1)} copy-done((f32[256,128]{1,0:T(8,128)S(1)}, f32[256,128]{1,0:T(8,128)}, u32[]{:S(2)}) %copy-start.1) | copy-done | bytes 131096
  17.1 0.6 %tables.1 = (f32[256,128]{1,0:T(8,128)S(1)}, s32[256,128]{1,0:T(8,128)S(1)}, f32[256,128]{1,0:T(8,128)S(1)}, s32[256,128]{1,0:T(8,128)S(1)}) custom-call(s32[1]{0:T(128)} %bitcast.refs_0_.place, f32[2,16,256]{2,1,0:T(8,128)S(1)} %collective-permute-done.2.refs_1_.side, f32[256,128]{1,0:T(8,128)S(1)} %copy-done, f32[256,128]{1,0:T(8,128)S(1)} %copy-done.1), custom_call_target="tpu_custom_call" | custom-call | tf_op jit(solution)/shard_map/tables/pallas_call | solution.py:498
  17.7 0.0 collective-permute-done.3.corner
  17.7 0.0 collective-permute-done.7.far
  17.8 0.2 copy-done.3
  18.0 8.5 %first_step.3 = (f32[176,256]{1,0:T(8,128)S(1)}, f32[200,128]{1,0:T(8,128)S(1)}) custom-call(s32[1]{0:T(128)} %bitcast.refs_0_.place, f32[160,256]{1,0:T(8,128)S(1)} %copy-done.3, f32[160,256]{1,0:T(8,128)S(1)} %collective-permute-done.6.near, f32[200,128]{1,0:T(8,128)S(1)} %collective-permute-done.7.far, ...), custom_call_target="tpu_custom_call" | custom-call | flops 8999999488 | bytes 29000000 | tf_op jit(solution)/shard_map/first_step/pallas_call | solution.py:415
  26.6 0.2 collective-permute-start.8
  26.8 3.4 %collective-permute-start.9 = (f32[200,128]{1,0:T(8,128)S(1)}, f32[200,128]{1,0:T(8,128)S(1)}, u32[]{:S(2)}, u32[]{:S(2)}) collective-permute-start(f32[200,128]{1,0:T(8,128)S(1)} %get-tuple-element.35), channel_id=1, source_target_pairs={{0,4},{2,6},{4,8},{6,10},{8,12},{10,14},{12,16},{14,18},{16,20},{1... | collective-permute-start | bytes 307208 | tf_op jit(solution)/shard_map/ppermute | solution.py:470
  30.2 0.0 collective-permute-done.near
  30.3 8.6 %first_step.2 = (f32[176,256]{1,0:T(8,128)S(1)}, f32[200,128]{1,0:T(8,128)S(1)}) custom-call(s32[1]{0:T(128)} %bitcast.refs_0_.place, f32[160,256]{1,0:T(8,128)S(1)} %copy-done.2, f32[160,256]{1,0:T(8,128)S(1)} %collective-permute-done.near, f32[200,128]{1,0:T(8,128)S(1)} %collective-permute-done.1.far, ...), custom_call_target="tpu_custom_call" | custom-call | flops 8999999488 | bytes 29000000 | tf_op jit(solution)/shard_map/first_step/pallas_call | solution.py:415
  38.8 1.2 %collective-permute-start.4 = (f32[176,256]{1,0:T(8,128)S(1)}, f32[176,256]{1,0:T(8,128)S(1)}, u32[]{:S(2)}, u32[]{:S(2)}) collective-permute-start(f32[176,256]{1,0:T(8,128)S(1)} %get-tuple-element.28.own), channel_id=1, source_target_pairs={{0,2},{2,4},{4,6},{6,8},{8,10},{10,12},{12,14},{14,16},{16,18},{18... | collective-permute-start | bytes 540680 | tf_op jit(solution)/shard_map/ppermute | solution.py:469
  40.1 3.4 %collective-permute-start.5 = (f32[200,128]{1,0:T(8,128)S(1)}, f32[200,128]{1,0:T(8,128)S(1)}, u32[]{:S(2)}, u32[]{:S(2)}) collective-permute-start(f32[200,128]{1,0:T(8,128)S(1)} %get-tuple-element.29), channel_id=1, source_target_pairs={{0,4},{2,6},{4,8},{6,10},{8,12},{10,14},{12,16},{14,18},{16,20},{1... | collective-permute-start | bytes 307208 | tf_op jit(solution)/shard_map/ppermute | solution.py:470
  43.5 7.9 %last_step.2 = (f32[2,32,256]{2,1,0:T(8,128)}, f32[2,2,32,256]{3,2,1,0:T(8,128)}, f32[2,2,32,256]{3,2,1,0:T(8,128)}) custom-call(s32[1]{0:T(128)} %bitcast.refs_0_.place, f32[176,256]{1,0:T(8,128)S(1)} %get-tuple-element.34.own, f32[176,256]{1,0:T(8,128)S(1)} %collective-permute-done.8.near, f32[200,128]{1,0:T(8,128)S(1)} %collective-permute-done.9.far, ...), custom_call_target="tpu_custom_call" | custom-call | flops 8999999488 | bytes 29000000 | tf_op jit(solution)/shard_map/last_step/pallas_call | solution.py:438
  51.4 7.9 %last_step.3 = (f32[2,32,256]{2,1,0:T(8,128)}, f32[2,2,32,256]{3,2,1,0:T(8,128)}, f32[2,2,32,256]{3,2,1,0:T(8,128)}) custom-call(s32[1]{0:T(128)} %bitcast.refs_0_.place, f32[176,256]{1,0:T(8,128)S(1)} %get-tuple-element.28.own, f32[176,256]{1,0:T(8,128)S(1)} %collective-permute-done.4.near, ...), custom_call_target="tpu_custom_call", output_to_operand_aliasing={{0}: (6, {}), {1}: (7, {}), {2}: (8, {})} | custom-call | flops 8999999488 | bytes 29000000 | tf_op jit(solution)/shard_map/last_step/pallas_call | solution.py:438
  (10 shorter events, 0.0 us)
Async XLA Ops:
  2.7 15.0 %collective-permute-start.6 = (f32[160,256]{1,0:T(8,128)}, f32[160,256]{1,0:T(8,128)S(1)}, u32[]{:S(2)}, u32[]{:S(2)}) collective-permute-start(f32[160,256]{1,0:T(8,128)} %get-tuple-element.32.own), channel_id=1, source_target_pairs={{0,2},{2,4},{4,6},{6,8},{8,10},{10,12},{12,14},{14,16},{16,18},{18... | collective-permute-start | bytes 491528 | tf_op jit(solution)/shard_map/ppermute | solution.py:469
  3.2 14.5 %collective-permute-start.7 = (f32[200,128]{1,0:T(8,128)}, f32[200,128]{1,0:T(8,128)S(1)}, u32[]{:S(2)}, u32[]{:S(2)}) collective-permute-start(f32[200,128]{1,0:T(8,128)} %get-tuple-element.33), channel_id=1, source_target_pairs={{0,4},{2,6},{4,8},{6,10},{8,12},{10,14},{12,16},{14,18},{16,20},{1... | collective-permute-start | bytes 307208 | tf_op jit(solution)/shard_map/ppermute | solution.py:470
  7.7 4.2 %collective-permute-start.2 = (f32[2,16,256]{2,1,0:T(8,128)}, f32[2,16,256]{2,1,0:T(8,128)S(1)}, u32[]{:S(2)}, u32[]{:S(2)}) collective-permute-start(f32[2,16,256]{2,1,0:T(8,128)} %get-tuple-element.23), channel_id=1, source_target_pairs={{0,1},{1,0},{2,3},{3,2},{4,5},{5,4},{6,7},{7,6},{8,9},{9,8},{10,11... | collective-permute-start | bytes 98312 | tf_op jit(solution)/shard_map/ppermute | solution.py:471
  7.7 10.0 %collective-permute-start.3 = (f32[2,16,256]{2,1,0:T(8,128)}, f32[2,16,256]{2,1,0:T(8,128)S(1)}, u32[]{:S(2)}, u32[]{:S(2)}) collective-permute-start(f32[2,16,256]{2,1,0:T(8,128)} %get-tuple-element.23), channel_id=1, source_target_pairs={{0,3},{1,2},{2,5},{3,4},{4,7},{5,6},{6,9},{7,8},{8,11},{9,10},{10,... | collective-permute-start | bytes 98312 | tf_op jit(solution)/shard_map/ppermute | solution.py:472
  10.4 19.8 %collective-permute-start = (f32[160,256]{1,0:T(8,128)}, f32[160,256]{1,0:T(8,128)S(1)}, u32[]{:S(2)}, u32[]{:S(2)}) collective-permute-start(f32[160,256]{1,0:T(8,128)} %get-tuple-element.21.own), channel_id=1, source_target_pairs={{0,2},{2,4},{4,6},{6,8},{8,10},{10,12},{12,14},{14,16},{16,18},{18... | collective-permute-start | bytes 491528 | tf_op jit(solution)/shard_map/ppermute | solution.py:469
  11.9 18.4 %collective-permute-start.1 = (f32[200,128]{1,0:T(8,128)}, f32[200,128]{1,0:T(8,128)S(1)}, u32[]{:S(2)}, u32[]{:S(2)}) collective-permute-start(f32[200,128]{1,0:T(8,128)} %get-tuple-element.22), channel_id=1, source_target_pairs={{0,4},{2,6},{4,8},{6,10},{8,12},{10,14},{12,16},{14,18},{16,20},{1... | collective-permute-start | bytes 307208 | tf_op jit(solution)/shard_map/ppermute | solution.py:470
  15.3 0.9 %copy-start = (f32[256,128]{1,0:T(8,128)S(1)}, f32[256,128]{1,0:T(8,128)}, u32[]{:S(2)}) copy-start(f32[256,128]{1,0:T(8,128)} %get-tuple-element.24.refs_2_) | copy-start | bytes 393220
  16.2 0.9 %copy-start.1 = (f32[256,128]{1,0:T(8,128)S(1)}, f32[256,128]{1,0:T(8,128)}, u32[]{:S(2)}) copy-start(f32[256,128]{1,0:T(8,128)} %get-tuple-element.25.refs_3_) | copy-start | bytes 393220
  17.1 0.9 %copy-start.3 = (f32[160,256]{1,0:T(8,128)S(1)}, f32[160,256]{1,0:T(8,128)}, u32[]{:S(2)}) copy-start(f32[160,256]{1,0:T(8,128)} %get-tuple-element.32.own) | copy-start | bytes 491524
  18.0 12.2 %copy-start.2 = (f32[160,256]{1,0:T(8,128)S(1)}, f32[160,256]{1,0:T(8,128)}, u32[]{:S(2)}) copy-start(f32[160,256]{1,0:T(8,128)} %get-tuple-element.21.own) | copy-start | bytes 491524
  26.6 16.9 %collective-permute-start.8 = (f32[176,256]{1,0:T(8,128)S(1)}, f32[176,256]{1,0:T(8,128)S(1)}, u32[]{:S(2)}, u32[]{:S(2)}) collective-permute-start(f32[176,256]{1,0:T(8,128)S(1)} %get-tuple-element.34.own), channel_id=1, source_target_pairs={{0,2},{2,4},{4,6},{6,8},{8,10},{10,12},{12,14},{14,16},{16,18},{18... | collective-permute-start | bytes 540680 | tf_op jit(solution)/shard_map/ppermute | solution.py:469
  26.8 16.7 %collective-permute-start.9 = (f32[200,128]{1,0:T(8,128)S(1)}, f32[200,128]{1,0:T(8,128)S(1)}, u32[]{:S(2)}, u32[]{:S(2)}) collective-permute-start(f32[200,128]{1,0:T(8,128)S(1)} %get-tuple-element.35), channel_id=1, source_target_pairs={{0,4},{2,6},{4,8},{6,10},{8,12},{10,14},{12,16},{14,18},{16,20},{1... | collective-permute-start | bytes 307208 | tf_op jit(solution)/shard_map/ppermute | solution.py:470
  38.8 12.6 %collective-permute-start.4 = (f32[176,256]{1,0:T(8,128)S(1)}, f32[176,256]{1,0:T(8,128)S(1)}, u32[]{:S(2)}, u32[]{:S(2)}) collective-permute-start(f32[176,256]{1,0:T(8,128)S(1)} %get-tuple-element.28.own), channel_id=1, source_target_pairs={{0,2},{2,4},{4,6},{6,8},{8,10},{10,12},{12,14},{14,16},{16,18},{18... | collective-permute-start | bytes 540680 | tf_op jit(solution)/shard_map/ppermute | solution.py:469
  40.1 11.4 %collective-permute-start.5 = (f32[200,128]{1,0:T(8,128)S(1)}, f32[200,128]{1,0:T(8,128)S(1)}, u32[]{:S(2)}, u32[]{:S(2)}) collective-permute-start(f32[200,128]{1,0:T(8,128)S(1)} %get-tuple-element.29), channel_id=1, source_target_pairs={{0,4},{2,6},{4,8},{6,10},{8,12},{10,14},{12,16},{14,18},{16,20},{1... | collective-permute-start | bytes 307208 | tf_op jit(solution)/shard_map/ppermute | solution.py:470

commit v6 on v5

--- a/solution.py
+++ b/solution.py
@@ -17,7 +17,8 @@
 SLOTS = 2 * SUB
 EXTRA = 2 * SUB
 TALL = 32
-ROWS = 4
+ROWS = 3
+PICKS = 4
 VMEM_LIMIT = 32 * 1024 * 1024
 PACK_LIMIT = 60 * 1024 * 1024
 
@@ -132,11 +133,10 @@
             for k in (1, 2):
                 stages[stage, f, tile(first - k), :] = jnp.where(low_mask, inner, stages[stage, f, tile(first - k), :])
                 stages[stage, f, tile(last + k), :] = jnp.where(high_mask, outer, stages[stage, f, tile(last + k), :])
-        lo = 2 * stage + 2
-        count = n + 2 * REACH - 4 - 4 * stage
-        before = radial_faces([[stages[stage, f, tile(lo + k), :] for f in range(FIELDS)] for k in range(-2, 2)])[0]
-        turns = lax.div(count + ROWS - 1, ROWS)
-        lax.fori_loop(0, turns, lambda c, carried: tuple(work(stage, lo + c * ROWS, ROWS, list(carried))), tuple(before))
+        lo = 2 * stage + 1
+        turns = lax.div(n + 2 * REACH - 3 - 4 * stage + ROWS - 1, ROWS)
+        before = (jnp.zeros((SUB, LANES), jnp.float32),) * FIELDS
+        lax.fori_loop(0, turns, lambda c, carried: tuple(work(stage, lo + c * ROWS, ROWS, list(carried))), before)
         return 0
 
     lax.fori_loop(0, STAGES, run, 0)
@@ -170,7 +170,7 @@
 
 def pack_kernel(spare, levels, place, density, momentum, magnetic, rotation, shifts, *rest):
     nears, fars, rest = rest[:levels], rest[levels : 2 * levels], rest[2 * levels :]
-    edge, spin_rows, shift_rows, spin_in, shift_in, arrived = rest
+    edge, spin_in, shift_in, arrived = rest
     own_cells, radius = density.shape[1:]
     on_low = place[0] == 0
     parts = radius // LANES
@@ -187,10 +187,6 @@
         copy.start()
     for copy in copies[:2]:
         copy.wait()
-    for part in range(parts):
-        rows = slice(part * LANES, (part + 1) * LANES)
-        spin_rows[rows, :] = jnp.broadcast_to(spin_in[part : part + 1, :], (LANES, LANES)).T * time_step
-        shift_rows[rows, :] = jnp.broadcast_to(shift_in[part : part + 1, :].astype(jnp.float32), (LANES, LANES)).T
     wide = lambda ref: jnp.broadcast_to(
         jnp.where(on_low, ref[parts - 1 : parts, :], ref[0:1, :]).astype(jnp.float32), (own_cells, LANES)
     )
@@ -223,7 +219,7 @@
         return slice(start, start + TALL)
 
 
-def table_kernel(plans, place, side, spin_rows, shift_rows, *rest):
+def table_kernel(plans, place, side, rotation, shifts, *rest):
     outs, held = rest[:-1], rest[-1]
     lane = lax.broadcasted_iota(jnp.int32, (SUB, LANES), 1)
     sublane = lax.broadcasted_iota(jnp.int32, (SUB, LANES), 0)
@@ -232,9 +228,12 @@
     for which, (n, radius, own_cells, total, spare, moved) in enumerate(plans):
         spin, pick = outs[2 * which : 2 * which + 2]
         blocks = Blocks(place[0], n, radius, total, moved)
-        held[0, pl.ds(blocks.own_at, radius), :] = spin_rows[...]
+        for part in range(radius // LANES):
+            rows = pl.ds(blocks.own_at + part * LANES, LANES)
+            along = lambda ref: jnp.broadcast_to(ref[part : part + 1, :].astype(jnp.float32), (LANES, LANES)).T
+            held[0, rows, :] = along(rotation) * time_step
+            held[1, rows, :] = along(shifts)
         held[0, pl.ds(blocks.edge_at, EXTRA), :] = spread(more, own_cells, own_cells)
-        held[1, pl.ds(blocks.own_at, radius), :] = shift_rows[...]
         held[1, pl.ds(blocks.edge_at, EXTRA), :] = spread(more, 2 * own_cells, own_cells)
         bound = jnp.zeros((SUB, LANES), jnp.int32)
         for j in range(SUB):
@@ -317,8 +316,8 @@
     even = (lane & own_cells) == 0
 
     def shift(turn, _):
-        for k in range(ROWS):
-            i = turn * ROWS + k
+        for k in range(PICKS):
+            i = turn * PICKS + k
             rows = tile(REACH + i)
             source = pick[rows, :]
             picks = [source & (LANES - 1), (source - own_cells) & (LANES - 1)]
@@ -331,7 +330,7 @@
             stages[2, 2, tile(i), :] = turned[4]
         return 0
 
-    lax.fori_loop(0, (n + ROWS - 1) // ROWS, shift, 0)
+    lax.fori_loop(0, (n + PICKS - 1) // PICKS, shift, 0)
     narrow = lax.broadcasted_iota(jnp.int32, (n, LANES), 1) < HALF
     for j in range(SUB):
         one, two, three = [stages[2, g, pl.ds(j, n, stride=SUB), :] for g in range(3)]
@@ -366,24 +365,30 @@
         pack_far(self.far, self.near, self.own_cells, self.spare)
 
 
-class ToResult:
-    def __init__(self, density, momentum, magnetic):
-        self.outs = (density, momentum, magnetic)
+class ToBuffer:
+    def __init__(self, buffer):
+        self.buffer = buffer
 
     def fields(self, columns, four, fifth):
-        density, momentum, magnetic = self.outs
-        cells = density.shape[1]
-        density[0, :, columns] = four[0:cells]
-        momentum[0, 0, :, columns] = four[cells : 2 * cells]
-        momentum[1, 0, :, columns] = four[2 * cells : 3 * cells]
-        magnetic[0, 0, :, columns] = four[3 * cells : 4 * cells]
-        magnetic[1, 0, :, columns] = fifth[0:cells]
+        split = four.shape[0]
+        self.buffer[0:split, columns] = four
+        self.buffer[split:, columns] = fifth[0 : self.buffer.shape[0] - split]
 
     def edge(self, first, second):
         pass
 
     def end(self):
         pass
+
+
+def copies_out(level, buffer, outs, sent):
+    density, momentum, magnetic = outs
+    cells = density.shape[1]
+    targets = [density.at[level]] + [x.at[k, level] for x in (momentum, magnetic) for k in range(2)]
+    return [
+        pltpu.make_async_copy(buffer.at[pl.ds(f * cells, cells), :], x, sent.at[level * FIELDS + f])
+        for f, x in enumerate(targets)
+    ]
 
 
 def tall_of(n):
@@ -424,29 +429,47 @@
     )(*operands)
 
 
-def last_step(plan, level, operands, results, levels):
+def last_step(plan, level, operands, done, levels):
     n, radius, own_cells, total, spare, moved = plan
     tail = pl.ds(FIELDS * own_cells, EXTRA)
-    count = len(results)
+    final = level == levels - 1
+    buffer = f32(FIELDS * own_cells, radius)
 
     def kernel(place, own, near, far, spin, pick, *rest):
-        outs, scratch = rest[count : count + 3], rest[count + 3 :]
         refs = (place, own, own.at[tail, :], near, near.at[tail, :], far, spin, pick)
-        step_kernel(plan, refs, ToResult(*outs), scratch)
-
-    pair = pl.BlockSpec((2, 1, own_cells, radius), lambda i: (0, level, 0, 0))
+        if not final:
+            step_kernel(plan, refs, ToBuffer(rest[0]), rest[1:])
+            return
+        ready, outs, scratch = rest[: levels - 1], rest[levels - 1 : levels + 2], rest[levels + 2 :]
+        last, sent = scratch[-2:]
+        copies = []
+        for k, x in enumerate(ready):
+            copies += copies_out(k, x, outs, sent)
+        for copy in copies:
+            copy.start()
+        step_kernel(plan, refs, ToBuffer(last), scratch[:-2])
+        rest_of = copies_out(level, last, outs, sent)
+        for copy in rest_of:
+            copy.start()
+        for copy in copies + rest_of:
+            copy.wait()
+
+    if final:
+        out_shape = [f32(levels, own_cells, radius), f32(2, levels, own_cells, radius), f32(2, levels, own_cells, radius)]
+        more = [pltpu.VMEM((FIELDS * own_cells, radius), jnp.float32), pltpu.SemaphoreType.DMA((levels * FIELDS,))]
+    else:
+        out_shape = buffer
+        more = []
     return pl.pallas_call(
         kernel,
-        grid=(1,),
-        out_shape=[f32(levels, own_cells, radius), f32(2, levels, own_cells, radius), f32(2, levels, own_cells, radius)],
-        in_specs=[smem] + [vmem] * 5 + [pl.BlockSpec(memory_space=pl.ANY)] * count,
-        out_specs=[pl.BlockSpec((1, own_cells, radius), lambda i: (level, 0, 0)), pair, pair],
-        scratch_shapes=step_scratch(n),
-        input_output_aliases={len(operands) + k: k for k in range(count)},
+        out_shape=out_shape,
+        in_specs=[smem] + [vmem] * (5 + len(done)),
+        out_specs=[pl.BlockSpec(memory_space=pltpu.HBM)] * 3 if final else vmem,
+        scratch_shapes=step_scratch(n) + more,
         compiler_params=params,
         cost_estimate=cost,
         name="last_step",
-    )(*operands, *results)
+    )(*operands, *done)
 
 
 def body(density, momentum, magnetic, rotation, shifts):
@@ -467,19 +490,20 @@
     everyone = [(p, r) for p in range(phi_count) for r in range(row_count)]
     both = ("phi", "row")
     send_near = lambda x: lax.ppermute(x, "phi", [(p, (p + 1) % phi_count) for p in range(phi_count)])
-    send_far = lambda x: lax.ppermute(x, both, [(here(p, 0), here(p + 2, 0)) for p in range(phi_count)])
+    send_far = lambda x: lax.ppermute(x, "phi", [(p, (p + 2) % phi_count) for p in range(phi_count)])
     send_side = lambda x: lax.ppermute(x, "row", [(0, 1), (1, 0)])
     send_corner = lambda x: lax.ppermute(x, both, [(here(p, r), here(p + 1, 1 - r)) for p, r in everyone])
 
+    spins, turns = rotation.reshape(parts, LANES), shifts.reshape(parts, LANES)
     near_message = f32(FIELDS * own_cells, radius)
     far_message = f32(FIELDS * (own_cells + SUB), LANES)
     packed = pl.pallas_call(
         lambda *refs: pack_kernel(spare, levels, *refs),
         out_shape=[near_message] * levels
         + [far_message] * levels
-        + [f32(levels, EXTRA, 2 * LANES), f32(radius, LANES), f32(radius, LANES)],
+        + [f32(levels, EXTRA, 2 * LANES)],
         in_specs=[smem] + [pl.BlockSpec(memory_space=pltpu.HBM)] * 5,
-        out_specs=[vmem] * (2 * levels + 3),
+        out_specs=[vmem] * (2 * levels + 1),
         scratch_shapes=[
             pltpu.VMEM((parts, LANES), jnp.float32),
             pltpu.VMEM((parts, LANES), jnp.int32),
@@ -487,8 +511,8 @@
         ],
         compiler_params=pltpu.CompilerParams(vmem_limit_bytes=PACK_LIMIT),
         name="pack",
-    )(place, density, momentum, magnetic, rotation.reshape(parts, LANES), shifts.reshape(parts, LANES))
-    owns, fars, (edge, spin_rows, shift_rows) = packed[:levels], packed[levels : 2 * levels], packed[2 * levels :]
+    )(place, density, momentum, magnetic, spins, turns)
+    owns, fars, edge = packed[:levels], packed[levels : 2 * levels], packed[2 * levels]
 
     side = send_side(edge)
     corner = send_corner(edge)
@@ -503,18 +527,20 @@
         scratch_shapes=[pltpu.VMEM((2, tall_of(n + 1), LANES), jnp.float32)],
         compiler_params=params,
         name="tables",
-    )(place, side, spin_rows, shift_rows)
+    )(place, side, spins, turns)
     moved = [(send_near(own), send_far(far)) for own, far in zip(owns, fars)]
     states = []
     for level in range(levels):
         near, far = moved[level]
         states.append(first_step(wide, level, (place, owns[level], near, far, side, corner, *tables[:2])))
     moved = [(send_near(own), send_far(far)) for own, far in states]
-    results = ()
+    done = ()
     for level in range(levels):
         near, far = moved[level]
-        results = last_step(plain, level, (place, states[level][0], near, far, *tables[2:]), results, levels)
-    return tuple(results)
+        operands = (place, states[level][0], near, far, *tables[2:])
+        result = last_step(plain, level, operands, done if level == levels - 1 else (), levels)
+        done += (result,)
+    return tuple(result)
 
 
 def solution(mesh):

time: 59.7 us -> 57.7 us (0.966)
  starting transfers between devices: 19.8 us -> 9.15 us
  Pallas kernels: 35.6 us -> 41.8 us
  waiting for transfers between devices: 1.05 us -> 4.46 us
  local copies, waits for them, and re-layouts: 2.05 us -> 0.93 us
    ppermute x4, starting transfers between devices: 14.7 us -> 4.45 us  [body(): lax.ppermute(x, 'phi', [(p, (p + 2) % phi_count) for p in range(phi_count)])]
    pallas_call x2, Pallas kernels: 15.8 us -> 19.3 us  [last_step(): pl.pallas_call(kernel, out_shape=out_shape, in_specs=[smem] + [vmem] * (5...]
    ppermute x1, waiting for transfers between devices: 0.01 us -> 3.39 us  [body(): lax.ppermute(x, both, [(here(p, r), here(p + 1, 1 - r)) for p, r in every...]
    pallas_call x2, Pallas kernels: 17.1 us -> 19.7 us  [first_step(): pl.pallas_call(kernel, out_shape=[f32(FIELDS * own_cells + EXTRA, radius)...]
    ppermute x1, starting transfers between devices: 2.67 us -> 1.15 us  [body(): lax.ppermute(x, both, [(here(p, r), here(p + 1, 1 - r)) for p, r in every...]
    ppermute x1, starting transfers between devices: 0.07 us -> 1.49 us  [body(): send_side = lambda x: lax.ppermute(x, 'row', [(0, 1), (1, 0)])]
    unnamed x8, local copies, waits for them, and re-layouts: 2.05 us -> 0.93 us
  transfers between devices with their start and end apart: 10 -> 10, of which waited for: 1 -> 2; matrix products, arithmetic and copies ran while one was open for 0% -> 0% of each run, Pallas kernels for 43% -> 52%
where the time goes in v6:
time: 57.7 us; the launch traced here: 57.1 us
  Pallas kernels  41.8 us (72%)
  starting transfers between devices  9.15 us (16%)
  waiting for transfers between devices  4.46 us (8%)
  local copies, waits for them, and re-layouts  0.93 us (2%)
  between operations  0.73 us (1%)
    pallas_call x2, Pallas kernels, first_step(): pl.pallas_call(kernel, out_shape=[f32(FIELDS * own_cells + EXTRA, radius)...  19.7 us
    pallas_call x2, Pallas kernels, last_step(): pl.pallas_call(kernel, out_shape=out_shape, in_specs=[smem] + [vmem] * (5...  19.3 us
    ppermute x4, starting transfers between devices, body(): lax.ppermute(x, 'phi', [(p, (p + 2) % phi_count) for p in range(phi_count)])  4.45 us
    ppermute x1, waiting for transfers between devices, body(): lax.ppermute(x, both, [(here(p, r), here(p + 1, 1 - r)) for p, r in every...  3.39 us
    ppermute x4, starting transfers between devices, body(): lax.ppermute(x, 'phi', [(p, (p + 1) % phi_count) for p in range(phi_count)])  2.05 us
    pallas_call x1, Pallas kernels, body(): pl.pallas_call(lambda *refs: pack_kernel(spare, levels, *refs), out_shape...  1.99 us
    ppermute x1, starting transfers between devices, body(): send_side = lambda x: lax.ppermute(x, 'row', [(0, 1), (1, 0)])  1.49 us
  transfers between devices with their start and end apart: 10, of which 2 were waited for; matrix products, arithmetic and copies ran while one was open for 0% of the time, Pallas kernels for 52%

profile of v6, /device:TPU:0, one launch (start us, length us, event | category | flops | bytes accessed | tf_op | source)
XLA Modules:
  0.0 57.1 jit_solution(3976002267903959500)
XLA Ops:
  0.6 2.0 %pack.1 = (f32[160,256]{1,0:T(8,128)}, f32[160,256]{1,0:T(8,128)}, f32[200,128]{1,0:T(8,128)}, f32[200,128]{1,0:T(8,128)}, f32[2,16,256]{2,1,0:T(8,128)}) custom-call(s32[1]{0:T(128)} %bitcast.refs_0_.place, f32[2,32,256]{2,1,0:T(8,128)} %refs_1_.1, f32[2,2,32,256]{3,2,1,0:T(8,128)} %refs_2_.1, f32[2,2,32,256]{3,2,1,0:T(8,128)} %refs_3_.1, ...), custom_call_target="tpu_custom_call" | custom-call | tf_op jit(solution)/shard_map/pack/pallas_call | solution.py:500
  2.6 0.5 collective-permute-start.6
  3.1 2.6 %collective-permute-start.7 = (f32[200,128]{1,0:T(8,128)}, f32[200,128]{1,0:T(8,128)S(1)}, u32[]{:S(2)}, u32[]{:S(2)}) collective-permute-start(f32[200,128]{1,0:T(8,128)} %get-tuple-element.26), channel_id=1, source_target_pairs={{0,4},{2,6},{4,8},{6,10},{8,12},{10,14},{12,16},{14,18},{16,20},{1... | collective-permute-start | bytes 307208 | tf_op jit(solution)/shard_map/ppermute | solution.py:493
  5.7 1.5 %collective-permute-start.2 = (f32[2,16,256]{2,1,0:T(8,128)}, f32[2,16,256]{2,1,0:T(8,128)S(1)}, u32[]{:S(2)}, u32[]{:S(2)}) collective-permute-start(f32[2,16,256]{2,1,0:T(8,128)} %get-tuple-element.18), channel_id=1, source_target_pairs={{0,1},{1,0},{2,3},{3,2},{4,5},{5,4},{6,7},{7,6},{8,9},{9,8},{10,11... | collective-permute-start | bytes 98312 | tf_op jit(solution)/shard_map/ppermute | solution.py:494
  7.2 1.1 %collective-permute-start.3 = (f32[2,16,256]{2,1,0:T(8,128)}, f32[2,16,256]{2,1,0:T(8,128)S(1)}, u32[]{:S(2)}, u32[]{:S(2)}) collective-permute-start(f32[2,16,256]{2,1,0:T(8,128)} %get-tuple-element.18), channel_id=1, source_target_pairs={{0,3},{1,2},{2,5},{3,4},{4,7},{5,6},{6,9},{7,8},{8,11},{9,10},{10,... | collective-permute-start | bytes 98312 | tf_op jit(solution)/shard_map/ppermute | solution.py:495
  8.4 0.5 collective-permute-start
  8.8 1.1 %collective-permute-done.2.refs_1_.side = f32[2,16,256]{2,1,0:T(8,128)S(1)} collective-permute-done((f32[2,16,256]{2,1,0:T(8,128)}, f32[2,16,256]{2,1,0:T(8,128)S(1)}, u32[]{:S(2)}, u32[]{:S(2)}) %collective-permute-start.2) | collective-permute-done | bytes 32800 | tf_op jit(solution)/shard_map/ppermute | solution.py:494
  9.9 1.5 %collective-permute-start.1 = (f32[200,128]{1,0:T(8,128)}, f32[200,128]{1,0:T(8,128)S(1)}, u32[]{:S(2)}, u32[]{:S(2)}) collective-permute-start(f32[200,128]{1,0:T(8,128)} %get-tuple-element.17), channel_id=1, source_target_pairs={{0,4},{2,6},{4,8},{6,10},{8,12},{10,14},{12,16},{14,18},{16,20},{1... | collective-permute-start | bytes 307208 | tf_op jit(solution)/shard_map/ppermute | solution.py:493
  11.4 0.8 %tables.1 = (f32[256,128]{1,0:T(8,128)S(1)}, s32[256,128]{1,0:T(8,128)S(1)}, f32[256,128]{1,0:T(8,128)S(1)}, s32[256,128]{1,0:T(8,128)S(1)}) custom-call(s32[1]{0:T(128)} %bitcast.refs_0_.place, f32[2,16,256]{2,1,0:T(8,128)S(1)} %collective-permute-done.2.refs_1_.side, f32[2,128]{1,0:T(2,128)S(1)} %bitcast.4, s32[2,128]{1,0:T(2,128)S(1)} %bitcast.6), custom_call_target="tpu_custom_call" | custom-call | tf_op jit(solution)/shard_map/tables/pallas_call | solution.py:522
  12.2 3.4 %collective-permute-done.3.corner = f32[2,16,256]{2,1,0:T(8,128)S(1)} collective-permute-done((f32[2,16,256]{2,1,0:T(8,128)}, f32[2,16,256]{2,1,0:T(8,128)S(1)}, u32[]{:S(2)}, u32[]{:S(2)}) %collective-permute-start.3) | collective-permute-done | bytes 32800 | tf_op jit(solution)/shard_map/ppermute | solution.py:495
  15.6 0.0 collective-permute-done.7.far
  15.6 0.0 collective-permute-done.6.near
  15.6 0.9 %copy-done.3 = f32[160,256]{1,0:T(8,128)S(1)} copy-done((f32[160,256]{1,0:T(8,128)S(1)}, f32[160,256]{1,0:T(8,128)}, u32[]{:S(2)}) %copy-start.3) | copy-done | bytes 163864
  16.5 9.8 %first_step.3 = (f32[176,256]{1,0:T(8,128)S(1)}, f32[200,128]{1,0:T(8,128)S(1)}) custom-call(s32[1]{0:T(128)} %bitcast.refs_0_.place, f32[160,256]{1,0:T(8,128)S(1)} %copy-done.3, f32[160,256]{1,0:T(8,128)S(1)} %collective-permute-done.6.near, f32[200,128]{1,0:T(8,128)S(1)} %collective-permute-done.7.far, ...), custom_call_target="tpu_custom_call" | custom-call | flops 8999999488 | bytes 29000000 | tf_op jit(solution)/shard_map/first_step/pallas_call | solution.py:420
  26.4 0.1 collective-permute-start.8
  26.4 0.1 collective-permute-start.9
  26.5 0.0 collective-permute-done.1.far
  26.5 9.9 %first_step.2 = (f32[176,256]{1,0:T(8,128)S(1)}, f32[200,128]{1,0:T(8,128)S(1)}) custom-call(s32[1]{0:T(128)} %bitcast.refs_0_.place, f32[160,256]{1,0:T(8,128)S(1)} %copy-done.2, f32[160,256]{1,0:T(8,128)S(1)} %collective-permute-done.near, f32[200,128]{1,0:T(8,128)S(1)} %collective-permute-done.1.far, ...), custom_call_target="tpu_custom_call" | custom-call | flops 8999999488 | bytes 29000000 | tf_op jit(solution)/shard_map/first_step/pallas_call | solution.py:420
  36.4 1.0 %collective-permute-start.4 = (f32[176,256]{1,0:T(8,128)S(1)}, f32[176,256]{1,0:T(8,128)S(1)}, u32[]{:S(2)}, u32[]{:S(2)}) collective-permute-start(f32[176,256]{1,0:T(8,128)S(1)} %get-tuple-element.21.own), channel_id=1, source_target_pairs={{0,2},{2,4},{4,6},{6,8},{8,10},{10,12},{12,14},{14,16},{16,18},{18... | collective-permute-start | bytes 540680 | tf_op jit(solution)/shard_map/ppermute | solution.py:492
  37.4 0.3 collective-permute-start.5
  37.7 0.0 collective-permute-done.9.far
  37.7 0.0 collective-permute-done.8.near
  37.7 9.3 %last_step.2.rest_0_ = f32[160,256]{1,0:T(8,128)S(1)} custom-call(s32[1]{0:T(128)} %bitcast.refs_0_.place, f32[176,256]{1,0:T(8,128)S(1)} %get-tuple-element.27.own, f32[176,256]{1,0:T(8,128)S(1)} %collective-permute-done.8.near, f32[200,128]{1,0:T(8,128)S(1)} %collective-permute-done.9.far, f32[256,128]{1,0:T(8,128)S(1)} %get-tuple-element.23.spin, ...), custom_call_target="tpu_custom_call" | custom-call | flops 8999999488 | bytes 29000000 | tf_op jit(solution)/shard_map/last_step/pallas_call | solution.py:463
  47.0 10.0 %last_step.3 = (f32[2,32,256]{2,1,0:T(8,128)}, f32[2,2,32,256]{3,2,1,0:T(8,128)}, f32[2,2,32,256]{3,2,1,0:T(8,128)}) custom-call(s32[1]{0:T(128)} %bitcast.refs_0_.place, f32[176,256]{1,0:T(8,128)S(1)} %get-tuple-element.21.own, f32[176,256]{1,0:T(8,128)S(1)} %collective-permute-done.4.near, f32[200,128]{1,0:T(8,128)S(1)} %collective-permute-done.5.far, ...), custom_call_target="tpu_custom_call" | custom-call | flops 8999999488 | bytes 29000000 | tf_op jit(solution)/shard_map/last_step/pallas_call | solution.py:463
  (10 shorter events, 0.0 us)
Async XLA Ops:
  2.6 13.0 %collective-permute-start.6 = (f32[160,256]{1,0:T(8,128)}, f32[160,256]{1,0:T(8,128)S(1)}, u32[]{:S(2)}, u32[]{:S(2)}) collective-permute-start(f32[160,256]{1,0:T(8,128)} %get-tuple-element.25.own), channel_id=1, source_target_pairs={{0,2},{2,4},{4,6},{6,8},{8,10},{10,12},{12,14},{14,16},{16,18},{18... | collective-permute-start | bytes 491528 | tf_op jit(solution)/shard_map/ppermute | solution.py:492
  3.1 12.5 %collective-permute-start.7 = (f32[200,128]{1,0:T(8,128)}, f32[200,128]{1,0:T(8,128)S(1)}, u32[]{:S(2)}, u32[]{:S(2)}) collective-permute-start(f32[200,128]{1,0:T(8,128)} %get-tuple-element.26), channel_id=1, source_target_pairs={{0,4},{2,6},{4,8},{6,10},{8,12},{10,14},{12,16},{14,18},{16,20},{1... | collective-permute-start | bytes 307208 | tf_op jit(solution)/shard_map/ppermute | solution.py:493
  5.7 4.2 %collective-permute-start.2 = (f32[2,16,256]{2,1,0:T(8,128)}, f32[2,16,256]{2,1,0:T(8,128)S(1)}, u32[]{:S(2)}, u32[]{:S(2)}) collective-permute-start(f32[2,16,256]{2,1,0:T(8,128)} %get-tuple-element.18), channel_id=1, source_target_pairs={{0,1},{1,0},{2,3},{3,2},{4,5},{5,4},{6,7},{7,6},{8,9},{9,8},{10,11... | collective-permute-start | bytes 98312 | tf_op jit(solution)/shard_map/ppermute | solution.py:494
  7.2 8.4 %collective-permute-start.3 = (f32[2,16,256]{2,1,0:T(8,128)}, f32[2,16,256]{2,1,0:T(8,128)S(1)}, u32[]{:S(2)}, u32[]{:S(2)}) collective-permute-start(f32[2,16,256]{2,1,0:T(8,128)} %get-tuple-element.18), channel_id=1, source_target_pairs={{0,3},{1,2},{2,5},{3,4},{4,7},{5,6},{6,9},{7,8},{8,11},{9,10},{10,... | collective-permute-start | bytes 98312 | tf_op jit(solution)/shard_map/ppermute | solution.py:495
  8.4 3.0 %copy-start.1 = (s32[256]{0:T(256)S(1)}, s32[256]{0:T(256)}, u32[]{:S(2)}) copy-start(s32[256]{0:T(256)} %param.9) | copy-start | bytes 3076
  8.4 3.0 %copy-start = (f32[256]{0:T(256)S(1)}, f32[256]{0:T(256)}, u32[]{:S(2)}) copy-start(f32[256]{0:T(256)} %param.8) | copy-start | bytes 3076
  8.4 18.2 %collective-permute-start = (f32[160,256]{1,0:T(8,128)}, f32[160,256]{1,0:T(8,128)S(1)}, u32[]{:S(2)}, u32[]{:S(2)}) collective-permute-start(f32[160,256]{1,0:T(8,128)} %get-tuple-element.16.own), channel_id=1, source_target_pairs={{0,2},{2,4},{4,6},{6,8},{8,10},{10,12},{12,14},{14,16},{16,18},{18... | collective-permute-start | bytes 491528 | tf_op jit(solution)/shard_map/ppermute | solution.py:492
  9.9 16.6 %collective-permute-start.1 = (f32[200,128]{1,0:T(8,128)}, f32[200,128]{1,0:T(8,128)S(1)}, u32[]{:S(2)}, u32[]{:S(2)}) collective-permute-start(f32[200,128]{1,0:T(8,128)} %get-tuple-element.17), channel_id=1, source_target_pairs={{0,4},{2,6},{4,8},{6,10},{8,12},{10,14},{12,16},{14,18},{16,20},{1... | collective-permute-start | bytes 307208 | tf_op jit(solution)/shard_map/ppermute | solution.py:493
  15.6 0.9 %copy-start.3 = (f32[160,256]{1,0:T(8,128)S(1)}, f32[160,256]{1,0:T(8,128)}, u32[]{:S(2)}) copy-start(f32[160,256]{1,0:T(8,128)} %get-tuple-element.25.own) | copy-start | bytes 491524
  16.5 10.0 %copy-start.2 = (f32[160,256]{1,0:T(8,128)S(1)}, f32[160,256]{1,0:T(8,128)}, u32[]{:S(2)}) copy-start(f32[160,256]{1,0:T(8,128)} %get-tuple-element.16.own) | copy-start | bytes 491524
  26.4 11.4 %collective-permute-start.8 = (f32[176,256]{1,0:T(8,128)S(1)}, f32[176,256]{1,0:T(8,128)S(1)}, u32[]{:S(2)}, u32[]{:S(2)}) collective-permute-start(f32[176,256]{1,0:T(8,128)S(1)} %get-tuple-element.27.own), channel_id=1, source_target_pairs={{0,2},{2,4},{4,6},{6,8},{8,10},{10,12},{12,14},{14,16},{16,18},{18... | collective-permute-start | bytes 540680 | tf_op jit(solution)/shard_map/ppermute | solution.py:492
  26.4 11.3 %collective-permute-start.9 = (f32[200,128]{1,0:T(8,128)S(1)}, f32[200,128]{1,0:T(8,128)S(1)}, u32[]{:S(2)}, u32[]{:S(2)}) collective-permute-start(f32[200,128]{1,0:T(8,128)S(1)} %get-tuple-element.28), channel_id=1, source_target_pairs={{0,4},{2,6},{4,8},{6,10},{8,12},{10,14},{12,16},{14,18},{16,20},{1... | collective-permute-start | bytes 307208 | tf_op jit(solution)/shard_map/ppermute | solution.py:493
  36.4 10.6 %collective-permute-start.4 = (f32[176,256]{1,0:T(8,128)S(1)}, f32[176,256]{1,0:T(8,128)S(1)}, u32[]{:S(2)}, u32[]{:S(2)}) collective-permute-start(f32[176,256]{1,0:T(8,128)S(1)} %get-tuple-element.21.own), channel_id=1, source_target_pairs={{0,2},{2,4},{4,6},{6,8},{8,10},{10,12},{12,14},{14,16},{16,18},{18... | collective-permute-start | bytes 540680 | tf_op jit(solution)/shard_map/ppermute | solution.py:492
  37.4 9.6 %collective-permute-start.5 = (f32[200,128]{1,0:T(8,128)S(1)}, f32[200,128]{1,0:T(8,128)S(1)}, u32[]{:S(2)}, u32[]{:S(2)}) collective-permute-start(f32[200,128]{1,0:T(8,128)S(1)} %get-tuple-element.22), channel_id=1, source_target_pairs={{0,4},{2,6},{4,8},{6,10},{8,12},{10,14},{12,16},{14,18},{16,20},{1... | collective-permute-start | bytes 307208 | tf_op jit(solution)/shard_map/ppermute | solution.py:493

commit v7 on v6

--- a/solution.py
+++ b/solution.py
@@ -17,10 +17,10 @@
 SLOTS = 2 * SUB
 EXTRA = 2 * SUB
 TALL = 32
-ROWS = 3
+ROWS = 4
 PICKS = 4
 VMEM_LIMIT = 32 * 1024 * 1024
-PACK_LIMIT = 60 * 1024 * 1024
+EDGE_LIMIT = 60 * 1024 * 1024
 
 time_step = 0.08
 
@@ -133,9 +133,16 @@
             for k in (1, 2):
                 stages[stage, f, tile(first - k), :] = jnp.where(low_mask, inner, stages[stage, f, tile(first - k), :])
                 stages[stage, f, tile(last + k), :] = jnp.where(high_mask, outer, stages[stage, f, tile(last + k), :])
-        lo = 2 * stage + 1
-        turns = lax.div(n + 2 * REACH - 3 - 4 * stage + ROWS - 1, ROWS)
-        before = (jnp.zeros((SUB, LANES), jnp.float32),) * FIELDS
+        count = n + 2 * REACH - 4 - 4 * stage
+        if n % ROWS == 0:
+            lo = 2 * stage + 2
+            ahead = [[stages[stage, f, tile(lo + k), :] for f in range(FIELDS)] for k in range(-2, 2)]
+            before = tuple(radial_faces(ahead)[0])
+        else:
+            lo = 2 * stage + 1
+            count = count + 1
+            before = (jnp.zeros((SUB, LANES), jnp.float32),) * FIELDS
+        turns = lax.div(count + ROWS - 1, ROWS)
         lax.fori_loop(0, turns, lambda c, carried: tuple(work(stage, lo + c * ROWS, ROWS, list(carried))), before)
         return 0
 
@@ -168,24 +175,24 @@
     lax.fori_loop(0, FIELDS, one, 0)
 
 
-def pack_kernel(spare, levels, place, density, momentum, magnetic, rotation, shifts, *rest):
-    nears, fars, rest = rest[:levels], rest[levels : 2 * levels], rest[2 * levels :]
-    edge, spin_in, shift_in, arrived = rest
-    own_cells, radius = density.shape[1:]
+def edge_kernel(place, density, momentum, magnetic, rotation, shifts, edge, ends, spin_in, shift_in, arrived):
+    levels, own_cells, radius = density.shape
     on_low = place[0] == 0
     parts = radius // LANES
+    split = 4 * own_cells
+    columns = pl.ds(pl.multiple_of(jnp.where(on_low, radius - LANES, 0), LANES), LANES)
     copies = [
         pltpu.make_async_copy(rotation, spin_in, arrived.at[levels * FIELDS]),
         pltpu.make_async_copy(shifts, shift_in, arrived.at[levels * FIELDS + 1]),
     ]
     for level in range(levels):
-        sources = [density.at[level]] + [x.at[k, level] for x in (momentum, magnetic) for k in range(2)]
+        sources = [density.at[level, :, columns]] + [x.at[k, level, :, columns] for x in (momentum, magnetic) for k in range(2)]
         for f, x in enumerate(sources):
-            at = nears[level].at[pl.ds(f * own_cells, own_cells), :]
+            at = ends.at[level, pl.ds(f * own_cells, own_cells), :]
             copies.append(pltpu.make_async_copy(x, at, arrived.at[level * FIELDS + f]))
     for copy in copies:
         copy.start()
-    for copy in copies[:2]:
+    for copy in copies:
         copy.wait()
     wide = lambda ref: jnp.broadcast_to(
         jnp.where(on_low, ref[parts - 1 : parts, :], ref[0:1, :]).astype(jnp.float32), (own_cells, LANES)
@@ -193,16 +200,22 @@
     turn = wide(spin_in) * time_step
     shift = wide(shift_in)
     zero = jnp.zeros((own_cells, LANES), jnp.float32)
-    for copy in copies[2:]:
-        copy.wait()
     for level in range(levels):
-        near = nears[level]
-        pack_far(fars[level], near, own_cells, spare)
-        block = jnp.where(on_low, near[:, radius - LANES :], near[:, 0:LANES])
-        split = 4 * own_cells
-        for side, group in enumerate((block[0:split], jnp.concatenate([block[split:], turn, shift, zero], axis=0))):
+        last = jnp.concatenate([ends[level, split:, :], turn, shift, zero], axis=0)
+        for side, group in enumerate((ends[level, 0:split, :], last)):
             turned = group.T
             edge[level, :, side * LANES : (side + 1) * LANES] = jnp.where(on_low, turned[LANES - EXTRA :], turned[0:EXTRA])
+
+
+def pack_kernel(spare, levels, density, momentum, magnetic, side, *outs):
+    nears, fars = outs[:levels], outs[levels:]
+    own_cells = density.shape[1]
+    for level in range(levels):
+        sources = [density.at[level]] + [x.at[k, level] for x in (momentum, magnetic) for k in range(2)]
+        for f, x in enumerate(sources):
+            nears[level][f * own_cells : (f + 1) * own_cells, :] = x[...]
+        nears[level][FIELDS * own_cells :, :] = side[level]
+        pack_far(fars[level], nears[level], own_cells, spare)
 
 
 class Blocks:
@@ -251,7 +264,8 @@
 
 def step_kernel(plan, refs, write, scratch):
     n, radius, own_cells, total, spare, moved = plan
-    place, own, own_edge, near, near_edge, far, spin, pick = refs
+    place, own, near, far, spin, pick = refs
+    tail = slice(FIELDS * own_cells, FIELDS * own_cells + EXTRA)
     cells, stages, packed = scratch
     row = place[0]
     lane = lax.broadcasted_iota(jnp.int32, (SUB, LANES), 1)
@@ -284,8 +298,8 @@
         lanes_at = lax.rem(f, 4) * own_cells
         cells[f, pl.ds(blocks.edge_at, EXTRA), :] = jnp.where(
             edge_lane < 2 * own_cells,
-            pltpu.roll(near_edge[:, columns], lax.rem(LANES + own_cells - lanes_at, LANES), 1),
-            pltpu.roll(own_edge[:, columns], lax.rem(LANES + 2 * own_cells - lanes_at, LANES), 1),
+            pltpu.roll(near[tail, columns], lax.rem(LANES + own_cells - lanes_at, LANES), 1),
+            pltpu.roll(own[tail, columns], lax.rem(LANES + 2 * own_cells - lanes_at, LANES), 1),
         )
         return 0
 
@@ -410,17 +424,17 @@
 cost = pl.CostEstimate(flops=9_000_000_000, bytes_accessed=29_000_000, transcendentals=0)
 
 
-def first_step(plan, level, operands):
+def first_step(plan, operands):
     n, radius, own_cells, total, spare, moved = plan
 
-    def kernel(place, own, near, far, side, corner, spin, pick, near_out, far_out, *scratch):
-        refs = (place, own, side.at[level], near, corner.at[level], far, spin, pick)
+    def kernel(place, own, near, far, spin, pick, near_out, far_out, *scratch):
+        refs = (place, own, near, far, spin, pick)
         step_kernel(plan, refs, ToMessage(near_out, far_out, own_cells, spare), scratch)
 
     return pl.pallas_call(
         kernel,
         out_shape=[f32(FIELDS * own_cells + EXTRA, radius), f32(FIELDS * (own_cells + SUB), LANES)],
-        in_specs=[smem] + [vmem] * 7,
+        in_specs=[smem] + [vmem] * 5,
         out_specs=[vmem] * 2,
         scratch_shapes=step_scratch(n),
         compiler_params=params,
@@ -431,12 +445,11 @@
 
 def last_step(plan, level, operands, done, levels):
     n, radius, own_cells, total, spare, moved = plan
-    tail = pl.ds(FIELDS * own_cells, EXTRA)
     final = level == levels - 1
     buffer = f32(FIELDS * own_cells, radius)
 
     def kernel(place, own, near, far, spin, pick, *rest):
-        refs = (place, own, own.at[tail, :], near, near.at[tail, :], far, spin, pick)
+        refs = (place, own, near, far, spin, pick)
         if not final:
             step_kernel(plan, refs, ToBuffer(rest[0]), rest[1:])
             return
@@ -486,36 +499,38 @@
 
     row = lax.axis_index("row")
     place = jnp.reshape(row, (1,)).astype(jnp.int32)
-    here = lambda p, r: (p % phi_count) * row_count + r
-    everyone = [(p, r) for p in range(phi_count) for r in range(row_count)]
-    both = ("phi", "row")
     send_near = lambda x: lax.ppermute(x, "phi", [(p, (p + 1) % phi_count) for p in range(phi_count)])
     send_far = lambda x: lax.ppermute(x, "phi", [(p, (p + 2) % phi_count) for p in range(phi_count)])
     send_side = lambda x: lax.ppermute(x, "row", [(0, 1), (1, 0)])
-    send_corner = lambda x: lax.ppermute(x, both, [(here(p, r), here(p + 1, 1 - r)) for p, r in everyone])
 
     spins, turns = rotation.reshape(parts, LANES), shifts.reshape(parts, LANES)
-    near_message = f32(FIELDS * own_cells, radius)
+    near_message = f32(FIELDS * own_cells + EXTRA, radius)
     far_message = f32(FIELDS * (own_cells + SUB), LANES)
-    packed = pl.pallas_call(
-        lambda *refs: pack_kernel(spare, levels, *refs),
-        out_shape=[near_message] * levels
-        + [far_message] * levels
-        + [f32(levels, EXTRA, 2 * LANES)],
+    edge = pl.pallas_call(
+        edge_kernel,
+        out_shape=f32(levels, EXTRA, 2 * LANES),
         in_specs=[smem] + [pl.BlockSpec(memory_space=pltpu.HBM)] * 5,
-        out_specs=[vmem] * (2 * levels + 1),
+        out_specs=vmem,
         scratch_shapes=[
+            pltpu.VMEM((levels, FIELDS * own_cells, LANES), jnp.float32),
             pltpu.VMEM((parts, LANES), jnp.float32),
             pltpu.VMEM((parts, LANES), jnp.int32),
             pltpu.SemaphoreType.DMA((levels * FIELDS + 2,)),
         ],
-        compiler_params=pltpu.CompilerParams(vmem_limit_bytes=PACK_LIMIT),
+        compiler_params=pltpu.CompilerParams(vmem_limit_bytes=EDGE_LIMIT),
+        name="edges",
+    )(place, density, momentum, magnetic, spins, turns)
+    side = send_side(edge)
+    packed = pl.pallas_call(
+        lambda *refs: pack_kernel(spare, levels, *refs),
+        out_shape=[near_message] * levels + [far_message] * levels,
+        in_specs=[vmem] * 4,
+        out_specs=[vmem] * (2 * levels),
+        compiler_params=params,
+        cost_estimate=cost,
         name="pack",
-    )(place, density, momentum, magnetic, spins, turns)
-    owns, fars, edge = packed[:levels], packed[levels : 2 * levels], packed[2 * levels]
-
-    side = send_side(edge)
-    corner = send_corner(edge)
+    )(density, momentum, magnetic, side)
+    owns, fars = packed[:levels], packed[levels:]
     wide = (n + 1, radius, own_cells, total, spare, EXTRA)
     plain = (n, radius, own_cells, total, spare, 0)
     i32 = jax.ShapeDtypeStruct((TALL * SUB, LANES), jnp.int32)
@@ -532,7 +547,7 @@
     states = []
     for level in range(levels):
         near, far = moved[level]
-        states.append(first_step(wide, level, (place, owns[level], near, far, side, corner, *tables[:2])))
+        states.append(first_step(wide, (place, owns[level], near, far, *tables[:2])))
     moved = [(send_near(own), send_far(far)) for own, far in states]
     done = ()
     for level in range(levels):

time: 57.7 us -> 53 us (0.919)
  Pallas kernels: 41.8 us -> 34.9 us
  starting transfers between devices: 9.15 us -> 11.5 us
  local copies, waits for them, and re-layouts: 0.93 us -> 0.02 us
  waiting for transfers between devices: 4.46 us -> 5.26 us
    pallas_call x2, Pallas kernels: 19.3 us -> 15.3 us  [last_step(): pl.pallas_call(kernel, out_shape=out_shape, in_specs=[smem] + [vmem] * (5...]
    ppermute x1 -> x0, waiting for transfers between devices: 3.39 us -> none  [body(): lax.ppermute(x, both, [(here(p, r), here(p + 1, 1 - r)) for p, r in every...]
    ppermute x4, waiting for transfers between devices: 0.01 us -> 3.14 us  [body(): lax.ppermute(x, 'phi', [(p, (p + 2) % phi_count) for p in range(phi_count)])]
    pallas_call x2, Pallas kernels: 19.7 us -> 17 us  [first_step(): pl.pallas_call(kernel, out_shape=[f32(FIELDS * own_cells + EXTRA, radius)...]
    pallas_call x1, Pallas kernels: 1.99 us -> 0.11 us  [body(): pl.pallas_call(lambda *refs: pack_kernel(spare, levels, *refs), out_shape...]
    pallas_call x0 -> x1, Pallas kernels: none -> 1.74 us  [body(): pl.pallas_call(edge_kernel, out_shape=f32(levels, EXTRA, 2 * LANES), in_s...]
    ppermute x1, starting transfers between devices: 1.49 us -> 3 us  [body(): send_side = lambda x: lax.ppermute(x, 'row', [(0, 1), (1, 0)])]
    ppermute x4, starting transfers between devices: 4.45 us -> 5.67 us  [body(): lax.ppermute(x, 'phi', [(p, (p + 2) % phi_count) for p in range(phi_count)])]
  transfers between devices with their start and end apart: 10 -> 9, of which waited for: 2 -> 2; matrix products, arithmetic and copies ran while one was open for 0% -> 0% of each run, Pallas kernels for 52% -> 48%
where the time goes in v7:
time: 53 us; the launch traced here: 52.4 us
  Pallas kernels  34.9 us (66%)
  starting transfers between devices  11.5 us (22%)
  waiting for transfers between devices  5.26 us (10%)
  between operations  0.74 us (1%)
    pallas_call x2, Pallas kernels, first_step(): pl.pallas_call(kernel, out_shape=[f32(FIELDS * own_cells + EXTRA, radius)...  17 us
    pallas_call x2, Pallas kernels, last_step(): pl.pallas_call(kernel, out_shape=out_shape, in_specs=[smem] + [vmem] * (5...  15.3 us
    ppermute x4, starting transfers between devices, body(): lax.ppermute(x, 'phi', [(p, (p + 2) % phi_count) for p in range(phi_count)])  5.67 us
    ppermute x4, waiting for transfers between devices, body(): lax.ppermute(x, 'phi', [(p, (p + 2) % phi_count) for p in range(phi_count)])  3.14 us
    ppermute x1, starting transfers between devices, body(): send_side = lambda x: lax.ppermute(x, 'row', [(0, 1), (1, 0)])  3 us
    ppermute x4, starting transfers between devices, body(): lax.ppermute(x, 'phi', [(p, (p + 1) % phi_count) for p in range(phi_count)])  2.86 us
    ppermute x1, waiting for transfers between devices, body(): send_side = lambda x: lax.ppermute(x, 'row', [(0, 1), (1, 0)])  2.1 us
    pallas_call x1, Pallas kernels, body(): pl.pallas_call(edge_kernel, out_shape=f32(levels, EXTRA, 2 * LANES), in_s...  1.74 us
  transfers between devices with their start and end apart: 9, of which 2 were waited for; matrix products, arithmetic and copies ran while one was open for 0% of the time, Pallas kernels for 48%

profile of v7, /device:TPU:0, one launch (start us, length us, event | category | flops | bytes accessed | tf_op | source)
XLA Modules:
  0.0 52.4 jit_solution(8642704038267911126)
XLA Ops:
  0.7 1.7 %edges.1 = f32[2,16,256]{2,1,0:T(8,128)} custom-call(s32[1]{0:T(128)} %bitcast.place.refs_0_, f32[2,32,256]{2,1,0:T(8,128)} %refs_0_.1, f32[2,2,32,256]{3,2,1,0:T(8,128)} %refs_1_.1, f32[2,2,32,256]{3,2,1,0:T(8,128)} %refs_2_.1, f32[2,128]{1,0:T(2,128)} %bitcast.3, s32[2,128]{1,0:T(2,128)} %bitcast.5), custom_call_target="tpu_custom_call" | custom-call | tf_op jit(solution)/shard_map/edges/pallas_call | solution.py:509
  2.4 3.0 %collective-permute-start = (f32[2,16,256]{2,1,0:T(8,128)}, f32[2,16,256]{2,1,0:T(8,128)S(1)}, u32[]{:S(2)}, u32[]{:S(2)}) collective-permute-start(f32[2,16,256]{2,1,0:T(8,128)} %edges.1), channel_id=1, source_target_pairs={{0,1},{1,0},{2,3},{3,2},{4,5},{5,4},{6,7},{7,6},{8,9},{9,8},{10,11... | collective-permute-start | bytes 98312 | tf_op jit(solution)/shard_map/ppermute | solution.py:504
  5.4 2.1 %collective-permute-done.refs_3_.refs_1_ = f32[2,16,256]{2,1,0:T(8,128)S(1)} collective-permute-done((f32[2,16,256]{2,1,0:T(8,128)}, f32[2,16,256]{2,1,0:T(8,128)S(1)}, u32[]{:S(2)}, u32[]{:S(2)}) %collective-permute-start) | collective-permute-done | bytes 32800 | tf_op jit(solution)/shard_map/ppermute | solution.py:504
  7.5 0.1 pack.1
  7.6 0.1 collective-permute-start.5
  7.7 2.1 %collective-permute-start.6 = (f32[200,128]{1,0:T(8,128)S(1)}, f32[200,128]{1,0:T(8,128)S(1)}, u32[]{:S(2)}, u32[]{:S(2)}) collective-permute-start(f32[200,128]{1,0:T(8,128)S(1)} %get-tuple-element.24), channel_id=1, source_target_pairs={{0,4},{2,6},{4,8},{6,10},{8,12},{10,14},{12,16},{14,18},{16,20},{1... | collective-permute-start | bytes 307208 | tf_op jit(solution)/shard_map/ppermute | solution.py:503
  9.8 1.3 %collective-permute-start.1 = (f32[176,256]{1,0:T(8,128)S(1)}, f32[176,256]{1,0:T(8,128)S(1)}, u32[]{:S(2)}, u32[]{:S(2)}) collective-permute-start(f32[176,256]{1,0:T(8,128)S(1)} %get-tuple-element.15.own), channel_id=1, source_target_pairs={{0,2},{2,4},{4,6},{6,8},{8,10},{10,12},{12,14},{14,16},{16,18},{18... | collective-permute-start | bytes 540680 | tf_op jit(solution)/shard_map/ppermute | solution.py:502
  11.1 1.5 %collective-permute-start.2 = (f32[200,128]{1,0:T(8,128)S(1)}, f32[200,128]{1,0:T(8,128)S(1)}, u32[]{:S(2)}, u32[]{:S(2)}) collective-permute-start(f32[200,128]{1,0:T(8,128)S(1)} %get-tuple-element.16), channel_id=1, source_target_pairs={{0,4},{2,6},{4,8},{6,10},{8,12},{10,14},{12,16},{14,18},{16,20},{1... | collective-permute-start | bytes 307208 | tf_op jit(solution)/shard_map/ppermute | solution.py:503
  12.6 0.8 %tables.1 = (f32[256,128]{1,0:T(8,128)S(1)}, s32[256,128]{1,0:T(8,128)S(1)}, f32[256,128]{1,0:T(8,128)S(1)}, s32[256,128]{1,0:T(8,128)S(1)}) custom-call(s32[1]{0:T(128)} %bitcast.place.refs_0_, f32[2,16,256]{2,1,0:T(8,128)S(1)} %collective-permute-done.refs_3_.refs_1_, f32[2,128]{1,0:T(2,128)S(1)} %bitcast.4, s32[2,128]{1,0:T(2,128)S(1)} %bitcast.6), custom_call_target="tpu_custom_call" | custom-call | tf_op jit(solution)/shard_map/tables/pallas_call | solution.py:537
  13.5 3.1 %collective-permute-done.6.far = f32[200,128]{1,0:T(8,128)S(1)} collective-permute-done((f32[200,128]{1,0:T(8,128)S(1)}, f32[200,128]{1,0:T(8,128)S(1)}, u32[]{:S(2)}, u32[]{:S(2)}) %collective-permute-start.6) | collective-permute-done | bytes 102432 | tf_op jit(solution)/shard_map/ppermute | solution.py:503
  16.6 0.0 collective-permute-done.5.near
  16.6 8.5 %first_step.3 = (f32[176,256]{1,0:T(8,128)S(1)}, f32[200,128]{1,0:T(8,128)S(1)}) custom-call(s32[1]{0:T(128)} %bitcast.place.refs_0_, f32[176,256]{1,0:T(8,128)S(1)} %get-tuple-element.23.own, f32[176,256]{1,0:T(8,128)S(1)} %collective-permute-done.5.near, f32[200,128]{1,0:T(8,128)S(1)} %collective-permute-done.6.far, ...), custom_call_target="tpu_custom_call" | custom-call | flops 8999999488 | bytes 29000000 | tf_op jit(solution)/shard_map/first_step/pallas_call | solution.py:434
  25.1 1.2 %collective-permute-start.7 = (f32[176,256]{1,0:T(8,128)S(1)}, f32[176,256]{1,0:T(8,128)S(1)}, u32[]{:S(2)}, u32[]{:S(2)}) collective-permute-start(f32[176,256]{1,0:T(8,128)S(1)} %get-tuple-element.25.own), channel_id=1, source_target_pairs={{0,2},{2,4},{4,6},{6,8},{8,10},{10,12},{12,14},{14,16},{16,18},{18... | collective-permute-start | bytes 540680 | tf_op jit(solution)/shard_map/ppermute | solution.py:502
  26.2 0.0 collective-permute-start.8
  26.2 0.0 collective-permute-done.2.far
  26.2 0.0 collective-permute-done.1.near
  26.2 8.5 %first_step.2 = (f32[176,256]{1,0:T(8,128)S(1)}, f32[200,128]{1,0:T(8,128)S(1)}) custom-call(s32[1]{0:T(128)} %bitcast.place.refs_0_, f32[176,256]{1,0:T(8,128)S(1)} %get-tuple-element.15.own, f32[176,256]{1,0:T(8,128)S(1)} %collective-permute-done.1.near, f32[200,128]{1,0:T(8,128)S(1)} %collective-permute-done.2.far, ...), custom_call_target="tpu_custom_call" | custom-call | flops 8999999488 | bytes 29000000 | tf_op jit(solution)/shard_map/first_step/pallas_call | solution.py:434
  34.7 0.4 collective-permute-start.3
  35.1 2.1 %collective-permute-start.4 = (f32[200,128]{1,0:T(8,128)S(1)}, f32[200,128]{1,0:T(8,128)S(1)}, u32[]{:S(2)}, u32[]{:S(2)}) collective-permute-start(f32[200,128]{1,0:T(8,128)S(1)} %get-tuple-element.20), channel_id=1, source_target_pairs={{0,4},{2,6},{4,8},{6,10},{8,12},{10,14},{12,16},{14,18},{16,20},{1... | collective-permute-start | bytes 307208 | tf_op jit(solution)/shard_map/ppermute | solution.py:503
  37.2 0.0 collective-permute-done.8.far
  37.2 7.2 %last_step.2.rest_0_ = f32[160,256]{1,0:T(8,128)S(1)} custom-call(s32[1]{0:T(128)} %bitcast.place.refs_0_, f32[176,256]{1,0:T(8,128)S(1)} %get-tuple-element.25.own, f32[176,256]{1,0:T(8,128)S(1)} %collective-permute-done.7.near, f32[200,128]{1,0:T(8,128)S(1)} %collective-permute-done.8.far, f32[256,128]{1,0:T(8,128)S(1)} %get-tuple-element.21.spin, ...), custom_call_target="tpu_custom_call" | custom-call | flops 8999999488 | bytes 29000000 | tf_op jit(solution)/shard_map/last_step/pallas_call | solution.py:476
  44.4 0.0 collective-permute-done.4.far
  44.4 0.0 collective-permute-done.3.near
  44.4 8.0 %last_step.3 = (f32[2,32,256]{2,1,0:T(8,128)}, f32[2,2,32,256]{3,2,1,0:T(8,128)}, f32[2,2,32,256]{3,2,1,0:T(8,128)}) custom-call(s32[1]{0:T(128)} %bitcast.place.refs_0_, f32[176,256]{1,0:T(8,128)S(1)} %get-tuple-element.19.own, f32[176,256]{1,0:T(8,128)S(1)} %collective-permute-done.3.near, f32[200,128]{1,0:T(8,128)S(1)} %collective-permute-done.4.far, ...), custom_call_target="tpu_custom_call" | custom-call | flops 8999999488 | bytes 29000000 | tf_op jit(solution)/shard_map/last_step/pallas_call | solution.py:476
  (11 shorter events, 0.0 us)
Async XLA Ops:
  0.6 6.9 %copy-start = (f32[2,2,32,256]{3,2,1,0:T(8,128)S(1)}, f32[2,2,32,256]{3,2,1,0:T(8,128)}, u32[]{:S(2)}) copy-start(f32[2,2,32,256]{3,2,1,0:T(8,128)} %refs_1_.1) | copy-start | bytes 393220
  0.6 6.9 %copy-start.1 = (f32[2,2,32,256]{3,2,1,0:T(8,128)S(1)}, f32[2,2,32,256]{3,2,1,0:T(8,128)}, u32[]{:S(2)}) copy-start(f32[2,2,32,256]{3,2,1,0:T(8,128)} %refs_2_.1) | copy-start | bytes 393220
  0.7 6.9 %copy-start.2 = (f32[2,32,256]{2,1,0:T(8,128)S(1)}, f32[2,32,256]{2,1,0:T(8,128)}, u32[]{:S(2)}) copy-start(f32[2,32,256]{2,1,0:T(8,128)} %refs_0_.1) | copy-start | bytes 196612
  2.4 5.1 %collective-permute-start = (f32[2,16,256]{2,1,0:T(8,128)}, f32[2,16,256]{2,1,0:T(8,128)S(1)}, u32[]{:S(2)}, u32[]{:S(2)}) collective-permute-start(f32[2,16,256]{2,1,0:T(8,128)} %edges.1), channel_id=1, source_target_pairs={{0,1},{1,0},{2,3},{3,2},{4,5},{5,4},{6,7},{7,6},{8,9},{9,8},{10,11... | collective-permute-start | bytes 98312 | tf_op jit(solution)/shard_map/ppermute | solution.py:504
  7.6 8.9 %collective-permute-start.5 = (f32[176,256]{1,0:T(8,128)S(1)}, f32[176,256]{1,0:T(8,128)S(1)}, u32[]{:S(2)}, u32[]{:S(2)}) collective-permute-start(f32[176,256]{1,0:T(8,128)S(1)} %get-tuple-element.23.own), channel_id=1, source_target_pairs={{0,2},{2,4},{4,6},{6,8},{8,10},{10,12},{12,14},{14,16},{16,18},{18... | collective-permute-start | bytes 540680 | tf_op jit(solution)/shard_map/ppermute | solution.py:502
  7.7 8.9 %collective-permute-start.6 = (f32[200,128]{1,0:T(8,128)S(1)}, f32[200,128]{1,0:T(8,128)S(1)}, u32[]{:S(2)}, u32[]{:S(2)}) collective-permute-start(f32[200,128]{1,0:T(8,128)S(1)} %get-tuple-element.24), channel_id=1, source_target_pairs={{0,4},{2,6},{4,8},{6,10},{8,12},{10,14},{12,16},{14,18},{16,20},{1... | collective-permute-start | bytes 307208 | tf_op jit(solution)/shard_map/ppermute | solution.py:503
  9.8 2.8 %copy-start.4 = (s32[256]{0:T(256)S(1)}, s32[256]{0:T(256)}, u32[]{:S(2)}) copy-start(s32[256]{0:T(256)} %param.9) | copy-start | bytes 3076
  9.8 2.8 %copy-start.3 = (f32[256]{0:T(256)S(1)}, f32[256]{0:T(256)}, u32[]{:S(2)}) copy-start(f32[256]{0:T(256)} %param.8) | copy-start | bytes 3076
  9.8 16.4 %collective-permute-start.1 = (f32[176,256]{1,0:T(8,128)S(1)}, f32[176,256]{1,0:T(8,128)S(1)}, u32[]{:S(2)}, u32[]{:S(2)}) collective-permute-start(f32[176,256]{1,0:T(8,128)S(1)} %get-tuple-element.15.own), channel_id=1, source_target_pairs={{0,2},{2,4},{4,6},{6,8},{8,10},{10,12},{12,14},{14,16},{16,18},{18... | collective-permute-start | bytes 540680 | tf_op jit(solution)/shard_map/ppermute | solution.py:502
  11.1 15.1 %collective-permute-start.2 = (f32[200,128]{1,0:T(8,128)S(1)}, f32[200,128]{1,0:T(8,128)S(1)}, u32[]{:S(2)}, u32[]{:S(2)}) collective-permute-start(f32[200,128]{1,0:T(8,128)S(1)} %get-tuple-element.16), channel_id=1, source_target_pairs={{0,4},{2,6},{4,8},{6,10},{8,12},{10,14},{12,16},{14,18},{16,20},{1... | collective-permute-start | bytes 307208 | tf_op jit(solution)/shard_map/ppermute | solution.py:503
  25.1 12.1 %collective-permute-start.7 = (f32[176,256]{1,0:T(8,128)S(1)}, f32[176,256]{1,0:T(8,128)S(1)}, u32[]{:S(2)}, u32[]{:S(2)}) collective-permute-start(f32[176,256]{1,0:T(8,128)S(1)} %get-tuple-element.25.own), channel_id=1, source_target_pairs={{0,2},{2,4},{4,6},{6,8},{8,10},{10,12},{12,14},{14,16},{16,18},{18... | collective-permute-start | bytes 540680 | tf_op jit(solution)/shard_map/ppermute | solution.py:502
  26.2 10.9 %collective-permute-start.8 = (f32[200,128]{1,0:T(8,128)S(1)}, f32[200,128]{1,0:T(8,128)S(1)}, u32[]{:S(2)}, u32[]{:S(2)}) collective-permute-start(f32[200,128]{1,0:T(8,128)S(1)} %get-tuple-element.26), channel_id=1, source_target_pairs={{0,4},{2,6},{4,8},{6,10},{8,12},{10,14},{12,16},{14,18},{16,20},{1... | collective-permute-start | bytes 307208 | tf_op jit(solution)/shard_map/ppermute | solution.py:503
  34.7 9.7 %collective-permute-start.3 = (f32[176,256]{1,0:T(8,128)S(1)}, f32[176,256]{1,0:T(8,128)S(1)}, u32[]{:S(2)}, u32[]{:S(2)}) collective-permute-start(f32[176,256]{1,0:T(8,128)S(1)} %get-tuple-element.19.own), channel_id=1, source_target_pairs={{0,2},{2,4},{4,6},{6,8},{8,10},{10,12},{12,14},{14,16},{16,18},{18... | collective-permute-start | bytes 540680 | tf_op jit(solution)/shard_map/ppermute | solution.py:502
  35.1 9.3 %collective-permute-start.4 = (f32[200,128]{1,0:T(8,128)S(1)}, f32[200,128]{1,0:T(8,128)S(1)}, u32[]{:S(2)}, u32[]{:S(2)}) collective-permute-start(f32[200,128]{1,0:T(8,128)S(1)} %get-tuple-element.20), channel_id=1, source_target_pairs={{0,4},{2,6},{4,8},{6,10},{8,12},{10,14},{12,16},{14,18},{16,20},{1... | collective-permute-start | bytes 307208 | tf_op jit(solution)/shard_map/ppermute | solution.py:503

commit v8 on v7

--- a/solution.py
+++ b/solution.py
@@ -95,7 +95,7 @@
     return pl.ds(pl.multiple_of(i * SUB, SUB), SUB)
 
 
-def run_stages(n, stages, spin, edges):
+def run_stages(n, stages, spin, edges, live):
     half_dt = 0.5 * time_step
     low_mask, high_mask = edges
     first, last = REACH, REACH + n - 1
@@ -142,11 +142,11 @@
             lo = 2 * stage + 1
             count = count + 1
             before = (jnp.zeros((SUB, LANES), jnp.float32),) * FIELDS
-        turns = lax.div(count + ROWS - 1, ROWS)
+        turns = jnp.where(live, lax.div(count + ROWS - 1, ROWS), 1)
         lax.fori_loop(0, turns, lambda c, carried: tuple(work(stage, lo + c * ROWS, ROWS, list(carried))), before)
         return 0
 
-    lax.fori_loop(0, STAGES, run, 0)
+    lax.fori_loop(0, jnp.where(live, STAGES, 1), run, 0)
 
 
 def spread(block, first, width):
@@ -303,7 +303,8 @@
         )
         return 0
 
-    lax.fori_loop(0, FIELDS, gather, 0)
+    live = place[1] > 0
+    lax.fori_loop(0, jnp.where(live, FIELDS, 1), gather, 0)
 
     front = lax.broadcasted_iota(jnp.int32, (TALL, LANES), 1) < HALF
 
@@ -319,13 +320,13 @@
             )
         return 0
 
-    lax.fori_loop(0, FIELDS, deal, 0)
+    lax.fori_loop(0, jnp.where(live, FIELDS, 1), deal, 0)
 
     edges = (
         (sublane == 0) & (lane < HALF) & (row == 0),
         (sublane == SUB - 1) & (lane >= HALF) & (row == total // radius - 1),
     )
-    run_stages(n, stages, spin, edges)
+    run_stages(n, stages, spin, edges, live)
 
     even = (lane & own_cells) == 0
 
@@ -344,7 +345,7 @@
             stages[2, 2, tile(i), :] = turned[4]
         return 0
 
-    lax.fori_loop(0, (n + PICKS - 1) // PICKS, shift, 0)
+    lax.fori_loop(0, jnp.where(live, (n + PICKS - 1) // PICKS, 1), shift, 0)
     narrow = lax.broadcasted_iota(jnp.int32, (n, LANES), 1) < HALF
     for j in range(SUB):
         one, two, three = [stages[2, g, pl.ds(j, n, stride=SUB), :] for g in range(3)]
@@ -379,22 +380,6 @@
         pack_far(self.far, self.near, self.own_cells, self.spare)
 
 
-class ToBuffer:
-    def __init__(self, buffer):
-        self.buffer = buffer
-
-    def fields(self, columns, four, fifth):
-        split = four.shape[0]
-        self.buffer[0:split, columns] = four
-        self.buffer[split:, columns] = fifth[0 : self.buffer.shape[0] - split]
-
-    def edge(self, first, second):
-        pass
-
-    def end(self):
-        pass
-
-
 def copies_out(level, buffer, outs, sent):
     density, momentum, magnetic = outs
     cells = density.shape[1]
@@ -424,12 +409,24 @@
 cost = pl.CostEstimate(flops=9_000_000_000, bytes_accessed=29_000_000, transcendentals=0)
 
 
-def first_step(plan, operands):
+def step(plan, operands):
     n, radius, own_cells, total, spare, moved = plan
 
     def kernel(place, own, near, far, spin, pick, near_out, far_out, *scratch):
         refs = (place, own, near, far, spin, pick)
         step_kernel(plan, refs, ToMessage(near_out, far_out, own_cells, spare), scratch)
+
+        @pl.when(place[1] == 0)
+        def _():
+            def hand(ref, out):
+                def one(i, _):
+                    out[tile(i), :] = ref[tile(i), :]
+                    return 0
+
+                lax.fori_loop(0, ref.shape[0] // SUB, one, 0)
+
+            hand(own, near_out)
+            hand(far, far_out)
 
     return pl.pallas_call(
         kernel,
@@ -439,50 +436,28 @@
         scratch_shapes=step_scratch(n),
         compiler_params=params,
         cost_estimate=cost,
-        name="first_step",
+        name="step",
     )(*operands)
 
 
-def last_step(plan, level, operands, done, levels):
-    n, radius, own_cells, total, spare, moved = plan
-    final = level == levels - 1
-    buffer = f32(FIELDS * own_cells, radius)
-
-    def kernel(place, own, near, far, spin, pick, *rest):
-        refs = (place, own, near, far, spin, pick)
-        if not final:
-            step_kernel(plan, refs, ToBuffer(rest[0]), rest[1:])
-            return
-        ready, outs, scratch = rest[: levels - 1], rest[levels - 1 : levels + 2], rest[levels + 2 :]
-        last, sent = scratch[-2:]
-        copies = []
-        for k, x in enumerate(ready):
-            copies += copies_out(k, x, outs, sent)
+def unpack(levels, own_cells, radius, states):
+    def kernel(*refs):
+        buffers, outs, sent = refs[:levels], refs[levels:-1], refs[-1]
+        copies = [copy for level in range(levels) for copy in copies_out(level, buffers[level], outs, sent)]
         for copy in copies:
             copy.start()
-        step_kernel(plan, refs, ToBuffer(last), scratch[:-2])
-        rest_of = copies_out(level, last, outs, sent)
-        for copy in rest_of:
-            copy.start()
-        for copy in copies + rest_of:
+        for copy in copies:
             copy.wait()
 
-    if final:
-        out_shape = [f32(levels, own_cells, radius), f32(2, levels, own_cells, radius), f32(2, levels, own_cells, radius)]
-        more = [pltpu.VMEM((FIELDS * own_cells, radius), jnp.float32), pltpu.SemaphoreType.DMA((levels * FIELDS,))]
-    else:
-        out_shape = buffer
-        more = []
     return pl.pallas_call(
         kernel,
-        out_shape=out_shape,
-        in_specs=[smem] + [vmem] * (5 + len(done)),
-        out_specs=[pl.BlockSpec(memory_space=pltpu.HBM)] * 3 if final else vmem,
-        scratch_shapes=step_scratch(n) + more,
+        out_shape=[f32(levels, own_cells, radius), f32(2, levels, own_cells, radius), f32(2, levels, own_cells, radius)],
+        in_specs=[vmem] * levels,
+        out_specs=[pl.BlockSpec(memory_space=pltpu.HBM)] * 3,
+        scratch_shapes=[pltpu.SemaphoreType.DMA((levels * FIELDS,))],
         compiler_params=params,
-        cost_estimate=cost,
-        name="last_step",
-    )(*operands, *done)
+        name="unpack",
+    )(*states)
 
 
 def body(density, momentum, magnetic, rotation, shifts):
@@ -532,30 +507,27 @@
     )(density, momentum, magnetic, side)
     owns, fars = packed[:levels], packed[levels:]
     wide = (n + 1, radius, own_cells, total, spare, EXTRA)
-    plain = (n, radius, own_cells, total, spare, 0)
     i32 = jax.ShapeDtypeStruct((TALL * SUB, LANES), jnp.int32)
     tables = pl.pallas_call(
-        lambda *refs: table_kernel((wide, plain), *refs),
-        out_shape=[f32(TALL * SUB, LANES), i32] * 2,
+        lambda *refs: table_kernel((wide,), *refs),
+        out_shape=[f32(TALL * SUB, LANES), i32],
         in_specs=[smem] + [vmem] * 3,
-        out_specs=[vmem] * 4,
+        out_specs=[vmem] * 2,
         scratch_shapes=[pltpu.VMEM((2, tall_of(n + 1), LANES), jnp.float32)],
         compiler_params=params,
         name="tables",
     )(place, side, spins, turns)
-    moved = [(send_near(own), send_far(far)) for own, far in zip(owns, fars)]
-    states = []
-    for level in range(levels):
-        near, far = moved[level]
-        states.append(first_step(wide, (place, owns[level], near, far, *tables[:2])))
-    moved = [(send_near(own), send_far(far)) for own, far in states]
-    done = ()
-    for level in range(levels):
-        near, far = moved[level]
-        operands = (place, states[level][0], near, far, *tables[2:])
-        result = last_step(plain, level, operands, done if level == levels - 1 else (), levels)
-        done += (result,)
-    return tuple(result)
+    def turn(i, carried):
+        send_own, send_beyond, own, near, far = carried
+        where = jnp.stack([row, i]).astype(jnp.int32)
+        sent = send_near(send_own), send_far(send_beyond)
+        new = step(wide, (where, own, near, far, *tables))
+        return (*new, send_own, *sent)
+
+    assert levels == 2
+    first = (owns[0], fars[0], owns[1], owns[1], fars[1])
+    carried = lax.fori_loop(0, STEPS * levels + 1, turn, first)
+    return tuple(unpack(levels, own_cells, radius, (carried[2], carried[0])))
 
 
 def solution(mesh):

time: 53 us -> 64.2 us (1.21)
  Pallas kernels: 34.9 us -> 41.2 us
  waiting for transfers between devices: 5.26 us -> 7.68 us
  starting transfers between devices: 11.5 us -> 12.6 us
  local copies, waits for them, and re-layouts: 0.02 us -> 0.97 us
    pallas_call x5 -> x7, Pallas kernels: 33 us -> 39.4 us  [the longest x5 38.1 us: step(): pl.pallas_call(kernel, out_shape=[f32(FIELDS * own_cells + EXTRA, radius)...]
    ppermute x4 -> x5, waiting for transfers between devices: 0.01 us -> 2.01 us  [body(): lax.ppermute(x, 'phi', [(p, (p + 1) % phi_count) for p in range(phi_count)])]
    ppermute x4 -> x5, starting transfers between devices: 5.67 us -> 6.66 us  [body(): lax.ppermute(x, 'phi', [(p, (p + 2) % phi_count) for p in range(phi_count)])]
    unnamed x10 -> x11, local copies, waits for them, and re-layouts: 0.02 us -> 0.69 us
    ppermute x4 -> x5, waiting for transfers between devices: 3.14 us -> 3.57 us  [body(): lax.ppermute(x, 'phi', [(p, (p + 2) % phi_count) for p in range(phi_count)])]
    ppermute x4 -> x5, starting transfers between devices: 2.86 us -> 2.97 us  [body(): lax.ppermute(x, 'phi', [(p, (p + 1) % phi_count) for p in range(phi_count)])]
  transfers between devices with their start and end apart: 9 -> 11, of which waited for: 2 -> 3; matrix products, arithmetic and copies ran while one was open for 0% -> 1% of each run, Pallas kernels for 48% -> 60%
where the time goes in v8:
time: 64.2 us; the launch traced here: 64 us
  Pallas kernels  41.2 us (64%)
  starting transfers between devices  12.6 us (20%)
  waiting for transfers between devices  7.68 us (12%)
  local copies, waits for them, and re-layouts  0.97 us (2%)
  between operations  0.72 us (1%)
    pallas_call x5, Pallas kernels, step(): pl.pallas_call(kernel, out_shape=[f32(FIELDS * own_cells + EXTRA, radius)...  38.1 us
    ppermute x5, starting transfers between devices, body(): lax.ppermute(x, 'phi', [(p, (p + 2) % phi_count) for p in range(phi_count)])  6.66 us
    ppermute x5, waiting for transfers between devices, body(): lax.ppermute(x, 'phi', [(p, (p + 2) % phi_count) for p in range(phi_count)])  3.57 us
    ppermute x1, starting transfers between devices, body(): send_side = lambda x: lax.ppermute(x, 'row', [(0, 1), (1, 0)])  3 us
    ppermute x5, starting transfers between devices, body(): lax.ppermute(x, 'phi', [(p, (p + 1) % phi_count) for p in range(phi_count)])  2.97 us
    ppermute x1, waiting for transfers between devices, body(): send_side = lambda x: lax.ppermute(x, 'row', [(0, 1), (1, 0)])  2.1 us
    ppermute x5, waiting for transfers between devices, body(): lax.ppermute(x, 'phi', [(p, (p + 1) % phi_count) for p in range(phi_count)])  2.01 us
    pallas_call x1, Pallas kernels, body(): pl.pallas_call(edge_kernel, out_shape=f32(levels, EXTRA, 2 * LANES), in_s...  1.74 us
  transfers between devices with their start and end apart: 11, of which 3 were waited for; matrix products, arithmetic and copies ran while one was open for 1% of the time, Pallas kernels for 60%

profile of v8, /device:TPU:0, one launch (start us, length us, event | category | flops | bytes accessed | tf_op | source)
XLA Modules:
  0.0 64.0 jit_solution(9797493831527415774)
XLA Ops:
  0.7 1.7 %edges.1 = f32[2,16,256]{2,1,0:T(8,128)} custom-call(s32[1]{0:T(128)} %bitcast.2.place.refs_0_, f32[2,32,256]{2,1,0:T(8,128)} %refs_0_.1, f32[2,2,32,256]{3,2,1,0:T(8,128)} %refs_1_.1, f32[2,2,32,256]{3,2,1,0:T(8,128)} %refs_2_.1, f32[2,128]{1,0:T(2,128)} %bitcast.9, s32[2,128]{1,0:T(2,128)} %bitcast.11), custom_call_target="tpu_custom_call" | custom-call | tf_op jit(solution)/shard_map/edges/pallas_call | solution.py:484
  2.4 3.0 %collective-permute-start.2 = (f32[2,16,256]{2,1,0:T(8,128)}, f32[2,16,256]{2,1,0:T(8,128)S(1)}, u32[]{:S(2)}, u32[]{:S(2)}) collective-permute-start(f32[2,16,256]{2,1,0:T(8,128)} %edges.1), channel_id=1, source_target_pairs={{0,1},{1,0},{2,3},{3,2},{4,5},{5,4},{6,7},{7,6},{8,9},{9,8},{10,11... | collective-permute-start | bytes 98312 | tf_op jit(solution)/shard_map/ppermute | solution.py:479
  5.4 2.1 %collective-permute-done.2.refs_3_.refs_1_ = f32[2,16,256]{2,1,0:T(8,128)S(1)} collective-permute-done((f32[2,16,256]{2,1,0:T(8,128)}, f32[2,16,256]{2,1,0:T(8,128)S(1)}, u32[]{:S(2)}, u32[]{:S(2)}) %collective-permute-start.2) | collective-permute-done | bytes 32800 | tf_op jit(solution)/shard_map/ppermute | solution.py:479
  7.5 0.1 pack.1
  7.7 0.6 copy-done.3
  8.3 0.5 tables.1
  8.8 54.4 %while.21 = (s32[]{:T(128)}, f32[176,256]{1,0:T(8,128)S(1)}, f32[200,128]{1,0:T(8,128)S(1)}, f32[176,256]{1,0:T(8,128)S(1)}, f32[176,256]{1,0:T(8,128)S(1)}, /*i...) while((s32[]{:T(128)}, f32[176,256]{1,0:T(8,128)S(1)}, ...), condition=%wide.region_1.0_spmd, body=%wide.region_0.0_spmd.sunk | while | flops 8999999488 | bytes 31621636 | solution.py:529
  8.8 2.1 %collective-permute-start.1 = (f32[200,128]{1,0:T(8,128)S(1)}, f32[200,128]{1,0:T(8,128)S(1)}, u32[]{:S(2)}, u32[]{:S(2)}) collective-permute-start(f32[200,128]{1,0:T(8,128)S(1)} %copy.16), channel_id=1, source_target_pairs={{0,4},{2,6},{4,8},{6,10},{8,12},{10,14},{12,16},{14,18},{16,20},{1... | collective-permute-start | bytes 307208 | tf_op jit(solution)/shard_map/while/body/eval_jaxpr/ppermute | solution.py:478
  11.0 0.1 pad_add_fusion.2.place
  11.1 1.9 %step.5 = (f32[176,256]{1,0:T(8,128)S(1)}, f32[200,128]{1,0:T(8,128)S(1)}) custom-call(s32[2]{0:T(128)S(1)} %pad_add_fusion.2.place, f32[176,256]{1,0:T(8,128)S(1)} %get-tuple-element.255.own, f32[176,256]{1,0:T(8,128)S(1)} %get-tuple-element.256.near, f32[200,128]{1,0:T(8,128)S(1)} %get-tuple-element.257.far, f32[256,128]{1,0:T(8,128)S(1)} %get-tuple-element.269.spin, ...), custom_call_target="tpu_custom_call" | custom-call | flops 8999999488 | bytes 29000000 | tf_op jit(solution)/shard_map/while/body/eval_jaxpr/step/pallas_call | solution.py:431
  13.1 3.6 %collective-permute-done.1 = f32[200,128]{1,0:T(8,128)S(1)} collective-permute-done((f32[200,128]{1,0:T(8,128)S(1)}, f32[200,128]{1,0:T(8,128)S(1)}, u32[]{:S(2)}, u32[]{:S(2)}) %collective-permute-start.1) | collective-permute-done | bytes 102432 | tf_op jit(solution)/shard_map/while/body/eval_jaxpr/ppermute | solution.py:478
  16.6 2.0 %collective-permute-done = f32[176,256]{1,0:T(8,128)S(1)} collective-permute-done((f32[176,256]{1,0:T(8,128)S(1)}, f32[176,256]{1,0:T(8,128)S(1)}, u32[]{:S(2)}, u32[]{:S(2)}) %collective-permute-start) | collective-permute-done | bytes 180256 | tf_op jit(solution)/shard_map/while/body/eval_jaxpr/ppermute | solution.py:477
  18.8 0.1 pad_add_fusion.2.place
  18.9 9.0 %step.5 = (f32[176,256]{1,0:T(8,128)S(1)}, f32[200,128]{1,0:T(8,128)S(1)}) custom-call(s32[2]{0:T(128)S(1)} %pad_add_fusion.2.place, f32[176,256]{1,0:T(8,128)S(1)} %get-tuple-element.255.own, f32[176,256]{1,0:T(8,128)S(1)} %get-tuple-element.256.near, f32[200,128]{1,0:T(8,128)S(1)} %get-tuple-element.257.far, f32[256,128]{1,0:T(8,128)S(1)} %get-tuple-element.269.spin, ...), custom_call_target="tpu_custom_call" | custom-call | flops 8999999488 | bytes 29000000 | tf_op jit(solution)/shard_map/while/body/eval_jaxpr/step/pallas_call | solution.py:431
  28.1 1.4 %collective-permute-start.1 = (f32[200,128]{1,0:T(8,128)S(1)}, f32[200,128]{1,0:T(8,128)S(1)}, u32[]{:S(2)}, u32[]{:S(2)}) collective-permute-start(f32[200,128]{1,0:T(8,128)S(1)} %copy.16), channel_id=1, source_target_pairs={{0,4},{2,6},{4,8},{6,10},{8,12},{10,14},{12,16},{14,18},{16,20},{1... | collective-permute-start | bytes 307208 | tf_op jit(solution)/shard_map/while/body/eval_jaxpr/ppermute | solution.py:478
  29.5 0.5 collective-permute-start
  29.9 0.1 pad_add_fusion.2.place
  30.0 9.0 %step.5 = (f32[176,256]{1,0:T(8,128)S(1)}, f32[200,128]{1,0:T(8,128)S(1)}) custom-call(s32[2]{0:T(128)S(1)} %pad_add_fusion.2.place, f32[176,256]{1,0:T(8,128)S(1)} %get-tuple-element.255.own, f32[176,256]{1,0:T(8,128)S(1)} %get-tuple-element.256.near, f32[200,128]{1,0:T(8,128)S(1)} %get-tuple-element.257.far, f32[256,128]{1,0:T(8,128)S(1)} %get-tuple-element.269.spin, ...), custom_call_target="tpu_custom_call" | custom-call | flops 8999999488 | bytes 29000000 | tf_op jit(solution)/shard_map/while/body/eval_jaxpr/step/pallas_call | solution.py:431
  39.2 2.5 %collective-permute-start.1 = (f32[200,128]{1,0:T(8,128)S(1)}, f32[200,128]{1,0:T(8,128)S(1)}, u32[]{:S(2)}, u32[]{:S(2)}) collective-permute-start(f32[200,128]{1,0:T(8,128)S(1)} %copy.16), channel_id=1, source_target_pairs={{0,4},{2,6},{4,8},{6,10},{8,12},{10,14},{12,16},{14,18},{16,20},{1... | collective-permute-start | bytes 307208 | tf_op jit(solution)/shard_map/while/body/eval_jaxpr/ppermute | solution.py:478
  41.8 9.0 %step.5 = (f32[176,256]{1,0:T(8,128)S(1)}, f32[200,128]{1,0:T(8,128)S(1)}) custom-call(s32[2]{0:T(128)S(1)} %pad_add_fusion.2.place, f32[176,256]{1,0:T(8,128)S(1)} %get-tuple-element.255.own, f32[176,256]{1,0:T(8,128)S(1)} %get-tuple-element.256.near, f32[200,128]{1,0:T(8,128)S(1)} %get-tuple-element.257.far, f32[256,128]{1,0:T(8,128)S(1)} %get-tuple-element.269.spin, ...), custom_call_target="tpu_custom_call" | custom-call | flops 8999999488 | bytes 29000000 | tf_op jit(solution)/shard_map/while/body/eval_jaxpr/step/pallas_call | solution.py:431
  51.0 0.7 %collective-permute-start.1 = (f32[200,128]{1,0:T(8,128)S(1)}, f32[200,128]{1,0:T(8,128)S(1)}, u32[]{:S(2)}, u32[]{:S(2)}) collective-permute-start(f32[200,128]{1,0:T(8,128)S(1)} %copy.16), channel_id=1, source_target_pairs={{0,4},{2,6},{4,8},{6,10},{8,12},{10,14},{12,16},{14,18},{16,20},{1... | collective-permute-start | bytes 307208 | tf_op jit(solution)/shard_map/while/body/eval_jaxpr/ppermute | solution.py:478
  51.7 2.3 %collective-permute-start = (f32[176,256]{1,0:T(8,128)S(1)}, f32[176,256]{1,0:T(8,128)S(1)}, u32[]{:S(2)}, u32[]{:S(2)}) collective-permute-start(f32[176,256]{1,0:T(8,128)S(1)} %copy.15), channel_id=1, source_target_pairs={{0,2},{2,4},{4,6},{6,8},{8,10},{10,12},{12,14},{14,16},{16,18},{18... | collective-permute-start | bytes 540680 | tf_op jit(solution)/shard_map/while/body/eval_jaxpr/ppermute | solution.py:477
  54.0 9.0 %step.5 = (f32[176,256]{1,0:T(8,128)S(1)}, f32[200,128]{1,0:T(8,128)S(1)}) custom-call(s32[2]{0:T(128)S(1)} %pad_add_fusion.2.place, f32[176,256]{1,0:T(8,128)S(1)} %get-tuple-element.255.own, f32[176,256]{1,0:T(8,128)S(1)} %get-tuple-element.256.near, f32[200,128]{1,0:T(8,128)S(1)} %get-tuple-element.257.far, f32[256,128]{1,0:T(8,128)S(1)} %get-tuple-element.269.spin, ...), custom_call_target="tpu_custom_call" | custom-call | flops 8999999488 | bytes 29000000 | tf_op jit(solution)/shard_map/while/body/eval_jaxpr/step/pallas_call | solution.py:431
  63.2 0.8 %unpack.1 = (f32[2,32,256]{2,1,0:T(8,128)}, f32[2,2,32,256]{3,2,1,0:T(8,128)}, f32[2,2,32,256]{3,2,1,0:T(8,128)}) custom-call(f32[176,256]{1,0:T(8,128)S(1)} %get-tuple-element.163.refs_0_, f32[176,256]{1,0:T(8,128)S(1)} %get-tuple-element.164.refs_1_), custom_call_target="tpu_custom_call" | custom-call | tf_op jit(solution)/shard_map/unpack/pallas_call | solution.py:452
  (49 shorter events, 0.8 us)
Async XLA Ops:
  0.6 6.9 %copy-start = (f32[2,2,32,256]{3,2,1,0:T(8,128)S(1)}, f32[2,2,32,256]{3,2,1,0:T(8,128)}, u32[]{:S(2)}) copy-start(f32[2,2,32,256]{3,2,1,0:T(8,128)} %refs_1_.1) | copy-start | bytes 393220
  0.6 6.9 %copy-start.1 = (f32[2,2,32,256]{3,2,1,0:T(8,128)S(1)}, f32[2,2,32,256]{3,2,1,0:T(8,128)}, u32[]{:S(2)}) copy-start(f32[2,2,32,256]{3,2,1,0:T(8,128)} %refs_2_.1) | copy-start | bytes 393220
  0.7 6.9 %copy-start.2 = (f32[2,32,256]{2,1,0:T(8,128)S(1)}, f32[2,32,256]{2,1,0:T(8,128)}, u32[]{:S(2)}) copy-start(f32[2,32,256]{2,1,0:T(8,128)} %refs_0_.1) | copy-start | bytes 196612
  2.4 5.1 %collective-permute-start.2 = (f32[2,16,256]{2,1,0:T(8,128)}, f32[2,16,256]{2,1,0:T(8,128)S(1)}, u32[]{:S(2)}, u32[]{:S(2)}) collective-permute-start(f32[2,16,256]{2,1,0:T(8,128)} %edges.1), channel_id=1, source_target_pairs={{0,1},{1,0},{2,3},{3,2},{4,5},{5,4},{6,7},{7,6},{8,9},{9,8},{10,11... | collective-permute-start | bytes 98312 | tf_op jit(solution)/shard_map/ppermute | solution.py:479
  7.6 0.7 %copy-start.3 = (f32[256]{0:T(256)S(1)}, f32[256]{0:T(256)}, u32[]{:S(2)}) copy-start(f32[256]{0:T(256)} %param.10) | copy-start | bytes 3076
  7.7 0.7 %copy-start.4 = (s32[256]{0:T(256)S(1)}, s32[256]{0:T(256)}, u32[]{:S(2)}) copy-start(s32[256]{0:T(256)} %param.11) | copy-start | bytes 3076
  8.8 7.8 %collective-permute-start.1 = (f32[200,128]{1,0:T(8,128)S(1)}, f32[200,128]{1,0:T(8,128)S(1)}, u32[]{:S(2)}, u32[]{:S(2)}) collective-permute-start(f32[200,128]{1,0:T(8,128)S(1)} %copy.16), channel_id=1, source_target_pairs={{0,4},{2,6},{4,8},{6,10},{8,12},{10,14},{12,16},{14,18},{16,20},{1... | collective-permute-start | bytes 307208 | tf_op jit(solution)/shard_map/while/body/eval_jaxpr/ppermute | solution.py:478
  11.0 7.7 %collective-permute-start = (f32[176,256]{1,0:T(8,128)S(1)}, f32[176,256]{1,0:T(8,128)S(1)}, u32[]{:S(2)}, u32[]{:S(2)}) collective-permute-start(f32[176,256]{1,0:T(8,128)S(1)} %copy.15), channel_id=1, source_target_pairs={{0,2},{2,4},{4,6},{6,8},{8,10},{10,12},{12,14},{14,16},{16,18},{18... | collective-permute-start | bytes 540680 | tf_op jit(solution)/shard_map/while/body/eval_jaxpr/ppermute | solution.py:477
  18.7 9.3 %collective-permute-start.1 = (f32[200,128]{1,0:T(8,128)S(1)}, f32[200,128]{1,0:T(8,128)S(1)}, u32[]{:S(2)}, u32[]{:S(2)}) collective-permute-start(f32[200,128]{1,0:T(8,128)S(1)} %copy.16), channel_id=1, source_target_pairs={{0,4},{2,6},{4,8},{6,10},{8,12},{10,14},{12,16},{14,18},{16,20},{1... | collective-permute-start | bytes 307208 | tf_op jit(solution)/shard_map/while/body/eval_jaxpr/ppermute | solution.py:478
  18.8 9.2 %collective-permute-start = (f32[176,256]{1,0:T(8,128)S(1)}, f32[176,256]{1,0:T(8,128)S(1)}, u32[]{:S(2)}, u32[]{:S(2)}) collective-permute-start(f32[176,256]{1,0:T(8,128)S(1)} %copy.15), channel_id=1, source_target_pairs={{0,2},{2,4},{4,6},{6,8},{8,10},{10,12},{12,14},{14,16},{16,18},{18... | collective-permute-start | bytes 540680 | tf_op jit(solution)/shard_map/while/body/eval_jaxpr/ppermute | solution.py:477
  28.1 11.0 %collective-permute-start.1 = (f32[200,128]{1,0:T(8,128)S(1)}, f32[200,128]{1,0:T(8,128)S(1)}, u32[]{:S(2)}, u32[]{:S(2)}) collective-permute-start(f32[200,128]{1,0:T(8,128)S(1)} %copy.16), channel_id=1, source_target_pairs={{0,4},{2,6},{4,8},{6,10},{8,12},{10,14},{12,16},{14,18},{16,20},{1... | collective-permute-start | bytes 307208 | tf_op jit(solution)/shard_map/while/body/eval_jaxpr/ppermute | solution.py:478
  29.5 9.7 %collective-permute-start = (f32[176,256]{1,0:T(8,128)S(1)}, f32[176,256]{1,0:T(8,128)S(1)}, u32[]{:S(2)}, u32[]{:S(2)}) collective-permute-start(f32[176,256]{1,0:T(8,128)S(1)} %copy.15), channel_id=1, source_target_pairs={{0,2},{2,4},{4,6},{6,8},{8,10},{10,12},{12,14},{14,16},{16,18},{18... | collective-permute-start | bytes 540680 | tf_op jit(solution)/shard_map/while/body/eval_jaxpr/ppermute | solution.py:477
  39.2 11.7 %collective-permute-start.1 = (f32[200,128]{1,0:T(8,128)S(1)}, f32[200,128]{1,0:T(8,128)S(1)}, u32[]{:S(2)}, u32[]{:S(2)}) collective-permute-start(f32[200,128]{1,0:T(8,128)S(1)} %copy.16), channel_id=1, source_target_pairs={{0,4},{2,6},{4,8},{6,10},{8,12},{10,14},{12,16},{14,18},{16,20},{1... | collective-permute-start | bytes 307208 | tf_op jit(solution)/shard_map/while/body/eval_jaxpr/ppermute | solution.py:478
  41.7 9.2 %collective-permute-start = (f32[176,256]{1,0:T(8,128)S(1)}, f32[176,256]{1,0:T(8,128)S(1)}, u32[]{:S(2)}, u32[]{:S(2)}) collective-permute-start(f32[176,256]{1,0:T(8,128)S(1)} %copy.15), channel_id=1, source_target_pairs={{0,2},{2,4},{4,6},{6,8},{8,10},{10,12},{12,14},{14,16},{16,18},{18... | collective-permute-start | bytes 540680 | tf_op jit(solution)/shard_map/while/body/eval_jaxpr/ppermute | solution.py:477
  51.0 12.1 %collective-permute-start.1 = (f32[200,128]{1,0:T(8,128)S(1)}, f32[200,128]{1,0:T(8,128)S(1)}, u32[]{:S(2)}, u32[]{:S(2)}) collective-permute-start(f32[200,128]{1,0:T(8,128)S(1)} %copy.16), channel_id=1, source_target_pairs={{0,4},{2,6},{4,8},{6,10},{8,12},{10,14},{12,16},{14,18},{16,20},{1... | collective-permute-start | bytes 307208 | tf_op jit(solution)/shard_map/while/body/eval_jaxpr/ppermute | solution.py:478
  51.7 11.5 %collective-permute-start = (f32[176,256]{1,0:T(8,128)S(1)}, f32[176,256]{1,0:T(8,128)S(1)}, u32[]{:S(2)}, u32[]{:S(2)}) collective-permute-start(f32[176,256]{1,0:T(8,128)S(1)} %copy.15), channel_id=1, source_target_pairs={{0,2},{2,4},{4,6},{6,8},{8,10},{10,12},{12,14},{14,16},{16,18},{18... | collective-permute-start | bytes 540680 | tf_op jit(solution)/shard_map/while/body/eval_jaxpr/ppermute | solution.py:477

commit v9 on v7

--- a/solution.py
+++ b/solution.py
@@ -239,7 +239,7 @@
     front = lax.broadcasted_iota(jnp.int32, (TALL, LANES), 1) < HALF
     more = side[0, :, LANES : 2 * LANES]
     for which, (n, radius, own_cells, total, spare, moved) in enumerate(plans):
-        spin, pick = outs[2 * which : 2 * which + 2]
+        spin, pick, frame = outs[3 * which : 3 * which + 3]
         blocks = Blocks(place[0], n, radius, total, moved)
         for part in range(radius // LANES):
             rows = pl.ds(blocks.own_at + part * LANES, LANES)
@@ -255,6 +255,10 @@
             pick[pl.ds(j, TALL, stride=SUB), :] = jnp.where(front, held[1, low, :], held[1, high, :]).astype(jnp.int32)
             bound = jnp.where(sublane == j, jnp.where(lane < HALF, blocks.bounds[j], blocks.bounds[SUB + j]), bound)
 
+        first = lane + (2 * own_cells - REACH) - bound
+        frame[0] = first & (LANES - 1)
+        frame[1] = (first + HALF) & (LANES - 1)
+
         def one(i, _):
             pick[tile(i), :] = (lane + (REACH + bound)) - pick[tile(i), :]
             return 0
@@ -262,9 +266,13 @@
         lax.fori_loop(0, TALL, one, 0)
 
 
+def lanes_of(x, index):
+    return jnp.take_along_axis(x, index, axis=1, mode="promise_in_bounds")
+
+
 def step_kernel(plan, refs, write, scratch):
     n, radius, own_cells, total, spare, moved = plan
-    place, own, near, far, spin, pick = refs
+    place, own, near, far, spin, pick, frame = refs
     tail = slice(FIELDS * own_cells, FIELDS * own_cells + EXTRA)
     cells, stages, packed = scratch
     row = place[0]
@@ -291,9 +299,8 @@
                     ],
                     axis=0,
                 )
-            fill = jnp.zeros((own_cells, LANES), jnp.float32)
-            block = jnp.concatenate([top, near[rows, columns], own[rows, columns], fill], axis=0)
-            cells[f, pl.ds(blocks.own_at + part * LANES, LANES), :] = block.T
+            block = jnp.concatenate([top, near[rows, columns], own[rows, columns]], axis=0)
+            cells[f, pl.ds(blocks.own_at + part * LANES, LANES), 0 : 3 * own_cells] = block.T
         columns = pl.ds(pl.multiple_of(lax.div(f, 4) * LANES, LANES), LANES)
         lanes_at = lax.rem(f, 4) * own_cells
         cells[f, pl.ds(blocks.edge_at, EXTRA), :] = jnp.where(
@@ -305,21 +312,20 @@
 
     lax.fori_loop(0, FIELDS, gather, 0)
 
-    front = lax.broadcasted_iota(jnp.int32, (TALL, LANES), 1) < HALF
-
-    def deal(f, _):
-        for j in range(SUB):
-            low, high = j, SUB + j
-            turn_low = (LANES - (2 * own_cells - REACH)) + blocks.bounds[low]
-            turn_high = (HALF - (2 * own_cells - REACH)) + blocks.bounds[high]
-            stages[0, f, pl.ds(j, TALL, stride=SUB), :] = jnp.where(
-                front,
-                pltpu.roll(cells[f, blocks.rows_of(low), :], turn_low, 1),
-                pltpu.roll(cells[f, blocks.rows_of(high), :], turn_high, 1),
-            )
+    front = lane < HALF
+
+    def deal(turn, _):
+        low, high = frame[0], frame[1]
+        for k in range(PICKS):
+            i = turn * PICKS + k
+            at = EXTRA - REACH + i
+            for f in range(FIELDS):
+                one = cells[f, pl.ds(at, SUB, stride=n), :]
+                two = cells[f, pl.ds(at + SUB * n, SUB, stride=n), :]
+                stages[0, f, tile(i), :] = jnp.where(front, lanes_of(one, low), lanes_of(two, high))
         return 0
 
-    lax.fori_loop(0, FIELDS, deal, 0)
+    lax.fori_loop(0, (n + 2 * REACH + PICKS - 1) // PICKS, deal, 0)
 
     edges = (
         (sublane == 0) & (lane < HALF) & (row == 0),
@@ -329,31 +335,26 @@
 
     even = (lane & own_cells) == 0
 
+    count = (n + PICKS - 1) // PICKS
+
     def shift(turn, _):
         for k in range(PICKS):
-            i = turn * PICKS + k
+            i = (count - turn) * PICKS - 1 - k
             rows = tile(REACH + i)
             source = pick[rows, :]
             picks = [source & (LANES - 1), (source - own_cells) & (LANES - 1)]
-            turned = [
-                jnp.take_along_axis(stages[1, f, rows, :], picks[f % 2], axis=1, mode="promise_in_bounds")
-                for f in range(FIELDS)
-            ]
-            stages[2, 0, tile(i), :] = jnp.where(even, turned[0], turned[1])
-            stages[2, 1, tile(i), :] = jnp.where(even, turned[2], turned[3])
-            stages[2, 2, tile(i), :] = turned[4]
+            turned = [lanes_of(stages[1, f, rows, :], picks[f % 2]) for f in range(FIELDS)]
+            one = jnp.where(even, turned[0], turned[1])
+            two = jnp.where(even, turned[2], turned[3])
+            low = pl.ds(EXTRA + i, SUB, stride=n)
+            high = pl.ds(EXTRA + SUB * n + i, SUB, stride=n)
+            packed[0, low, :] = jnp.where(front, one, pltpu.roll(two, HALF, 1))
+            packed[0, high, :] = jnp.where(front, pltpu.roll(one, HALF, 1), two)
+            packed[1, low, :] = turned[4]
+            packed[1, high, :] = pltpu.roll(turned[4], HALF, 1)
         return 0
 
-    lax.fori_loop(0, (n + PICKS - 1) // PICKS, shift, 0)
-    narrow = lax.broadcasted_iota(jnp.int32, (n, LANES), 1) < HALF
-    for j in range(SUB):
-        one, two, three = [stages[2, g, pl.ds(j, n, stride=SUB), :] for g in range(3)]
-        low = slice(EXTRA + n * j, EXTRA + n * (j + 1))
-        high = slice(EXTRA + n * (SUB + j), EXTRA + n * (SUB + j + 1))
-        packed[0, low, :] = jnp.where(narrow, one, pltpu.roll(two, HALF, 1))
-        packed[0, high, :] = jnp.where(narrow, pltpu.roll(one, HALF, 1), two)
-        packed[1, low, :] = three
-        packed[1, high, :] = pltpu.roll(three, HALF, 1)
+    lax.fori_loop(0, count, shift, 0)
     for part in range(parts):
         rows = pl.ds(blocks.own_at + part * LANES, LANES)
         write.fields(slice(part * LANES, (part + 1) * LANES), packed[0, rows, :].T, packed[1, rows, :].T)
@@ -427,14 +428,14 @@
 def first_step(plan, operands):
     n, radius, own_cells, total, spare, moved = plan
 
-    def kernel(place, own, near, far, spin, pick, near_out, far_out, *scratch):
-        refs = (place, own, near, far, spin, pick)
+    def kernel(place, own, near, far, spin, pick, frame, near_out, far_out, *scratch):
+        refs = (place, own, near, far, spin, pick, frame)
         step_kernel(plan, refs, ToMessage(near_out, far_out, own_cells, spare), scratch)
 
     return pl.pallas_call(
         kernel,
         out_shape=[f32(FIELDS * own_cells + EXTRA, radius), f32(FIELDS * (own_cells + SUB), LANES)],
-        in_specs=[smem] + [vmem] * 5,
+        in_specs=[smem] + [vmem] * 6,
         out_specs=[vmem] * 2,
         scratch_shapes=step_scratch(n),
         compiler_params=params,
@@ -448,8 +449,8 @@
     final = level == levels - 1
     buffer = f32(FIELDS * own_cells, radius)
 
-    def kernel(place, own, near, far, spin, pick, *rest):
-        refs = (place, own, near, far, spin, pick)
+    def kernel(place, own, near, far, spin, pick, frame, *rest):
+        refs = (place, own, near, far, spin, pick, frame)
         if not final:
             step_kernel(plan, refs, ToBuffer(rest[0]), rest[1:])
             return
@@ -476,7 +477,7 @@
     return pl.pallas_call(
         kernel,
         out_shape=out_shape,
-        in_specs=[smem] + [vmem] * (5 + len(done)),
+        in_specs=[smem] + [vmem] * (6 + len(done)),
         out_specs=[pl.BlockSpec(memory_space=pltpu.HBM)] * 3 if final else vmem,
         scratch_shapes=step_scratch(n) + more,
         compiler_params=params,
@@ -534,11 +535,12 @@
     wide = (n + 1, radius, own_cells, total, spare, EXTRA)
     plain = (n, radius, own_cells, total, spare, 0)
     i32 = jax.ShapeDtypeStruct((TALL * SUB, LANES), jnp.int32)
+    frames = jax.ShapeDtypeStruct((2, SUB, LANES), jnp.int32)
     tables = pl.pallas_call(
         lambda *refs: table_kernel((wide, plain), *refs),
-        out_shape=[f32(TALL * SUB, LANES), i32] * 2,
+        out_shape=[f32(TALL * SUB, LANES), i32, frames] * 2,
         in_specs=[smem] + [vmem] * 3,
-        out_specs=[vmem] * 4,
+        out_specs=[vmem] * 6,
         scratch_shapes=[pltpu.VMEM((2, tall_of(n + 1), LANES), jnp.float32)],
         compiler_params=params,
         name="tables",
@@ -547,12 +549,12 @@
     states = []
     for level in range(levels):
         near, far = moved[level]
-        states.append(first_step(wide, (place, owns[level], near, far, *tables[:2])))
+        states.append(first_step(wide, (place, owns[level], near, far, *tables[:3])))
     moved = [(send_near(own), send_far(far)) for own, far in states]
     done = ()
     for level in range(levels):
         near, far = moved[level]
-        operands = (place, states[level][0], near, far, *tables[2:])
+        operands = (place, states[level][0], near, far, *tables[3:])
         result = last_step(plain, level, operands, done if level == levels - 1 else (), levels)
         done += (result,)
     return tuple(result)

time: 53 us -> 54.5 us (1.028)
  Pallas kernels: 34.9 us -> 36.3 us
    pallas_call x2, Pallas kernels: 15.3 us -> 16 us  [last_step(): pl.pallas_call(kernel, out_shape=out_shape, in_specs=[smem] + [vmem] * (6...]
    pallas_call x2, Pallas kernels: 17 us -> 17.7 us  [first_step(): pl.pallas_call(kernel, out_shape=[f32(FIELDS * own_cells + EXTRA, radius)...]
where the time goes in v9:
time: 54.5 us; the launch traced here: 53.9 us
  Pallas kernels  36.3 us (67%)
  starting transfers between devices  11.5 us (21%)
  waiting for transfers between devices  5.26 us (10%)
  between operations  0.74 us (1%)
    pallas_call x2, Pallas kernels, first_step(): pl.pallas_call(kernel, out_shape=[f32(FIELDS * own_cells + EXTRA, radius)...  17.7 us
    pallas_call x2, Pallas kernels, last_step(): pl.pallas_call(kernel, out_shape=out_shape, in_specs=[smem] + [vmem] * (6...  16 us
    ppermute x4, starting transfers between devices, body(): lax.ppermute(x, 'phi', [(p, (p + 2) % phi_count) for p in range(phi_count)])  5.67 us
    ppermute x4, waiting for transfers between devices, body(): lax.ppermute(x, 'phi', [(p, (p + 2) % phi_count) for p in range(phi_count)])  3.14 us
    ppermute x1, starting transfers between devices, body(): send_side = lambda x: lax.ppermute(x, 'row', [(0, 1), (1, 0)])  3 us
    ppermute x4, starting transfers between devices, body(): lax.ppermute(x, 'phi', [(p, (p + 1) % phi_count) for p in range(phi_count)])  2.87 us
    ppermute x1, waiting for transfers between devices, body(): send_side = lambda x: lax.ppermute(x, 'row', [(0, 1), (1, 0)])  2.1 us
    pallas_call x1, Pallas kernels, body(): pl.pallas_call(edge_kernel, out_shape=f32(levels, EXTRA, 2 * LANES), in_s...  1.74 us
  transfers between devices with their start and end apart: 9, of which 2 were waited for; matrix products, arithmetic and copies ran while one was open for 0% of the time, Pallas kernels for 48%

profile of v9, /device:TPU:0, one launch (start us, length us, event | category | flops | bytes accessed | tf_op | source)
XLA Modules:
  0.0 53.9 jit_solution(2652503475752776391)
XLA Ops:
  0.7 1.7 %edges.1 = f32[2,16,256]{2,1,0:T(8,128)} custom-call(s32[1]{0:T(128)} %bitcast.place.refs_0_, f32[2,32,256]{2,1,0:T(8,128)} %refs_0_.1, f32[2,2,32,256]{3,2,1,0:T(8,128)} %refs_1_.1, f32[2,2,32,256]{3,2,1,0:T(8,128)} %refs_2_.1, f32[2,128]{1,0:T(2,128)} %bitcast.3, s32[2,128]{1,0:T(2,128)} %bitcast.5), custom_call_target="tpu_custom_call" | custom-call | tf_op jit(solution)/shard_map/edges/pallas_call | solution.py:510
  2.4 3.0 %collective-permute-start = (f32[2,16,256]{2,1,0:T(8,128)}, f32[2,16,256]{2,1,0:T(8,128)S(1)}, u32[]{:S(2)}, u32[]{:S(2)}) collective-permute-start(f32[2,16,256]{2,1,0:T(8,128)} %edges.1), channel_id=1, source_target_pairs={{0,1},{1,0},{2,3},{3,2},{4,5},{5,4},{6,7},{7,6},{8,9},{9,8},{10,11... | collective-permute-start | bytes 98312 | tf_op jit(solution)/shard_map/ppermute | solution.py:505
  5.4 2.1 %collective-permute-done.refs_3_.refs_1_ = f32[2,16,256]{2,1,0:T(8,128)S(1)} collective-permute-done((f32[2,16,256]{2,1,0:T(8,128)}, f32[2,16,256]{2,1,0:T(8,128)S(1)}, u32[]{:S(2)}, u32[]{:S(2)}) %collective-permute-start) | collective-permute-done | bytes 32800 | tf_op jit(solution)/shard_map/ppermute | solution.py:505
  7.5 0.1 pack.1
  7.6 0.1 collective-permute-start.5
  7.7 2.1 %collective-permute-start.6 = (f32[200,128]{1,0:T(8,128)S(1)}, f32[200,128]{1,0:T(8,128)S(1)}, u32[]{:S(2)}, u32[]{:S(2)}) collective-permute-start(f32[200,128]{1,0:T(8,128)S(1)} %get-tuple-element.28), channel_id=1, source_target_pairs={{0,4},{2,6},{4,8},{6,10},{8,12},{10,14},{12,16},{14,18},{16,20},{1... | collective-permute-start | bytes 307208 | tf_op jit(solution)/shard_map/ppermute | solution.py:504
  9.8 1.3 %collective-permute-start.1 = (f32[176,256]{1,0:T(8,128)S(1)}, f32[176,256]{1,0:T(8,128)S(1)}, u32[]{:S(2)}, u32[]{:S(2)}) collective-permute-start(f32[176,256]{1,0:T(8,128)S(1)} %get-tuple-element.17.own), channel_id=1, source_target_pairs={{0,2},{2,4},{4,6},{6,8},{8,10},{10,12},{12,14},{14,16},{16,18},{18... | collective-permute-start | bytes 540680 | tf_op jit(solution)/shard_map/ppermute | solution.py:503
  11.1 1.5 %collective-permute-start.2 = (f32[200,128]{1,0:T(8,128)S(1)}, f32[200,128]{1,0:T(8,128)S(1)}, u32[]{:S(2)}, u32[]{:S(2)}) collective-permute-start(f32[200,128]{1,0:T(8,128)S(1)} %get-tuple-element.18), channel_id=1, source_target_pairs={{0,4},{2,6},{4,8},{6,10},{8,12},{10,14},{12,16},{14,18},{16,20},{1... | collective-permute-start | bytes 307208 | tf_op jit(solution)/shard_map/ppermute | solution.py:504
  12.6 0.8 %tables.1 = (f32[256,128]{1,0:T(8,128)S(1)}, s32[256,128]{1,0:T(8,128)S(1)}, s32[2,8,128]{2,1,0:T(8,128)S(1)}, f32[256,128]{1,0:T(8,128)S(1)}, s32[256,128]{1,0:T(8,128)S(1)}, /*index=5*/s32[2,8,128]{2,1,0:T(8,128)S(1)}) custom-call(s32[1]{0:T(128)} %bitcast.place.refs_0_, f32[2,16,256]{2,1,0:T(8,128)S(1)} %collective-permute-done.refs_3_.refs_1_, ...), custom_call_target="tpu_custom_call" | custom-call | tf_op jit(solution)/shard_map/tables/pallas_call | solution.py:539
  13.5 3.1 %collective-permute-done.6.far = f32[200,128]{1,0:T(8,128)S(1)} collective-permute-done((f32[200,128]{1,0:T(8,128)S(1)}, f32[200,128]{1,0:T(8,128)S(1)}, u32[]{:S(2)}, u32[]{:S(2)}) %collective-permute-start.6) | collective-permute-done | bytes 102432 | tf_op jit(solution)/shard_map/ppermute | solution.py:504
  16.6 0.0 collective-permute-done.5.near
  16.6 8.8 %first_step.3 = (f32[176,256]{1,0:T(8,128)S(1)}, f32[200,128]{1,0:T(8,128)S(1)}) custom-call(s32[1]{0:T(128)} %bitcast.place.refs_0_, f32[176,256]{1,0:T(8,128)S(1)} %get-tuple-element.27.own, f32[176,256]{1,0:T(8,128)S(1)} %collective-permute-done.5.near, f32[200,128]{1,0:T(8,128)S(1)} %collective-permute-done.6.far, ...), custom_call_target="tpu_custom_call" | custom-call | flops 8999999488 | bytes 29000000 | tf_op jit(solution)/shard_map/first_step/pallas_call | solution.py:435
  25.4 1.2 %collective-permute-start.7 = (f32[176,256]{1,0:T(8,128)S(1)}, f32[176,256]{1,0:T(8,128)S(1)}, u32[]{:S(2)}, u32[]{:S(2)}) collective-permute-start(f32[176,256]{1,0:T(8,128)S(1)} %get-tuple-element.29.own), channel_id=1, source_target_pairs={{0,2},{2,4},{4,6},{6,8},{8,10},{10,12},{12,14},{14,16},{16,18},{18... | collective-permute-start | bytes 540680 | tf_op jit(solution)/shard_map/ppermute | solution.py:503
  26.6 0.0 collective-permute-start.8
  26.6 0.0 collective-permute-done.2.far
  26.6 0.0 collective-permute-done.1.near
  26.6 8.8 %first_step.2 = (f32[176,256]{1,0:T(8,128)S(1)}, f32[200,128]{1,0:T(8,128)S(1)}) custom-call(s32[1]{0:T(128)} %bitcast.place.refs_0_, f32[176,256]{1,0:T(8,128)S(1)} %get-tuple-element.17.own, f32[176,256]{1,0:T(8,128)S(1)} %collective-permute-done.1.near, f32[200,128]{1,0:T(8,128)S(1)} %collective-permute-done.2.far, ...), custom_call_target="tpu_custom_call" | custom-call | flops 8999999488 | bytes 29000000 | tf_op jit(solution)/shard_map/first_step/pallas_call | solution.py:435
  35.5 0.4 collective-permute-start.3
  35.8 2.1 %collective-permute-start.4 = (f32[200,128]{1,0:T(8,128)S(1)}, f32[200,128]{1,0:T(8,128)S(1)}, u32[]{:S(2)}, u32[]{:S(2)}) collective-permute-start(f32[200,128]{1,0:T(8,128)S(1)} %get-tuple-element.23), channel_id=1, source_target_pairs={{0,4},{2,6},{4,8},{6,10},{8,12},{10,14},{12,16},{14,18},{16,20},{1... | collective-permute-start | bytes 307208 | tf_op jit(solution)/shard_map/ppermute | solution.py:504
  37.9 0.0 collective-permute-done.8.far
  37.9 0.0 collective-permute-done.7.near
  37.9 7.6 %last_step.2.rest_0_ = f32[160,256]{1,0:T(8,128)S(1)} custom-call(s32[1]{0:T(128)} %bitcast.place.refs_0_, f32[176,256]{1,0:T(8,128)S(1)} %get-tuple-element.29.own, f32[176,256]{1,0:T(8,128)S(1)} %collective-permute-done.7.near, f32[200,128]{1,0:T(8,128)S(1)} %collective-permute-done.8.far, f32[256,128]{1,0:T(8,128)S(1)} %get-tuple-element.24.spin, ...), custom_call_target="tpu_custom_call" | custom-call | flops 8999999488 | bytes 29000000 | tf_op jit(solution)/shard_map/last_step/pallas_call | solution.py:477
  45.5 0.0 collective-permute-done.4.far
  45.5 8.4 %last_step.3 = (f32[2,32,256]{2,1,0:T(8,128)}, f32[2,2,32,256]{3,2,1,0:T(8,128)}, f32[2,2,32,256]{3,2,1,0:T(8,128)}) custom-call(s32[1]{0:T(128)} %bitcast.place.refs_0_, f32[176,256]{1,0:T(8,128)S(1)} %get-tuple-element.22.own, f32[176,256]{1,0:T(8,128)S(1)} %collective-permute-done.3.near, f32[200,128]{1,0:T(8,128)S(1)} %collective-permute-done.4.far, ...), custom_call_target="tpu_custom_call" | custom-call | flops 8999999488 | bytes 29000000 | tf_op jit(solution)/shard_map/last_step/pallas_call | solution.py:477
  (11 shorter events, 0.0 us)
Async XLA Ops:
  0.6 6.9 %copy-start = (f32[2,2,32,256]{3,2,1,0:T(8,128)S(1)}, f32[2,2,32,256]{3,2,1,0:T(8,128)}, u32[]{:S(2)}) copy-start(f32[2,2,32,256]{3,2,1,0:T(8,128)} %refs_1_.1) | copy-start | bytes 393220
  0.6 6.9 %copy-start.1 = (f32[2,2,32,256]{3,2,1,0:T(8,128)S(1)}, f32[2,2,32,256]{3,2,1,0:T(8,128)}, u32[]{:S(2)}) copy-start(f32[2,2,32,256]{3,2,1,0:T(8,128)} %refs_2_.1) | copy-start | bytes 393220
  0.7 6.9 %copy-start.2 = (f32[2,32,256]{2,1,0:T(8,128)S(1)}, f32[2,32,256]{2,1,0:T(8,128)}, u32[]{:S(2)}) copy-start(f32[2,32,256]{2,1,0:T(8,128)} %refs_0_.1) | copy-start | bytes 196612
  2.4 5.1 %collective-permute-start = (f32[2,16,256]{2,1,0:T(8,128)}, f32[2,16,256]{2,1,0:T(8,128)S(1)}, u32[]{:S(2)}, u32[]{:S(2)}) collective-permute-start(f32[2,16,256]{2,1,0:T(8,128)} %edges.1), channel_id=1, source_target_pairs={{0,1},{1,0},{2,3},{3,2},{4,5},{5,4},{6,7},{7,6},{8,9},{9,8},{10,11... | collective-permute-start | bytes 98312 | tf_op jit(solution)/shard_map/ppermute | solution.py:505
  7.6 8.9 %collective-permute-start.5 = (f32[176,256]{1,0:T(8,128)S(1)}, f32[176,256]{1,0:T(8,128)S(1)}, u32[]{:S(2)}, u32[]{:S(2)}) collective-permute-start(f32[176,256]{1,0:T(8,128)S(1)} %get-tuple-element.27.own), channel_id=1, source_target_pairs={{0,2},{2,4},{4,6},{6,8},{8,10},{10,12},{12,14},{14,16},{16,18},{18... | collective-permute-start | bytes 540680 | tf_op jit(solution)/shard_map/ppermute | solution.py:503
  7.7 8.9 %collective-permute-start.6 = (f32[200,128]{1,0:T(8,128)S(1)}, f32[200,128]{1,0:T(8,128)S(1)}, u32[]{:S(2)}, u32[]{:S(2)}) collective-permute-start(f32[200,128]{1,0:T(8,128)S(1)} %get-tuple-element.28), channel_id=1, source_target_pairs={{0,4},{2,6},{4,8},{6,10},{8,12},{10,14},{12,16},{14,18},{16,20},{1... | collective-permute-start | bytes 307208 | tf_op jit(solution)/shard_map/ppermute | solution.py:504
  9.8 2.8 %copy-start.4 = (s32[256]{0:T(256)S(1)}, s32[256]{0:T(256)}, u32[]{:S(2)}) copy-start(s32[256]{0:T(256)} %param.9) | copy-start | bytes 3076
  9.8 2.8 %copy-start.3 = (f32[256]{0:T(256)S(1)}, f32[256]{0:T(256)}, u32[]{:S(2)}) copy-start(f32[256]{0:T(256)} %param.8) | copy-start | bytes 3076
  9.8 16.8 %collective-permute-start.1 = (f32[176,256]{1,0:T(8,128)S(1)}, f32[176,256]{1,0:T(8,128)S(1)}, u32[]{:S(2)}, u32[]{:S(2)}) collective-permute-start(f32[176,256]{1,0:T(8,128)S(1)} %get-tuple-element.17.own), channel_id=1, source_target_pairs={{0,2},{2,4},{4,6},{6,8},{8,10},{10,12},{12,14},{14,16},{16,18},{18... | collective-permute-start | bytes 540680 | tf_op jit(solution)/shard_map/ppermute | solution.py:503
  11.1 15.5 %collective-permute-start.2 = (f32[200,128]{1,0:T(8,128)S(1)}, f32[200,128]{1,0:T(8,128)S(1)}, u32[]{:S(2)}, u32[]{:S(2)}) collective-permute-start(f32[200,128]{1,0:T(8,128)S(1)} %get-tuple-element.18), channel_id=1, source_target_pairs={{0,4},{2,6},{4,8},{6,10},{8,12},{10,14},{12,16},{14,18},{16,20},{1... | collective-permute-start | bytes 307208 | tf_op jit(solution)/shard_map/ppermute | solution.py:504
  25.4 12.4 %collective-permute-start.7 = (f32[176,256]{1,0:T(8,128)S(1)}, f32[176,256]{1,0:T(8,128)S(1)}, u32[]{:S(2)}, u32[]{:S(2)}) collective-permute-start(f32[176,256]{1,0:T(8,128)S(1)} %get-tuple-element.29.own), channel_id=1, source_target_pairs={{0,2},{2,4},{4,6},{6,8},{8,10},{10,12},{12,14},{14,16},{16,18},{18... | collective-permute-start | bytes 540680 | tf_op jit(solution)/shard_map/ppermute | solution.py:503
  26.6 11.3 %collective-permute-start.8 = (f32[200,128]{1,0:T(8,128)S(1)}, f32[200,128]{1,0:T(8,128)S(1)}, u32[]{:S(2)}, u32[]{:S(2)}) collective-permute-start(f32[200,128]{1,0:T(8,128)S(1)} %get-tuple-element.30), channel_id=1, source_target_pairs={{0,4},{2,6},{4,8},{6,10},{8,12},{10,14},{12,16},{14,18},{16,20},{1... | collective-permute-start | bytes 307208 | tf_op jit(solution)/shard_map/ppermute | solution.py:504
  35.5 10.1 %collective-permute-start.3 = (f32[176,256]{1,0:T(8,128)S(1)}, f32[176,256]{1,0:T(8,128)S(1)}, u32[]{:S(2)}, u32[]{:S(2)}) collective-permute-start(f32[176,256]{1,0:T(8,128)S(1)} %get-tuple-element.22.own), channel_id=1, source_target_pairs={{0,2},{2,4},{4,6},{6,8},{8,10},{10,12},{12,14},{14,16},{16,18},{18... | collective-permute-start | bytes 540680 | tf_op jit(solution)/shard_map/ppermute | solution.py:503
  35.8 9.7 %collective-permute-start.4 = (f32[200,128]{1,0:T(8,128)S(1)}, f32[200,128]{1,0:T(8,128)S(1)}, u32[]{:S(2)}, u32[]{:S(2)}) collective-permute-start(f32[200,128]{1,0:T(8,128)S(1)} %get-tuple-element.23), channel_id=1, source_target_pairs={{0,4},{2,6},{4,8},{6,10},{8,12},{10,14},{12,16},{14,18},{16,20},{1... | collective-permute-start | bytes 307208 | tf_op jit(solution)/shard_map/ppermute | solution.py:504

commit v10 on v7

--- a/solution.py
+++ b/solution.py
@@ -37,22 +37,23 @@
 def physical(state):
     rho, mn, mt, bn, bt = state
     inverse = pltpu.reciprocal(rho, approx=True)
+    bn_sq = bn * bn
+    bt_sq = bt * bt
     vn = mn * inverse
     vt = mt * inverse
-    bn_sq = bn * bn
-    bt_sq = bt * bt
+    inside = (bn_sq + bt_sq) * inverse + 1.0
+    root = lax.rsqrt(inside)
     ram = mn * vn + rho
     tension = bt_sq - bn_sq
     flux_t = mt * vn - bn * bt
     flux_b = bt * vn - bn * vt
-    inside = (bn_sq + bt_sq) * inverse + 1.0
-    speed = jnp.abs(vn) + inside * lax.rsqrt(inside)
+    speed = jnp.abs(vn) + inside * root
     return ram, tension, flux_t, flux_b, speed
 
 
-def face_twice(left, right):
-    left_ram, left_tension, left_t, left_b, left_speed = physical(left)
-    right_ram, right_tension, right_t, right_b, right_speed = physical(right)
+def face_twice(left, right, of_left, of_right):
+    left_ram, left_tension, left_t, left_b, left_speed = of_left
+    right_ram, right_tension, right_t, right_b, right_speed = of_right
     bound = jnp.maximum(left_speed, right_speed)
     jumps = [bound * (l - r) for l, r in zip(left, right)]
     return [
@@ -68,29 +69,6 @@
     return [five[0], five[2], five[1], five[4], five[3]]
 
 
-def radial_faces(rows):
-    halves = [[0.5 * x for x in r] for r in rows]
-    jumps = [[b - a for a, b in zip(p, q)] for p, q in zip(halves[:-1], halves[1:])]
-    slopes = [[minmod(a, b) for a, b in zip(p, q)] for p, q in zip(jumps[:-1], jumps[1:])]
-    upper = [[x + s for x, s in zip(r, sl)] for r, sl in zip(rows[1:-1], slopes)]
-    lower = [[x - s for x, s in zip(r, sl)] for r, sl in zip(rows[1:-1], slopes)]
-    return [swapped(face_twice(swapped(u), swapped(l))) for u, l in zip(upper[:-1], lower[1:])]
-
-
-def azimuth_change(fields):
-    right_of = lambda x: pltpu.roll(x, LANES - 1, 1)
-    left_of = lambda x: pltpu.roll(x, 1, 1)
-    lower = []
-    upper = []
-    for x in fields:
-        half = 0.5 * x
-        jump = right_of(half) - half
-        slope = minmod(left_of(jump), jump)
-        upper.append(x + slope)
-        lower.append(right_of(x - slope))
-    return [x - left_of(x) for x in face_twice(upper, lower)]
-
-
 def tile(i):
     return pl.ds(pl.multiple_of(i * SUB, SUB), SUB)
 
@@ -100,31 +78,50 @@
     low_mask, high_mask = edges
     first, last = REACH, REACH + n - 1
 
-    def work(stage, i0, count, before):
+    right_of = lambda x: pltpu.roll(x, LANES - 1, 1)
+    left_of = lambda x: pltpu.roll(x, 1, 1)
+
+    def radial_states(halves, centres):
+        jumps = [h[SUB:] - h[:-SUB] for h in halves]
+        slopes = [minmod(d[:-SUB], d[SUB:]) for d in jumps]
+        lower = [x - g for x, g in zip(centres, slopes)]
+        upper = [x + g for x, g in zip(centres, slopes)]
+        return swapped([x[:-SUB] for x in upper]), swapped([x[SUB:] for x in lower])
+
+    def work(stage, i0, before):
         src, dst = stage, (stage & 1) + 1
         weight = jnp.where(stage == 0, 1.0, jnp.where(stage == 1, 0.25, 2.0 / 3.0))
         keep = jnp.where(stage == 0, 0.0, jnp.where(stage == 1, 0.75, 1.0 / 3.0))
-        rows = [[stages[src, f, tile(i0 + k), :] for f in range(FIELDS)] for k in range(-1, count + 2)]
-        starts = [[stages[0, f, tile(i0 + k), :] for f in range(FIELDS)] for k in range(count)]
-        turns = [spin[tile(i0 + k), :] for k in range(count)]
-        faces = [before] + radial_faces(rows)
-        for k in range(count):
-            fields = rows[k + 1]
-            change = azimuth_change(fields)
-            turn = turns[k]
-            source = [
-                None,
-                (-0.5 * turn) * fields[2],
-                (2.0 * turn) * fields[1],
-                (-1.5 * turn) * fields[4],
-                None,
-            ]
-            for f in range(FIELDS):
-                new = fields[f] - half_dt * (change[f] + (faces[k + 1][f] - faces[k][f]))
-                if source[f] is not None:
-                    new = new + source[f]
-                stages[dst, f, tile(i0 + k), :] = weight * new + keep * starts[k][f]
-        return faces[-1]
+        some = lambda first, count: pl.ds(pl.multiple_of((i0 + first) * SUB, SUB), count * SUB)
+        here = some(0, ROWS)
+        size = ROWS * SUB
+        rows = [stages[src, f, some(-1, ROWS + 3), :] for f in range(FIELDS)]
+        halves = [0.5 * x for x in rows]
+        own = [x[SUB : SUB + size] for x in rows]
+        half = [x[SUB : SUB + size] for x in halves]
+        after = [right_of(x) for x in half]
+        left, right = radial_states(halves, [x[SUB:-SUB] for x in rows])
+        jump = [x - y for x, y in zip(after, half)]
+        behind = [left_of(x) for x in jump]
+        of_left = physical(left)
+        of_right = physical(right)
+        slopes = [minmod(x, y) for x, y in zip(behind, jump)]
+        lower = [right_of(x - y) for x, y in zip(own, slopes)]
+        upper = [x + y for x, y in zip(own, slopes)]
+        of_upper = physical(upper)
+        faces = swapped(face_twice(left, right, of_left, of_right))
+        of_lower = physical(lower)
+        azimuth = face_twice(upper, lower, of_upper, of_lower)
+        shifted = [left_of(x) for x in azimuth]
+        change = [x - jnp.concatenate([y, x[:-SUB]], axis=0) for x, y in zip(faces, before)]
+        turn = spin[here, :]
+        source = [None, (-0.5 * turn) * own[2], (2.0 * turn) * own[1], (-1.5 * turn) * own[4], None]
+        partial = [x if y is None else x + y for x, y in zip(own, source)]
+        starts = [keep * stages[0, f, here, :] for f in range(FIELDS)]
+        for f in range(FIELDS):
+            new = partial[f] - half_dt * ((azimuth[f] - shifted[f]) + change[f])
+            stages[dst, f, here, :] = weight * new + starts[f]
+        return [x[-SUB:] for x in faces]
 
     def run(stage, _):
         for f in range(FIELDS):
@@ -136,14 +133,15 @@
         count = n + 2 * REACH - 4 - 4 * stage
         if n % ROWS == 0:
             lo = 2 * stage + 2
-            ahead = [[stages[stage, f, tile(lo + k), :] for f in range(FIELDS)] for k in range(-2, 2)]
-            before = tuple(radial_faces(ahead)[0])
+            rows = [stages[stage, f, pl.ds(pl.multiple_of((lo - 2) * SUB, SUB), 4 * SUB), :] for f in range(FIELDS)]
+            left, right = radial_states([0.5 * x for x in rows], [x[SUB:-SUB] for x in rows])
+            before = tuple(swapped(face_twice(left, right, physical(left), physical(right))))
         else:
             lo = 2 * stage + 1
             count = count + 1
             before = (jnp.zeros((SUB, LANES), jnp.float32),) * FIELDS
         turns = lax.div(count + ROWS - 1, ROWS)
-        lax.fori_loop(0, turns, lambda c, carried: tuple(work(stage, lo + c * ROWS, ROWS, list(carried))), before)
+        lax.fori_loop(0, turns, lambda c, carried: tuple(work(stage, lo + c * ROWS, list(carried))), before)
         return 0
 
     lax.fori_loop(0, STAGES, run, 0)

time: 53 us -> 53.1 us (level)
  no operation moved by 1% of the time
where the time goes in v10:
time: 53.1 us; the launch traced here: 52.5 us
  Pallas kernels  35 us (66%)
  starting transfers between devices  11.5 us (22%)
  waiting for transfers between devices  5.26 us (10%)
  between operations  0.74 us (1%)
    pallas_call x2, Pallas kernels, first_step(): pl.pallas_call(kernel, out_shape=[f32(FIELDS * own_cells + EXTRA, radius)...  17 us
    pallas_call x2, Pallas kernels, last_step(): pl.pallas_call(kernel, out_shape=out_shape, in_specs=[smem] + [vmem] * (5...  15.3 us
    ppermute x4, starting transfers between devices, body(): lax.ppermute(x, 'phi', [(p, (p + 2) % phi_count) for p in range(phi_count)])  5.67 us
    ppermute x4, waiting for transfers between devices, body(): lax.ppermute(x, 'phi', [(p, (p + 2) % phi_count) for p in range(phi_count)])  3.14 us
    ppermute x1, starting transfers between devices, body(): send_side = lambda x: lax.ppermute(x, 'row', [(0, 1), (1, 0)])  3 us
    ppermute x4, starting transfers between devices, body(): lax.ppermute(x, 'phi', [(p, (p + 1) % phi_count) for p in range(phi_count)])  2.86 us
    ppermute x1, waiting for transfers between devices, body(): send_side = lambda x: lax.ppermute(x, 'row', [(0, 1), (1, 0)])  2.1 us
    pallas_call x1, Pallas kernels, body(): pl.pallas_call(edge_kernel, out_shape=f32(levels, EXTRA, 2 * LANES), in_s...  1.74 us
  transfers between devices with their start and end apart: 9, of which 2 were waited for; matrix products, arithmetic and copies ran while one was open for 0% of the time, Pallas kernels for 48%

profile of v10, /device:TPU:0, one launch (start us, length us, event | category | flops | bytes accessed | tf_op | source)
XLA Modules:
  0.0 52.5 jit_solution(6850517280170155058)
XLA Ops:
  0.7 1.7 %edges.1 = f32[2,16,256]{2,1,0:T(8,128)} custom-call(s32[1]{0:T(128)} %bitcast.place.refs_0_, f32[2,32,256]{2,1,0:T(8,128)} %refs_0_.1, f32[2,2,32,256]{3,2,1,0:T(8,128)} %refs_1_.1, f32[2,2,32,256]{3,2,1,0:T(8,128)} %refs_2_.1, f32[2,128]{1,0:T(2,128)} %bitcast.3, s32[2,128]{1,0:T(2,128)} %bitcast.5), custom_call_target="tpu_custom_call" | custom-call | tf_op jit(solution)/shard_map/edges/pallas_call | solution.py:507
  2.4 3.0 %collective-permute-start = (f32[2,16,256]{2,1,0:T(8,128)}, f32[2,16,256]{2,1,0:T(8,128)S(1)}, u32[]{:S(2)}, u32[]{:S(2)}) collective-permute-start(f32[2,16,256]{2,1,0:T(8,128)} %edges.1), channel_id=1, source_target_pairs={{0,1},{1,0},{2,3},{3,2},{4,5},{5,4},{6,7},{7,6},{8,9},{9,8},{10,11... | collective-permute-start | bytes 98312 | tf_op jit(solution)/shard_map/ppermute | solution.py:502
  5.4 2.1 %collective-permute-done.refs_3_.refs_1_ = f32[2,16,256]{2,1,0:T(8,128)S(1)} collective-permute-done((f32[2,16,256]{2,1,0:T(8,128)}, f32[2,16,256]{2,1,0:T(8,128)S(1)}, u32[]{:S(2)}, u32[]{:S(2)}) %collective-permute-start) | collective-permute-done | bytes 32800 | tf_op jit(solution)/shard_map/ppermute | solution.py:502
  7.5 0.1 pack.1
  7.6 0.1 collective-permute-start.5
  7.7 2.1 %collective-permute-start.6 = (f32[200,128]{1,0:T(8,128)S(1)}, f32[200,128]{1,0:T(8,128)S(1)}, u32[]{:S(2)}, u32[]{:S(2)}) collective-permute-start(f32[200,128]{1,0:T(8,128)S(1)} %get-tuple-element.24), channel_id=1, source_target_pairs={{0,4},{2,6},{4,8},{6,10},{8,12},{10,14},{12,16},{14,18},{16,20},{1... | collective-permute-start | bytes 307208 | tf_op jit(solution)/shard_map/ppermute | solution.py:501
  9.8 1.3 %collective-permute-start.1 = (f32[176,256]{1,0:T(8,128)S(1)}, f32[176,256]{1,0:T(8,128)S(1)}, u32[]{:S(2)}, u32[]{:S(2)}) collective-permute-start(f32[176,256]{1,0:T(8,128)S(1)} %get-tuple-element.15.own), channel_id=1, source_target_pairs={{0,2},{2,4},{4,6},{6,8},{8,10},{10,12},{12,14},{14,16},{16,18},{18... | collective-permute-start | bytes 540680 | tf_op jit(solution)/shard_map/ppermute | solution.py:500
  11.1 1.5 %collective-permute-start.2 = (f32[200,128]{1,0:T(8,128)S(1)}, f32[200,128]{1,0:T(8,128)S(1)}, u32[]{:S(2)}, u32[]{:S(2)}) collective-permute-start(f32[200,128]{1,0:T(8,128)S(1)} %get-tuple-element.16), channel_id=1, source_target_pairs={{0,4},{2,6},{4,8},{6,10},{8,12},{10,14},{12,16},{14,18},{16,20},{1... | collective-permute-start | bytes 307208 | tf_op jit(solution)/shard_map/ppermute | solution.py:501
  12.6 0.8 %tables.1 = (f32[256,128]{1,0:T(8,128)S(1)}, s32[256,128]{1,0:T(8,128)S(1)}, f32[256,128]{1,0:T(8,128)S(1)}, s32[256,128]{1,0:T(8,128)S(1)}) custom-call(s32[1]{0:T(128)} %bitcast.place.refs_0_, f32[2,16,256]{2,1,0:T(8,128)S(1)} %collective-permute-done.refs_3_.refs_1_, f32[2,128]{1,0:T(2,128)S(1)} %bitcast.4, s32[2,128]{1,0:T(2,128)S(1)} %bitcast.6), custom_call_target="tpu_custom_call" | custom-call | tf_op jit(solution)/shard_map/tables/pallas_call | solution.py:535
  13.5 3.1 %collective-permute-done.6.far = f32[200,128]{1,0:T(8,128)S(1)} collective-permute-done((f32[200,128]{1,0:T(8,128)S(1)}, f32[200,128]{1,0:T(8,128)S(1)}, u32[]{:S(2)}, u32[]{:S(2)}) %collective-permute-start.6) | collective-permute-done | bytes 102432 | tf_op jit(solution)/shard_map/ppermute | solution.py:501
  16.6 0.0 collective-permute-done.5.near
  16.6 8.5 %first_step.3 = (f32[176,256]{1,0:T(8,128)S(1)}, f32[200,128]{1,0:T(8,128)S(1)}) custom-call(s32[1]{0:T(128)} %bitcast.place.refs_0_, f32[176,256]{1,0:T(8,128)S(1)} %get-tuple-element.23.own, f32[176,256]{1,0:T(8,128)S(1)} %collective-permute-done.5.near, f32[200,128]{1,0:T(8,128)S(1)} %collective-permute-done.6.far, ...), custom_call_target="tpu_custom_call" | custom-call | flops 8999999488 | bytes 29000000 | tf_op jit(solution)/shard_map/first_step/pallas_call | solution.py:432
  25.1 1.2 %collective-permute-start.7 = (f32[176,256]{1,0:T(8,128)S(1)}, f32[176,256]{1,0:T(8,128)S(1)}, u32[]{:S(2)}, u32[]{:S(2)}) collective-permute-start(f32[176,256]{1,0:T(8,128)S(1)} %get-tuple-element.25.own), channel_id=1, source_target_pairs={{0,2},{2,4},{4,6},{6,8},{8,10},{10,12},{12,14},{14,16},{16,18},{18... | collective-permute-start | bytes 540680 | tf_op jit(solution)/shard_map/ppermute | solution.py:500
  26.3 0.0 collective-permute-start.8
  26.3 0.0 collective-permute-done.2.far
  26.3 8.5 %first_step.2 = (f32[176,256]{1,0:T(8,128)S(1)}, f32[200,128]{1,0:T(8,128)S(1)}) custom-call(s32[1]{0:T(128)} %bitcast.place.refs_0_, f32[176,256]{1,0:T(8,128)S(1)} %get-tuple-element.15.own, f32[176,256]{1,0:T(8,128)S(1)} %collective-permute-done.1.near, f32[200,128]{1,0:T(8,128)S(1)} %collective-permute-done.2.far, ...), custom_call_target="tpu_custom_call" | custom-call | flops 8999999488 | bytes 29000000 | tf_op jit(solution)/shard_map/first_step/pallas_call | solution.py:432
  34.8 0.4 collective-permute-start.3
  35.2 2.1 %collective-permute-start.4 = (f32[200,128]{1,0:T(8,128)S(1)}, f32[200,128]{1,0:T(8,128)S(1)}, u32[]{:S(2)}, u32[]{:S(2)}) collective-permute-start(f32[200,128]{1,0:T(8,128)S(1)} %get-tuple-element.20), channel_id=1, source_target_pairs={{0,4},{2,6},{4,8},{6,10},{8,12},{10,14},{12,16},{14,18},{16,20},{1... | collective-permute-start | bytes 307208 | tf_op jit(solution)/shard_map/ppermute | solution.py:501
  37.2 0.0 collective-permute-done.8.far
  37.2 0.0 collective-permute-done.7.near
  37.2 7.3 %last_step.2.rest_0_ = f32[160,256]{1,0:T(8,128)S(1)} custom-call(s32[1]{0:T(128)} %bitcast.place.refs_0_, f32[176,256]{1,0:T(8,128)S(1)} %get-tuple-element.25.own, f32[176,256]{1,0:T(8,128)S(1)} %collective-permute-done.7.near, f32[200,128]{1,0:T(8,128)S(1)} %collective-permute-done.8.far, f32[256,128]{1,0:T(8,128)S(1)} %get-tuple-element.21.spin, ...), custom_call_target="tpu_custom_call" | custom-call | flops 8999999488 | bytes 29000000 | tf_op jit(solution)/shard_map/last_step/pallas_call | solution.py:474
  44.5 0.0 collective-permute-done.4.far
  44.5 0.0 collective-permute-done.3.near
  44.5 8.0 %last_step.3 = (f32[2,32,256]{2,1,0:T(8,128)}, f32[2,2,32,256]{3,2,1,0:T(8,128)}, f32[2,2,32,256]{3,2,1,0:T(8,128)}) custom-call(s32[1]{0:T(128)} %bitcast.place.refs_0_, f32[176,256]{1,0:T(8,128)S(1)} %get-tuple-element.19.own, f32[176,256]{1,0:T(8,128)S(1)} %collective-permute-done.3.near, f32[200,128]{1,0:T(8,128)S(1)} %collective-permute-done.4.far, ...), custom_call_target="tpu_custom_call" | custom-call | flops 8999999488 | bytes 29000000 | tf_op jit(solution)/shard_map/last_step/pallas_call | solution.py:474
  (11 shorter events, 0.0 us)
Async XLA Ops:
  0.6 6.9 %copy-start = (f32[2,2,32,256]{3,2,1,0:T(8,128)S(1)}, f32[2,2,32,256]{3,2,1,0:T(8,128)}, u32[]{:S(2)}) copy-start(f32[2,2,32,256]{3,2,1,0:T(8,128)} %refs_1_.1) | copy-start | bytes 393220
  0.6 6.9 %copy-start.1 = (f32[2,2,32,256]{3,2,1,0:T(8,128)S(1)}, f32[2,2,32,256]{3,2,1,0:T(8,128)}, u32[]{:S(2)}) copy-start(f32[2,2,32,256]{3,2,1,0:T(8,128)} %refs_2_.1) | copy-start | bytes 393220
  0.7 6.9 %copy-start.2 = (f32[2,32,256]{2,1,0:T(8,128)S(1)}, f32[2,32,256]{2,1,0:T(8,128)}, u32[]{:S(2)}) copy-start(f32[2,32,256]{2,1,0:T(8,128)} %refs_0_.1) | copy-start | bytes 196612
  2.4 5.1 %collective-permute-start = (f32[2,16,256]{2,1,0:T(8,128)}, f32[2,16,256]{2,1,0:T(8,128)S(1)}, u32[]{:S(2)}, u32[]{:S(2)}) collective-permute-start(f32[2,16,256]{2,1,0:T(8,128)} %edges.1), channel_id=1, source_target_pairs={{0,1},{1,0},{2,3},{3,2},{4,5},{5,4},{6,7},{7,6},{8,9},{9,8},{10,11... | collective-permute-start | bytes 98312 | tf_op jit(solution)/shard_map/ppermute | solution.py:502
  7.6 8.9 %collective-permute-start.5 = (f32[176,256]{1,0:T(8,128)S(1)}, f32[176,256]{1,0:T(8,128)S(1)}, u32[]{:S(2)}, u32[]{:S(2)}) collective-permute-start(f32[176,256]{1,0:T(8,128)S(1)} %get-tuple-element.23.own), channel_id=1, source_target_pairs={{0,2},{2,4},{4,6},{6,8},{8,10},{10,12},{12,14},{14,16},{16,18},{18... | collective-permute-start | bytes 540680 | tf_op jit(solution)/shard_map/ppermute | solution.py:500
  7.7 8.9 %collective-permute-start.6 = (f32[200,128]{1,0:T(8,128)S(1)}, f32[200,128]{1,0:T(8,128)S(1)}, u32[]{:S(2)}, u32[]{:S(2)}) collective-permute-start(f32[200,128]{1,0:T(8,128)S(1)} %get-tuple-element.24), channel_id=1, source_target_pairs={{0,4},{2,6},{4,8},{6,10},{8,12},{10,14},{12,16},{14,18},{16,20},{1... | collective-permute-start | bytes 307208 | tf_op jit(solution)/shard_map/ppermute | solution.py:501
  9.8 2.8 %copy-start.4 = (s32[256]{0:T(256)S(1)}, s32[256]{0:T(256)}, u32[]{:S(2)}) copy-start(s32[256]{0:T(256)} %param.9) | copy-start | bytes 3076
  9.8 2.8 %copy-start.3 = (f32[256]{0:T(256)S(1)}, f32[256]{0:T(256)}, u32[]{:S(2)}) copy-start(f32[256]{0:T(256)} %param.8) | copy-start | bytes 3076
  9.8 16.5 %collective-permute-start.1 = (f32[176,256]{1,0:T(8,128)S(1)}, f32[176,256]{1,0:T(8,128)S(1)}, u32[]{:S(2)}, u32[]{:S(2)}) collective-permute-start(f32[176,256]{1,0:T(8,128)S(1)} %get-tuple-element.15.own), channel_id=1, source_target_pairs={{0,2},{2,4},{4,6},{6,8},{8,10},{10,12},{12,14},{14,16},{16,18},{18... | collective-permute-start | bytes 540680 | tf_op jit(solution)/shard_map/ppermute | solution.py:500
  11.1 15.2 %collective-permute-start.2 = (f32[200,128]{1,0:T(8,128)S(1)}, f32[200,128]{1,0:T(8,128)S(1)}, u32[]{:S(2)}, u32[]{:S(2)}) collective-permute-start(f32[200,128]{1,0:T(8,128)S(1)} %get-tuple-element.16), channel_id=1, source_target_pairs={{0,4},{2,6},{4,8},{6,10},{8,12},{10,14},{12,16},{14,18},{16,20},{1... | collective-permute-start | bytes 307208 | tf_op jit(solution)/shard_map/ppermute | solution.py:501
  25.1 12.1 %collective-permute-start.7 = (f32[176,256]{1,0:T(8,128)S(1)}, f32[176,256]{1,0:T(8,128)S(1)}, u32[]{:S(2)}, u32[]{:S(2)}) collective-permute-start(f32[176,256]{1,0:T(8,128)S(1)} %get-tuple-element.25.own), channel_id=1, source_target_pairs={{0,2},{2,4},{4,6},{6,8},{8,10},{10,12},{12,14},{14,16},{16,18},{18... | collective-permute-start | bytes 540680 | tf_op jit(solution)/shard_map/ppermute | solution.py:500
  26.3 11.0 %collective-permute-start.8 = (f32[200,128]{1,0:T(8,128)S(1)}, f32[200,128]{1,0:T(8,128)S(1)}, u32[]{:S(2)}, u32[]{:S(2)}) collective-permute-start(f32[200,128]{1,0:T(8,128)S(1)} %get-tuple-element.26), channel_id=1, source_target_pairs={{0,4},{2,6},{4,8},{6,10},{8,12},{10,14},{12,16},{14,18},{16,20},{1... | collective-permute-start | bytes 307208 | tf_op jit(solution)/shard_map/ppermute | solution.py:501
  34.8 9.7 %collective-permute-start.3 = (f32[176,256]{1,0:T(8,128)S(1)}, f32[176,256]{1,0:T(8,128)S(1)}, u32[]{:S(2)}, u32[]{:S(2)}) collective-permute-start(f32[176,256]{1,0:T(8,128)S(1)} %get-tuple-element.19.own), channel_id=1, source_target_pairs={{0,2},{2,4},{4,6},{6,8},{8,10},{10,12},{12,14},{14,16},{16,18},{18... | collective-permute-start | bytes 540680 | tf_op jit(solution)/shard_map/ppermute | solution.py:500
  35.2 9.3 %collective-permute-start.4 = (f32[200,128]{1,0:T(8,128)S(1)}, f32[200,128]{1,0:T(8,128)S(1)}, u32[]{:S(2)}, u32[]{:S(2)}) collective-permute-start(f32[200,128]{1,0:T(8,128)S(1)} %get-tuple-element.20), channel_id=1, source_target_pairs={{0,4},{2,6},{4,8},{6,10},{8,12},{10,14},{12,16},{14,18},{16,20},{1... | collective-permute-start | bytes 307208 | tf_op jit(solution)/shard_map/ppermute | solution.py:501

commit v11 on v10

--- a/solution.py
+++ b/solution.py
@@ -16,8 +16,9 @@
 HALF = LANES // 2
 SLOTS = 2 * SUB
 EXTRA = 2 * SUB
-TALL = 32
-ROWS = 4
+DEALT = 32
+TALL = 40
+ROWS = 8
 PICKS = 4
 VMEM_LIMIT = 32 * 1024 * 1024
 EDGE_LIMIT = 60 * 1024 * 1024
@@ -227,14 +228,14 @@
 
     def rows_of(self, k):
         start = EXTRA - REACH + self.n * k
-        return slice(start, start + TALL)
+        return slice(start, start + DEALT)
 
 
 def table_kernel(plans, place, side, rotation, shifts, *rest):
     outs, held = rest[:-1], rest[-1]
     lane = lax.broadcasted_iota(jnp.int32, (SUB, LANES), 1)
     sublane = lax.broadcasted_iota(jnp.int32, (SUB, LANES), 0)
-    front = lax.broadcasted_iota(jnp.int32, (TALL, LANES), 1) < HALF
+    front = lax.broadcasted_iota(jnp.int32, (DEALT, LANES), 1) < HALF
     more = side[0, :, LANES : 2 * LANES]
     for which, (n, radius, own_cells, total, spare, moved) in enumerate(plans):
         spin, pick = outs[2 * which : 2 * which + 2]
@@ -249,8 +250,8 @@
         bound = jnp.zeros((SUB, LANES), jnp.int32)
         for j in range(SUB):
             low, high = blocks.rows_of(j), blocks.rows_of(SUB + j)
-            spin[pl.ds(j, TALL, stride=SUB), :] = jnp.where(front, held[0, low, :], held[0, high, :])
-            pick[pl.ds(j, TALL, stride=SUB), :] = jnp.where(front, held[1, low, :], held[1, high, :]).astype(jnp.int32)
+            spin[pl.ds(j, DEALT, stride=SUB), :] = jnp.where(front, held[0, low, :], held[0, high, :])
+            pick[pl.ds(j, DEALT, stride=SUB), :] = jnp.where(front, held[1, low, :], held[1, high, :]).astype(jnp.int32)
             bound = jnp.where(sublane == j, jnp.where(lane < HALF, blocks.bounds[j], blocks.bounds[SUB + j]), bound)
 
         def one(i, _):
@@ -303,14 +304,14 @@
 
     lax.fori_loop(0, FIELDS, gather, 0)
 
-    front = lax.broadcasted_iota(jnp.int32, (TALL, LANES), 1) < HALF
+    front = lax.broadcasted_iota(jnp.int32, (DEALT, LANES), 1) < HALF
 
     def deal(f, _):
         for j in range(SUB):
             low, high = j, SUB + j
             turn_low = (LANES - (2 * own_cells - REACH)) + blocks.bounds[low]
             turn_high = (HALF - (2 * own_cells - REACH)) + blocks.bounds[high]
-            stages[0, f, pl.ds(j, TALL, stride=SUB), :] = jnp.where(
+            stages[0, f, pl.ds(j, DEALT, stride=SUB), :] = jnp.where(
                 front,
                 pltpu.roll(cells[f, blocks.rows_of(low), :], turn_low, 1),
                 pltpu.roll(cells[f, blocks.rows_of(high), :], turn_high, 1),

time: 53.1 us -> 47.5 us (0.89)
  Pallas kernels: 35 us -> 28.4 us
  waiting for transfers between devices: 5.26 us -> 5.96 us
    pallas_call x2, Pallas kernels: 15.3 us -> 11.9 us  [last_step(): pl.pallas_call(kernel, out_shape=out_shape, in_specs=[smem] + [vmem] * (5...]
    pallas_call x2, Pallas kernels: 17 us -> 13.8 us  [first_step(): pl.pallas_call(kernel, out_shape=[f32(FIELDS * own_cells + EXTRA, radius)...]
    ppermute x4, waiting for transfers between devices: 3.14 us -> 3.85 us  [body(): lax.ppermute(x, 'phi', [(p, (p + 2) % phi_count) for p in range(phi_count)])]
  transfers between devices with their start and end apart: 9 -> 9, of which waited for: 2 -> 3; matrix products, arithmetic and copies ran while one was open for 0% -> 0% of each run, Pallas kernels for 48% -> 43%
where the time goes in v11:
time: 47.5 us; the launch traced here: 46.7 us
  Pallas kernels  28.4 us (60%)
  starting transfers between devices  11.5 us (24%)
  waiting for transfers between devices  5.96 us (13%)
  between operations  0.72 us (2%)
    pallas_call x2, Pallas kernels, first_step(): pl.pallas_call(kernel, out_shape=[f32(FIELDS * own_cells + EXTRA, radius)...  13.8 us
    pallas_call x2, Pallas kernels, last_step(): pl.pallas_call(kernel, out_shape=out_shape, in_specs=[smem] + [vmem] * (5...  11.9 us
    ppermute x4, starting transfers between devices, body(): lax.ppermute(x, 'phi', [(p, (p + 2) % phi_count) for p in range(phi_count)])  5.67 us
    ppermute x4, waiting for transfers between devices, body(): lax.ppermute(x, 'phi', [(p, (p + 2) % phi_count) for p in range(phi_count)])  3.85 us
    ppermute x1, starting transfers between devices, body(): send_side = lambda x: lax.ppermute(x, 'row', [(0, 1), (1, 0)])  3 us
    ppermute x4, starting transfers between devices, body(): lax.ppermute(x, 'phi', [(p, (p + 1) % phi_count) for p in range(phi_count)])  2.86 us
    ppermute x1, waiting for transfers between devices, body(): send_side = lambda x: lax.ppermute(x, 'row', [(0, 1), (1, 0)])  2.1 us
    pallas_call x1, Pallas kernels, body(): pl.pallas_call(edge_kernel, out_shape=f32(levels, EXTRA, 2 * LANES), in_s...  1.74 us
  transfers between devices with their start and end apart: 9, of which 3 were waited for; matrix products, arithmetic and copies ran while one was open for 0% of the time, Pallas kernels for 43%

profile of v11, /device:TPU:0, one launch (start us, length us, event | category | flops | bytes accessed | tf_op | source)
XLA Modules:
  0.0 46.7 jit_solution(17104063334056540962)
XLA Ops:
  0.7 1.7 %edges.1 = f32[2,16,256]{2,1,0:T(8,128)} custom-call(s32[1]{0:T(128)} %bitcast.place.refs_0_, f32[2,32,256]{2,1,0:T(8,128)} %refs_0_.1, f32[2,2,32,256]{3,2,1,0:T(8,128)} %refs_1_.1, f32[2,2,32,256]{3,2,1,0:T(8,128)} %refs_2_.1, f32[2,128]{1,0:T(2,128)} %bitcast.3, s32[2,128]{1,0:T(2,128)} %bitcast.5), custom_call_target="tpu_custom_call" | custom-call | tf_op jit(solution)/shard_map/edges/pallas_call | solution.py:508
  2.4 3.0 %collective-permute-start = (f32[2,16,256]{2,1,0:T(8,128)}, f32[2,16,256]{2,1,0:T(8,128)S(1)}, u32[]{:S(2)}, u32[]{:S(2)}) collective-permute-start(f32[2,16,256]{2,1,0:T(8,128)} %edges.1), channel_id=1, source_target_pairs={{0,1},{1,0},{2,3},{3,2},{4,5},{5,4},{6,7},{7,6},{8,9},{9,8},{10,11... | collective-permute-start | bytes 98312 | tf_op jit(solution)/shard_map/ppermute | solution.py:503
  5.4 2.1 %collective-permute-done.refs_3_.refs_1_ = f32[2,16,256]{2,1,0:T(8,128)S(1)} collective-permute-done((f32[2,16,256]{2,1,0:T(8,128)}, f32[2,16,256]{2,1,0:T(8,128)S(1)}, u32[]{:S(2)}, u32[]{:S(2)}) %collective-permute-start) | collective-permute-done | bytes 32800 | tf_op jit(solution)/shard_map/ppermute | solution.py:503
  7.5 0.1 pack.1
  7.6 0.1 collective-permute-start.5
  7.7 2.1 %collective-permute-start.6 = (f32[200,128]{1,0:T(8,128)S(1)}, f32[200,128]{1,0:T(8,128)S(1)}, u32[]{:S(2)}, u32[]{:S(2)}) collective-permute-start(f32[200,128]{1,0:T(8,128)S(1)} %get-tuple-element.24), channel_id=1, source_target_pairs={{0,4},{2,6},{4,8},{6,10},{8,12},{10,14},{12,16},{14,18},{16,20},{1... | collective-permute-start | bytes 307208 | tf_op jit(solution)/shard_map/ppermute | solution.py:502
  9.8 1.3 %collective-permute-start.1 = (f32[176,256]{1,0:T(8,128)S(1)}, f32[176,256]{1,0:T(8,128)S(1)}, u32[]{:S(2)}, u32[]{:S(2)}) collective-permute-start(f32[176,256]{1,0:T(8,128)S(1)} %get-tuple-element.15.own), channel_id=1, source_target_pairs={{0,2},{2,4},{4,6},{6,8},{8,10},{10,12},{12,14},{14,16},{16,18},{18... | collective-permute-start | bytes 540680 | tf_op jit(solution)/shard_map/ppermute | solution.py:501
  11.1 1.5 %collective-permute-start.2 = (f32[200,128]{1,0:T(8,128)S(1)}, f32[200,128]{1,0:T(8,128)S(1)}, u32[]{:S(2)}, u32[]{:S(2)}) collective-permute-start(f32[200,128]{1,0:T(8,128)S(1)} %get-tuple-element.16), channel_id=1, source_target_pairs={{0,4},{2,6},{4,8},{6,10},{8,12},{10,14},{12,16},{14,18},{16,20},{1... | collective-permute-start | bytes 307208 | tf_op jit(solution)/shard_map/ppermute | solution.py:502
  12.6 0.9 %tables.1 = (f32[320,128]{1,0:T(8,128)S(1)}, s32[320,128]{1,0:T(8,128)S(1)}, f32[320,128]{1,0:T(8,128)S(1)}, s32[320,128]{1,0:T(8,128)S(1)}) custom-call(s32[1]{0:T(128)} %bitcast.place.refs_0_, f32[2,16,256]{2,1,0:T(8,128)S(1)} %collective-permute-done.refs_3_.refs_1_, f32[2,128]{1,0:T(2,128)S(1)} %bitcast.4, s32[2,128]{1,0:T(2,128)S(1)} %bitcast.6), custom_call_target="tpu_custom_call" | custom-call | tf_op jit(solution)/shard_map/tables/pallas_call | solution.py:536
  13.5 3.0 %collective-permute-done.6.far = f32[200,128]{1,0:T(8,128)S(1)} collective-permute-done((f32[200,128]{1,0:T(8,128)S(1)}, f32[200,128]{1,0:T(8,128)S(1)}, u32[]{:S(2)}, u32[]{:S(2)}) %collective-permute-start.6) | collective-permute-done | bytes 102432 | tf_op jit(solution)/shard_map/ppermute | solution.py:502
  16.6 0.0 collective-permute-done.5.near
  16.6 6.9 %first_step.3 = (f32[176,256]{1,0:T(8,128)S(1)}, f32[200,128]{1,0:T(8,128)S(1)}) custom-call(s32[1]{0:T(128)} %bitcast.place.refs_0_, f32[176,256]{1,0:T(8,128)S(1)} %get-tuple-element.23.own, f32[176,256]{1,0:T(8,128)S(1)} %collective-permute-done.5.near, f32[200,128]{1,0:T(8,128)S(1)} %collective-permute-done.6.far, ...), custom_call_target="tpu_custom_call" | custom-call | flops 8999999488 | bytes 29000000 | tf_op jit(solution)/shard_map/first_step/pallas_call | solution.py:433
  23.5 1.2 %collective-permute-start.7 = (f32[176,256]{1,0:T(8,128)S(1)}, f32[176,256]{1,0:T(8,128)S(1)}, u32[]{:S(2)}, u32[]{:S(2)}) collective-permute-start(f32[176,256]{1,0:T(8,128)S(1)} %get-tuple-element.25.own), channel_id=1, source_target_pairs={{0,2},{2,4},{4,6},{6,8},{8,10},{10,12},{12,14},{14,16},{16,18},{18... | collective-permute-start | bytes 540680 | tf_op jit(solution)/shard_map/ppermute | solution.py:501
  24.6 0.0 collective-permute-start.8
  24.6 0.0 collective-permute-done.2.far
  24.6 6.9 %first_step.2 = (f32[176,256]{1,0:T(8,128)S(1)}, f32[200,128]{1,0:T(8,128)S(1)}) custom-call(s32[1]{0:T(128)} %bitcast.place.refs_0_, f32[176,256]{1,0:T(8,128)S(1)} %get-tuple-element.15.own, f32[176,256]{1,0:T(8,128)S(1)} %collective-permute-done.1.near, f32[200,128]{1,0:T(8,128)S(1)} %collective-permute-done.2.far, ...), custom_call_target="tpu_custom_call" | custom-call | flops 8999999488 | bytes 29000000 | tf_op jit(solution)/shard_map/first_step/pallas_call | solution.py:433
  31.5 0.4 collective-permute-start.3
  31.9 2.1 %collective-permute-start.4 = (f32[200,128]{1,0:T(8,128)S(1)}, f32[200,128]{1,0:T(8,128)S(1)}, u32[]{:S(2)}, u32[]{:S(2)}) collective-permute-start(f32[200,128]{1,0:T(8,128)S(1)} %get-tuple-element.20), channel_id=1, source_target_pairs={{0,4},{2,6},{4,8},{6,10},{8,12},{10,14},{12,16},{14,18},{16,20},{1... | collective-permute-start | bytes 307208 | tf_op jit(solution)/shard_map/ppermute | solution.py:502
  33.9 0.0 collective-permute-done.8.far
  33.9 0.0 collective-permute-done.7.near
  34.0 5.6 %last_step.2.rest_0_ = f32[160,256]{1,0:T(8,128)S(1)} custom-call(s32[1]{0:T(128)} %bitcast.place.refs_0_, f32[176,256]{1,0:T(8,128)S(1)} %get-tuple-element.25.own, f32[176,256]{1,0:T(8,128)S(1)} %collective-permute-done.7.near, f32[200,128]{1,0:T(8,128)S(1)} %collective-permute-done.8.far, f32[320,128]{1,0:T(8,128)S(1)} %get-tuple-element.21.spin, ...), custom_call_target="tpu_custom_call" | custom-call | flops 8999999488 | bytes 29000000 | tf_op jit(solution)/shard_map/last_step/pallas_call | solution.py:475
  39.5 0.8 %collective-permute-done.4.far = f32[200,128]{1,0:T(8,128)S(1)} collective-permute-done((f32[200,128]{1,0:T(8,128)S(1)}, f32[200,128]{1,0:T(8,128)S(1)}, u32[]{:S(2)}, u32[]{:S(2)}) %collective-permute-start.4) | collective-permute-done | bytes 102432 | tf_op jit(solution)/shard_map/ppermute | solution.py:502
  40.3 0.0 collective-permute-done.3.near
  40.3 6.3 %last_step.3 = (f32[2,32,256]{2,1,0:T(8,128)}, f32[2,2,32,256]{3,2,1,0:T(8,128)}, f32[2,2,32,256]{3,2,1,0:T(8,128)}) custom-call(s32[1]{0:T(128)} %bitcast.place.refs_0_, f32[176,256]{1,0:T(8,128)S(1)} %get-tuple-element.19.own, f32[176,256]{1,0:T(8,128)S(1)} %collective-permute-done.3.near, f32[200,128]{1,0:T(8,128)S(1)} %collective-permute-done.4.far, ...), custom_call_target="tpu_custom_call" | custom-call | flops 8999999488 | bytes 29000000 | tf_op jit(solution)/shard_map/last_step/pallas_call | solution.py:475
  (11 shorter events, 0.0 us)
Async XLA Ops:
  0.6 6.9 %copy-start = (f32[2,2,32,256]{3,2,1,0:T(8,128)S(1)}, f32[2,2,32,256]{3,2,1,0:T(8,128)}, u32[]{:S(2)}) copy-start(f32[2,2,32,256]{3,2,1,0:T(8,128)} %refs_1_.1) | copy-start | bytes 393220
  0.6 6.9 %copy-start.1 = (f32[2,2,32,256]{3,2,1,0:T(8,128)S(1)}, f32[2,2,32,256]{3,2,1,0:T(8,128)}, u32[]{:S(2)}) copy-start(f32[2,2,32,256]{3,2,1,0:T(8,128)} %refs_2_.1) | copy-start | bytes 393220
  0.7 6.9 %copy-start.2 = (f32[2,32,256]{2,1,0:T(8,128)S(1)}, f32[2,32,256]{2,1,0:T(8,128)}, u32[]{:S(2)}) copy-start(f32[2,32,256]{2,1,0:T(8,128)} %refs_0_.1) | copy-start | bytes 196612
  2.4 5.1 %collective-permute-start = (f32[2,16,256]{2,1,0:T(8,128)}, f32[2,16,256]{2,1,0:T(8,128)S(1)}, u32[]{:S(2)}, u32[]{:S(2)}) collective-permute-start(f32[2,16,256]{2,1,0:T(8,128)} %edges.1), channel_id=1, source_target_pairs={{0,1},{1,0},{2,3},{3,2},{4,5},{5,4},{6,7},{7,6},{8,9},{9,8},{10,11... | collective-permute-start | bytes 98312 | tf_op jit(solution)/shard_map/ppermute | solution.py:503
  7.6 8.9 %collective-permute-start.5 = (f32[176,256]{1,0:T(8,128)S(1)}, f32[176,256]{1,0:T(8,128)S(1)}, u32[]{:S(2)}, u32[]{:S(2)}) collective-permute-start(f32[176,256]{1,0:T(8,128)S(1)} %get-tuple-element.23.own), channel_id=1, source_target_pairs={{0,2},{2,4},{4,6},{6,8},{8,10},{10,12},{12,14},{14,16},{16,18},{18... | collective-permute-start | bytes 540680 | tf_op jit(solution)/shard_map/ppermute | solution.py:501
  7.7 8.9 %collective-permute-start.6 = (f32[200,128]{1,0:T(8,128)S(1)}, f32[200,128]{1,0:T(8,128)S(1)}, u32[]{:S(2)}, u32[]{:S(2)}) collective-permute-start(f32[200,128]{1,0:T(8,128)S(1)} %get-tuple-element.24), channel_id=1, source_target_pairs={{0,4},{2,6},{4,8},{6,10},{8,12},{10,14},{12,16},{14,18},{16,20},{1... | collective-permute-start | bytes 307208 | tf_op jit(solution)/shard_map/ppermute | solution.py:502
  9.8 2.8 %copy-start.4 = (s32[256]{0:T(256)S(1)}, s32[256]{0:T(256)}, u32[]{:S(2)}) copy-start(s32[256]{0:T(256)} %param.9) | copy-start | bytes 3076
  9.8 2.8 %copy-start.3 = (f32[256]{0:T(256)S(1)}, f32[256]{0:T(256)}, u32[]{:S(2)}) copy-start(f32[256]{0:T(256)} %param.8) | copy-start | bytes 3076
  9.8 14.8 %collective-permute-start.1 = (f32[176,256]{1,0:T(8,128)S(1)}, f32[176,256]{1,0:T(8,128)S(1)}, u32[]{:S(2)}, u32[]{:S(2)}) collective-permute-start(f32[176,256]{1,0:T(8,128)S(1)} %get-tuple-element.15.own), channel_id=1, source_target_pairs={{0,2},{2,4},{4,6},{6,8},{8,10},{10,12},{12,14},{14,16},{16,18},{18... | collective-permute-start | bytes 540680 | tf_op jit(solution)/shard_map/ppermute | solution.py:501
  11.1 13.5 %collective-permute-start.2 = (f32[200,128]{1,0:T(8,128)S(1)}, f32[200,128]{1,0:T(8,128)S(1)}, u32[]{:S(2)}, u32[]{:S(2)}) collective-permute-start(f32[200,128]{1,0:T(8,128)S(1)} %get-tuple-element.16), channel_id=1, source_target_pairs={{0,4},{2,6},{4,8},{6,10},{8,12},{10,14},{12,16},{14,18},{16,20},{1... | collective-permute-start | bytes 307208 | tf_op jit(solution)/shard_map/ppermute | solution.py:502
  23.5 10.5 %collective-permute-start.7 = (f32[176,256]{1,0:T(8,128)S(1)}, f32[176,256]{1,0:T(8,128)S(1)}, u32[]{:S(2)}, u32[]{:S(2)}) collective-permute-start(f32[176,256]{1,0:T(8,128)S(1)} %get-tuple-element.25.own), channel_id=1, source_target_pairs={{0,2},{2,4},{4,6},{6,8},{8,10},{10,12},{12,14},{14,16},{16,18},{18... | collective-permute-start | bytes 540680 | tf_op jit(solution)/shard_map/ppermute | solution.py:501
  24.6 9.3 %collective-permute-start.8 = (f32[200,128]{1,0:T(8,128)S(1)}, f32[200,128]{1,0:T(8,128)S(1)}, u32[]{:S(2)}, u32[]{:S(2)}) collective-permute-start(f32[200,128]{1,0:T(8,128)S(1)} %get-tuple-element.26), channel_id=1, source_target_pairs={{0,4},{2,6},{4,8},{6,10},{8,12},{10,14},{12,16},{14,18},{16,20},{1... | collective-permute-start | bytes 307208 | tf_op jit(solution)/shard_map/ppermute | solution.py:502
  31.5 8.8 %collective-permute-start.3 = (f32[176,256]{1,0:T(8,128)S(1)}, f32[176,256]{1,0:T(8,128)S(1)}, u32[]{:S(2)}, u32[]{:S(2)}) collective-permute-start(f32[176,256]{1,0:T(8,128)S(1)} %get-tuple-element.19.own), channel_id=1, source_target_pairs={{0,2},{2,4},{4,6},{6,8},{8,10},{10,12},{12,14},{14,16},{16,18},{18... | collective-permute-start | bytes 540680 | tf_op jit(solution)/shard_map/ppermute | solution.py:501
  31.9 8.4 %collective-permute-start.4 = (f32[200,128]{1,0:T(8,128)S(1)}, f32[200,128]{1,0:T(8,128)S(1)}, u32[]{:S(2)}, u32[]{:S(2)}) collective-permute-start(f32[200,128]{1,0:T(8,128)S(1)} %get-tuple-element.20), channel_id=1, source_target_pairs={{0,4},{2,6},{4,8},{6,10},{8,12},{10,14},{12,16},{14,18},{16,20},{1... | collective-permute-start | bytes 307208 | tf_op jit(solution)/shard_map/ppermute | solution.py:502

commit v12 on v11

--- a/solution.py
+++ b/solution.py
@@ -100,15 +100,17 @@
         halves = [0.5 * x for x in rows]
         own = [x[SUB : SUB + size] for x in rows]
         half = [x[SUB : SUB + size] for x in halves]
-        after = [right_of(x) for x in half]
+        before_half = [left_of(x) for x in half]
+        after_half = [right_of(x) for x in half]
+        second_half = [pltpu.roll(x, LANES - 2, 1) for x in half]
         left, right = radial_states(halves, [x[SUB:-SUB] for x in rows])
-        jump = [x - y for x, y in zip(after, half)]
-        behind = [left_of(x) for x in jump]
         of_left = physical(left)
         of_right = physical(right)
-        slopes = [minmod(x, y) for x, y in zip(behind, jump)]
-        lower = [right_of(x - y) for x, y in zip(own, slopes)]
-        upper = [x + y for x, y in zip(own, slopes)]
+        behind = [x - y for x, y in zip(half, before_half)]
+        jump = [x - y for x, y in zip(after_half, half)]
+        ahead = [x - y for x, y in zip(second_half, after_half)]
+        upper = [x + minmod(p, q) for x, p, q in zip(own, behind, jump)]
+        lower = [(x + x) - minmod(p, q) for x, p, q in zip(after_half, jump, ahead)]
         of_upper = physical(upper)
         faces = swapped(face_twice(left, right, of_left, of_right))
         of_lower = physical(lower)

time: 47.5 us -> 47.6 us (level)
  no operation moved by 1% of the time
where the time goes in v12:
time: 47.6 us; the launch traced here: 46.8 us
  Pallas kernels  28.7 us (60%)
  starting transfers between devices  11.5 us (24%)
  waiting for transfers between devices  5.79 us (12%)
  between operations  0.72 us (2%)
    pallas_call x2, Pallas kernels, first_step(): pl.pallas_call(kernel, out_shape=[f32(FIELDS * own_cells + EXTRA, radius)...  13.7 us
    pallas_call x2, Pallas kernels, last_step(): pl.pallas_call(kernel, out_shape=out_shape, in_specs=[smem] + [vmem] * (5...  12.3 us
    ppermute x4, starting transfers between devices, body(): lax.ppermute(x, 'phi', [(p, (p + 2) % phi_count) for p in range(phi_count)])  5.67 us
    ppermute x4, waiting for transfers between devices, body(): lax.ppermute(x, 'phi', [(p, (p + 2) % phi_count) for p in range(phi_count)])  3.67 us
    ppermute x1, starting transfers between devices, body(): send_side = lambda x: lax.ppermute(x, 'row', [(0, 1), (1, 0)])  3 us
    ppermute x4, starting transfers between devices, body(): lax.ppermute(x, 'phi', [(p, (p + 1) % phi_count) for p in range(phi_count)])  2.86 us
    ppermute x1, waiting for transfers between devices, body(): send_side = lambda x: lax.ppermute(x, 'row', [(0, 1), (1, 0)])  2.1 us
    pallas_call x1, Pallas kernels, body(): pl.pallas_call(edge_kernel, out_shape=f32(levels, EXTRA, 2 * LANES), in_s...  1.74 us
  transfers between devices with their start and end apart: 9, of which 3 were waited for; matrix products, arithmetic and copies ran while one was open for 0% of the time, Pallas kernels for 43%

profile of v12, /device:TPU:0, one launch (start us, length us, event | category | flops | bytes accessed | tf_op | source)
XLA Modules:
  0.0 46.8 jit_solution(4833611646083260409)
XLA Ops:
  0.7 1.7 %edges.1 = f32[2,16,256]{2,1,0:T(8,128)} custom-call(s32[1]{0:T(128)} %bitcast.place.refs_0_, f32[2,32,256]{2,1,0:T(8,128)} %refs_0_.1, f32[2,2,32,256]{3,2,1,0:T(8,128)} %refs_1_.1, f32[2,2,32,256]{3,2,1,0:T(8,128)} %refs_2_.1, f32[2,128]{1,0:T(2,128)} %bitcast.3, s32[2,128]{1,0:T(2,128)} %bitcast.5), custom_call_target="tpu_custom_call" | custom-call | tf_op jit(solution)/shard_map/edges/pallas_call | solution.py:510
  2.4 3.0 %collective-permute-start = (f32[2,16,256]{2,1,0:T(8,128)}, f32[2,16,256]{2,1,0:T(8,128)S(1)}, u32[]{:S(2)}, u32[]{:S(2)}) collective-permute-start(f32[2,16,256]{2,1,0:T(8,128)} %edges.1), channel_id=1, source_target_pairs={{0,1},{1,0},{2,3},{3,2},{4,5},{5,4},{6,7},{7,6},{8,9},{9,8},{10,11... | collective-permute-start | bytes 98312 | tf_op jit(solution)/shard_map/ppermute | solution.py:505
  5.4 2.1 %collective-permute-done.refs_3_.refs_1_ = f32[2,16,256]{2,1,0:T(8,128)S(1)} collective-permute-done((f32[2,16,256]{2,1,0:T(8,128)}, f32[2,16,256]{2,1,0:T(8,128)S(1)}, u32[]{:S(2)}, u32[]{:S(2)}) %collective-permute-start) | collective-permute-done | bytes 32800 | tf_op jit(solution)/shard_map/ppermute | solution.py:505
  7.5 0.1 pack.1
  7.6 0.1 collective-permute-start.5
  7.7 2.1 %collective-permute-start.6 = (f32[200,128]{1,0:T(8,128)S(1)}, f32[200,128]{1,0:T(8,128)S(1)}, u32[]{:S(2)}, u32[]{:S(2)}) collective-permute-start(f32[200,128]{1,0:T(8,128)S(1)} %get-tuple-element.24), channel_id=1, source_target_pairs={{0,4},{2,6},{4,8},{6,10},{8,12},{10,14},{12,16},{14,18},{16,20},{1... | collective-permute-start | bytes 307208 | tf_op jit(solution)/shard_map/ppermute | solution.py:504
  9.8 1.3 %collective-permute-start.1 = (f32[176,256]{1,0:T(8,128)S(1)}, f32[176,256]{1,0:T(8,128)S(1)}, u32[]{:S(2)}, u32[]{:S(2)}) collective-permute-start(f32[176,256]{1,0:T(8,128)S(1)} %get-tuple-element.15.own), channel_id=1, source_target_pairs={{0,2},{2,4},{4,6},{6,8},{8,10},{10,12},{12,14},{14,16},{16,18},{18... | collective-permute-start | bytes 540680 | tf_op jit(solution)/shard_map/ppermute | solution.py:503
  11.1 1.5 %collective-permute-start.2 = (f32[200,128]{1,0:T(8,128)S(1)}, f32[200,128]{1,0:T(8,128)S(1)}, u32[]{:S(2)}, u32[]{:S(2)}) collective-permute-start(f32[200,128]{1,0:T(8,128)S(1)} %get-tuple-element.16), channel_id=1, source_target_pairs={{0,4},{2,6},{4,8},{6,10},{8,12},{10,14},{12,16},{14,18},{16,20},{1... | collective-permute-start | bytes 307208 | tf_op jit(solution)/shard_map/ppermute | solution.py:504
  12.6 0.9 %tables.1 = (f32[320,128]{1,0:T(8,128)S(1)}, s32[320,128]{1,0:T(8,128)S(1)}, f32[320,128]{1,0:T(8,128)S(1)}, s32[320,128]{1,0:T(8,128)S(1)}) custom-call(s32[1]{0:T(128)} %bitcast.place.refs_0_, f32[2,16,256]{2,1,0:T(8,128)S(1)} %collective-permute-done.refs_3_.refs_1_, f32[2,128]{1,0:T(2,128)S(1)} %bitcast.4, s32[2,128]{1,0:T(2,128)S(1)} %bitcast.6), custom_call_target="tpu_custom_call" | custom-call | tf_op jit(solution)/shard_map/tables/pallas_call | solution.py:538
  13.5 3.0 %collective-permute-done.6.far = f32[200,128]{1,0:T(8,128)S(1)} collective-permute-done((f32[200,128]{1,0:T(8,128)S(1)}, f32[200,128]{1,0:T(8,128)S(1)}, u32[]{:S(2)}, u32[]{:S(2)}) %collective-permute-start.6) | collective-permute-done | bytes 102432 | tf_op jit(solution)/shard_map/ppermute | solution.py:504
  16.6 0.0 collective-permute-done.5.near
  16.6 6.8 %first_step.3 = (f32[176,256]{1,0:T(8,128)S(1)}, f32[200,128]{1,0:T(8,128)S(1)}) custom-call(s32[1]{0:T(128)} %bitcast.place.refs_0_, f32[176,256]{1,0:T(8,128)S(1)} %get-tuple-element.23.own, f32[176,256]{1,0:T(8,128)S(1)} %collective-permute-done.5.near, f32[200,128]{1,0:T(8,128)S(1)} %collective-permute-done.6.far, ...), custom_call_target="tpu_custom_call" | custom-call | flops 8999999488 | bytes 29000000 | tf_op jit(solution)/shard_map/first_step/pallas_call | solution.py:435
  23.4 1.2 %collective-permute-start.7 = (f32[176,256]{1,0:T(8,128)S(1)}, f32[176,256]{1,0:T(8,128)S(1)}, u32[]{:S(2)}, u32[]{:S(2)}) collective-permute-start(f32[176,256]{1,0:T(8,128)S(1)} %get-tuple-element.25.own), channel_id=1, source_target_pairs={{0,2},{2,4},{4,6},{6,8},{8,10},{10,12},{12,14},{14,16},{16,18},{18... | collective-permute-start | bytes 540680 | tf_op jit(solution)/shard_map/ppermute | solution.py:503
  24.6 0.0 collective-permute-start.8
  24.6 0.0 collective-permute-done.2.far
  24.6 0.0 collective-permute-done.1.near
  24.6 6.8 %first_step.2 = (f32[176,256]{1,0:T(8,128)S(1)}, f32[200,128]{1,0:T(8,128)S(1)}) custom-call(s32[1]{0:T(128)} %bitcast.place.refs_0_, f32[176,256]{1,0:T(8,128)S(1)} %get-tuple-element.15.own, f32[176,256]{1,0:T(8,128)S(1)} %collective-permute-done.1.near, f32[200,128]{1,0:T(8,128)S(1)} %collective-permute-done.2.far, ...), custom_call_target="tpu_custom_call" | custom-call | flops 8999999488 | bytes 29000000 | tf_op jit(solution)/shard_map/first_step/pallas_call | solution.py:435
  31.5 0.4 collective-permute-start.3
  31.8 2.1 %collective-permute-start.4 = (f32[200,128]{1,0:T(8,128)S(1)}, f32[200,128]{1,0:T(8,128)S(1)}, u32[]{:S(2)}, u32[]{:S(2)}) collective-permute-start(f32[200,128]{1,0:T(8,128)S(1)} %get-tuple-element.20), channel_id=1, source_target_pairs={{0,4},{2,6},{4,8},{6,10},{8,12},{10,14},{12,16},{14,18},{16,20},{1... | collective-permute-start | bytes 307208 | tf_op jit(solution)/shard_map/ppermute | solution.py:504
  33.9 0.0 collective-permute-done.8.far
  33.9 0.0 collective-permute-done.7.near
  33.9 5.8 %last_step.2.rest_0_ = f32[160,256]{1,0:T(8,128)S(1)} custom-call(s32[1]{0:T(128)} %bitcast.place.refs_0_, f32[176,256]{1,0:T(8,128)S(1)} %get-tuple-element.25.own, f32[176,256]{1,0:T(8,128)S(1)} %collective-permute-done.7.near, f32[200,128]{1,0:T(8,128)S(1)} %collective-permute-done.8.far, f32[320,128]{1,0:T(8,128)S(1)} %get-tuple-element.21.spin, ...), custom_call_target="tpu_custom_call" | custom-call | flops 8999999488 | bytes 29000000 | tf_op jit(solution)/shard_map/last_step/pallas_call | solution.py:477
  39.6 0.6 %collective-permute-done.4.far = f32[200,128]{1,0:T(8,128)S(1)} collective-permute-done((f32[200,128]{1,0:T(8,128)S(1)}, f32[200,128]{1,0:T(8,128)S(1)}, u32[]{:S(2)}, u32[]{:S(2)}) %collective-permute-start.4) | collective-permute-done | bytes 102432 | tf_op jit(solution)/shard_map/ppermute | solution.py:504
  40.3 6.5 %last_step.3 = (f32[2,32,256]{2,1,0:T(8,128)}, f32[2,2,32,256]{3,2,1,0:T(8,128)}, f32[2,2,32,256]{3,2,1,0:T(8,128)}) custom-call(s32[1]{0:T(128)} %bitcast.place.refs_0_, f32[176,256]{1,0:T(8,128)S(1)} %get-tuple-element.19.own, f32[176,256]{1,0:T(8,128)S(1)} %collective-permute-done.3.near, f32[200,128]{1,0:T(8,128)S(1)} %collective-permute-done.4.far, ...), custom_call_target="tpu_custom_call" | custom-call | flops 8999999488 | bytes 29000000 | tf_op jit(solution)/shard_map/last_step/pallas_call | solution.py:477
  (11 shorter events, 0.0 us)
Async XLA Ops:
  0.6 6.9 %copy-start = (f32[2,2,32,256]{3,2,1,0:T(8,128)S(1)}, f32[2,2,32,256]{3,2,1,0:T(8,128)}, u32[]{:S(2)}) copy-start(f32[2,2,32,256]{3,2,1,0:T(8,128)} %refs_1_.1) | copy-start | bytes 393220
  0.6 6.9 %copy-start.1 = (f32[2,2,32,256]{3,2,1,0:T(8,128)S(1)}, f32[2,2,32,256]{3,2,1,0:T(8,128)}, u32[]{:S(2)}) copy-start(f32[2,2,32,256]{3,2,1,0:T(8,128)} %refs_2_.1) | copy-start | bytes 393220
  0.7 6.9 %copy-start.2 = (f32[2,32,256]{2,1,0:T(8,128)S(1)}, f32[2,32,256]{2,1,0:T(8,128)}, u32[]{:S(2)}) copy-start(f32[2,32,256]{2,1,0:T(8,128)} %refs_0_.1) | copy-start | bytes 196612
  2.4 5.1 %collective-permute-start = (f32[2,16,256]{2,1,0:T(8,128)}, f32[2,16,256]{2,1,0:T(8,128)S(1)}, u32[]{:S(2)}, u32[]{:S(2)}) collective-permute-start(f32[2,16,256]{2,1,0:T(8,128)} %edges.1), channel_id=1, source_target_pairs={{0,1},{1,0},{2,3},{3,2},{4,5},{5,4},{6,7},{7,6},{8,9},{9,8},{10,11... | collective-permute-start | bytes 98312 | tf_op jit(solution)/shard_map/ppermute | solution.py:505
  7.6 8.9 %collective-permute-start.5 = (f32[176,256]{1,0:T(8,128)S(1)}, f32[176,256]{1,0:T(8,128)S(1)}, u32[]{:S(2)}, u32[]{:S(2)}) collective-permute-start(f32[176,256]{1,0:T(8,128)S(1)} %get-tuple-element.23.own), channel_id=1, source_target_pairs={{0,2},{2,4},{4,6},{6,8},{8,10},{10,12},{12,14},{14,16},{16,18},{18... | collective-permute-start | bytes 540680 | tf_op jit(solution)/shard_map/ppermute | solution.py:503
  7.7 8.9 %collective-permute-start.6 = (f32[200,128]{1,0:T(8,128)S(1)}, f32[200,128]{1,0:T(8,128)S(1)}, u32[]{:S(2)}, u32[]{:S(2)}) collective-permute-start(f32[200,128]{1,0:T(8,128)S(1)} %get-tuple-element.24), channel_id=1, source_target_pairs={{0,4},{2,6},{4,8},{6,10},{8,12},{10,14},{12,16},{14,18},{16,20},{1... | collective-permute-start | bytes 307208 | tf_op jit(solution)/shard_map/ppermute | solution.py:504
  9.8 2.8 %copy-start.4 = (s32[256]{0:T(256)S(1)}, s32[256]{0:T(256)}, u32[]{:S(2)}) copy-start(s32[256]{0:T(256)} %param.9) | copy-start | bytes 3076
  9.8 2.8 %copy-start.3 = (f32[256]{0:T(256)S(1)}, f32[256]{0:T(256)}, u32[]{:S(2)}) copy-start(f32[256]{0:T(256)} %param.8) | copy-start | bytes 3076
  9.8 14.8 %collective-permute-start.1 = (f32[176,256]{1,0:T(8,128)S(1)}, f32[176,256]{1,0:T(8,128)S(1)}, u32[]{:S(2)}, u32[]{:S(2)}) collective-permute-start(f32[176,256]{1,0:T(8,128)S(1)} %get-tuple-element.15.own), channel_id=1, source_target_pairs={{0,2},{2,4},{4,6},{6,8},{8,10},{10,12},{12,14},{14,16},{16,18},{18... | collective-permute-start | bytes 540680 | tf_op jit(solution)/shard_map/ppermute | solution.py:503
  11.1 13.5 %collective-permute-start.2 = (f32[200,128]{1,0:T(8,128)S(1)}, f32[200,128]{1,0:T(8,128)S(1)}, u32[]{:S(2)}, u32[]{:S(2)}) collective-permute-start(f32[200,128]{1,0:T(8,128)S(1)} %get-tuple-element.16), channel_id=1, source_target_pairs={{0,4},{2,6},{4,8},{6,10},{8,12},{10,14},{12,16},{14,18},{16,20},{1... | collective-permute-start | bytes 307208 | tf_op jit(solution)/shard_map/ppermute | solution.py:504
  23.4 10.4 %collective-permute-start.7 = (f32[176,256]{1,0:T(8,128)S(1)}, f32[176,256]{1,0:T(8,128)S(1)}, u32[]{:S(2)}, u32[]{:S(2)}) collective-permute-start(f32[176,256]{1,0:T(8,128)S(1)} %get-tuple-element.25.own), channel_id=1, source_target_pairs={{0,2},{2,4},{4,6},{6,8},{8,10},{10,12},{12,14},{14,16},{16,18},{18... | collective-permute-start | bytes 540680 | tf_op jit(solution)/shard_map/ppermute | solution.py:503
  24.6 9.3 %collective-permute-start.8 = (f32[200,128]{1,0:T(8,128)S(1)}, f32[200,128]{1,0:T(8,128)S(1)}, u32[]{:S(2)}, u32[]{:S(2)}) collective-permute-start(f32[200,128]{1,0:T(8,128)S(1)} %get-tuple-element.26), channel_id=1, source_target_pairs={{0,4},{2,6},{4,8},{6,10},{8,12},{10,14},{12,16},{14,18},{16,20},{1... | collective-permute-start | bytes 307208 | tf_op jit(solution)/shard_map/ppermute | solution.py:504
  31.5 8.8 %collective-permute-start.3 = (f32[176,256]{1,0:T(8,128)S(1)}, f32[176,256]{1,0:T(8,128)S(1)}, u32[]{:S(2)}, u32[]{:S(2)}) collective-permute-start(f32[176,256]{1,0:T(8,128)S(1)} %get-tuple-element.19.own), channel_id=1, source_target_pairs={{0,2},{2,4},{4,6},{6,8},{8,10},{10,12},{12,14},{14,16},{16,18},{18... | collective-permute-start | bytes 540680 | tf_op jit(solution)/shard_map/ppermute | solution.py:503
  31.8 8.4 %collective-permute-start.4 = (f32[200,128]{1,0:T(8,128)S(1)}, f32[200,128]{1,0:T(8,128)S(1)}, u32[]{:S(2)}, u32[]{:S(2)}) collective-permute-start(f32[200,128]{1,0:T(8,128)S(1)} %get-tuple-element.20), channel_id=1, source_target_pairs={{0,4},{2,6},{4,8},{6,10},{8,12},{10,14},{12,16},{14,18},{16,20},{1... | collective-permute-start | bytes 307208 | tf_op jit(solution)/shard_map/ppermute | solution.py:504

commit v13 on v11

--- a/solution.py
+++ b/solution.py
@@ -206,14 +206,14 @@
             edge[level, :, side * LANES : (side + 1) * LANES] = jnp.where(on_low, turned[LANES - EXTRA :], turned[0:EXTRA])
 
 
-def pack_kernel(spare, levels, density, momentum, magnetic, side, *outs):
+def pack_kernel(spare, levels, density, momentum, magnetic, edge, *outs):
+    del edge
     nears, fars = outs[:levels], outs[levels:]
     own_cells = density.shape[1]
     for level in range(levels):
         sources = [density.at[level]] + [x.at[k, level] for x in (momentum, magnetic) for k in range(2)]
         for f, x in enumerate(sources):
             nears[level][f * own_cells : (f + 1) * own_cells, :] = x[...]
-        nears[level][FIELDS * own_cells :, :] = side[level]
         pack_far(fars[level], nears[level], own_cells, spare)
 
 
@@ -263,8 +263,7 @@
 
 def step_kernel(plan, refs, write, scratch):
     n, radius, own_cells, total, spare, moved = plan
-    place, own, near, far, spin, pick = refs
-    tail = slice(FIELDS * own_cells, FIELDS * own_cells + EXTRA)
+    place, own, own_edge, near, near_edge, far, spin, pick = refs
     cells, stages, packed = scratch
     row = place[0]
     lane = lax.broadcasted_iota(jnp.int32, (SUB, LANES), 1)
@@ -297,8 +296,8 @@
         lanes_at = lax.rem(f, 4) * own_cells
         cells[f, pl.ds(blocks.edge_at, EXTRA), :] = jnp.where(
             edge_lane < 2 * own_cells,
-            pltpu.roll(near[tail, columns], lax.rem(LANES + own_cells - lanes_at, LANES), 1),
-            pltpu.roll(own[tail, columns], lax.rem(LANES + 2 * own_cells - lanes_at, LANES), 1),
+            pltpu.roll(near_edge[:, columns], lax.rem(LANES + own_cells - lanes_at, LANES), 1),
+            pltpu.roll(own_edge[:, columns], lax.rem(LANES + 2 * own_cells - lanes_at, LANES), 1),
         )
         return 0
 
@@ -423,17 +422,17 @@
 cost = pl.CostEstimate(flops=9_000_000_000, bytes_accessed=29_000_000, transcendentals=0)
 
 
-def first_step(plan, operands):
+def first_step(plan, level, operands):
     n, radius, own_cells, total, spare, moved = plan
 
-    def kernel(place, own, near, far, spin, pick, near_out, far_out, *scratch):
-        refs = (place, own, near, far, spin, pick)
+    def kernel(place, own, near, far, side, corner, spin, pick, near_out, far_out, *scratch):
+        refs = (place, own, side.at[level], near, corner.at[level], far, spin, pick)
         step_kernel(plan, refs, ToMessage(near_out, far_out, own_cells, spare), scratch)
 
     return pl.pallas_call(
         kernel,
         out_shape=[f32(FIELDS * own_cells + EXTRA, radius), f32(FIELDS * (own_cells + SUB), LANES)],
-        in_specs=[smem] + [vmem] * 5,
+        in_specs=[smem] + [vmem] * 7,
         out_specs=[vmem] * 2,
         scratch_shapes=step_scratch(n),
         compiler_params=params,
@@ -445,10 +444,11 @@
 def last_step(plan, level, operands, done, levels):
     n, radius, own_cells, total, spare, moved = plan
     final = level == levels - 1
+    tail = pl.ds(FIELDS * own_cells, EXTRA)
     buffer = f32(FIELDS * own_cells, radius)
 
     def kernel(place, own, near, far, spin, pick, *rest):
-        refs = (place, own, near, far, spin, pick)
+        refs = (place, own, own.at[tail, :], near, near.at[tail, :], far, spin, pick)
         if not final:
             step_kernel(plan, refs, ToBuffer(rest[0]), rest[1:])
             return
@@ -503,7 +503,7 @@
     send_side = lambda x: lax.ppermute(x, "row", [(0, 1), (1, 0)])
 
     spins, turns = rotation.reshape(parts, LANES), shifts.reshape(parts, LANES)
-    near_message = f32(FIELDS * own_cells + EXTRA, radius)
+    near_message = f32(FIELDS * own_cells, radius)
     far_message = f32(FIELDS * (own_cells + SUB), LANES)
     edge = pl.pallas_call(
         edge_kernel,
@@ -519,17 +519,18 @@
         compiler_params=pltpu.CompilerParams(vmem_limit_bytes=EDGE_LIMIT),
         name="edges",
     )(place, density, momentum, magnetic, spins, turns)
-    side = send_side(edge)
     packed = pl.pallas_call(
         lambda *refs: pack_kernel(spare, levels, *refs),
         out_shape=[near_message] * levels + [far_message] * levels,
-        in_specs=[vmem] * 4,
+        in_specs=[vmem] * 3 + [pl.BlockSpec(memory_space=pl.ANY)],
         out_specs=[vmem] * (2 * levels),
         compiler_params=params,
         cost_estimate=cost,
         name="pack",
-    )(density, momentum, magnetic, side)
+    )(density, momentum, magnetic, edge)
     owns, fars = packed[:levels], packed[levels:]
+    side = send_side(edge)
+    corner = send_near(side)
     wide = (n + 1, radius, own_cells, total, spare, EXTRA)
     plain = (n, radius, own_cells, total, spare, 0)
     i32 = jax.ShapeDtypeStruct((TALL * SUB, LANES), jnp.int32)
@@ -542,11 +543,15 @@
         compiler_params=params,
         name="tables",
     )(place, side, spins, turns)
-    moved = [(send_near(own), send_far(far)) for own, far in zip(owns, fars)]
+    moved = []
+    for own, far in zip(owns, fars):
+        if moved:
+            own, far, _ = lax.optimization_barrier((own, far, tables[0]))
+        moved.append((send_near(own), send_far(far)))
     states = []
     for level in range(levels):
         near, far = moved[level]
-        states.append(first_step(wide, (place, owns[level], near, far, *tables[:2])))
+        states.append(first_step(wide, level, (place, owns[level], near, far, side, corner, *tables[:2])))
     moved = [(send_near(own), send_far(far)) for own, far in states]
     done = ()
     for level in range(levels):

time: 47.5 us -> 46.5 us (0.979); the launches traced: 46.7 us -> 46.2 us
  starting transfers between devices: 11.5 us -> 10.3 us
  local copies, waits for them, and re-layouts: 0.02 us -> 0.78 us
    ppermute x4, waiting for transfers between devices: 3.85 us -> 1.5 us  [body(): lax.ppermute(x, 'phi', [(p, (p + 2) % phi_count) for p in range(phi_count)])]
    ppermute x4 -> x5, waiting for transfers between devices: 0.01 us -> 1.92 us  [body(): lax.ppermute(x, 'phi', [(p, (p + 1) % phi_count) for p in range(phi_count)])]
    ppermute x1, starting transfers between devices: 3 us -> 1.49 us  [body(): send_side = lambda x: lax.ppermute(x, 'row', [(0, 1), (1, 0)])]
    unnamed x10 -> x12, local copies, waits for them, and re-layouts: 0.02 us -> 0.78 us
    ppermute x4 -> x5, starting transfers between devices: 2.86 us -> 3.27 us  [body(): lax.ppermute(x, 'phi', [(p, (p + 1) % phi_count) for p in range(phi_count)])]
  transfers between devices with their start and end apart: 9 -> 10, of which waited for: 3 -> 3; matrix products, arithmetic and copies ran while one was open for 0% -> 0% of each run, Pallas kernels for 43% -> 44%
where the time goes in v13:
time: 46.5 us; the launch traced here: 46.2 us
  Pallas kernels  28.5 us (61%)
  starting transfers between devices  10.3 us (22%)
  waiting for transfers between devices  5.88 us (13%)
  between operations  0.79 us (2%)
  local copies, waits for them, and re-layouts  0.78 us (2%)
    pallas_call x2, Pallas kernels, first_step(): pl.pallas_call(kernel, out_shape=[f32(FIELDS * own_cells + EXTRA, radius)...  13.8 us
    pallas_call x2, Pallas kernels, last_step(): pl.pallas_call(kernel, out_shape=out_shape, in_specs=[smem] + [vmem] * (5...  12 us
    ppermute x4, starting transfers between devices, body(): lax.ppermute(x, 'phi', [(p, (p + 2) % phi_count) for p in range(phi_count)])  5.58 us
    ppermute x5, starting transfers between devices, body(): lax.ppermute(x, 'phi', [(p, (p + 1) % phi_count) for p in range(phi_count)])  3.27 us
    ppermute x1, waiting for transfers between devices, body(): send_side = lambda x: lax.ppermute(x, 'row', [(0, 1), (1, 0)])  2.45 us
    ppermute x5, waiting for transfers between devices, body(): lax.ppermute(x, 'phi', [(p, (p + 1) % phi_count) for p in range(phi_count)])  1.92 us
    pallas_call x1, Pallas kernels, body(): pl.pallas_call(edge_kernel, out_shape=f32(levels, EXTRA, 2 * LANES), in_s...  1.74 us
    ppermute x4, waiting for transfers between devices, body(): lax.ppermute(x, 'phi', [(p, (p + 2) % phi_count) for p in range(phi_count)])  1.5 us
  transfers between devices with their start and end apart: 10, of which 3 were waited for; matrix products, arithmetic and copies ran while one was open for 0% of the time, Pallas kernels for 44%

profile of v13, /device:TPU:0, one launch (start us, length us, event | category | flops | bytes accessed | tf_op | source)
XLA Modules:
  0.0 46.2 jit_solution(13422069862477106329)
XLA Ops:
  0.7 1.7 %edges.1.refs_3_ = f32[2,16,256]{2,1,0:T(8,128)} custom-call(s32[1]{0:T(128)} %bitcast.place.refs_0_, f32[2,32,256]{2,1,0:T(8,128)} %refs_0_.1, f32[2,2,32,256]{3,2,1,0:T(8,128)} %refs_1_.1, f32[2,2,32,256]{3,2,1,0:T(8,128)} %refs_2_.1, f32[2,128]{1,0:T(2,128)} %bitcast.3, s32[2,128]{1,0:T(2,128)} %bitcast.5), custom_call_target="tpu_custom_call" | custom-call | tf_op jit(solution)/shard_map/edges/pallas_call | solution.py:508
  2.4 0.0 copy-start.3
  2.5 0.7 %copy-done.3 = f32[2,16,256]{2,1,0:T(8,128)S(1)} copy-done((f32[2,16,256]{2,1,0:T(8,128)S(1)}, f32[2,16,256]{2,1,0:T(8,128)}, u32[]{:S(2)}) %copy-start.3) | copy-done | bytes 32792
  3.2 0.1 pack.1
  3.3 0.0 copy-start.5
  3.3 0.0 copy-start.4
  3.3 0.5 %collective-permute-start.6 = (f32[160,256]{1,0:T(8,128)S(1)}, f32[160,256]{1,0:T(8,128)S(1)}, u32[]{:S(2)}, u32[]{:S(2)}) collective-permute-start(f32[160,256]{1,0:T(8,128)S(1)} %get-tuple-element.27.own), channel_id=1, source_target_pairs={{0,2},{2,4},{4,6},{6,8},{8,10},{10,12},{12,14},{14,16},{16,18},{18... | collective-permute-start | bytes 491528 | tf_op jit(solution)/shard_map/ppermute | solution.py:501
  3.8 2.6 %collective-permute-start.7 = (f32[200,128]{1,0:T(8,128)S(1)}, f32[200,128]{1,0:T(8,128)S(1)}, u32[]{:S(2)}, u32[]{:S(2)}) collective-permute-start(f32[200,128]{1,0:T(8,128)S(1)} %get-tuple-element.28), channel_id=1, source_target_pairs={{0,4},{2,6},{4,8},{6,10},{8,12},{10,14},{12,16},{14,18},{16,20},{1... | collective-permute-start | bytes 307208 | tf_op jit(solution)/shard_map/ppermute | solution.py:502
  6.4 1.5 %collective-permute-start = (f32[2,16,256]{2,1,0:T(8,128)S(1)}, f32[2,16,256]{2,1,0:T(8,128)S(1)}, u32[]{:S(2)}, u32[]{:S(2)}) collective-permute-start(f32[2,16,256]{2,1,0:T(8,128)S(1)} %copy-done.3), channel_id=1, source_target_pairs={{0,1},{1,0},{2,3},{3,2},{4,5},{5,4},{6,7},{7,6},{8,9},{9,8},{10,11... | collective-permute-start | bytes 98312 | tf_op jit(solution)/shard_map/ppermute | solution.py:503
  7.9 2.5 %collective-permute-done.refs_1_.side = f32[2,16,256]{2,1,0:T(8,128)S(1)} collective-permute-done((f32[2,16,256]{2,1,0:T(8,128)S(1)}, f32[2,16,256]{2,1,0:T(8,128)S(1)}, u32[]{:S(2)}, u32[]{:S(2)}) %collective-permute-start) | collective-permute-done | bytes 32800 | tf_op jit(solution)/shard_map/ppermute | solution.py:503
  10.4 0.4 collective-permute-start.3
  10.8 0.9 %tables.1 = (f32[320,128]{1,0:T(8,128)S(1)}, s32[320,128]{1,0:T(8,128)S(1)}, f32[320,128]{1,0:T(8,128)S(1)}, s32[320,128]{1,0:T(8,128)S(1)}) custom-call(s32[1]{0:T(128)} %bitcast.place.refs_0_, f32[2,16,256]{2,1,0:T(8,128)S(1)} %collective-permute-done.refs_1_.side, f32[2,128]{1,0:T(2,128)S(1)} %bitcast.4, s32[2,128]{1,0:T(2,128)S(1)} %bitcast.6), custom_call_target="tpu_custom_call" | custom-call | tf_op jit(solution)/shard_map/tables/pallas_call | solution.py:537
  11.7 1.2 %collective-permute-start.1 = (f32[160,256]{1,0:T(8,128)S(1)}, f32[160,256]{1,0:T(8,128)S(1)}, u32[]{:S(2)}, u32[]{:S(2)}) collective-permute-start(f32[160,256]{1,0:T(8,128)S(1)} %get-tuple-element.20.own), channel_id=1, source_target_pairs={{0,2},{2,4},{4,6},{6,8},{8,10},{10,12},{12,14},{14,16},{16,18},{18... | collective-permute-start | bytes 491528 | tf_op jit(solution)/shard_map/ppermute | solution.py:501
  13.0 1.5 %collective-permute-start.2 = (f32[200,128]{1,0:T(8,128)S(1)}, f32[200,128]{1,0:T(8,128)S(1)}, u32[]{:S(2)}, u32[]{:S(2)}) collective-permute-start(f32[200,128]{1,0:T(8,128)S(1)} %get-tuple-element.21), channel_id=1, source_target_pairs={{0,4},{2,6},{4,8},{6,10},{8,12},{10,14},{12,16},{14,18},{16,20},{1... | collective-permute-start | bytes 307208 | tf_op jit(solution)/shard_map/ppermute | solution.py:502
  14.5 1.9 %collective-permute-done.3.corner = f32[2,16,256]{2,1,0:T(8,128)S(1)} collective-permute-done((f32[2,16,256]{2,1,0:T(8,128)S(1)}, f32[2,16,256]{2,1,0:T(8,128)S(1)}, u32[]{:S(2)}, u32[]{:S(2)}) %collective-permute-start.3) | collective-permute-done | bytes 32800 | tf_op jit(solution)/shard_map/ppermute | solution.py:501
  16.4 6.9 %first_step.3 = (f32[176,256]{1,0:T(8,128)S(1)}, f32[200,128]{1,0:T(8,128)S(1)}) custom-call(s32[1]{0:T(128)} %bitcast.place.refs_0_, f32[160,256]{1,0:T(8,128)S(1)} %get-tuple-element.27.own, f32[160,256]{1,0:T(8,128)S(1)} %collective-permute-done.6.near, f32[200,128]{1,0:T(8,128)S(1)} %collective-permute-done.7.far, ...), custom_call_target="tpu_custom_call" | custom-call | flops 8999999488 | bytes 29000000 | tf_op jit(solution)/shard_map/first_step/pallas_call | solution.py:432
  23.3 0.1 collective-permute-start.8
  23.4 0.1 collective-permute-start.9
  23.4 6.9 %first_step.2 = (f32[176,256]{1,0:T(8,128)S(1)}, f32[200,128]{1,0:T(8,128)S(1)}) custom-call(s32[1]{0:T(128)} %bitcast.place.refs_0_, f32[160,256]{1,0:T(8,128)S(1)} %get-tuple-element.20.own, f32[160,256]{1,0:T(8,128)S(1)} %collective-permute-done.1.near, f32[200,128]{1,0:T(8,128)S(1)} %collective-permute-done.2.far, ...), custom_call_target="tpu_custom_call" | custom-call | flops 8999999488 | bytes 29000000 | tf_op jit(solution)/shard_map/first_step/pallas_call | solution.py:432
  30.3 1.0 %collective-permute-start.4 = (f32[176,256]{1,0:T(8,128)S(1)}, f32[176,256]{1,0:T(8,128)S(1)}, u32[]{:S(2)}, u32[]{:S(2)}) collective-permute-start(f32[176,256]{1,0:T(8,128)S(1)} %get-tuple-element.23.own), channel_id=1, source_target_pairs={{0,2},{2,4},{4,6},{6,8},{8,10},{10,12},{12,14},{14,16},{16,18},{18... | collective-permute-start | bytes 540680 | tf_op jit(solution)/shard_map/ppermute | solution.py:501
  31.4 1.4 %collective-permute-start.5 = (f32[200,128]{1,0:T(8,128)S(1)}, f32[200,128]{1,0:T(8,128)S(1)}, u32[]{:S(2)}, u32[]{:S(2)}) collective-permute-start(f32[200,128]{1,0:T(8,128)S(1)} %get-tuple-element.24), channel_id=1, source_target_pairs={{0,4},{2,6},{4,8},{6,10},{8,12},{10,14},{12,16},{14,18},{16,20},{1... | collective-permute-start | bytes 307208 | tf_op jit(solution)/shard_map/ppermute | solution.py:502
  32.8 5.6 %last_step.2.rest_0_ = f32[160,256]{1,0:T(8,128)S(1)} custom-call(s32[1]{0:T(128)} %bitcast.place.refs_0_, f32[176,256]{1,0:T(8,128)S(1)} %get-tuple-element.29.own, f32[176,256]{1,0:T(8,128)S(1)} %collective-permute-done.8.near, f32[200,128]{1,0:T(8,128)S(1)} %collective-permute-done.9.far, f32[320,128]{1,0:T(8,128)S(1)} %get-tuple-element.25.spin, ...), custom_call_target="tpu_custom_call" | custom-call | flops 8999999488 | bytes 29000000 | tf_op jit(solution)/shard_map/last_step/pallas_call | solution.py:475
  38.4 1.5 %collective-permute-done.5.far = f32[200,128]{1,0:T(8,128)S(1)} collective-permute-done((f32[200,128]{1,0:T(8,128)S(1)}, f32[200,128]{1,0:T(8,128)S(1)}, u32[]{:S(2)}, u32[]{:S(2)}) %collective-permute-start.5) | collective-permute-done | bytes 102432 | tf_op jit(solution)/shard_map/ppermute | solution.py:502
  39.9 6.4 %last_step.3 = (f32[2,32,256]{2,1,0:T(8,128)}, f32[2,2,32,256]{3,2,1,0:T(8,128)}, f32[2,2,32,256]{3,2,1,0:T(8,128)}) custom-call(s32[1]{0:T(128)} %bitcast.place.refs_0_, f32[176,256]{1,0:T(8,128)S(1)} %get-tuple-element.23.own, f32[176,256]{1,0:T(8,128)S(1)} %collective-permute-done.4.near, f32[200,128]{1,0:T(8,128)S(1)} %collective-permute-done.5.far, ...), custom_call_target="tpu_custom_call" | custom-call | flops 8999999488 | bytes 29000000 | tf_op jit(solution)/shard_map/last_step/pallas_call | solution.py:475
  (15 shorter events, 0.0 us)
Async XLA Ops:
  0.6 1.8 %copy-start = (f32[2,2,32,256]{3,2,1,0:T(8,128)S(1)}, f32[2,2,32,256]{3,2,1,0:T(8,128)}, u32[]{:S(2)}) copy-start(f32[2,2,32,256]{3,2,1,0:T(8,128)} %refs_1_.1) | copy-start | bytes 393220
  0.6 1.8 %copy-start.1 = (f32[2,2,32,256]{3,2,1,0:T(8,128)S(1)}, f32[2,2,32,256]{3,2,1,0:T(8,128)}, u32[]{:S(2)}) copy-start(f32[2,2,32,256]{3,2,1,0:T(8,128)} %refs_2_.1) | copy-start | bytes 393220
  0.7 1.8 %copy-start.2 = (f32[2,32,256]{2,1,0:T(8,128)S(1)}, f32[2,32,256]{2,1,0:T(8,128)}, u32[]{:S(2)}) copy-start(f32[2,32,256]{2,1,0:T(8,128)} %refs_0_.1) | copy-start | bytes 196612
  2.4 0.8 %copy-start.3 = (f32[2,16,256]{2,1,0:T(8,128)S(1)}, f32[2,16,256]{2,1,0:T(8,128)}, u32[]{:S(2)}) copy-start(f32[2,16,256]{2,1,0:T(8,128)} %edges.1.refs_3_) | copy-start | bytes 98308
  3.3 7.5 %copy-start.5 = (s32[256]{0:T(256)S(1)}, s32[256]{0:T(256)}, u32[]{:S(2)}) copy-start(s32[256]{0:T(256)} %param.9) | copy-start | bytes 3076
  3.3 7.5 %copy-start.4 = (f32[256]{0:T(256)S(1)}, f32[256]{0:T(256)}, u32[]{:S(2)}) copy-start(f32[256]{0:T(256)} %param.8) | copy-start | bytes 3076
  3.3 13.1 %collective-permute-start.6 = (f32[160,256]{1,0:T(8,128)S(1)}, f32[160,256]{1,0:T(8,128)S(1)}, u32[]{:S(2)}, u32[]{:S(2)}) collective-permute-start(f32[160,256]{1,0:T(8,128)S(1)} %get-tuple-element.27.own), channel_id=1, source_target_pairs={{0,2},{2,4},{4,6},{6,8},{8,10},{10,12},{12,14},{14,16},{16,18},{18... | collective-permute-start | bytes 491528 | tf_op jit(solution)/shard_map/ppermute | solution.py:501
  3.8 12.6 %collective-permute-start.7 = (f32[200,128]{1,0:T(8,128)S(1)}, f32[200,128]{1,0:T(8,128)S(1)}, u32[]{:S(2)}, u32[]{:S(2)}) collective-permute-start(f32[200,128]{1,0:T(8,128)S(1)} %get-tuple-element.28), channel_id=1, source_target_pairs={{0,4},{2,6},{4,8},{6,10},{8,12},{10,14},{12,16},{14,18},{16,20},{1... | collective-permute-start | bytes 307208 | tf_op jit(solution)/shard_map/ppermute | solution.py:502
  6.4 3.9 %collective-permute-start = (f32[2,16,256]{2,1,0:T(8,128)S(1)}, f32[2,16,256]{2,1,0:T(8,128)S(1)}, u32[]{:S(2)}, u32[]{:S(2)}) collective-permute-start(f32[2,16,256]{2,1,0:T(8,128)S(1)} %copy-done.3), channel_id=1, source_target_pairs={{0,1},{1,0},{2,3},{3,2},{4,5},{5,4},{6,7},{7,6},{8,9},{9,8},{10,11... | collective-permute-start | bytes 98312 | tf_op jit(solution)/shard_map/ppermute | solution.py:503
  10.4 6.0 %collective-permute-start.3 = (f32[2,16,256]{2,1,0:T(8,128)S(1)}, f32[2,16,256]{2,1,0:T(8,128)S(1)}, u32[]{:S(2)}, u32[]{:S(2)}) collective-permute-start(f32[2,16,256]{2,1,0:T(8,128)S(1)} %collective-permute-done.refs_1_.side), channel_id=1, source_target_pairs={{0,2},{2,4},{4,6},{6,8},{8,10},{10,12},{12,14},{14,16},{16,18},{18... | collective-permute-start | bytes 98312 | tf_op jit(solution)/shard_map/ppermute | solution.py:501
  11.7 11.7 %collective-permute-start.1 = (f32[160,256]{1,0:T(8,128)S(1)}, f32[160,256]{1,0:T(8,128)S(1)}, u32[]{:S(2)}, u32[]{:S(2)}) collective-permute-start(f32[160,256]{1,0:T(8,128)S(1)} %get-tuple-element.20.own), channel_id=1, source_target_pairs={{0,2},{2,4},{4,6},{6,8},{8,10},{10,12},{12,14},{14,16},{16,18},{18... | collective-permute-start | bytes 491528 | tf_op jit(solution)/shard_map/ppermute | solution.py:501
  13.0 10.5 %collective-permute-start.2 = (f32[200,128]{1,0:T(8,128)S(1)}, f32[200,128]{1,0:T(8,128)S(1)}, u32[]{:S(2)}, u32[]{:S(2)}) collective-permute-start(f32[200,128]{1,0:T(8,128)S(1)} %get-tuple-element.21), channel_id=1, source_target_pairs={{0,4},{2,6},{4,8},{6,10},{8,12},{10,14},{12,16},{14,18},{16,20},{1... | collective-permute-start | bytes 307208 | tf_op jit(solution)/shard_map/ppermute | solution.py:502
  23.3 9.5 %collective-permute-start.8 = (f32[176,256]{1,0:T(8,128)S(1)}, f32[176,256]{1,0:T(8,128)S(1)}, u32[]{:S(2)}, u32[]{:S(2)}) collective-permute-start(f32[176,256]{1,0:T(8,128)S(1)} %get-tuple-element.29.own), channel_id=1, source_target_pairs={{0,2},{2,4},{4,6},{6,8},{8,10},{10,12},{12,14},{14,16},{16,18},{18... | collective-permute-start | bytes 540680 | tf_op jit(solution)/shard_map/ppermute | solution.py:501
  23.4 9.4 %collective-permute-start.9 = (f32[200,128]{1,0:T(8,128)S(1)}, f32[200,128]{1,0:T(8,128)S(1)}, u32[]{:S(2)}, u32[]{:S(2)}) collective-permute-start(f32[200,128]{1,0:T(8,128)S(1)} %get-tuple-element.30), channel_id=1, source_target_pairs={{0,4},{2,6},{4,8},{6,10},{8,12},{10,14},{12,16},{14,18},{16,20},{1... | collective-permute-start | bytes 307208 | tf_op jit(solution)/shard_map/ppermute | solution.py:502
  30.3 9.5 %collective-permute-start.4 = (f32[176,256]{1,0:T(8,128)S(1)}, f32[176,256]{1,0:T(8,128)S(1)}, u32[]{:S(2)}, u32[]{:S(2)}) collective-permute-start(f32[176,256]{1,0:T(8,128)S(1)} %get-tuple-element.23.own), channel_id=1, source_target_pairs={{0,2},{2,4},{4,6},{6,8},{8,10},{10,12},{12,14},{14,16},{16,18},{18... | collective-permute-start | bytes 540680 | tf_op jit(solution)/shard_map/ppermute | solution.py:501
  31.4 8.5 %collective-permute-start.5 = (f32[200,128]{1,0:T(8,128)S(1)}, f32[200,128]{1,0:T(8,128)S(1)}, u32[]{:S(2)}, u32[]{:S(2)}) collective-permute-start(f32[200,128]{1,0:T(8,128)S(1)} %get-tuple-element.24), channel_id=1, source_target_pairs={{0,4},{2,6},{4,8},{6,10},{8,12},{10,14},{12,16},{14,18},{16,20},{1... | collective-permute-start | bytes 307208 | tf_op jit(solution)/shard_map/ppermute | solution.py:502

commit v14 on v13

--- a/solution.py
+++ b/solution.py
@@ -500,6 +500,9 @@
     place = jnp.reshape(row, (1,)).astype(jnp.int32)
     send_near = lambda x: lax.ppermute(x, "phi", [(p, (p + 1) % phi_count) for p in range(phi_count)])
     send_far = lambda x: lax.ppermute(x, "phi", [(p, (p + 2) % phi_count) for p in range(phi_count)])
+    here = lambda p, r: (p % phi_count) * row_count + r
+    diagonal = [(here(p, r), here(p + 1, 1 - r)) for p in range(phi_count) for r in range(row_count)]
+    send_corner = lambda x: lax.ppermute(x, ("phi", "row"), diagonal)
     send_side = lambda x: lax.ppermute(x, "row", [(0, 1), (1, 0)])
 
     spins, turns = rotation.reshape(parts, LANES), shifts.reshape(parts, LANES)
@@ -530,7 +533,7 @@
     )(density, momentum, magnetic, edge)
     owns, fars = packed[:levels], packed[levels:]
     side = send_side(edge)
-    corner = send_near(side)
+    corner = send_corner(edge)
     wide = (n + 1, radius, own_cells, total, spare, EXTRA)
     plain = (n, radius, own_cells, total, spare, 0)
     i32 = jax.ShapeDtypeStruct((TALL * SUB, LANES), jnp.int32)

time: 46.5 us -> 45 us (0.968)
  local copies, waits for them, and re-layouts: 0.78 us -> 0.03 us
  starting transfers between devices: 10.3 us -> 9.77 us
    ppermute x0 -> x1, waiting for transfers between devices: none -> 2.47 us  [body(): send_corner = lambda x: lax.ppermute(x, ('phi', 'row'), diagonal)]
    ppermute x5 -> x4, waiting for transfers between devices: 1.92 us -> 0.01 us  [body(): lax.ppermute(x, 'phi', [(p, (p + 1) % phi_count) for p in range(phi_count)])]
    ppermute x5 -> x4, starting transfers between devices: 3.27 us -> 1.99 us  [body(): lax.ppermute(x, 'phi', [(p, (p + 1) % phi_count) for p in range(phi_count)])]
    ppermute x0 -> x1, starting transfers between devices: none -> 1.15 us  [body(): send_corner = lambda x: lax.ppermute(x, ('phi', 'row'), diagonal)]
    ppermute x1, waiting for transfers between devices: 2.45 us -> 1.51 us  [body(): send_side = lambda x: lax.ppermute(x, 'row', [(0, 1), (1, 0)])]
    unnamed x12 -> x10, local copies, waits for them, and re-layouts: 0.78 us -> 0.03 us
  transfers between devices with their start and end apart: 10 -> 10, of which waited for: 3 -> 3; matrix products, arithmetic and copies ran while one was open for 0% -> 0% of each run, Pallas kernels for 44% -> 45%
where the time goes in v14:
time: 45 us; the launch traced here: 44.8 us
  Pallas kernels  28.5 us (63%)
  starting transfers between devices  9.77 us (22%)
  waiting for transfers between devices  5.83 us (13%)
  between operations  0.76 us (2%)
    pallas_call x2, Pallas kernels, first_step(): pl.pallas_call(kernel, out_shape=[f32(FIELDS * own_cells + EXTRA, radius)...  13.8 us
    pallas_call x2, Pallas kernels, last_step(): pl.pallas_call(kernel, out_shape=out_shape, in_specs=[smem] + [vmem] * (5...  12 us
    ppermute x4, starting transfers between devices, body(): lax.ppermute(x, 'phi', [(p, (p + 2) % phi_count) for p in range(phi_count)])  5.15 us
    ppermute x1, waiting for transfers between devices, body(): send_corner = lambda x: lax.ppermute(x, ('phi', 'row'), diagonal)  2.47 us
    ppermute x4, starting transfers between devices, body(): lax.ppermute(x, 'phi', [(p, (p + 1) % phi_count) for p in range(phi_count)])  1.99 us
    ppermute x4, waiting for transfers between devices, body(): lax.ppermute(x, 'phi', [(p, (p + 2) % phi_count) for p in range(phi_count)])  1.83 us
    pallas_call x1, Pallas kernels, body(): pl.pallas_call(edge_kernel, out_shape=f32(levels, EXTRA, 2 * LANES), in_s...  1.74 us
    ppermute x1, waiting for transfers between devices, body(): send_side = lambda x: lax.ppermute(x, 'row', [(0, 1), (1, 0)])  1.51 us
  transfers between devices with their start and end apart: 10, of which 3 were waited for; matrix products, arithmetic and copies ran while one was open for 0% of the time, Pallas kernels for 45%

profile of v14, /device:TPU:0, one launch (start us, length us, event | category | flops | bytes accessed | tf_op | source)
XLA Modules:
  0.0 44.8 jit_solution(12654616611899941242)
XLA Ops:
  0.7 1.7 %edges.1.refs_3_ = f32[2,16,256]{2,1,0:T(8,128)} custom-call(s32[1]{0:T(128)} %bitcast.place.refs_0_, f32[2,32,256]{2,1,0:T(8,128)} %refs_0_.1, f32[2,2,32,256]{3,2,1,0:T(8,128)} %refs_1_.1, f32[2,2,32,256]{3,2,1,0:T(8,128)} %refs_2_.1, f32[2,128]{1,0:T(2,128)} %bitcast.3, s32[2,128]{1,0:T(2,128)} %bitcast.5), custom_call_target="tpu_custom_call" | custom-call | tf_op jit(solution)/shard_map/edges/pallas_call | solution.py:511
  2.4 0.1 pack.1
  2.6 0.0 copy-start.4
  2.6 0.0 copy-start.3
  2.6 0.5 %collective-permute-start.6 = (f32[160,256]{1,0:T(8,128)S(1)}, f32[160,256]{1,0:T(8,128)S(1)}, u32[]{:S(2)}, u32[]{:S(2)}) collective-permute-start(f32[160,256]{1,0:T(8,128)S(1)} %get-tuple-element.27.own), channel_id=1, source_target_pairs={{0,2},{2,4},{4,6},{6,8},{8,10},{10,12},{12,14},{14,16},{16,18},{18... | collective-permute-start | bytes 491528 | tf_op jit(solution)/shard_map/ppermute | solution.py:501
  3.1 2.6 %collective-permute-start.7 = (f32[200,128]{1,0:T(8,128)S(1)}, f32[200,128]{1,0:T(8,128)S(1)}, u32[]{:S(2)}, u32[]{:S(2)}) collective-permute-start(f32[200,128]{1,0:T(8,128)S(1)} %get-tuple-element.28), channel_id=1, source_target_pairs={{0,4},{2,6},{4,8},{6,10},{8,12},{10,14},{12,16},{14,18},{16,20},{1... | collective-permute-start | bytes 307208 | tf_op jit(solution)/shard_map/ppermute | solution.py:502
  5.7 1.5 %collective-permute-start = (f32[2,16,256]{2,1,0:T(8,128)}, f32[2,16,256]{2,1,0:T(8,128)S(1)}, u32[]{:S(2)}, u32[]{:S(2)}) collective-permute-start(f32[2,16,256]{2,1,0:T(8,128)} %edges.1.refs_3_), channel_id=1, source_target_pairs={{0,1},{1,0},{2,3},{3,2},{4,5},{5,4},{6,7},{7,6},{8,9},{9,8},{10,11... | collective-permute-start | bytes 98312 | tf_op jit(solution)/shard_map/ppermute | solution.py:506
  7.2 1.1 %collective-permute-start.3 = (f32[2,16,256]{2,1,0:T(8,128)}, f32[2,16,256]{2,1,0:T(8,128)S(1)}, u32[]{:S(2)}, u32[]{:S(2)}) collective-permute-start(f32[2,16,256]{2,1,0:T(8,128)} %edges.1.refs_3_), channel_id=1, source_target_pairs={{0,3},{1,2},{2,5},{3,4},{4,7},{5,6},{6,9},{7,8},{8,11},{9,10},{10,... | collective-permute-start | bytes 98312 | tf_op jit(solution)/shard_map/ppermute | solution.py:505
  8.3 1.5 %collective-permute-done.refs_1_.side = f32[2,16,256]{2,1,0:T(8,128)S(1)} collective-permute-done((f32[2,16,256]{2,1,0:T(8,128)}, f32[2,16,256]{2,1,0:T(8,128)S(1)}, u32[]{:S(2)}, u32[]{:S(2)}) %collective-permute-start) | collective-permute-done | bytes 32800 | tf_op jit(solution)/shard_map/ppermute | solution.py:506
  9.8 0.9 %tables.1 = (f32[320,128]{1,0:T(8,128)S(1)}, s32[320,128]{1,0:T(8,128)S(1)}, f32[320,128]{1,0:T(8,128)S(1)}, s32[320,128]{1,0:T(8,128)S(1)}) custom-call(s32[1]{0:T(128)} %bitcast.place.refs_0_, f32[2,16,256]{2,1,0:T(8,128)S(1)} %collective-permute-done.refs_1_.side, f32[2,128]{1,0:T(2,128)S(1)} %bitcast.4, s32[2,128]{1,0:T(2,128)S(1)} %bitcast.6), custom_call_target="tpu_custom_call" | custom-call | tf_op jit(solution)/shard_map/tables/pallas_call | solution.py:540
  10.7 0.5 %collective-permute-start.1 = (f32[160,256]{1,0:T(8,128)S(1)}, f32[160,256]{1,0:T(8,128)S(1)}, u32[]{:S(2)}, u32[]{:S(2)}) collective-permute-start(f32[160,256]{1,0:T(8,128)S(1)} %get-tuple-element.20.own), channel_id=1, source_target_pairs={{0,2},{2,4},{4,6},{6,8},{8,10},{10,12},{12,14},{14,16},{16,18},{18... | collective-permute-start | bytes 491528 | tf_op jit(solution)/shard_map/ppermute | solution.py:501
  11.2 1.3 %collective-permute-start.2 = (f32[200,128]{1,0:T(8,128)S(1)}, f32[200,128]{1,0:T(8,128)S(1)}, u32[]{:S(2)}, u32[]{:S(2)}) collective-permute-start(f32[200,128]{1,0:T(8,128)S(1)} %get-tuple-element.21), channel_id=1, source_target_pairs={{0,4},{2,6},{4,8},{6,10},{8,12},{10,14},{12,16},{14,18},{16,20},{1... | collective-permute-start | bytes 307208 | tf_op jit(solution)/shard_map/ppermute | solution.py:502
  12.5 2.5 %collective-permute-done.3.corner = f32[2,16,256]{2,1,0:T(8,128)S(1)} collective-permute-done((f32[2,16,256]{2,1,0:T(8,128)}, f32[2,16,256]{2,1,0:T(8,128)S(1)}, u32[]{:S(2)}, u32[]{:S(2)}) %collective-permute-start.3) | collective-permute-done | bytes 32800 | tf_op jit(solution)/shard_map/ppermute | solution.py:505
  15.0 0.0 collective-permute-done.7.far
  15.0 0.0 collective-permute-done.6.near
  15.0 6.9 %first_step.3 = (f32[176,256]{1,0:T(8,128)S(1)}, f32[200,128]{1,0:T(8,128)S(1)}) custom-call(s32[1]{0:T(128)} %bitcast.place.refs_0_, f32[160,256]{1,0:T(8,128)S(1)} %get-tuple-element.27.own, f32[160,256]{1,0:T(8,128)S(1)} %collective-permute-done.6.near, f32[200,128]{1,0:T(8,128)S(1)} %collective-permute-done.7.far, ...), custom_call_target="tpu_custom_call" | custom-call | flops 8999999488 | bytes 29000000 | tf_op jit(solution)/shard_map/first_step/pallas_call | solution.py:432
  21.9 0.1 collective-permute-start.8
  22.0 0.2 collective-permute-start.9
  22.2 6.9 %first_step.2 = (f32[176,256]{1,0:T(8,128)S(1)}, f32[200,128]{1,0:T(8,128)S(1)}) custom-call(s32[1]{0:T(128)} %bitcast.place.refs_0_, f32[160,256]{1,0:T(8,128)S(1)} %get-tuple-element.20.own, f32[160,256]{1,0:T(8,128)S(1)} %collective-permute-done.1.near, f32[200,128]{1,0:T(8,128)S(1)} %collective-permute-done.2.far, ...), custom_call_target="tpu_custom_call" | custom-call | flops 8999999488 | bytes 29000000 | tf_op jit(solution)/shard_map/first_step/pallas_call | solution.py:432
  29.0 0.9 %collective-permute-start.4 = (f32[176,256]{1,0:T(8,128)S(1)}, f32[176,256]{1,0:T(8,128)S(1)}, u32[]{:S(2)}, u32[]{:S(2)}) collective-permute-start(f32[176,256]{1,0:T(8,128)S(1)} %get-tuple-element.23.own), channel_id=1, source_target_pairs={{0,2},{2,4},{4,6},{6,8},{8,10},{10,12},{12,14},{14,16},{16,18},{18... | collective-permute-start | bytes 540680 | tf_op jit(solution)/shard_map/ppermute | solution.py:501
  30.0 1.1 %collective-permute-start.5 = (f32[200,128]{1,0:T(8,128)S(1)}, f32[200,128]{1,0:T(8,128)S(1)}, u32[]{:S(2)}, u32[]{:S(2)}) collective-permute-start(f32[200,128]{1,0:T(8,128)S(1)} %get-tuple-element.24), channel_id=1, source_target_pairs={{0,4},{2,6},{4,8},{6,10},{8,12},{10,14},{12,16},{14,18},{16,20},{1... | collective-permute-start | bytes 307208 | tf_op jit(solution)/shard_map/ppermute | solution.py:502
  31.1 5.6 %last_step.2.rest_0_ = f32[160,256]{1,0:T(8,128)S(1)} custom-call(s32[1]{0:T(128)} %bitcast.place.refs_0_, f32[176,256]{1,0:T(8,128)S(1)} %get-tuple-element.29.own, f32[176,256]{1,0:T(8,128)S(1)} %collective-permute-done.8.near, f32[200,128]{1,0:T(8,128)S(1)} %collective-permute-done.9.far, f32[320,128]{1,0:T(8,128)S(1)} %get-tuple-element.25.spin, ...), custom_call_target="tpu_custom_call" | custom-call | flops 8999999488 | bytes 29000000 | tf_op jit(solution)/shard_map/last_step/pallas_call | solution.py:475
  36.7 1.8 %collective-permute-done.5.far = f32[200,128]{1,0:T(8,128)S(1)} collective-permute-done((f32[200,128]{1,0:T(8,128)S(1)}, f32[200,128]{1,0:T(8,128)S(1)}, u32[]{:S(2)}, u32[]{:S(2)}) %collective-permute-start.5) | collective-permute-done | bytes 102432 | tf_op jit(solution)/shard_map/ppermute | solution.py:502
  38.5 6.4 %last_step.3 = (f32[2,32,256]{2,1,0:T(8,128)}, f32[2,2,32,256]{3,2,1,0:T(8,128)}, f32[2,2,32,256]{3,2,1,0:T(8,128)}) custom-call(s32[1]{0:T(128)} %bitcast.place.refs_0_, f32[176,256]{1,0:T(8,128)S(1)} %get-tuple-element.23.own, f32[176,256]{1,0:T(8,128)S(1)} %collective-permute-done.4.near, f32[200,128]{1,0:T(8,128)S(1)} %collective-permute-done.5.far, ...), custom_call_target="tpu_custom_call" | custom-call | flops 8999999488 | bytes 29000000 | tf_op jit(solution)/shard_map/last_step/pallas_call | solution.py:475
  (13 shorter events, 0.0 us)
Async XLA Ops:
  0.6 1.8 %copy-start = (f32[2,2,32,256]{3,2,1,0:T(8,128)S(1)}, f32[2,2,32,256]{3,2,1,0:T(8,128)}, u32[]{:S(2)}) copy-start(f32[2,2,32,256]{3,2,1,0:T(8,128)} %refs_1_.1) | copy-start | bytes 393220
  0.6 1.8 %copy-start.1 = (f32[2,2,32,256]{3,2,1,0:T(8,128)S(1)}, f32[2,2,32,256]{3,2,1,0:T(8,128)}, u32[]{:S(2)}) copy-start(f32[2,2,32,256]{3,2,1,0:T(8,128)} %refs_2_.1) | copy-start | bytes 393220
  0.7 1.8 %copy-start.2 = (f32[2,32,256]{2,1,0:T(8,128)S(1)}, f32[2,32,256]{2,1,0:T(8,128)}, u32[]{:S(2)}) copy-start(f32[2,32,256]{2,1,0:T(8,128)} %refs_0_.1) | copy-start | bytes 196612
  2.6 7.3 %copy-start.4 = (s32[256]{0:T(256)S(1)}, s32[256]{0:T(256)}, u32[]{:S(2)}) copy-start(s32[256]{0:T(256)} %param.9) | copy-start | bytes 3076
  2.6 7.3 %copy-start.3 = (f32[256]{0:T(256)S(1)}, f32[256]{0:T(256)}, u32[]{:S(2)}) copy-start(f32[256]{0:T(256)} %param.8) | copy-start | bytes 3076
  2.6 12.4 %collective-permute-start.6 = (f32[160,256]{1,0:T(8,128)S(1)}, f32[160,256]{1,0:T(8,128)S(1)}, u32[]{:S(2)}, u32[]{:S(2)}) collective-permute-start(f32[160,256]{1,0:T(8,128)S(1)} %get-tuple-element.27.own), channel_id=1, source_target_pairs={{0,2},{2,4},{4,6},{6,8},{8,10},{10,12},{12,14},{14,16},{16,18},{18... | collective-permute-start | bytes 491528 | tf_op jit(solution)/shard_map/ppermute | solution.py:501
  3.1 11.9 %collective-permute-start.7 = (f32[200,128]{1,0:T(8,128)S(1)}, f32[200,128]{1,0:T(8,128)S(1)}, u32[]{:S(2)}, u32[]{:S(2)}) collective-permute-start(f32[200,128]{1,0:T(8,128)S(1)} %get-tuple-element.28), channel_id=1, source_target_pairs={{0,4},{2,6},{4,8},{6,10},{8,12},{10,14},{12,16},{14,18},{16,20},{1... | collective-permute-start | bytes 307208 | tf_op jit(solution)/shard_map/ppermute | solution.py:502
  5.7 4.2 %collective-permute-start = (f32[2,16,256]{2,1,0:T(8,128)}, f32[2,16,256]{2,1,0:T(8,128)S(1)}, u32[]{:S(2)}, u32[]{:S(2)}) collective-permute-start(f32[2,16,256]{2,1,0:T(8,128)} %edges.1.refs_3_), channel_id=1, source_target_pairs={{0,1},{1,0},{2,3},{3,2},{4,5},{5,4},{6,7},{7,6},{8,9},{9,8},{10,11... | collective-permute-start | bytes 98312 | tf_op jit(solution)/shard_map/ppermute | solution.py:506
  7.2 7.8 %collective-permute-start.3 = (f32[2,16,256]{2,1,0:T(8,128)}, f32[2,16,256]{2,1,0:T(8,128)S(1)}, u32[]{:S(2)}, u32[]{:S(2)}) collective-permute-start(f32[2,16,256]{2,1,0:T(8,128)} %edges.1.refs_3_), channel_id=1, source_target_pairs={{0,3},{1,2},{2,5},{3,4},{4,7},{5,6},{6,9},{7,8},{8,11},{9,10},{10,... | collective-permute-start | bytes 98312 | tf_op jit(solution)/shard_map/ppermute | solution.py:505
  10.7 11.4 %collective-permute-start.1 = (f32[160,256]{1,0:T(8,128)S(1)}, f32[160,256]{1,0:T(8,128)S(1)}, u32[]{:S(2)}, u32[]{:S(2)}) collective-permute-start(f32[160,256]{1,0:T(8,128)S(1)} %get-tuple-element.20.own), channel_id=1, source_target_pairs={{0,2},{2,4},{4,6},{6,8},{8,10},{10,12},{12,14},{14,16},{16,18},{18... | collective-permute-start | bytes 491528 | tf_op jit(solution)/shard_map/ppermute | solution.py:501
  11.2 10.9 %collective-permute-start.2 = (f32[200,128]{1,0:T(8,128)S(1)}, f32[200,128]{1,0:T(8,128)S(1)}, u32[]{:S(2)}, u32[]{:S(2)}) collective-permute-start(f32[200,128]{1,0:T(8,128)S(1)} %get-tuple-element.21), channel_id=1, source_target_pairs={{0,4},{2,6},{4,8},{6,10},{8,12},{10,14},{12,16},{14,18},{16,20},{1... | collective-permute-start | bytes 307208 | tf_op jit(solution)/shard_map/ppermute | solution.py:502
  21.9 9.2 %collective-permute-start.8 = (f32[176,256]{1,0:T(8,128)S(1)}, f32[176,256]{1,0:T(8,128)S(1)}, u32[]{:S(2)}, u32[]{:S(2)}) collective-permute-start(f32[176,256]{1,0:T(8,128)S(1)} %get-tuple-element.29.own), channel_id=1, source_target_pairs={{0,2},{2,4},{4,6},{6,8},{8,10},{10,12},{12,14},{14,16},{16,18},{18... | collective-permute-start | bytes 540680 | tf_op jit(solution)/shard_map/ppermute | solution.py:501
  22.0 9.1 %collective-permute-start.9 = (f32[200,128]{1,0:T(8,128)S(1)}, f32[200,128]{1,0:T(8,128)S(1)}, u32[]{:S(2)}, u32[]{:S(2)}) collective-permute-start(f32[200,128]{1,0:T(8,128)S(1)} %get-tuple-element.30), channel_id=1, source_target_pairs={{0,4},{2,6},{4,8},{6,10},{8,12},{10,14},{12,16},{14,18},{16,20},{1... | collective-permute-start | bytes 307208 | tf_op jit(solution)/shard_map/ppermute | solution.py:502
  29.0 9.4 %collective-permute-start.4 = (f32[176,256]{1,0:T(8,128)S(1)}, f32[176,256]{1,0:T(8,128)S(1)}, u32[]{:S(2)}, u32[]{:S(2)}) collective-permute-start(f32[176,256]{1,0:T(8,128)S(1)} %get-tuple-element.23.own), channel_id=1, source_target_pairs={{0,2},{2,4},{4,6},{6,8},{8,10},{10,12},{12,14},{14,16},{16,18},{18... | collective-permute-start | bytes 540680 | tf_op jit(solution)/shard_map/ppermute | solution.py:501
  30.0 8.5 %collective-permute-start.5 = (f32[200,128]{1,0:T(8,128)S(1)}, f32[200,128]{1,0:T(8,128)S(1)}, u32[]{:S(2)}, u32[]{:S(2)}) collective-permute-start(f32[200,128]{1,0:T(8,128)S(1)} %get-tuple-element.24), channel_id=1, source_target_pairs={{0,4},{2,6},{4,8},{6,10},{8,12},{10,14},{12,16},{14,18},{16,20},{1... | collective-permute-start | bytes 307208 | tf_op jit(solution)/shard_map/ppermute | solution.py:502

commit v15 on v14

--- a/solution.py
+++ b/solution.py
@@ -18,8 +18,6 @@
 EXTRA = 2 * SUB
 DEALT = 32
 TALL = 40
-ROWS = 8
-PICKS = 4
 VMEM_LIMIT = 32 * 1024 * 1024
 EDGE_LIMIT = 60 * 1024 * 1024
 
@@ -74,7 +72,12 @@
     return pl.ds(pl.multiple_of(i * SUB, SUB), SUB)
 
 
+def rows_a_turn(n):
+    return (n + 2 * REACH - 4 + 1) // 2
+
+
 def run_stages(n, stages, spin, edges):
+    each = rows_a_turn(n)
     half_dt = 0.5 * time_step
     low_mask, high_mask = edges
     first, last = REACH, REACH + n - 1
@@ -94,9 +97,9 @@
         weight = jnp.where(stage == 0, 1.0, jnp.where(stage == 1, 0.25, 2.0 / 3.0))
         keep = jnp.where(stage == 0, 0.0, jnp.where(stage == 1, 0.75, 1.0 / 3.0))
         some = lambda first, count: pl.ds(pl.multiple_of((i0 + first) * SUB, SUB), count * SUB)
-        here = some(0, ROWS)
-        size = ROWS * SUB
-        rows = [stages[src, f, some(-1, ROWS + 3), :] for f in range(FIELDS)]
+        here = some(0, each)
+        size = each * SUB
+        rows = [stages[src, f, some(-1, each + 3), :] for f in range(FIELDS)]
         halves = [0.5 * x for x in rows]
         own = [x[SUB : SUB + size] for x in rows]
         half = [x[SUB : SUB + size] for x in halves]
@@ -132,7 +135,7 @@
                 stages[stage, f, tile(first - k), :] = jnp.where(low_mask, inner, stages[stage, f, tile(first - k), :])
                 stages[stage, f, tile(last + k), :] = jnp.where(high_mask, outer, stages[stage, f, tile(last + k), :])
         count = n + 2 * REACH - 4 - 4 * stage
-        if n % ROWS == 0:
+        if n % 2 == 0:
             lo = 2 * stage + 2
             rows = [stages[stage, f, pl.ds(pl.multiple_of((lo - 2) * SUB, SUB), 4 * SUB), :] for f in range(FIELDS)]
             left, right = radial_states([0.5 * x for x in rows], [x[SUB:-SUB] for x in rows])
@@ -141,8 +144,8 @@
             lo = 2 * stage + 1
             count = count + 1
             before = (jnp.zeros((SUB, LANES), jnp.float32),) * FIELDS
-        turns = lax.div(count + ROWS - 1, ROWS)
-        lax.fori_loop(0, turns, lambda c, carried: tuple(work(stage, lo + c * ROWS, list(carried))), before)
+        turns = lax.div(count + each - 1, each)
+        lax.fori_loop(0, turns, lambda c, carried: tuple(work(stage, lo + c * each, list(carried))), before)
         return 0
 
     lax.fori_loop(0, STAGES, run, 0)
@@ -327,9 +330,11 @@
 
     even = (lane & own_cells) == 0
 
+    picked = (n + 1) // 2
+
     def shift(turn, _):
-        for k in range(PICKS):
-            i = turn * PICKS + k
+        for k in range(picked):
+            i = turn * picked + k
             rows = tile(REACH + i)
             source = pick[rows, :]
             picks = [source & (LANES - 1), (source - own_cells) & (LANES - 1)]
@@ -342,7 +347,7 @@
             stages[2, 2, tile(i), :] = turned[4]
         return 0
 
-    lax.fori_loop(0, (n + PICKS - 1) // PICKS, shift, 0)
+    lax.fori_loop(0, (n + picked - 1) // picked, shift, 0)
     narrow = lax.broadcasted_iota(jnp.int32, (n, LANES), 1) < HALF
     for j in range(SUB):
         one, two, three = [stages[2, g, pl.ds(j, n, stride=SUB), :] for g in range(3)]

time: 45 us -> 42.9 us (0.953)
  Pallas kernels: 28.5 us -> 26.3 us
    pallas_call x2, Pallas kernels: 13.8 us -> 11.7 us  [first_step(): pl.pallas_call(kernel, out_shape=[f32(FIELDS * own_cells + EXTRA, radius)...]
  transfers between devices with their start and end apart: 10 -> 10, of which waited for: 3 -> 5; matrix products, arithmetic and copies ran while one was open for 0% -> 0% of each run, Pallas kernels for 45% -> 42%
where the time goes in v15:
time: 42.9 us; the launch traced here: 42.7 us
  Pallas kernels  26.3 us (61%)
  starting transfers between devices  9.77 us (23%)
  waiting for transfers between devices  5.9 us (14%)
  between operations  0.76 us (2%)
    pallas_call x2, Pallas kernels, last_step(): pl.pallas_call(kernel, out_shape=out_shape, in_specs=[smem] + [vmem] * (5...  11.8 us
    pallas_call x2, Pallas kernels, first_step(): pl.pallas_call(kernel, out_shape=[f32(FIELDS * own_cells + EXTRA, radius)...  11.7 us
    ppermute x4, starting transfers between devices, body(): lax.ppermute(x, 'phi', [(p, (p + 2) % phi_count) for p in range(phi_count)])  5.15 us
    ppermute x1, waiting for transfers between devices, body(): send_corner = lambda x: lax.ppermute(x, ('phi', 'row'), diagonal)  2.47 us
    ppermute x4, starting transfers between devices, body(): lax.ppermute(x, 'phi', [(p, (p + 1) % phi_count) for p in range(phi_count)])  1.99 us
    pallas_call x1, Pallas kernels, body(): pl.pallas_call(edge_kernel, out_shape=f32(levels, EXTRA, 2 * LANES), in_s...  1.74 us
    ppermute x4, waiting for transfers between devices, body(): lax.ppermute(x, 'phi', [(p, (p + 2) % phi_count) for p in range(phi_count)])  1.66 us
    ppermute x1, waiting for transfers between devices, body(): send_side = lambda x: lax.ppermute(x, 'row', [(0, 1), (1, 0)])  1.51 us
  transfers between devices with their start and end apart: 10, of which 5 were waited for; matrix products, arithmetic and copies ran while one was open for 0% of the time, Pallas kernels for 42%

profile of v15, /device:TPU:0, one launch (start us, length us, event | category | flops | bytes accessed | tf_op | source)
XLA Modules:
  0.0 42.7 jit_solution(13125484645252464250)
XLA Ops:
  0.7 1.7 %edges.1.refs_3_ = f32[2,16,256]{2,1,0:T(8,128)} custom-call(s32[1]{0:T(128)} %bitcast.place.refs_0_, f32[2,32,256]{2,1,0:T(8,128)} %refs_0_.1, f32[2,2,32,256]{3,2,1,0:T(8,128)} %refs_1_.1, f32[2,2,32,256]{3,2,1,0:T(8,128)} %refs_2_.1, f32[2,128]{1,0:T(2,128)} %bitcast.3, s32[2,128]{1,0:T(2,128)} %bitcast.5), custom_call_target="tpu_custom_call" | custom-call | tf_op jit(solution)/shard_map/edges/pallas_call | solution.py:516
  2.4 0.1 pack.1
  2.6 0.0 copy-start.4
  2.6 0.0 copy-start.3
  2.6 0.5 %collective-permute-start.6 = (f32[160,256]{1,0:T(8,128)S(1)}, f32[160,256]{1,0:T(8,128)S(1)}, u32[]{:S(2)}, u32[]{:S(2)}) collective-permute-start(f32[160,256]{1,0:T(8,128)S(1)} %get-tuple-element.27.own), channel_id=1, source_target_pairs={{0,2},{2,4},{4,6},{6,8},{8,10},{10,12},{12,14},{14,16},{16,18},{18... | collective-permute-start | bytes 491528 | tf_op jit(solution)/shard_map/ppermute | solution.py:506
  3.1 2.6 %collective-permute-start.7 = (f32[200,128]{1,0:T(8,128)S(1)}, f32[200,128]{1,0:T(8,128)S(1)}, u32[]{:S(2)}, u32[]{:S(2)}) collective-permute-start(f32[200,128]{1,0:T(8,128)S(1)} %get-tuple-element.28), channel_id=1, source_target_pairs={{0,4},{2,6},{4,8},{6,10},{8,12},{10,14},{12,16},{14,18},{16,20},{1... | collective-permute-start | bytes 307208 | tf_op jit(solution)/shard_map/ppermute | solution.py:507
  5.7 1.5 %collective-permute-start = (f32[2,16,256]{2,1,0:T(8,128)}, f32[2,16,256]{2,1,0:T(8,128)S(1)}, u32[]{:S(2)}, u32[]{:S(2)}) collective-permute-start(f32[2,16,256]{2,1,0:T(8,128)} %edges.1.refs_3_), channel_id=1, source_target_pairs={{0,1},{1,0},{2,3},{3,2},{4,5},{5,4},{6,7},{7,6},{8,9},{9,8},{10,11... | collective-permute-start | bytes 98312 | tf_op jit(solution)/shard_map/ppermute | solution.py:511
  7.2 1.1 %collective-permute-start.3 = (f32[2,16,256]{2,1,0:T(8,128)}, f32[2,16,256]{2,1,0:T(8,128)S(1)}, u32[]{:S(2)}, u32[]{:S(2)}) collective-permute-start(f32[2,16,256]{2,1,0:T(8,128)} %edges.1.refs_3_), channel_id=1, source_target_pairs={{0,3},{1,2},{2,5},{3,4},{4,7},{5,6},{6,9},{7,8},{8,11},{9,10},{10,... | collective-permute-start | bytes 98312 | tf_op jit(solution)/shard_map/ppermute | solution.py:510
  8.3 1.5 %collective-permute-done.refs_1_.side = f32[2,16,256]{2,1,0:T(8,128)S(1)} collective-permute-done((f32[2,16,256]{2,1,0:T(8,128)}, f32[2,16,256]{2,1,0:T(8,128)S(1)}, u32[]{:S(2)}, u32[]{:S(2)}) %collective-permute-start) | collective-permute-done | bytes 32800 | tf_op jit(solution)/shard_map/ppermute | solution.py:511
  9.8 0.9 %tables.1 = (f32[320,128]{1,0:T(8,128)S(1)}, s32[320,128]{1,0:T(8,128)S(1)}, f32[320,128]{1,0:T(8,128)S(1)}, s32[320,128]{1,0:T(8,128)S(1)}) custom-call(s32[1]{0:T(128)} %bitcast.place.refs_0_, f32[2,16,256]{2,1,0:T(8,128)S(1)} %collective-permute-done.refs_1_.side, f32[2,128]{1,0:T(2,128)S(1)} %bitcast.4, s32[2,128]{1,0:T(2,128)S(1)} %bitcast.6), custom_call_target="tpu_custom_call" | custom-call | tf_op jit(solution)/shard_map/tables/pallas_call | solution.py:545
  10.7 0.5 %collective-permute-start.1 = (f32[160,256]{1,0:T(8,128)S(1)}, f32[160,256]{1,0:T(8,128)S(1)}, u32[]{:S(2)}, u32[]{:S(2)}) collective-permute-start(f32[160,256]{1,0:T(8,128)S(1)} %get-tuple-element.20.own), channel_id=1, source_target_pairs={{0,2},{2,4},{4,6},{6,8},{8,10},{10,12},{12,14},{14,16},{16,18},{18... | collective-permute-start | bytes 491528 | tf_op jit(solution)/shard_map/ppermute | solution.py:506
  11.2 1.3 %collective-permute-start.2 = (f32[200,128]{1,0:T(8,128)S(1)}, f32[200,128]{1,0:T(8,128)S(1)}, u32[]{:S(2)}, u32[]{:S(2)}) collective-permute-start(f32[200,128]{1,0:T(8,128)S(1)} %get-tuple-element.21), channel_id=1, source_target_pairs={{0,4},{2,6},{4,8},{6,10},{8,12},{10,14},{12,16},{14,18},{16,20},{1... | collective-permute-start | bytes 307208 | tf_op jit(solution)/shard_map/ppermute | solution.py:507
  12.5 2.5 %collective-permute-done.3.corner = f32[2,16,256]{2,1,0:T(8,128)S(1)} collective-permute-done((f32[2,16,256]{2,1,0:T(8,128)}, f32[2,16,256]{2,1,0:T(8,128)S(1)}, u32[]{:S(2)}, u32[]{:S(2)}) %collective-permute-start.3) | collective-permute-done | bytes 32800 | tf_op jit(solution)/shard_map/ppermute | solution.py:510
  15.0 5.9 %first_step.3 = (f32[176,256]{1,0:T(8,128)S(1)}, f32[200,128]{1,0:T(8,128)S(1)}) custom-call(s32[1]{0:T(128)} %bitcast.place.refs_0_, f32[160,256]{1,0:T(8,128)S(1)} %get-tuple-element.27.own, f32[160,256]{1,0:T(8,128)S(1)} %collective-permute-done.6.near, f32[200,128]{1,0:T(8,128)S(1)} %collective-permute-done.7.far, ...), custom_call_target="tpu_custom_call" | custom-call | flops 8999999488 | bytes 29000000 | tf_op jit(solution)/shard_map/first_step/pallas_call | solution.py:437
  20.9 0.1 collective-permute-start.8
  20.9 0.2 collective-permute-start.9
  21.1 5.8 %first_step.2 = (f32[176,256]{1,0:T(8,128)S(1)}, f32[200,128]{1,0:T(8,128)S(1)}) custom-call(s32[1]{0:T(128)} %bitcast.place.refs_0_, f32[160,256]{1,0:T(8,128)S(1)} %get-tuple-element.20.own, f32[160,256]{1,0:T(8,128)S(1)} %collective-permute-done.1.near, f32[200,128]{1,0:T(8,128)S(1)} %collective-permute-done.2.far, ...), custom_call_target="tpu_custom_call" | custom-call | flops 8999999488 | bytes 29000000 | tf_op jit(solution)/shard_map/first_step/pallas_call | solution.py:437
  27.0 0.9 %collective-permute-start.4 = (f32[176,256]{1,0:T(8,128)S(1)}, f32[176,256]{1,0:T(8,128)S(1)}, u32[]{:S(2)}, u32[]{:S(2)}) collective-permute-start(f32[176,256]{1,0:T(8,128)S(1)} %get-tuple-element.23.own), channel_id=1, source_target_pairs={{0,2},{2,4},{4,6},{6,8},{8,10},{10,12},{12,14},{14,16},{16,18},{18... | collective-permute-start | bytes 540680 | tf_op jit(solution)/shard_map/ppermute | solution.py:506
  27.9 1.1 %collective-permute-start.5 = (f32[200,128]{1,0:T(8,128)S(1)}, f32[200,128]{1,0:T(8,128)S(1)}, u32[]{:S(2)}, u32[]{:S(2)}) collective-permute-start(f32[200,128]{1,0:T(8,128)S(1)} %get-tuple-element.24), channel_id=1, source_target_pairs={{0,4},{2,6},{4,8},{6,10},{8,12},{10,14},{12,16},{14,18},{16,20},{1... | collective-permute-start | bytes 307208 | tf_op jit(solution)/shard_map/ppermute | solution.py:507
  29.0 0.4 collective-permute-done.9.far
  29.4 0.3 collective-permute-done.8.near
  29.6 5.5 %last_step.2.rest_0_ = f32[160,256]{1,0:T(8,128)S(1)} custom-call(s32[1]{0:T(128)} %bitcast.place.refs_0_, f32[176,256]{1,0:T(8,128)S(1)} %get-tuple-element.29.own, f32[176,256]{1,0:T(8,128)S(1)} %collective-permute-done.8.near, f32[200,128]{1,0:T(8,128)S(1)} %collective-permute-done.9.far, f32[320,128]{1,0:T(8,128)S(1)} %get-tuple-element.25.spin, ...), custom_call_target="tpu_custom_call" | custom-call | flops 8999999488 | bytes 29000000 | tf_op jit(solution)/shard_map/last_step/pallas_call | solution.py:480
  35.2 1.3 %collective-permute-done.5.far = f32[200,128]{1,0:T(8,128)S(1)} collective-permute-done((f32[200,128]{1,0:T(8,128)S(1)}, f32[200,128]{1,0:T(8,128)S(1)}, u32[]{:S(2)}, u32[]{:S(2)}) %collective-permute-start.5) | collective-permute-done | bytes 102432 | tf_op jit(solution)/shard_map/ppermute | solution.py:507
  36.4 6.3 %last_step.3 = (f32[2,32,256]{2,1,0:T(8,128)}, f32[2,2,32,256]{3,2,1,0:T(8,128)}, f32[2,2,32,256]{3,2,1,0:T(8,128)}) custom-call(s32[1]{0:T(128)} %bitcast.place.refs_0_, f32[176,256]{1,0:T(8,128)S(1)} %get-tuple-element.23.own, f32[176,256]{1,0:T(8,128)S(1)} %collective-permute-done.4.near, f32[200,128]{1,0:T(8,128)S(1)} %collective-permute-done.5.far, ...), custom_call_target="tpu_custom_call" | custom-call | flops 8999999488 | bytes 29000000 | tf_op jit(solution)/shard_map/last_step/pallas_call | solution.py:480
  (13 shorter events, 0.0 us)
Async XLA Ops:
  0.6 1.8 %copy-start = (f32[2,2,32,256]{3,2,1,0:T(8,128)S(1)}, f32[2,2,32,256]{3,2,1,0:T(8,128)}, u32[]{:S(2)}) copy-start(f32[2,2,32,256]{3,2,1,0:T(8,128)} %refs_1_.1) | copy-start | bytes 393220
  0.6 1.8 %copy-start.1 = (f32[2,2,32,256]{3,2,1,0:T(8,128)S(1)}, f32[2,2,32,256]{3,2,1,0:T(8,128)}, u32[]{:S(2)}) copy-start(f32[2,2,32,256]{3,2,1,0:T(8,128)} %refs_2_.1) | copy-start | bytes 393220
  0.7 1.8 %copy-start.2 = (f32[2,32,256]{2,1,0:T(8,128)S(1)}, f32[2,32,256]{2,1,0:T(8,128)}, u32[]{:S(2)}) copy-start(f32[2,32,256]{2,1,0:T(8,128)} %refs_0_.1) | copy-start | bytes 196612
  2.6 7.3 %copy-start.4 = (s32[256]{0:T(256)S(1)}, s32[256]{0:T(256)}, u32[]{:S(2)}) copy-start(s32[256]{0:T(256)} %param.9) | copy-start | bytes 3076
  2.6 7.3 %copy-start.3 = (f32[256]{0:T(256)S(1)}, f32[256]{0:T(256)}, u32[]{:S(2)}) copy-start(f32[256]{0:T(256)} %param.8) | copy-start | bytes 3076
  2.6 12.4 %collective-permute-start.6 = (f32[160,256]{1,0:T(8,128)S(1)}, f32[160,256]{1,0:T(8,128)S(1)}, u32[]{:S(2)}, u32[]{:S(2)}) collective-permute-start(f32[160,256]{1,0:T(8,128)S(1)} %get-tuple-element.27.own), channel_id=1, source_target_pairs={{0,2},{2,4},{4,6},{6,8},{8,10},{10,12},{12,14},{14,16},{16,18},{18... | collective-permute-start | bytes 491528 | tf_op jit(solution)/shard_map/ppermute | solution.py:506
  3.1 11.9 %collective-permute-start.7 = (f32[200,128]{1,0:T(8,128)S(1)}, f32[200,128]{1,0:T(8,128)S(1)}, u32[]{:S(2)}, u32[]{:S(2)}) collective-permute-start(f32[200,128]{1,0:T(8,128)S(1)} %get-tuple-element.28), channel_id=1, source_target_pairs={{0,4},{2,6},{4,8},{6,10},{8,12},{10,14},{12,16},{14,18},{16,20},{1... | collective-permute-start | bytes 307208 | tf_op jit(solution)/shard_map/ppermute | solution.py:507
  5.7 4.2 %collective-permute-start = (f32[2,16,256]{2,1,0:T(8,128)}, f32[2,16,256]{2,1,0:T(8,128)S(1)}, u32[]{:S(2)}, u32[]{:S(2)}) collective-permute-start(f32[2,16,256]{2,1,0:T(8,128)} %edges.1.refs_3_), channel_id=1, source_target_pairs={{0,1},{1,0},{2,3},{3,2},{4,5},{5,4},{6,7},{7,6},{8,9},{9,8},{10,11... | collective-permute-start | bytes 98312 | tf_op jit(solution)/shard_map/ppermute | solution.py:511
  7.2 7.8 %collective-permute-start.3 = (f32[2,16,256]{2,1,0:T(8,128)}, f32[2,16,256]{2,1,0:T(8,128)S(1)}, u32[]{:S(2)}, u32[]{:S(2)}) collective-permute-start(f32[2,16,256]{2,1,0:T(8,128)} %edges.1.refs_3_), channel_id=1, source_target_pairs={{0,3},{1,2},{2,5},{3,4},{4,7},{5,6},{6,9},{7,8},{8,11},{9,10},{10,... | collective-permute-start | bytes 98312 | tf_op jit(solution)/shard_map/ppermute | solution.py:510
  10.7 10.4 %collective-permute-start.1 = (f32[160,256]{1,0:T(8,128)S(1)}, f32[160,256]{1,0:T(8,128)S(1)}, u32[]{:S(2)}, u32[]{:S(2)}) collective-permute-start(f32[160,256]{1,0:T(8,128)S(1)} %get-tuple-element.20.own), channel_id=1, source_target_pairs={{0,2},{2,4},{4,6},{6,8},{8,10},{10,12},{12,14},{14,16},{16,18},{18... | collective-permute-start | bytes 491528 | tf_op jit(solution)/shard_map/ppermute | solution.py:506
  11.2 9.9 %collective-permute-start.2 = (f32[200,128]{1,0:T(8,128)S(1)}, f32[200,128]{1,0:T(8,128)S(1)}, u32[]{:S(2)}, u32[]{:S(2)}) collective-permute-start(f32[200,128]{1,0:T(8,128)S(1)} %get-tuple-element.21), channel_id=1, source_target_pairs={{0,4},{2,6},{4,8},{6,10},{8,12},{10,14},{12,16},{14,18},{16,20},{1... | collective-permute-start | bytes 307208 | tf_op jit(solution)/shard_map/ppermute | solution.py:507
  20.9 8.8 %collective-permute-start.8 = (f32[176,256]{1,0:T(8,128)S(1)}, f32[176,256]{1,0:T(8,128)S(1)}, u32[]{:S(2)}, u32[]{:S(2)}) collective-permute-start(f32[176,256]{1,0:T(8,128)S(1)} %get-tuple-element.29.own), channel_id=1, source_target_pairs={{0,2},{2,4},{4,6},{6,8},{8,10},{10,12},{12,14},{14,16},{16,18},{18... | collective-permute-start | bytes 540680 | tf_op jit(solution)/shard_map/ppermute | solution.py:506
  20.9 8.4 %collective-permute-start.9 = (f32[200,128]{1,0:T(8,128)S(1)}, f32[200,128]{1,0:T(8,128)S(1)}, u32[]{:S(2)}, u32[]{:S(2)}) collective-permute-start(f32[200,128]{1,0:T(8,128)S(1)} %get-tuple-element.30), channel_id=1, source_target_pairs={{0,4},{2,6},{4,8},{6,10},{8,12},{10,14},{12,16},{14,18},{16,20},{1... | collective-permute-start | bytes 307208 | tf_op jit(solution)/shard_map/ppermute | solution.py:507
  27.0 9.4 %collective-permute-start.4 = (f32[176,256]{1,0:T(8,128)S(1)}, f32[176,256]{1,0:T(8,128)S(1)}, u32[]{:S(2)}, u32[]{:S(2)}) collective-permute-start(f32[176,256]{1,0:T(8,128)S(1)} %get-tuple-element.23.own), channel_id=1, source_target_pairs={{0,2},{2,4},{4,6},{6,8},{8,10},{10,12},{12,14},{14,16},{16,18},{18... | collective-permute-start | bytes 540680 | tf_op jit(solution)/shard_map/ppermute | solution.py:506
  27.9 8.5 %collective-permute-start.5 = (f32[200,128]{1,0:T(8,128)S(1)}, f32[200,128]{1,0:T(8,128)S(1)}, u32[]{:S(2)}, u32[]{:S(2)}) collective-permute-start(f32[200,128]{1,0:T(8,128)S(1)} %get-tuple-element.24), channel_id=1, source_target_pairs={{0,4},{2,6},{4,8},{6,10},{8,12},{10,14},{12,16},{14,18},{16,20},{1... | collective-permute-start | bytes 307208 | tf_op jit(solution)/shard_map/ppermute | solution.py:507

commit v16 on v15

--- a/solution.py
+++ b/solution.py
@@ -236,32 +236,29 @@
 
 def table_kernel(plans, place, side, rotation, shifts, *rest):
     outs, held = rest[:-1], rest[-1]
-    lane = lax.broadcasted_iota(jnp.int32, (SUB, LANES), 1)
-    sublane = lax.broadcasted_iota(jnp.int32, (SUB, LANES), 0)
-    front = lax.broadcasted_iota(jnp.int32, (DEALT, LANES), 1) < HALF
+    radius = plans[0][1]
+    own_cells = plans[0][2]
+    wide_lane = lax.broadcasted_iota(jnp.int32, (DEALT, LANES), 1)
+    front = wide_lane < HALF
     more = side[0, :, LANES : 2 * LANES]
+    edges = [spread(more, own_cells, own_cells), spread(more, 2 * own_cells, own_cells)]
+    own = []
+    for ref, scale in ((rotation, time_step), (shifts, 1.0)):
+        along = lambda part: jnp.broadcast_to(ref[part : part + 1, :].astype(jnp.float32), (LANES, LANES)).T
+        own.append([along(part) * scale for part in range(radius // LANES)])
     for which, (n, radius, own_cells, total, spare, moved) in enumerate(plans):
         spin, pick = outs[2 * which : 2 * which + 2]
         blocks = Blocks(place[0], n, radius, total, moved)
-        for part in range(radius // LANES):
-            rows = pl.ds(blocks.own_at + part * LANES, LANES)
-            along = lambda ref: jnp.broadcast_to(ref[part : part + 1, :].astype(jnp.float32), (LANES, LANES)).T
-            held[0, rows, :] = along(rotation) * time_step
-            held[1, rows, :] = along(shifts)
-        held[0, pl.ds(blocks.edge_at, EXTRA), :] = spread(more, own_cells, own_cells)
-        held[1, pl.ds(blocks.edge_at, EXTRA), :] = spread(more, 2 * own_cells, own_cells)
-        bound = jnp.zeros((SUB, LANES), jnp.int32)
+        for k in range(2):
+            for part, x in enumerate(own[k]):
+                held[2 * which + k, pl.ds(blocks.own_at + part * LANES, LANES), :] = x
+            held[2 * which + k, pl.ds(blocks.edge_at, EXTRA), :] = edges[k]
         for j in range(SUB):
             low, high = blocks.rows_of(j), blocks.rows_of(SUB + j)
-            spin[pl.ds(j, DEALT, stride=SUB), :] = jnp.where(front, held[0, low, :], held[0, high, :])
-            pick[pl.ds(j, DEALT, stride=SUB), :] = jnp.where(front, held[1, low, :], held[1, high, :]).astype(jnp.int32)
-            bound = jnp.where(sublane == j, jnp.where(lane < HALF, blocks.bounds[j], blocks.bounds[SUB + j]), bound)
-
-        def one(i, _):
-            pick[tile(i), :] = (lane + (REACH + bound)) - pick[tile(i), :]
-            return 0
-
-        lax.fori_loop(0, TALL, one, 0)
+            turns = [jnp.where(front, held[2 * which + k, low, :], held[2 * which + k, high, :]) for k in range(2)]
+            spin[pl.ds(j, DEALT, stride=SUB), :] = turns[0]
+            bound = jnp.where(front, blocks.bounds[j], blocks.bounds[SUB + j])
+            pick[pl.ds(j, DEALT, stride=SUB), :] = (wide_lane + (REACH + bound)) - turns[1].astype(jnp.int32)
 
 
 def step_kernel(plan, refs, write, scratch):
@@ -276,7 +273,9 @@
     edge_lane = lax.broadcasted_iota(jnp.int32, (EXTRA, LANES), 1)
     parts = radius // LANES
 
-    def gather(f, _):
+    front = lax.broadcasted_iota(jnp.int32, (DEALT, LANES), 1) < HALF
+
+    def bring(f, _):
         rows = pl.ds(pl.multiple_of(f * own_cells, SUB), own_cells)
         start = pl.multiple_of(f * (own_cells + SUB), SUB)
         for part in range(parts):
@@ -302,13 +301,7 @@
             pltpu.roll(near_edge[:, columns], lax.rem(LANES + own_cells - lanes_at, LANES), 1),
             pltpu.roll(own_edge[:, columns], lax.rem(LANES + 2 * own_cells - lanes_at, LANES), 1),
         )
-        return 0
-
-    lax.fori_loop(0, FIELDS, gather, 0)
-
-    front = lax.broadcasted_iota(jnp.int32, (DEALT, LANES), 1) < HALF
-
-    def deal(f, _):
+
         for j in range(SUB):
             low, high = j, SUB + j
             turn_low = (LANES - (2 * own_cells - REACH)) + blocks.bounds[low]
@@ -320,7 +313,7 @@
             )
         return 0
 
-    lax.fori_loop(0, FIELDS, deal, 0)
+    lax.fori_loop(0, FIELDS, bring, 0)
 
     edges = (
         (sublane == 0) & (lane < HALF) & (row == 0),
@@ -547,7 +540,7 @@
         out_shape=[f32(TALL * SUB, LANES), i32] * 2,
         in_specs=[smem] + [vmem] * 3,
         out_specs=[vmem] * 4,
-        scratch_shapes=[pltpu.VMEM((2, tall_of(n + 1), LANES), jnp.float32)],
+        scratch_shapes=[pltpu.VMEM((4, tall_of(n + 1), LANES), jnp.float32)],
         compiler_params=params,
         name="tables",
     )(place, side, spins, turns)

time: 42.9 us -> 42.9 us (level)
  waiting for transfers between devices: 5.9 us -> 6.99 us
  Pallas kernels: 26.3 us -> 25.7 us
  starting transfers between devices: 9.77 us -> 9.2 us
    ppermute x4, starting transfers between devices: 5.15 us -> 4.47 us  [body(): lax.ppermute(x, 'phi', [(p, (p + 2) % phi_count) for p in range(phi_count)])]
    ppermute x4, waiting for transfers between devices: 1.66 us -> 2.21 us  [body(): lax.ppermute(x, 'phi', [(p, (p + 2) % phi_count) for p in range(phi_count)])]
    pallas_call x1, Pallas kernels: 0.9 us -> 0.36 us  [body(): pl.pallas_call(lambda *refs: table_kernel((wide, plain), *refs), out_shap...]
    ppermute x1, waiting for transfers between devices: 2.47 us -> 3.01 us  [body(): send_corner = lambda x: lax.ppermute(x, ('phi', 'row'), diagonal)]
  transfers between devices with their start and end apart: 10 -> 10, of which waited for: 5 -> 5; matrix products, arithmetic and copies ran while one was open for 0% -> 0% of each run, Pallas kernels for 42% -> 41%
where the time goes in v16:
time: 42.9 us; the launch traced here: 42.7 us
  Pallas kernels  25.7 us (60%)
  starting transfers between devices  9.2 us (21%)
  waiting for transfers between devices  6.99 us (16%)
  between operations  0.78 us (2%)
    pallas_call x2, Pallas kernels, last_step(): pl.pallas_call(kernel, out_shape=out_shape, in_specs=[smem] + [vmem] * (5...  11.8 us
    pallas_call x2, Pallas kernels, first_step(): pl.pallas_call(kernel, out_shape=[f32(FIELDS * own_cells + EXTRA, radius)...  11.7 us
    ppermute x4, starting transfers between devices, body(): lax.ppermute(x, 'phi', [(p, (p + 2) % phi_count) for p in range(phi_count)])  4.47 us
    ppermute x1, waiting for transfers between devices, body(): send_corner = lambda x: lax.ppermute(x, ('phi', 'row'), diagonal)  3.01 us
    ppermute x4, waiting for transfers between devices, body(): lax.ppermute(x, 'phi', [(p, (p + 2) % phi_count) for p in range(phi_count)])  2.21 us
    ppermute x4, starting transfers between devices, body(): lax.ppermute(x, 'phi', [(p, (p + 1) % phi_count) for p in range(phi_count)])  2.09 us
    pallas_call x1, Pallas kernels, body(): pl.pallas_call(edge_kernel, out_shape=f32(levels, EXTRA, 2 * LANES), in_s...  1.74 us
    ppermute x1, waiting for transfers between devices, body(): send_side = lambda x: lax.ppermute(x, 'row', [(0, 1), (1, 0)])  1.51 us
  transfers between devices with their start and end apart: 10, of which 5 were waited for; matrix products, arithmetic and copies ran while one was open for 0% of the time, Pallas kernels for 41%

profile of v16, /device:TPU:0, one launch (start us, length us, event | category | flops | bytes accessed | tf_op | source)
XLA Modules:
  0.0 42.7 jit_solution(5518874642928233822)
XLA Ops:
  0.7 1.7 %edges.1.refs_3_ = f32[2,16,256]{2,1,0:T(8,128)} custom-call(s32[1]{0:T(128)} %bitcast.place.refs_0_, f32[2,32,256]{2,1,0:T(8,128)} %refs_0_.1, f32[2,2,32,256]{3,2,1,0:T(8,128)} %refs_1_.1, f32[2,2,32,256]{3,2,1,0:T(8,128)} %refs_2_.1, f32[2,128]{1,0:T(2,128)} %bitcast.3, s32[2,128]{1,0:T(2,128)} %bitcast.5), custom_call_target="tpu_custom_call" | custom-call | tf_op jit(solution)/shard_map/edges/pallas_call | solution.py:509
  2.4 0.1 pack.1
  2.6 0.0 copy-start.4
  2.6 0.0 copy-start.3
  2.6 0.5 %collective-permute-start.6 = (f32[160,256]{1,0:T(8,128)S(1)}, f32[160,256]{1,0:T(8,128)S(1)}, u32[]{:S(2)}, u32[]{:S(2)}) collective-permute-start(f32[160,256]{1,0:T(8,128)S(1)} %get-tuple-element.27.own), channel_id=1, source_target_pairs={{0,2},{2,4},{4,6},{6,8},{8,10},{10,12},{12,14},{14,16},{16,18},{18... | collective-permute-start | bytes 491528 | tf_op jit(solution)/shard_map/ppermute | solution.py:499
  3.1 2.6 %collective-permute-start.7 = (f32[200,128]{1,0:T(8,128)S(1)}, f32[200,128]{1,0:T(8,128)S(1)}, u32[]{:S(2)}, u32[]{:S(2)}) collective-permute-start(f32[200,128]{1,0:T(8,128)S(1)} %get-tuple-element.28), channel_id=1, source_target_pairs={{0,4},{2,6},{4,8},{6,10},{8,12},{10,14},{12,16},{14,18},{16,20},{1... | collective-permute-start | bytes 307208 | tf_op jit(solution)/shard_map/ppermute | solution.py:500
  5.7 1.5 %collective-permute-start = (f32[2,16,256]{2,1,0:T(8,128)}, f32[2,16,256]{2,1,0:T(8,128)S(1)}, u32[]{:S(2)}, u32[]{:S(2)}) collective-permute-start(f32[2,16,256]{2,1,0:T(8,128)} %edges.1.refs_3_), channel_id=1, source_target_pairs={{0,1},{1,0},{2,3},{3,2},{4,5},{5,4},{6,7},{7,6},{8,9},{9,8},{10,11... | collective-permute-start | bytes 98312 | tf_op jit(solution)/shard_map/ppermute | solution.py:504
  7.2 1.1 %collective-permute-start.3 = (f32[2,16,256]{2,1,0:T(8,128)}, f32[2,16,256]{2,1,0:T(8,128)S(1)}, u32[]{:S(2)}, u32[]{:S(2)}) collective-permute-start(f32[2,16,256]{2,1,0:T(8,128)} %edges.1.refs_3_), channel_id=1, source_target_pairs={{0,3},{1,2},{2,5},{3,4},{4,7},{5,6},{6,9},{7,8},{8,11},{9,10},{10,... | collective-permute-start | bytes 98312 | tf_op jit(solution)/shard_map/ppermute | solution.py:503
  8.3 1.5 %collective-permute-done.refs_1_.side = f32[2,16,256]{2,1,0:T(8,128)S(1)} collective-permute-done((f32[2,16,256]{2,1,0:T(8,128)}, f32[2,16,256]{2,1,0:T(8,128)S(1)}, u32[]{:S(2)}, u32[]{:S(2)}) %collective-permute-start) | collective-permute-done | bytes 32800 | tf_op jit(solution)/shard_map/ppermute | solution.py:504
  9.8 0.4 tables.1
  10.2 0.5 %collective-permute-start.1 = (f32[160,256]{1,0:T(8,128)S(1)}, f32[160,256]{1,0:T(8,128)S(1)}, u32[]{:S(2)}, u32[]{:S(2)}) collective-permute-start(f32[160,256]{1,0:T(8,128)S(1)} %get-tuple-element.20.own), channel_id=1, source_target_pairs={{0,2},{2,4},{4,6},{6,8},{8,10},{10,12},{12,14},{14,16},{16,18},{18... | collective-permute-start | bytes 491528 | tf_op jit(solution)/shard_map/ppermute | solution.py:499
  10.7 1.3 %collective-permute-start.2 = (f32[200,128]{1,0:T(8,128)S(1)}, f32[200,128]{1,0:T(8,128)S(1)}, u32[]{:S(2)}, u32[]{:S(2)}) collective-permute-start(f32[200,128]{1,0:T(8,128)S(1)} %get-tuple-element.21), channel_id=1, source_target_pairs={{0,4},{2,6},{4,8},{6,10},{8,12},{10,14},{12,16},{14,18},{16,20},{1... | collective-permute-start | bytes 307208 | tf_op jit(solution)/shard_map/ppermute | solution.py:500
  12.0 3.0 %collective-permute-done.3.corner = f32[2,16,256]{2,1,0:T(8,128)S(1)} collective-permute-done((f32[2,16,256]{2,1,0:T(8,128)}, f32[2,16,256]{2,1,0:T(8,128)S(1)}, u32[]{:S(2)}, u32[]{:S(2)}) %collective-permute-start.3) | collective-permute-done | bytes 32800 | tf_op jit(solution)/shard_map/ppermute | solution.py:503
  15.0 5.9 %first_step.3 = (f32[176,256]{1,0:T(8,128)S(1)}, f32[200,128]{1,0:T(8,128)S(1)}) custom-call(s32[1]{0:T(128)} %bitcast.place.refs_0_, f32[160,256]{1,0:T(8,128)S(1)} %get-tuple-element.27.own, f32[160,256]{1,0:T(8,128)S(1)} %collective-permute-done.6.near, f32[200,128]{1,0:T(8,128)S(1)} %collective-permute-done.7.far, ...), custom_call_target="tpu_custom_call" | custom-call | flops 8999999488 | bytes 29000000 | tf_op jit(solution)/shard_map/first_step/pallas_call | solution.py:430
  20.9 0.1 collective-permute-start.8
  20.9 0.1 collective-permute-start.9
  21.0 5.9 %first_step.2 = (f32[176,256]{1,0:T(8,128)S(1)}, f32[200,128]{1,0:T(8,128)S(1)}) custom-call(s32[1]{0:T(128)} %bitcast.place.refs_0_, f32[160,256]{1,0:T(8,128)S(1)} %get-tuple-element.20.own, f32[160,256]{1,0:T(8,128)S(1)} %collective-permute-done.1.near, f32[200,128]{1,0:T(8,128)S(1)} %collective-permute-done.2.far, ...), custom_call_target="tpu_custom_call" | custom-call | flops 8999999488 | bytes 29000000 | tf_op jit(solution)/shard_map/first_step/pallas_call | solution.py:430
  26.9 1.0 %collective-permute-start.4 = (f32[176,256]{1,0:T(8,128)S(1)}, f32[176,256]{1,0:T(8,128)S(1)}, u32[]{:S(2)}, u32[]{:S(2)}) collective-permute-start(f32[176,256]{1,0:T(8,128)S(1)} %get-tuple-element.23.own), channel_id=1, source_target_pairs={{0,2},{2,4},{4,6},{6,8},{8,10},{10,12},{12,14},{14,16},{16,18},{18... | collective-permute-start | bytes 540680 | tf_op jit(solution)/shard_map/ppermute | solution.py:499
  27.9 0.5 %collective-permute-start.5 = (f32[200,128]{1,0:T(8,128)S(1)}, f32[200,128]{1,0:T(8,128)S(1)}, u32[]{:S(2)}, u32[]{:S(2)}) collective-permute-start(f32[200,128]{1,0:T(8,128)S(1)} %get-tuple-element.24), channel_id=1, source_target_pairs={{0,4},{2,6},{4,8},{6,10},{8,12},{10,14},{12,16},{14,18},{16,20},{1... | collective-permute-start | bytes 307208 | tf_op jit(solution)/shard_map/ppermute | solution.py:500
  28.4 0.9 %collective-permute-done.9.far = f32[200,128]{1,0:T(8,128)S(1)} collective-permute-done((f32[200,128]{1,0:T(8,128)S(1)}, f32[200,128]{1,0:T(8,128)S(1)}, u32[]{:S(2)}, u32[]{:S(2)}) %collective-permute-start.9) | collective-permute-done | bytes 102432 | tf_op jit(solution)/shard_map/ppermute | solution.py:500
  29.4 0.3 collective-permute-done.8.near
  29.6 5.5 %last_step.2.rest_0_ = f32[160,256]{1,0:T(8,128)S(1)} custom-call(s32[1]{0:T(128)} %bitcast.place.refs_0_, f32[176,256]{1,0:T(8,128)S(1)} %get-tuple-element.29.own, f32[176,256]{1,0:T(8,128)S(1)} %collective-permute-done.8.near, f32[200,128]{1,0:T(8,128)S(1)} %collective-permute-done.9.far, f32[320,128]{1,0:T(8,128)S(1)} %get-tuple-element.25.spin, ...), custom_call_target="tpu_custom_call" | custom-call | flops 8999999488 | bytes 29000000 | tf_op jit(solution)/shard_map/last_step/pallas_call | solution.py:473
  35.2 1.3 %collective-permute-done.5.far = f32[200,128]{1,0:T(8,128)S(1)} collective-permute-done((f32[200,128]{1,0:T(8,128)S(1)}, f32[200,128]{1,0:T(8,128)S(1)}, u32[]{:S(2)}, u32[]{:S(2)}) %collective-permute-start.5) | collective-permute-done | bytes 102432 | tf_op jit(solution)/shard_map/ppermute | solution.py:500
  36.4 6.3 %last_step.3 = (f32[2,32,256]{2,1,0:T(8,128)}, f32[2,2,32,256]{3,2,1,0:T(8,128)}, f32[2,2,32,256]{3,2,1,0:T(8,128)}) custom-call(s32[1]{0:T(128)} %bitcast.place.refs_0_, f32[176,256]{1,0:T(8,128)S(1)} %get-tuple-element.23.own, f32[176,256]{1,0:T(8,128)S(1)} %collective-permute-done.4.near, f32[200,128]{1,0:T(8,128)S(1)} %collective-permute-done.5.far, ...), custom_call_target="tpu_custom_call" | custom-call | flops 8999999488 | bytes 29000000 | tf_op jit(solution)/shard_map/last_step/pallas_call | solution.py:473
  (13 shorter events, 0.0 us)
Async XLA Ops:
  0.6 1.8 %copy-start = (f32[2,2,32,256]{3,2,1,0:T(8,128)S(1)}, f32[2,2,32,256]{3,2,1,0:T(8,128)}, u32[]{:S(2)}) copy-start(f32[2,2,32,256]{3,2,1,0:T(8,128)} %refs_1_.1) | copy-start | bytes 393220
  0.6 1.8 %copy-start.1 = (f32[2,2,32,256]{3,2,1,0:T(8,128)S(1)}, f32[2,2,32,256]{3,2,1,0:T(8,128)}, u32[]{:S(2)}) copy-start(f32[2,2,32,256]{3,2,1,0:T(8,128)} %refs_2_.1) | copy-start | bytes 393220
  0.7 1.8 %copy-start.2 = (f32[2,32,256]{2,1,0:T(8,128)S(1)}, f32[2,32,256]{2,1,0:T(8,128)}, u32[]{:S(2)}) copy-start(f32[2,32,256]{2,1,0:T(8,128)} %refs_0_.1) | copy-start | bytes 196612
  2.6 7.3 %copy-start.4 = (s32[256]{0:T(256)S(1)}, s32[256]{0:T(256)}, u32[]{:S(2)}) copy-start(s32[256]{0:T(256)} %param.9) | copy-start | bytes 3076
  2.6 7.3 %copy-start.3 = (f32[256]{0:T(256)S(1)}, f32[256]{0:T(256)}, u32[]{:S(2)}) copy-start(f32[256]{0:T(256)} %param.8) | copy-start | bytes 3076
  2.6 12.4 %collective-permute-start.6 = (f32[160,256]{1,0:T(8,128)S(1)}, f32[160,256]{1,0:T(8,128)S(1)}, u32[]{:S(2)}, u32[]{:S(2)}) collective-permute-start(f32[160,256]{1,0:T(8,128)S(1)} %get-tuple-element.27.own), channel_id=1, source_target_pairs={{0,2},{2,4},{4,6},{6,8},{8,10},{10,12},{12,14},{14,16},{16,18},{18... | collective-permute-start | bytes 491528 | tf_op jit(solution)/shard_map/ppermute | solution.py:499
  3.1 11.9 %collective-permute-start.7 = (f32[200,128]{1,0:T(8,128)S(1)}, f32[200,128]{1,0:T(8,128)S(1)}, u32[]{:S(2)}, u32[]{:S(2)}) collective-permute-start(f32[200,128]{1,0:T(8,128)S(1)} %get-tuple-element.28), channel_id=1, source_target_pairs={{0,4},{2,6},{4,8},{6,10},{8,12},{10,14},{12,16},{14,18},{16,20},{1... | collective-permute-start | bytes 307208 | tf_op jit(solution)/shard_map/ppermute | solution.py:500
  5.7 4.2 %collective-permute-start = (f32[2,16,256]{2,1,0:T(8,128)}, f32[2,16,256]{2,1,0:T(8,128)S(1)}, u32[]{:S(2)}, u32[]{:S(2)}) collective-permute-start(f32[2,16,256]{2,1,0:T(8,128)} %edges.1.refs_3_), channel_id=1, source_target_pairs={{0,1},{1,0},{2,3},{3,2},{4,5},{5,4},{6,7},{7,6},{8,9},{9,8},{10,11... | collective-permute-start | bytes 98312 | tf_op jit(solution)/shard_map/ppermute | solution.py:504
  7.2 7.8 %collective-permute-start.3 = (f32[2,16,256]{2,1,0:T(8,128)}, f32[2,16,256]{2,1,0:T(8,128)S(1)}, u32[]{:S(2)}, u32[]{:S(2)}) collective-permute-start(f32[2,16,256]{2,1,0:T(8,128)} %edges.1.refs_3_), channel_id=1, source_target_pairs={{0,3},{1,2},{2,5},{3,4},{4,7},{5,6},{6,9},{7,8},{8,11},{9,10},{10,... | collective-permute-start | bytes 98312 | tf_op jit(solution)/shard_map/ppermute | solution.py:503
  10.2 10.8 %collective-permute-start.1 = (f32[160,256]{1,0:T(8,128)S(1)}, f32[160,256]{1,0:T(8,128)S(1)}, u32[]{:S(2)}, u32[]{:S(2)}) collective-permute-start(f32[160,256]{1,0:T(8,128)S(1)} %get-tuple-element.20.own), channel_id=1, source_target_pairs={{0,2},{2,4},{4,6},{6,8},{8,10},{10,12},{12,14},{14,16},{16,18},{18... | collective-permute-start | bytes 491528 | tf_op jit(solution)/shard_map/ppermute | solution.py:499
  10.7 10.3 %collective-permute-start.2 = (f32[200,128]{1,0:T(8,128)S(1)}, f32[200,128]{1,0:T(8,128)S(1)}, u32[]{:S(2)}, u32[]{:S(2)}) collective-permute-start(f32[200,128]{1,0:T(8,128)S(1)} %get-tuple-element.21), channel_id=1, source_target_pairs={{0,4},{2,6},{4,8},{6,10},{8,12},{10,14},{12,16},{14,18},{16,20},{1... | collective-permute-start | bytes 307208 | tf_op jit(solution)/shard_map/ppermute | solution.py:500
  20.9 8.8 %collective-permute-start.8 = (f32[176,256]{1,0:T(8,128)S(1)}, f32[176,256]{1,0:T(8,128)S(1)}, u32[]{:S(2)}, u32[]{:S(2)}) collective-permute-start(f32[176,256]{1,0:T(8,128)S(1)} %get-tuple-element.29.own), channel_id=1, source_target_pairs={{0,2},{2,4},{4,6},{6,8},{8,10},{10,12},{12,14},{14,16},{16,18},{18... | collective-permute-start | bytes 540680 | tf_op jit(solution)/shard_map/ppermute | solution.py:499
  20.9 8.4 %collective-permute-start.9 = (f32[200,128]{1,0:T(8,128)S(1)}, f32[200,128]{1,0:T(8,128)S(1)}, u32[]{:S(2)}, u32[]{:S(2)}) collective-permute-start(f32[200,128]{1,0:T(8,128)S(1)} %get-tuple-element.30), channel_id=1, source_target_pairs={{0,4},{2,6},{4,8},{6,10},{8,12},{10,14},{12,16},{14,18},{16,20},{1... | collective-permute-start | bytes 307208 | tf_op jit(solution)/shard_map/ppermute | solution.py:500
  26.9 9.6 %collective-permute-start.4 = (f32[176,256]{1,0:T(8,128)S(1)}, f32[176,256]{1,0:T(8,128)S(1)}, u32[]{:S(2)}, u32[]{:S(2)}) collective-permute-start(f32[176,256]{1,0:T(8,128)S(1)} %get-tuple-element.23.own), channel_id=1, source_target_pairs={{0,2},{2,4},{4,6},{6,8},{8,10},{10,12},{12,14},{14,16},{16,18},{18... | collective-permute-start | bytes 540680 | tf_op jit(solution)/shard_map/ppermute | solution.py:499
  27.9 8.5 %collective-permute-start.5 = (f32[200,128]{1,0:T(8,128)S(1)}, f32[200,128]{1,0:T(8,128)S(1)}, u32[]{:S(2)}, u32[]{:S(2)}) collective-permute-start(f32[200,128]{1,0:T(8,128)S(1)} %get-tuple-element.24), channel_id=1, source_target_pairs={{0,4},{2,6},{4,8},{6,10},{8,12},{10,14},{12,16},{14,18},{16,20},{1... | collective-permute-start | bytes 307208 | tf_op jit(solution)/shard_map/ppermute | solution.py:500

commit v17 on v16

--- a/solution.py
+++ b/solution.py
@@ -160,21 +160,34 @@
     return block
 
 
-def pack_far(far, near, own_cells, spare):
+def pack_far(far, near, own_cells):
     sublane = lax.broadcasted_iota(jnp.int32, (SUB, LANES), 0)
+    left = lax.broadcasted_iota(jnp.int32, (SUB, LANES), 1) < HALF
 
     def one(f, _):
         start = pl.multiple_of(f * own_cells, SUB)
-        base = pl.multiple_of(f * (own_cells + SUB), SUB)
         low = near[pl.ds(start, own_cells), 0:LANES]
         high = near[pl.ds(start + own_cells - 2 * SUB, 2 * SUB), LANES : 2 * LANES]
-        moved = pltpu.roll(high[0:SUB], spare, 0)
-        far[pl.ds(base, SUB), :] = jnp.where(sublane < spare, moved, low[0:SUB])
-        far[pl.ds(base + SUB, own_cells - SUB), :] = low[SUB:]
-        far[pl.ds(base + own_cells, SUB), :] = high[SUB:]
+        before, last = high[0:SUB], high[SUB:]
+        far[pl.ds(start, SUB), :] = jnp.where(left, low[0:SUB], pltpu.roll(last, HALF, 1))
+        third = pltpu.roll(pltpu.roll(before, 1, 0), HALF, 1)
+        fourth = pltpu.roll(last, 2, 0)
+        second = low[SUB : 2 * SUB]
+        mixed = jnp.where(sublane == 0, third, jnp.where(sublane == 1, fourth, second))
+        far[pl.ds(start + SUB, SUB), :] = jnp.where(left, second, mixed)
+        far[pl.ds(start + 2 * SUB, own_cells - 2 * SUB), :] = low[2 * SUB :]
         return 0
 
     lax.fori_loop(0, FIELDS, one, 0)
+
+
+def far_rows(far, start, own_cells):
+    left = lax.broadcasted_iota(jnp.int32, (SUB, LANES), 1) < HALF
+    first = far[pl.ds(start, SUB), :]
+    mixed = far[pl.ds(start + SUB, SUB), :]
+    before = pltpu.roll(pltpu.roll(mixed, SUB - 1, 0), HALF, 1)
+    last = jnp.where(left, pltpu.roll(first, HALF, 1), pltpu.roll(mixed, SUB - 2, 0))
+    return before, last
 
 
 def edge_kernel(place, density, momentum, magnetic, rotation, shifts, edge, ends, spin_in, shift_in, arrived):
@@ -209,7 +222,7 @@
             edge[level, :, side * LANES : (side + 1) * LANES] = jnp.where(on_low, turned[LANES - EXTRA :], turned[0:EXTRA])
 
 
-def pack_kernel(spare, levels, density, momentum, magnetic, edge, *outs):
+def pack_kernel(levels, density, momentum, magnetic, edge, *outs):
     del edge
     nears, fars = outs[:levels], outs[levels:]
     own_cells = density.shape[1]
@@ -217,7 +230,7 @@
         sources = [density.at[level]] + [x.at[k, level] for x in (momentum, magnetic) for k in range(2)]
         for f, x in enumerate(sources):
             nears[level][f * own_cells : (f + 1) * own_cells, :] = x[...]
-        pack_far(fars[level], nears[level], own_cells, spare)
+        pack_far(fars[level], nears[level], own_cells)
 
 
 class Blocks:
@@ -246,7 +259,7 @@
     for ref, scale in ((rotation, time_step), (shifts, 1.0)):
         along = lambda part: jnp.broadcast_to(ref[part : part + 1, :].astype(jnp.float32), (LANES, LANES)).T
         own.append([along(part) * scale for part in range(radius // LANES)])
-    for which, (n, radius, own_cells, total, spare, moved) in enumerate(plans):
+    for which, (n, radius, own_cells, total, moved) in enumerate(plans):
         spin, pick = outs[2 * which : 2 * which + 2]
         blocks = Blocks(place[0], n, radius, total, moved)
         for k in range(2):
@@ -262,7 +275,7 @@
 
 
 def step_kernel(plan, refs, write, scratch):
-    n, radius, own_cells, total, spare, moved = plan
+    n, radius, own_cells, total, moved = plan
     place, own, own_edge, near, near_edge, far, spin, pick = refs
     cells, stages, packed = scratch
     row = place[0]
@@ -277,20 +290,14 @@
 
     def bring(f, _):
         rows = pl.ds(pl.multiple_of(f * own_cells, SUB), own_cells)
-        start = pl.multiple_of(f * (own_cells + SUB), SUB)
+        start = pl.multiple_of(f * own_cells, SUB)
         for part in range(parts):
             columns = slice(part * LANES, (part + 1) * LANES)
             if part == 0:
                 top = far[pl.ds(start, own_cells), :]
             else:
-                top = jnp.concatenate(
-                    [
-                        jnp.zeros((own_cells - 2 * SUB, LANES), jnp.float32),
-                        pltpu.roll(far[pl.ds(start, SUB), :], SUB - spare, 0),
-                        far[pl.ds(start + own_cells, SUB), :],
-                    ],
-                    axis=0,
-                )
+                gap = jnp.zeros((own_cells - 2 * SUB, LANES), jnp.float32)
+                top = jnp.concatenate([gap, *far_rows(far, start, own_cells)], axis=0)
             fill = jnp.zeros((own_cells, LANES), jnp.float32)
             block = jnp.concatenate([top, near[rows, columns], own[rows, columns], fill], axis=0)
             cells[f, pl.ds(blocks.own_at + part * LANES, LANES), :] = block.T
@@ -358,8 +365,8 @@
 
 
 class ToMessage:
-    def __init__(self, near, far, own_cells, spare):
-        self.near, self.far, self.own_cells, self.spare = near, far, own_cells, spare
+    def __init__(self, near, far, own_cells):
+        self.near, self.far, self.own_cells = near, far, own_cells
 
     def fields(self, columns, four, fifth):
         split = 4 * self.own_cells
@@ -372,7 +379,7 @@
         self.near[tail : tail + EXTRA, LANES : 2 * LANES] = second
 
     def end(self):
-        pack_far(self.far, self.near, self.own_cells, self.spare)
+        pack_far(self.far, self.near, self.own_cells)
 
 
 class ToBuffer:
@@ -421,15 +428,15 @@
 
 
 def first_step(plan, level, operands):
-    n, radius, own_cells, total, spare, moved = plan
+    n, radius, own_cells, total, moved = plan
 
     def kernel(place, own, near, far, side, corner, spin, pick, near_out, far_out, *scratch):
         refs = (place, own, side.at[level], near, corner.at[level], far, spin, pick)
-        step_kernel(plan, refs, ToMessage(near_out, far_out, own_cells, spare), scratch)
+        step_kernel(plan, refs, ToMessage(near_out, far_out, own_cells), scratch)
 
     return pl.pallas_call(
         kernel,
-        out_shape=[f32(FIELDS * own_cells + EXTRA, radius), f32(FIELDS * (own_cells + SUB), LANES)],
+        out_shape=[f32(FIELDS * own_cells + EXTRA, radius), f32(FIELDS * own_cells, LANES)],
         in_specs=[smem] + [vmem] * 7,
         out_specs=[vmem] * 2,
         scratch_shapes=step_scratch(n),
@@ -440,7 +447,7 @@
 
 
 def last_step(plan, level, operands, done, levels):
-    n, radius, own_cells, total, spare, moved = plan
+    n, radius, own_cells, total, moved = plan
     final = level == levels - 1
     tail = pl.ds(FIELDS * own_cells, EXTRA)
     buffer = f32(FIELDS * own_cells, radius)
@@ -489,10 +496,9 @@
     total = radius * row_count
     parts = radius // LANES
     n = radius // SLOTS
-    need = [max(shift_bound(part * LANES, total) + REACH - own_cells, 0) for part in range(parts)]
-    spare = own_cells - need[0]
+    need = [max(shift_bound(k * HALF, total) + REACH - own_cells, 0) for k in range(radius // HALF)]
     assert row_count == 2 and radius == 2 * LANES and own_cells == HALF // 2
-    assert 0 < need[0] < own_cells and need[1] <= SUB + spare and spare <= SUB
+    assert need[0] <= own_cells and need[1] <= own_cells - SUB - 2 and need[2] <= SUB + 1 and need[3] <= 1
 
     row = lax.axis_index("row")
     place = jnp.reshape(row, (1,)).astype(jnp.int32)
@@ -505,7 +511,7 @@
 
     spins, turns = rotation.reshape(parts, LANES), shifts.reshape(parts, LANES)
     near_message = f32(FIELDS * own_cells, radius)
-    far_message = f32(FIELDS * (own_cells + SUB), LANES)
+    far_message = f32(FIELDS * own_cells, LANES)
     edge = pl.pallas_call(
         edge_kernel,
         out_shape=f32(levels, EXTRA, 2 * LANES),
@@ -521,7 +527,7 @@
         name="edges",
     )(place, density, momentum, magnetic, spins, turns)
     packed = pl.pallas_call(
-        lambda *refs: pack_kernel(spare, levels, *refs),
+        lambda *refs: pack_kernel(levels, *refs),
         out_shape=[near_message] * levels + [far_message] * levels,
         in_specs=[vmem] * 3 + [pl.BlockSpec(memory_space=pl.ANY)],
         out_specs=[vmem] * (2 * levels),
@@ -532,8 +538,8 @@
     owns, fars = packed[:levels], packed[levels:]
     side = send_side(edge)
     corner = send_corner(edge)
-    wide = (n + 1, radius, own_cells, total, spare, EXTRA)
-    plain = (n, radius, own_cells, total, spare, 0)
+    wide = (n + 1, radius, own_cells, total, EXTRA)
+    plain = (n, radius, own_cells, total, 0)
     i32 = jax.ShapeDtypeStruct((TALL * SUB, LANES), jnp.int32)
     tables = pl.pallas_call(
         lambda *refs: table_kernel((wide, plain), *refs),

time: 42.9 us -> 43.8 us (1.021)
  Pallas kernels: 25.7 us -> 27.9 us
  waiting for transfers between devices: 6.99 us -> 5.54 us
    pallas_call x2, Pallas kernels: 11.7 us -> 12.8 us  [first_step(): pl.pallas_call(kernel, out_shape=[f32(FIELDS * own_cells + EXTRA, radius)...]
    ppermute x4, waiting for transfers between devices: 2.21 us -> 1.36 us  [body(): lax.ppermute(x, 'phi', [(p, (p + 2) % phi_count) for p in range(phi_count)])]
    pallas_call x1, Pallas kernels: 0.1 us -> 0.73 us  [body(): pl.pallas_call(lambda *refs: pack_kernel(levels, *refs), out_shape=[near_...]
    pallas_call x2, Pallas kernels: 11.8 us -> 12.3 us  [last_step(): pl.pallas_call(kernel, out_shape=out_shape, in_specs=[smem] + [vmem] * (5...]
  transfers between devices with their start and end apart: 10 -> 10, of which waited for: 5 -> 3; matrix products, arithmetic and copies ran while one was open for 0% -> 0% of each run, Pallas kernels for 41% -> 43%
where the time goes in v17:
time: 43.8 us; the launch traced here: 43.7 us
  Pallas kernels  27.9 us (64%)
  starting transfers between devices  9.5 us (22%)
  waiting for transfers between devices  5.54 us (13%)
  between operations  0.72 us (2%)
    pallas_call x2, Pallas kernels, first_step(): pl.pallas_call(kernel, out_shape=[f32(FIELDS * own_cells + EXTRA, radius)...  12.8 us
    pallas_call x2, Pallas kernels, last_step(): pl.pallas_call(kernel, out_shape=out_shape, in_specs=[smem] + [vmem] * (5...  12.3 us
    ppermute x4, starting transfers between devices, body(): lax.ppermute(x, 'phi', [(p, (p + 2) % phi_count) for p in range(phi_count)])  4.86 us
    ppermute x1, waiting for transfers between devices, body(): send_corner = lambda x: lax.ppermute(x, ('phi', 'row'), diagonal)  2.65 us
    ppermute x4, starting transfers between devices, body(): lax.ppermute(x, 'phi', [(p, (p + 1) % phi_count) for p in range(phi_count)])  2 us
    pallas_call x1, Pallas kernels, body(): pl.pallas_call(edge_kernel, out_shape=f32(levels, EXTRA, 2 * LANES), in_s...  1.74 us
    ppermute x1, waiting for transfers between devices, body(): send_side = lambda x: lax.ppermute(x, 'row', [(0, 1), (1, 0)])  1.51 us
    ppermute x1, starting transfers between devices, body(): send_side = lambda x: lax.ppermute(x, 'row', [(0, 1), (1, 0)])  1.49 us
  transfers between devices with their start and end apart: 10, of which 3 were waited for; matrix products, arithmetic and copies ran while one was open for 0% of the time, Pallas kernels for 43%

profile of v17, /device:TPU:0, one launch (start us, length us, event | category | flops | bytes accessed | tf_op | source)
XLA Modules:
  0.0 43.7 jit_solution(17334862764945329054)
XLA Ops:
  0.7 1.7 %edges.1.refs_3_ = f32[2,16,256]{2,1,0:T(8,128)} custom-call(s32[1]{0:T(128)} %bitcast.place.refs_0_, f32[2,32,256]{2,1,0:T(8,128)} %refs_0_.1, f32[2,2,32,256]{3,2,1,0:T(8,128)} %refs_1_.1, f32[2,2,32,256]{3,2,1,0:T(8,128)} %refs_2_.1, f32[2,128]{1,0:T(2,128)} %bitcast.3, s32[2,128]{1,0:T(2,128)} %bitcast.5), custom_call_target="tpu_custom_call" | custom-call | tf_op jit(solution)/shard_map/edges/pallas_call | solution.py:515
  2.4 0.7 %pack.1 = (f32[160,256]{1,0:T(8,128)S(1)}, f32[160,256]{1,0:T(8,128)S(1)}, f32[160,128]{1,0:T(8,128)S(1)}, f32[160,128]{1,0:T(8,128)S(1)}) custom-call(f32[2,32,256]{2,1,0:T(8,128)S(1)} %copy-done.2, f32[2,2,32,256]{3,2,1,0:T(8,128)S(1)} %copy-done, f32[2,2,32,256]{3,2,1,0:T(8,128)S(1)} %copy-done.1, f32[2,16,256]{2,1,0:T(8,128)} %edges.1.refs_3_), custom_call_target="tpu_custom_call" | custom-call | flops 8999999488 | bytes 29000000 | tf_op jit(solution)/shard_map/pack/pallas_call | solution.py:529
  3.2 0.5 %collective-permute-start.6 = (f32[160,256]{1,0:T(8,128)S(1)}, f32[160,256]{1,0:T(8,128)S(1)}, u32[]{:S(2)}, u32[]{:S(2)}) collective-permute-start(f32[160,256]{1,0:T(8,128)S(1)} %get-tuple-element.27.own), channel_id=1, source_target_pairs={{0,2},{2,4},{4,6},{6,8},{8,10},{10,12},{12,14},{14,16},{16,18},{18... | collective-permute-start | bytes 491528 | tf_op jit(solution)/shard_map/ppermute | solution.py:505
  3.7 2.6 %collective-permute-start.7 = (f32[160,128]{1,0:T(8,128)S(1)}, f32[160,128]{1,0:T(8,128)S(1)}, u32[]{:S(2)}, u32[]{:S(2)}) collective-permute-start(f32[160,128]{1,0:T(8,128)S(1)} %get-tuple-element.28), channel_id=1, source_target_pairs={{0,4},{2,6},{4,8},{6,10},{8,12},{10,14},{12,16},{14,18},{16,20},{1... | collective-permute-start | bytes 245768 | tf_op jit(solution)/shard_map/ppermute | solution.py:506
  6.2 1.5 %collective-permute-start = (f32[2,16,256]{2,1,0:T(8,128)}, f32[2,16,256]{2,1,0:T(8,128)S(1)}, u32[]{:S(2)}, u32[]{:S(2)}) collective-permute-start(f32[2,16,256]{2,1,0:T(8,128)} %edges.1.refs_3_), channel_id=1, source_target_pairs={{0,1},{1,0},{2,3},{3,2},{4,5},{5,4},{6,7},{7,6},{8,9},{9,8},{10,11... | collective-permute-start | bytes 98312 | tf_op jit(solution)/shard_map/ppermute | solution.py:510
  7.7 1.1 %collective-permute-start.3 = (f32[2,16,256]{2,1,0:T(8,128)}, f32[2,16,256]{2,1,0:T(8,128)S(1)}, u32[]{:S(2)}, u32[]{:S(2)}) collective-permute-start(f32[2,16,256]{2,1,0:T(8,128)} %edges.1.refs_3_), channel_id=1, source_target_pairs={{0,3},{1,2},{2,5},{3,4},{4,7},{5,6},{6,9},{7,8},{8,11},{9,10},{10,... | collective-permute-start | bytes 98312 | tf_op jit(solution)/shard_map/ppermute | solution.py:509
  8.9 1.5 %collective-permute-done.refs_1_.side = f32[2,16,256]{2,1,0:T(8,128)S(1)} collective-permute-done((f32[2,16,256]{2,1,0:T(8,128)}, f32[2,16,256]{2,1,0:T(8,128)S(1)}, u32[]{:S(2)}, u32[]{:S(2)}) %collective-permute-start) | collective-permute-done | bytes 32800 | tf_op jit(solution)/shard_map/ppermute | solution.py:510
  10.4 0.4 tables.1
  10.8 0.5 %collective-permute-start.1 = (f32[160,256]{1,0:T(8,128)S(1)}, f32[160,256]{1,0:T(8,128)S(1)}, u32[]{:S(2)}, u32[]{:S(2)}) collective-permute-start(f32[160,256]{1,0:T(8,128)S(1)} %get-tuple-element.20.own), channel_id=1, source_target_pairs={{0,2},{2,4},{4,6},{6,8},{8,10},{10,12},{12,14},{14,16},{16,18},{18... | collective-permute-start | bytes 491528 | tf_op jit(solution)/shard_map/ppermute | solution.py:505
  11.3 1.2 %collective-permute-start.2 = (f32[160,128]{1,0:T(8,128)S(1)}, f32[160,128]{1,0:T(8,128)S(1)}, u32[]{:S(2)}, u32[]{:S(2)}) collective-permute-start(f32[160,128]{1,0:T(8,128)S(1)} %get-tuple-element.21), channel_id=1, source_target_pairs={{0,4},{2,6},{4,8},{6,10},{8,12},{10,14},{12,16},{14,18},{16,20},{1... | collective-permute-start | bytes 245768 | tf_op jit(solution)/shard_map/ppermute | solution.py:506
  12.5 2.6 %collective-permute-done.3.corner = f32[2,16,256]{2,1,0:T(8,128)S(1)} collective-permute-done((f32[2,16,256]{2,1,0:T(8,128)}, f32[2,16,256]{2,1,0:T(8,128)S(1)}, u32[]{:S(2)}, u32[]{:S(2)}) %collective-permute-start.3) | collective-permute-done | bytes 32800 | tf_op jit(solution)/shard_map/ppermute | solution.py:509
  15.1 0.0 collective-permute-done.7.far
  15.1 0.0 collective-permute-done.6.near
  15.1 6.4 %first_step.3 = (f32[176,256]{1,0:T(8,128)S(1)}, f32[160,128]{1,0:T(8,128)S(1)}) custom-call(s32[1]{0:T(128)} %bitcast.place.refs_0_, f32[160,256]{1,0:T(8,128)S(1)} %get-tuple-element.27.own, f32[160,256]{1,0:T(8,128)S(1)} %collective-permute-done.6.near, f32[160,128]{1,0:T(8,128)S(1)} %collective-permute-done.7.far, ...), custom_call_target="tpu_custom_call" | custom-call | flops 8999999488 | bytes 29000000 | tf_op jit(solution)/shard_map/first_step/pallas_call | solution.py:437
  21.5 0.0 collective-permute-start.8
  21.6 0.1 collective-permute-start.9
  21.7 0.0 collective-permute-done.2.far
  21.7 6.4 %first_step.2 = (f32[176,256]{1,0:T(8,128)S(1)}, f32[160,128]{1,0:T(8,128)S(1)}) custom-call(s32[1]{0:T(128)} %bitcast.place.refs_0_, f32[160,256]{1,0:T(8,128)S(1)} %get-tuple-element.20.own, f32[160,256]{1,0:T(8,128)S(1)} %collective-permute-done.1.near, f32[160,128]{1,0:T(8,128)S(1)} %collective-permute-done.2.far, ...), custom_call_target="tpu_custom_call" | custom-call | flops 8999999488 | bytes 29000000 | tf_op jit(solution)/shard_map/first_step/pallas_call | solution.py:437
  28.1 1.0 %collective-permute-start.4 = (f32[176,256]{1,0:T(8,128)S(1)}, f32[176,256]{1,0:T(8,128)S(1)}, u32[]{:S(2)}, u32[]{:S(2)}) collective-permute-start(f32[176,256]{1,0:T(8,128)S(1)} %get-tuple-element.23.own), channel_id=1, source_target_pairs={{0,2},{2,4},{4,6},{6,8},{8,10},{10,12},{12,14},{14,16},{16,18},{18... | collective-permute-start | bytes 540680 | tf_op jit(solution)/shard_map/ppermute | solution.py:505
  29.1 1.0 %collective-permute-start.5 = (f32[160,128]{1,0:T(8,128)S(1)}, f32[160,128]{1,0:T(8,128)S(1)}, u32[]{:S(2)}, u32[]{:S(2)}) collective-permute-start(f32[160,128]{1,0:T(8,128)S(1)} %get-tuple-element.24), channel_id=1, source_target_pairs={{0,4},{2,6},{4,8},{6,10},{8,12},{10,14},{12,16},{14,18},{16,20},{1... | collective-permute-start | bytes 245768 | tf_op jit(solution)/shard_map/ppermute | solution.py:506
  30.1 0.0 collective-permute-done.8.near
  30.1 5.8 %last_step.2.rest_0_ = f32[160,256]{1,0:T(8,128)S(1)} custom-call(s32[1]{0:T(128)} %bitcast.place.refs_0_, f32[176,256]{1,0:T(8,128)S(1)} %get-tuple-element.29.own, f32[176,256]{1,0:T(8,128)S(1)} %collective-permute-done.8.near, f32[160,128]{1,0:T(8,128)S(1)} %collective-permute-done.9.far, f32[320,128]{1,0:T(8,128)S(1)} %get-tuple-element.25.spin, ...), custom_call_target="tpu_custom_call" | custom-call | flops 8999999488 | bytes 29000000 | tf_op jit(solution)/shard_map/last_step/pallas_call | solution.py:480
  35.8 1.4 %collective-permute-done.5.far = f32[160,128]{1,0:T(8,128)S(1)} collective-permute-done((f32[160,128]{1,0:T(8,128)S(1)}, f32[160,128]{1,0:T(8,128)S(1)}, u32[]{:S(2)}, u32[]{:S(2)}) %collective-permute-start.5) | collective-permute-done | bytes 81952 | tf_op jit(solution)/shard_map/ppermute | solution.py:506
  37.2 6.5 %last_step.3 = (f32[2,32,256]{2,1,0:T(8,128)}, f32[2,2,32,256]{3,2,1,0:T(8,128)}, f32[2,2,32,256]{3,2,1,0:T(8,128)}) custom-call(s32[1]{0:T(128)} %bitcast.place.refs_0_, f32[176,256]{1,0:T(8,128)S(1)} %get-tuple-element.23.own, f32[176,256]{1,0:T(8,128)S(1)} %collective-permute-done.4.near, f32[160,128]{1,0:T(8,128)S(1)} %collective-permute-done.5.far, ...), custom_call_target="tpu_custom_call" | custom-call | flops 8999999488 | bytes 29000000 | tf_op jit(solution)/shard_map/last_step/pallas_call | solution.py:480
  (13 shorter events, 0.0 us)
Async XLA Ops:
  0.6 1.8 %copy-start = (f32[2,2,32,256]{3,2,1,0:T(8,128)S(1)}, f32[2,2,32,256]{3,2,1,0:T(8,128)}, u32[]{:S(2)}) copy-start(f32[2,2,32,256]{3,2,1,0:T(8,128)} %refs_1_.1) | copy-start | bytes 393220
  0.6 1.8 %copy-start.1 = (f32[2,2,32,256]{3,2,1,0:T(8,128)S(1)}, f32[2,2,32,256]{3,2,1,0:T(8,128)}, u32[]{:S(2)}) copy-start(f32[2,2,32,256]{3,2,1,0:T(8,128)} %refs_2_.1) | copy-start | bytes 393220
  0.7 1.8 %copy-start.2 = (f32[2,32,256]{2,1,0:T(8,128)S(1)}, f32[2,32,256]{2,1,0:T(8,128)}, u32[]{:S(2)}) copy-start(f32[2,32,256]{2,1,0:T(8,128)} %refs_0_.1) | copy-start | bytes 196612
  3.2 7.2 %copy-start.4 = (s32[256]{0:T(256)S(1)}, s32[256]{0:T(256)}, u32[]{:S(2)}) copy-start(s32[256]{0:T(256)} %param.9) | copy-start | bytes 3076
  3.2 7.2 %copy-start.3 = (f32[256]{0:T(256)S(1)}, f32[256]{0:T(256)}, u32[]{:S(2)}) copy-start(f32[256]{0:T(256)} %param.8) | copy-start | bytes 3076
  3.2 12.0 %collective-permute-start.6 = (f32[160,256]{1,0:T(8,128)S(1)}, f32[160,256]{1,0:T(8,128)S(1)}, u32[]{:S(2)}, u32[]{:S(2)}) collective-permute-start(f32[160,256]{1,0:T(8,128)S(1)} %get-tuple-element.27.own), channel_id=1, source_target_pairs={{0,2},{2,4},{4,6},{6,8},{8,10},{10,12},{12,14},{14,16},{16,18},{18... | collective-permute-start | bytes 491528 | tf_op jit(solution)/shard_map/ppermute | solution.py:505
  3.7 11.5 %collective-permute-start.7 = (f32[160,128]{1,0:T(8,128)S(1)}, f32[160,128]{1,0:T(8,128)S(1)}, u32[]{:S(2)}, u32[]{:S(2)}) collective-permute-start(f32[160,128]{1,0:T(8,128)S(1)} %get-tuple-element.28), channel_id=1, source_target_pairs={{0,4},{2,6},{4,8},{6,10},{8,12},{10,14},{12,16},{14,18},{16,20},{1... | collective-permute-start | bytes 245768 | tf_op jit(solution)/shard_map/ppermute | solution.py:506
  6.2 4.2 %collective-permute-start = (f32[2,16,256]{2,1,0:T(8,128)}, f32[2,16,256]{2,1,0:T(8,128)S(1)}, u32[]{:S(2)}, u32[]{:S(2)}) collective-permute-start(f32[2,16,256]{2,1,0:T(8,128)} %edges.1.refs_3_), channel_id=1, source_target_pairs={{0,1},{1,0},{2,3},{3,2},{4,5},{5,4},{6,7},{7,6},{8,9},{9,8},{10,11... | collective-permute-start | bytes 98312 | tf_op jit(solution)/shard_map/ppermute | solution.py:510
  7.7 7.4 %collective-permute-start.3 = (f32[2,16,256]{2,1,0:T(8,128)}, f32[2,16,256]{2,1,0:T(8,128)S(1)}, u32[]{:S(2)}, u32[]{:S(2)}) collective-permute-start(f32[2,16,256]{2,1,0:T(8,128)} %edges.1.refs_3_), channel_id=1, source_target_pairs={{0,3},{1,2},{2,5},{3,4},{4,7},{5,6},{6,9},{7,8},{8,11},{9,10},{10,... | collective-permute-start | bytes 98312 | tf_op jit(solution)/shard_map/ppermute | solution.py:509
  10.8 10.9 %collective-permute-start.1 = (f32[160,256]{1,0:T(8,128)S(1)}, f32[160,256]{1,0:T(8,128)S(1)}, u32[]{:S(2)}, u32[]{:S(2)}) collective-permute-start(f32[160,256]{1,0:T(8,128)S(1)} %get-tuple-element.20.own), channel_id=1, source_target_pairs={{0,2},{2,4},{4,6},{6,8},{8,10},{10,12},{12,14},{14,16},{16,18},{18... | collective-permute-start | bytes 491528 | tf_op jit(solution)/shard_map/ppermute | solution.py:505
  11.3 10.4 %collective-permute-start.2 = (f32[160,128]{1,0:T(8,128)S(1)}, f32[160,128]{1,0:T(8,128)S(1)}, u32[]{:S(2)}, u32[]{:S(2)}) collective-permute-start(f32[160,128]{1,0:T(8,128)S(1)} %get-tuple-element.21), channel_id=1, source_target_pairs={{0,4},{2,6},{4,8},{6,10},{8,12},{10,14},{12,16},{14,18},{16,20},{1... | collective-permute-start | bytes 245768 | tf_op jit(solution)/shard_map/ppermute | solution.py:506
  21.5 8.5 %collective-permute-start.8 = (f32[176,256]{1,0:T(8,128)S(1)}, f32[176,256]{1,0:T(8,128)S(1)}, u32[]{:S(2)}, u32[]{:S(2)}) collective-permute-start(f32[176,256]{1,0:T(8,128)S(1)} %get-tuple-element.29.own), channel_id=1, source_target_pairs={{0,2},{2,4},{4,6},{6,8},{8,10},{10,12},{12,14},{14,16},{16,18},{18... | collective-permute-start | bytes 540680 | tf_op jit(solution)/shard_map/ppermute | solution.py:505
  21.6 8.5 %collective-permute-start.9 = (f32[160,128]{1,0:T(8,128)S(1)}, f32[160,128]{1,0:T(8,128)S(1)}, u32[]{:S(2)}, u32[]{:S(2)}) collective-permute-start(f32[160,128]{1,0:T(8,128)S(1)} %get-tuple-element.30), channel_id=1, source_target_pairs={{0,4},{2,6},{4,8},{6,10},{8,12},{10,14},{12,16},{14,18},{16,20},{1... | collective-permute-start | bytes 245768 | tf_op jit(solution)/shard_map/ppermute | solution.py:506
  28.1 9.1 %collective-permute-start.4 = (f32[176,256]{1,0:T(8,128)S(1)}, f32[176,256]{1,0:T(8,128)S(1)}, u32[]{:S(2)}, u32[]{:S(2)}) collective-permute-start(f32[176,256]{1,0:T(8,128)S(1)} %get-tuple-element.23.own), channel_id=1, source_target_pairs={{0,2},{2,4},{4,6},{6,8},{8,10},{10,12},{12,14},{14,16},{16,18},{18... | collective-permute-start | bytes 540680 | tf_op jit(solution)/shard_map/ppermute | solution.py:505
  29.1 8.1 %collective-permute-start.5 = (f32[160,128]{1,0:T(8,128)S(1)}, f32[160,128]{1,0:T(8,128)S(1)}, u32[]{:S(2)}, u32[]{:S(2)}) collective-permute-start(f32[160,128]{1,0:T(8,128)S(1)} %get-tuple-element.24), channel_id=1, source_target_pairs={{0,4},{2,6},{4,8},{6,10},{8,12},{10,14},{12,16},{14,18},{16,20},{1... | collective-permute-start | bytes 245768 | tf_op jit(solution)/shard_map/ppermute | solution.py:506

commit v18 on v17

--- a/solution.py
+++ b/solution.py
@@ -164,27 +164,24 @@
     sublane = lax.broadcasted_iota(jnp.int32, (SUB, LANES), 0)
     left = lax.broadcasted_iota(jnp.int32, (SUB, LANES), 1) < HALF
 
-    def one(f, _):
-        start = pl.multiple_of(f * own_cells, SUB)
-        low = near[pl.ds(start, own_cells), 0:LANES]
-        high = near[pl.ds(start + own_cells - 2 * SUB, 2 * SUB), LANES : 2 * LANES]
+    for f in range(FIELDS):
+        start = f * own_cells
+        low = near[start : start + own_cells, 0:LANES]
+        high = near[start + own_cells - 2 * SUB : start + own_cells, LANES : 2 * LANES]
         before, last = high[0:SUB], high[SUB:]
-        far[pl.ds(start, SUB), :] = jnp.where(left, low[0:SUB], pltpu.roll(last, HALF, 1))
+        far[start : start + SUB, :] = jnp.where(left, low[0:SUB], pltpu.roll(last, HALF, 1))
         third = pltpu.roll(pltpu.roll(before, 1, 0), HALF, 1)
         fourth = pltpu.roll(last, 2, 0)
         second = low[SUB : 2 * SUB]
         mixed = jnp.where(sublane == 0, third, jnp.where(sublane == 1, fourth, second))
-        far[pl.ds(start + SUB, SUB), :] = jnp.where(left, second, mixed)
-        far[pl.ds(start + 2 * SUB, own_cells - 2 * SUB), :] = low[2 * SUB :]
-        return 0
-
-    lax.fori_loop(0, FIELDS, one, 0)
-
-
-def far_rows(far, start, own_cells):
+        far[start + SUB : start + 2 * SUB, :] = jnp.where(left, second, mixed)
+        far[start + 2 * SUB : start + own_cells, :] = low[2 * SUB :]
+
+
+def far_rows(far, start):
     left = lax.broadcasted_iota(jnp.int32, (SUB, LANES), 1) < HALF
-    first = far[pl.ds(start, SUB), :]
-    mixed = far[pl.ds(start + SUB, SUB), :]
+    first = far[start : start + SUB, :]
+    mixed = far[start + SUB : start + 2 * SUB, :]
     before = pltpu.roll(pltpu.roll(mixed, SUB - 1, 0), HALF, 1)
     last = jnp.where(left, pltpu.roll(first, HALF, 1), pltpu.roll(mixed, SUB - 2, 0))
     return before, last
@@ -277,7 +274,7 @@
 def step_kernel(plan, refs, write, scratch):
     n, radius, own_cells, total, moved = plan
     place, own, own_edge, near, near_edge, far, spin, pick = refs
-    cells, stages, packed = scratch
+    cells, stages, packed, tops = scratch
     row = place[0]
     lane = lax.broadcasted_iota(jnp.int32, (SUB, LANES), 1)
     sublane = lax.broadcasted_iota(jnp.int32, (SUB, LANES), 0)
@@ -287,6 +284,9 @@
     parts = radius // LANES
 
     front = lax.broadcasted_iota(jnp.int32, (DEALT, LANES), 1) < HALF
+
+    for f in range(FIELDS):
+        tops[f] = jnp.concatenate(far_rows(far, f * own_cells), axis=0)
 
     def bring(f, _):
         rows = pl.ds(pl.multiple_of(f * own_cells, SUB), own_cells)
@@ -297,7 +297,7 @@
                 top = far[pl.ds(start, own_cells), :]
             else:
                 gap = jnp.zeros((own_cells - 2 * SUB, LANES), jnp.float32)
-                top = jnp.concatenate([gap, *far_rows(far, start, own_cells)], axis=0)
+                top = jnp.concatenate([gap, tops[f]], axis=0)
             fill = jnp.zeros((own_cells, LANES), jnp.float32)
             block = jnp.concatenate([top, near[rows, columns], own[rows, columns], fill], axis=0)
             cells[f, pl.ds(blocks.own_at + part * LANES, LANES), :] = block.T
@@ -417,6 +417,7 @@
         pltpu.VMEM((FIELDS, tall_of(n), LANES), jnp.float32),
         pltpu.VMEM((STAGES, FIELDS, TALL * SUB, LANES), jnp.float32),
         pltpu.VMEM((2, tall_of(n), LANES), jnp.float32),
+        pltpu.VMEM((FIELDS, 2 * SUB, LANES), jnp.float32),
     ]
 
 

time: 43.8 us -> 42.2 us (0.963)
  Pallas kernels: 27.9 us -> 26 us
    pallas_call x2, Pallas kernels: 12.8 us -> 11.8 us  [first_step(): pl.pallas_call(kernel, out_shape=[f32(FIELDS * own_cells + EXTRA, radius)...]
    pallas_call x1, Pallas kernels: 0.73 us -> 0.1 us  [body(): pl.pallas_call(lambda *refs: pack_kernel(levels, *refs), out_shape=[near_...]
    ppermute x4, waiting for transfers between devices: 0.01 us -> 0.48 us  [body(): lax.ppermute(x, 'phi', [(p, (p + 1) % phi_count) for p in range(phi_count)])]
  transfers between devices with their start and end apart: 10 -> 10, of which waited for: 3 -> 4; matrix products, arithmetic and copies ran while one was open for 0% -> 0% of each run, Pallas kernels for 43% -> 42%
where the time goes in v18:
time: 42.2 us; the launch traced here: 42 us
  Pallas kernels  26 us (62%)
  starting transfers between devices  9.58 us (23%)
  waiting for transfers between devices  5.69 us (13%)
  between operations  0.75 us (2%)
    pallas_call x2, Pallas kernels, last_step(): pl.pallas_call(kernel, out_shape=out_shape, in_specs=[smem] + [vmem] * (5...  12 us
    pallas_call x2, Pallas kernels, first_step(): pl.pallas_call(kernel, out_shape=[f32(FIELDS * own_cells + EXTRA, radius)...  11.8 us
    ppermute x4, starting transfers between devices, body(): lax.ppermute(x, 'phi', [(p, (p + 2) % phi_count) for p in range(phi_count)])  4.83 us
    ppermute x1, waiting for transfers between devices, body(): send_corner = lambda x: lax.ppermute(x, ('phi', 'row'), diagonal)  2.65 us
    ppermute x4, starting transfers between devices, body(): lax.ppermute(x, 'phi', [(p, (p + 1) % phi_count) for p in range(phi_count)])  2.11 us
    pallas_call x1, Pallas kernels, body(): pl.pallas_call(edge_kernel, out_shape=f32(levels, EXTRA, 2 * LANES), in_s...  1.74 us
    ppermute x1, waiting for transfers between devices, body(): send_side = lambda x: lax.ppermute(x, 'row', [(0, 1), (1, 0)])  1.51 us
    ppermute x1, starting transfers between devices, body(): send_side = lambda x: lax.ppermute(x, 'row', [(0, 1), (1, 0)])  1.49 us
  transfers between devices with their start and end apart: 10, of which 4 were waited for; matrix products, arithmetic and copies ran while one was open for 0% of the time, Pallas kernels for 42%

profile of v18, /device:TPU:0, one launch (start us, length us, event | category | flops | bytes accessed | tf_op | source)
XLA Modules:
  0.0 42.0 jit_solution(3751667987531095690)
XLA Ops:
  0.7 1.7 %edges.1.refs_3_ = f32[2,16,256]{2,1,0:T(8,128)} custom-call(s32[1]{0:T(128)} %bitcast.place.refs_0_, f32[2,32,256]{2,1,0:T(8,128)} %refs_0_.1, f32[2,2,32,256]{3,2,1,0:T(8,128)} %refs_1_.1, f32[2,2,32,256]{3,2,1,0:T(8,128)} %refs_2_.1, f32[2,128]{1,0:T(2,128)} %bitcast.3, s32[2,128]{1,0:T(2,128)} %bitcast.5), custom_call_target="tpu_custom_call" | custom-call | tf_op jit(solution)/shard_map/edges/pallas_call | solution.py:516
  2.4 0.1 pack.1
  2.5 0.0 copy-start.4
  2.6 0.0 copy-start.3
  2.6 0.5 %collective-permute-start.6 = (f32[160,256]{1,0:T(8,128)S(1)}, f32[160,256]{1,0:T(8,128)S(1)}, u32[]{:S(2)}, u32[]{:S(2)}) collective-permute-start(f32[160,256]{1,0:T(8,128)S(1)} %get-tuple-element.27.own), channel_id=1, source_target_pairs={{0,2},{2,4},{4,6},{6,8},{8,10},{10,12},{12,14},{14,16},{16,18},{18... | collective-permute-start | bytes 491528 | tf_op jit(solution)/shard_map/ppermute | solution.py:506
  3.1 2.6 %collective-permute-start.7 = (f32[160,128]{1,0:T(8,128)S(1)}, f32[160,128]{1,0:T(8,128)S(1)}, u32[]{:S(2)}, u32[]{:S(2)}) collective-permute-start(f32[160,128]{1,0:T(8,128)S(1)} %get-tuple-element.28), channel_id=1, source_target_pairs={{0,4},{2,6},{4,8},{6,10},{8,12},{10,14},{12,16},{14,18},{16,20},{1... | collective-permute-start | bytes 245768 | tf_op jit(solution)/shard_map/ppermute | solution.py:507
  5.7 1.5 %collective-permute-start = (f32[2,16,256]{2,1,0:T(8,128)}, f32[2,16,256]{2,1,0:T(8,128)S(1)}, u32[]{:S(2)}, u32[]{:S(2)}) collective-permute-start(f32[2,16,256]{2,1,0:T(8,128)} %edges.1.refs_3_), channel_id=1, source_target_pairs={{0,1},{1,0},{2,3},{3,2},{4,5},{5,4},{6,7},{7,6},{8,9},{9,8},{10,11... | collective-permute-start | bytes 98312 | tf_op jit(solution)/shard_map/ppermute | solution.py:511
  7.2 1.1 %collective-permute-start.3 = (f32[2,16,256]{2,1,0:T(8,128)}, f32[2,16,256]{2,1,0:T(8,128)S(1)}, u32[]{:S(2)}, u32[]{:S(2)}) collective-permute-start(f32[2,16,256]{2,1,0:T(8,128)} %edges.1.refs_3_), channel_id=1, source_target_pairs={{0,3},{1,2},{2,5},{3,4},{4,7},{5,6},{6,9},{7,8},{8,11},{9,10},{10,... | collective-permute-start | bytes 98312 | tf_op jit(solution)/shard_map/ppermute | solution.py:510
  8.3 1.5 %collective-permute-done.refs_1_.side = f32[2,16,256]{2,1,0:T(8,128)S(1)} collective-permute-done((f32[2,16,256]{2,1,0:T(8,128)}, f32[2,16,256]{2,1,0:T(8,128)S(1)}, u32[]{:S(2)}, u32[]{:S(2)}) %collective-permute-start) | collective-permute-done | bytes 32800 | tf_op jit(solution)/shard_map/ppermute | solution.py:511
  9.8 0.4 tables.1
  10.2 0.5 %collective-permute-start.1 = (f32[160,256]{1,0:T(8,128)S(1)}, f32[160,256]{1,0:T(8,128)S(1)}, u32[]{:S(2)}, u32[]{:S(2)}) collective-permute-start(f32[160,256]{1,0:T(8,128)S(1)} %get-tuple-element.20.own), channel_id=1, source_target_pairs={{0,2},{2,4},{4,6},{6,8},{8,10},{10,12},{12,14},{14,16},{16,18},{18... | collective-permute-start | bytes 491528 | tf_op jit(solution)/shard_map/ppermute | solution.py:506
  10.7 1.2 %collective-permute-start.2 = (f32[160,128]{1,0:T(8,128)S(1)}, f32[160,128]{1,0:T(8,128)S(1)}, u32[]{:S(2)}, u32[]{:S(2)}) collective-permute-start(f32[160,128]{1,0:T(8,128)S(1)} %get-tuple-element.21), channel_id=1, source_target_pairs={{0,4},{2,6},{4,8},{6,10},{8,12},{10,14},{12,16},{14,18},{16,20},{1... | collective-permute-start | bytes 245768 | tf_op jit(solution)/shard_map/ppermute | solution.py:507
  11.9 2.6 %collective-permute-done.3.corner = f32[2,16,256]{2,1,0:T(8,128)S(1)} collective-permute-done((f32[2,16,256]{2,1,0:T(8,128)}, f32[2,16,256]{2,1,0:T(8,128)S(1)}, u32[]{:S(2)}, u32[]{:S(2)}) %collective-permute-start.3) | collective-permute-done | bytes 32800 | tf_op jit(solution)/shard_map/ppermute | solution.py:510
  14.6 5.9 %first_step.3 = (f32[176,256]{1,0:T(8,128)S(1)}, f32[160,128]{1,0:T(8,128)S(1)}) custom-call(s32[1]{0:T(128)} %bitcast.place.refs_0_, f32[160,256]{1,0:T(8,128)S(1)} %get-tuple-element.27.own, f32[160,256]{1,0:T(8,128)S(1)} %collective-permute-done.6.near, f32[160,128]{1,0:T(8,128)S(1)} %collective-permute-done.7.far, ...), custom_call_target="tpu_custom_call" | custom-call | flops 8999999488 | bytes 29000000 | tf_op jit(solution)/shard_map/first_step/pallas_call | solution.py:438
  20.5 0.1 collective-permute-start.8
  20.5 0.1 collective-permute-start.9
  20.6 5.9 %first_step.2 = (f32[176,256]{1,0:T(8,128)S(1)}, f32[160,128]{1,0:T(8,128)S(1)}) custom-call(s32[1]{0:T(128)} %bitcast.place.refs_0_, f32[160,256]{1,0:T(8,128)S(1)} %get-tuple-element.20.own, f32[160,256]{1,0:T(8,128)S(1)} %collective-permute-done.1.near, f32[160,128]{1,0:T(8,128)S(1)} %collective-permute-done.2.far, ...), custom_call_target="tpu_custom_call" | custom-call | flops 8999999488 | bytes 29000000 | tf_op jit(solution)/shard_map/first_step/pallas_call | solution.py:438
  26.5 1.1 %collective-permute-start.4 = (f32[176,256]{1,0:T(8,128)S(1)}, f32[176,256]{1,0:T(8,128)S(1)}, u32[]{:S(2)}, u32[]{:S(2)}) collective-permute-start(f32[176,256]{1,0:T(8,128)S(1)} %get-tuple-element.23.own), channel_id=1, source_target_pairs={{0,2},{2,4},{4,6},{6,8},{8,10},{10,12},{12,14},{14,16},{16,18},{18... | collective-permute-start | bytes 540680 | tf_op jit(solution)/shard_map/ppermute | solution.py:506
  27.6 1.0 %collective-permute-start.5 = (f32[160,128]{1,0:T(8,128)S(1)}, f32[160,128]{1,0:T(8,128)S(1)}, u32[]{:S(2)}, u32[]{:S(2)}) collective-permute-start(f32[160,128]{1,0:T(8,128)S(1)} %get-tuple-element.24), channel_id=1, source_target_pairs={{0,4},{2,6},{4,8},{6,10},{8,12},{10,14},{12,16},{14,18},{16,20},{1... | collective-permute-start | bytes 245768 | tf_op jit(solution)/shard_map/ppermute | solution.py:507
  28.5 0.0 collective-permute-done.9.far
  28.5 0.5 %collective-permute-done.8.near = f32[176,256]{1,0:T(8,128)S(1)} collective-permute-done((f32[176,256]{1,0:T(8,128)S(1)}, f32[176,256]{1,0:T(8,128)S(1)}, u32[]{:S(2)}, u32[]{:S(2)}) %collective-permute-start.8) | collective-permute-done | bytes 180256 | tf_op jit(solution)/shard_map/ppermute | solution.py:506
  29.0 5.6 %last_step.2.rest_0_ = f32[160,256]{1,0:T(8,128)S(1)} custom-call(s32[1]{0:T(128)} %bitcast.place.refs_0_, f32[176,256]{1,0:T(8,128)S(1)} %get-tuple-element.29.own, f32[176,256]{1,0:T(8,128)S(1)} %collective-permute-done.8.near, f32[160,128]{1,0:T(8,128)S(1)} %collective-permute-done.9.far, f32[320,128]{1,0:T(8,128)S(1)} %get-tuple-element.25.spin, ...), custom_call_target="tpu_custom_call" | custom-call | flops 8999999488 | bytes 29000000 | tf_op jit(solution)/shard_map/last_step/pallas_call | solution.py:481
  34.6 1.0 %collective-permute-done.5.far = f32[160,128]{1,0:T(8,128)S(1)} collective-permute-done((f32[160,128]{1,0:T(8,128)S(1)}, f32[160,128]{1,0:T(8,128)S(1)}, u32[]{:S(2)}, u32[]{:S(2)}) %collective-permute-start.5) | collective-permute-done | bytes 81952 | tf_op jit(solution)/shard_map/ppermute | solution.py:507
  35.7 6.4 %last_step.3 = (f32[2,32,256]{2,1,0:T(8,128)}, f32[2,2,32,256]{3,2,1,0:T(8,128)}, f32[2,2,32,256]{3,2,1,0:T(8,128)}) custom-call(s32[1]{0:T(128)} %bitcast.place.refs_0_, f32[176,256]{1,0:T(8,128)S(1)} %get-tuple-element.23.own, f32[176,256]{1,0:T(8,128)S(1)} %collective-permute-done.4.near, f32[160,128]{1,0:T(8,128)S(1)} %collective-permute-done.5.far, ...), custom_call_target="tpu_custom_call" | custom-call | flops 8999999488 | bytes 29000000 | tf_op jit(solution)/shard_map/last_step/pallas_call | solution.py:481
  (13 shorter events, 0.0 us)
Async XLA Ops:
  0.6 1.8 %copy-start = (f32[2,2,32,256]{3,2,1,0:T(8,128)S(1)}, f32[2,2,32,256]{3,2,1,0:T(8,128)}, u32[]{:S(2)}) copy-start(f32[2,2,32,256]{3,2,1,0:T(8,128)} %refs_1_.1) | copy-start | bytes 393220
  0.6 1.8 %copy-start.1 = (f32[2,2,32,256]{3,2,1,0:T(8,128)S(1)}, f32[2,2,32,256]{3,2,1,0:T(8,128)}, u32[]{:S(2)}) copy-start(f32[2,2,32,256]{3,2,1,0:T(8,128)} %refs_2_.1) | copy-start | bytes 393220
  0.7 1.8 %copy-start.2 = (f32[2,32,256]{2,1,0:T(8,128)S(1)}, f32[2,32,256]{2,1,0:T(8,128)}, u32[]{:S(2)}) copy-start(f32[2,32,256]{2,1,0:T(8,128)} %refs_0_.1) | copy-start | bytes 196612
  2.5 7.3 %copy-start.4 = (s32[256]{0:T(256)S(1)}, s32[256]{0:T(256)}, u32[]{:S(2)}) copy-start(s32[256]{0:T(256)} %param.9) | copy-start | bytes 3076
  2.6 7.3 %copy-start.3 = (f32[256]{0:T(256)S(1)}, f32[256]{0:T(256)}, u32[]{:S(2)}) copy-start(f32[256]{0:T(256)} %param.8) | copy-start | bytes 3076
  2.6 12.0 %collective-permute-start.6 = (f32[160,256]{1,0:T(8,128)S(1)}, f32[160,256]{1,0:T(8,128)S(1)}, u32[]{:S(2)}, u32[]{:S(2)}) collective-permute-start(f32[160,256]{1,0:T(8,128)S(1)} %get-tuple-element.27.own), channel_id=1, source_target_pairs={{0,2},{2,4},{4,6},{6,8},{8,10},{10,12},{12,14},{14,16},{16,18},{18... | collective-permute-start | bytes 491528 | tf_op jit(solution)/shard_map/ppermute | solution.py:506
  3.1 11.5 %collective-permute-start.7 = (f32[160,128]{1,0:T(8,128)S(1)}, f32[160,128]{1,0:T(8,128)S(1)}, u32[]{:S(2)}, u32[]{:S(2)}) collective-permute-start(f32[160,128]{1,0:T(8,128)S(1)} %get-tuple-element.28), channel_id=1, source_target_pairs={{0,4},{2,6},{4,8},{6,10},{8,12},{10,14},{12,16},{14,18},{16,20},{1... | collective-permute-start | bytes 245768 | tf_op jit(solution)/shard_map/ppermute | solution.py:507
  5.7 4.2 %collective-permute-start = (f32[2,16,256]{2,1,0:T(8,128)}, f32[2,16,256]{2,1,0:T(8,128)S(1)}, u32[]{:S(2)}, u32[]{:S(2)}) collective-permute-start(f32[2,16,256]{2,1,0:T(8,128)} %edges.1.refs_3_), channel_id=1, source_target_pairs={{0,1},{1,0},{2,3},{3,2},{4,5},{5,4},{6,7},{7,6},{8,9},{9,8},{10,11... | collective-permute-start | bytes 98312 | tf_op jit(solution)/shard_map/ppermute | solution.py:511
  7.2 7.4 %collective-permute-start.3 = (f32[2,16,256]{2,1,0:T(8,128)}, f32[2,16,256]{2,1,0:T(8,128)S(1)}, u32[]{:S(2)}, u32[]{:S(2)}) collective-permute-start(f32[2,16,256]{2,1,0:T(8,128)} %edges.1.refs_3_), channel_id=1, source_target_pairs={{0,3},{1,2},{2,5},{3,4},{4,7},{5,6},{6,9},{7,8},{8,11},{9,10},{10,... | collective-permute-start | bytes 98312 | tf_op jit(solution)/shard_map/ppermute | solution.py:510
  10.2 10.4 %collective-permute-start.1 = (f32[160,256]{1,0:T(8,128)S(1)}, f32[160,256]{1,0:T(8,128)S(1)}, u32[]{:S(2)}, u32[]{:S(2)}) collective-permute-start(f32[160,256]{1,0:T(8,128)S(1)} %get-tuple-element.20.own), channel_id=1, source_target_pairs={{0,2},{2,4},{4,6},{6,8},{8,10},{10,12},{12,14},{14,16},{16,18},{18... | collective-permute-start | bytes 491528 | tf_op jit(solution)/shard_map/ppermute | solution.py:506
  10.7 9.9 %collective-permute-start.2 = (f32[160,128]{1,0:T(8,128)S(1)}, f32[160,128]{1,0:T(8,128)S(1)}, u32[]{:S(2)}, u32[]{:S(2)}) collective-permute-start(f32[160,128]{1,0:T(8,128)S(1)} %get-tuple-element.21), channel_id=1, source_target_pairs={{0,4},{2,6},{4,8},{6,10},{8,12},{10,14},{12,16},{14,18},{16,20},{1... | collective-permute-start | bytes 245768 | tf_op jit(solution)/shard_map/ppermute | solution.py:507
  20.5 8.5 %collective-permute-start.8 = (f32[176,256]{1,0:T(8,128)S(1)}, f32[176,256]{1,0:T(8,128)S(1)}, u32[]{:S(2)}, u32[]{:S(2)}) collective-permute-start(f32[176,256]{1,0:T(8,128)S(1)} %get-tuple-element.29.own), channel_id=1, source_target_pairs={{0,2},{2,4},{4,6},{6,8},{8,10},{10,12},{12,14},{14,16},{16,18},{18... | collective-permute-start | bytes 540680 | tf_op jit(solution)/shard_map/ppermute | solution.py:506
  20.5 8.0 %collective-permute-start.9 = (f32[160,128]{1,0:T(8,128)S(1)}, f32[160,128]{1,0:T(8,128)S(1)}, u32[]{:S(2)}, u32[]{:S(2)}) collective-permute-start(f32[160,128]{1,0:T(8,128)S(1)} %get-tuple-element.30), channel_id=1, source_target_pairs={{0,4},{2,6},{4,8},{6,10},{8,12},{10,14},{12,16},{14,18},{16,20},{1... | collective-permute-start | bytes 245768 | tf_op jit(solution)/shard_map/ppermute | solution.py:507
  26.5 9.1 %collective-permute-start.4 = (f32[176,256]{1,0:T(8,128)S(1)}, f32[176,256]{1,0:T(8,128)S(1)}, u32[]{:S(2)}, u32[]{:S(2)}) collective-permute-start(f32[176,256]{1,0:T(8,128)S(1)} %get-tuple-element.23.own), channel_id=1, source_target_pairs={{0,2},{2,4},{4,6},{6,8},{8,10},{10,12},{12,14},{14,16},{16,18},{18... | collective-permute-start | bytes 540680 | tf_op jit(solution)/shard_map/ppermute | solution.py:506
  27.6 8.1 %collective-permute-start.5 = (f32[160,128]{1,0:T(8,128)S(1)}, f32[160,128]{1,0:T(8,128)S(1)}, u32[]{:S(2)}, u32[]{:S(2)}) collective-permute-start(f32[160,128]{1,0:T(8,128)S(1)} %get-tuple-element.24), channel_id=1, source_target_pairs={{0,4},{2,6},{4,8},{6,10},{8,12},{10,14},{12,16},{14,18},{16,20},{1... | collective-permute-start | bytes 245768 | tf_op jit(solution)/shard_map/ppermute | solution.py:507

commit v19 on v18

--- a/solution.py
+++ b/solution.py
@@ -73,7 +73,7 @@
 
 
 def rows_a_turn(n):
-    return (n + 2 * REACH - 4 + 1) // 2
+    return (n + 2 * REACH - 3 + 1) // 2
 
 
 def run_stages(n, stages, spin, edges):
@@ -134,16 +134,9 @@
             for k in (1, 2):
                 stages[stage, f, tile(first - k), :] = jnp.where(low_mask, inner, stages[stage, f, tile(first - k), :])
                 stages[stage, f, tile(last + k), :] = jnp.where(high_mask, outer, stages[stage, f, tile(last + k), :])
-        count = n + 2 * REACH - 4 - 4 * stage
-        if n % 2 == 0:
-            lo = 2 * stage + 2
-            rows = [stages[stage, f, pl.ds(pl.multiple_of((lo - 2) * SUB, SUB), 4 * SUB), :] for f in range(FIELDS)]
-            left, right = radial_states([0.5 * x for x in rows], [x[SUB:-SUB] for x in rows])
-            before = tuple(swapped(face_twice(left, right, physical(left), physical(right))))
-        else:
-            lo = 2 * stage + 1
-            count = count + 1
-            before = (jnp.zeros((SUB, LANES), jnp.float32),) * FIELDS
+        lo = 2 * stage + 1
+        count = n + 2 * REACH - 3 - 4 * stage
+        before = (jnp.zeros((SUB, LANES), jnp.float32),) * FIELDS
         turns = lax.div(count + each - 1, each)
         lax.fori_loop(0, turns, lambda c, carried: tuple(work(stage, lo + c * each, list(carried))), before)
         return 0
@@ -298,9 +291,8 @@
             else:
                 gap = jnp.zeros((own_cells - 2 * SUB, LANES), jnp.float32)
                 top = jnp.concatenate([gap, tops[f]], axis=0)
-            fill = jnp.zeros((own_cells, LANES), jnp.float32)
-            block = jnp.concatenate([top, near[rows, columns], own[rows, columns], fill], axis=0)
-            cells[f, pl.ds(blocks.own_at + part * LANES, LANES), :] = block.T
+            block = jnp.concatenate([top, near[rows, columns], own[rows, columns]], axis=0)
+            cells[f, pl.ds(blocks.own_at + part * LANES, LANES), 0 : 3 * own_cells] = block.T
         columns = pl.ds(pl.multiple_of(lax.div(f, 4) * LANES, LANES), LANES)
         lanes_at = lax.rem(f, 4) * own_cells
         cells[f, pl.ds(blocks.edge_at, EXTRA), :] = jnp.where(

time: 42.2 us -> 42.3 us (level)
  no operation moved by 1% of the time
where the time goes in v19:
time: 42.3 us; the launch traced here: 42.2 us
  Pallas kernels  26.3 us (62%)
  starting transfers between devices  9.58 us (23%)
  waiting for transfers between devices  5.54 us (13%)
  between operations  0.75 us (2%)
    pallas_call x2, Pallas kernels, last_step(): pl.pallas_call(kernel, out_shape=out_shape, in_specs=[smem] + [vmem] * (5...  12.3 us
    pallas_call x2, Pallas kernels, first_step(): pl.pallas_call(kernel, out_shape=[f32(FIELDS * own_cells + EXTRA, radius)...  11.8 us
    ppermute x4, starting transfers between devices, body(): lax.ppermute(x, 'phi', [(p, (p + 2) % phi_count) for p in range(phi_count)])  4.83 us
    ppermute x1, waiting for transfers between devices, body(): send_corner = lambda x: lax.ppermute(x, ('phi', 'row'), diagonal)  2.65 us
    ppermute x4, starting transfers between devices, body(): lax.ppermute(x, 'phi', [(p, (p + 1) % phi_count) for p in range(phi_count)])  2.11 us
    pallas_call x1, Pallas kernels, body(): pl.pallas_call(edge_kernel, out_shape=f32(levels, EXTRA, 2 * LANES), in_s...  1.74 us
    ppermute x1, waiting for transfers between devices, body(): send_side = lambda x: lax.ppermute(x, 'row', [(0, 1), (1, 0)])  1.51 us
    ppermute x1, starting transfers between devices, body(): send_side = lambda x: lax.ppermute(x, 'row', [(0, 1), (1, 0)])  1.49 us
  transfers between devices with their start and end apart: 10, of which 4 were waited for; matrix products, arithmetic and copies ran while one was open for 0% of the time, Pallas kernels for 42%

profile of v19, /device:TPU:0, one launch (start us, length us, event | category | flops | bytes accessed | tf_op | source)
XLA Modules:
  0.0 42.2 jit_solution(4577283040798031125)
XLA Ops:
  0.7 1.7 %edges.1.refs_3_ = f32[2,16,256]{2,1,0:T(8,128)} custom-call(s32[1]{0:T(128)} %bitcast.place.refs_0_, f32[2,32,256]{2,1,0:T(8,128)} %refs_0_.1, f32[2,2,32,256]{3,2,1,0:T(8,128)} %refs_1_.1, f32[2,2,32,256]{3,2,1,0:T(8,128)} %refs_2_.1, f32[2,128]{1,0:T(2,128)} %bitcast.3, s32[2,128]{1,0:T(2,128)} %bitcast.5), custom_call_target="tpu_custom_call" | custom-call | tf_op jit(solution)/shard_map/edges/pallas_call | solution.py:508
  2.4 0.1 pack.1
  2.5 0.0 copy-start.4
  2.6 0.0 copy-start.3
  2.6 0.5 %collective-permute-start.6 = (f32[160,256]{1,0:T(8,128)S(1)}, f32[160,256]{1,0:T(8,128)S(1)}, u32[]{:S(2)}, u32[]{:S(2)}) collective-permute-start(f32[160,256]{1,0:T(8,128)S(1)} %get-tuple-element.27.own), channel_id=1, source_target_pairs={{0,2},{2,4},{4,6},{6,8},{8,10},{10,12},{12,14},{14,16},{16,18},{18... | collective-permute-start | bytes 491528 | tf_op jit(solution)/shard_map/ppermute | solution.py:498
  3.1 2.6 %collective-permute-start.7 = (f32[160,128]{1,0:T(8,128)S(1)}, f32[160,128]{1,0:T(8,128)S(1)}, u32[]{:S(2)}, u32[]{:S(2)}) collective-permute-start(f32[160,128]{1,0:T(8,128)S(1)} %get-tuple-element.28), channel_id=1, source_target_pairs={{0,4},{2,6},{4,8},{6,10},{8,12},{10,14},{12,16},{14,18},{16,20},{1... | collective-permute-start | bytes 245768 | tf_op jit(solution)/shard_map/ppermute | solution.py:499
  5.7 1.5 %collective-permute-start = (f32[2,16,256]{2,1,0:T(8,128)}, f32[2,16,256]{2,1,0:T(8,128)S(1)}, u32[]{:S(2)}, u32[]{:S(2)}) collective-permute-start(f32[2,16,256]{2,1,0:T(8,128)} %edges.1.refs_3_), channel_id=1, source_target_pairs={{0,1},{1,0},{2,3},{3,2},{4,5},{5,4},{6,7},{7,6},{8,9},{9,8},{10,11... | collective-permute-start | bytes 98312 | tf_op jit(solution)/shard_map/ppermute | solution.py:503
  7.2 1.1 %collective-permute-start.3 = (f32[2,16,256]{2,1,0:T(8,128)}, f32[2,16,256]{2,1,0:T(8,128)S(1)}, u32[]{:S(2)}, u32[]{:S(2)}) collective-permute-start(f32[2,16,256]{2,1,0:T(8,128)} %edges.1.refs_3_), channel_id=1, source_target_pairs={{0,3},{1,2},{2,5},{3,4},{4,7},{5,6},{6,9},{7,8},{8,11},{9,10},{10,... | collective-permute-start | bytes 98312 | tf_op jit(solution)/shard_map/ppermute | solution.py:502
  8.3 1.5 %collective-permute-done.refs_1_.side = f32[2,16,256]{2,1,0:T(8,128)S(1)} collective-permute-done((f32[2,16,256]{2,1,0:T(8,128)}, f32[2,16,256]{2,1,0:T(8,128)S(1)}, u32[]{:S(2)}, u32[]{:S(2)}) %collective-permute-start) | collective-permute-done | bytes 32800 | tf_op jit(solution)/shard_map/ppermute | solution.py:503
  9.8 0.4 tables.1
  10.2 0.5 %collective-permute-start.1 = (f32[160,256]{1,0:T(8,128)S(1)}, f32[160,256]{1,0:T(8,128)S(1)}, u32[]{:S(2)}, u32[]{:S(2)}) collective-permute-start(f32[160,256]{1,0:T(8,128)S(1)} %get-tuple-element.20.own), channel_id=1, source_target_pairs={{0,2},{2,4},{4,6},{6,8},{8,10},{10,12},{12,14},{14,16},{16,18},{18... | collective-permute-start | bytes 491528 | tf_op jit(solution)/shard_map/ppermute | solution.py:498
  10.7 1.2 %collective-permute-start.2 = (f32[160,128]{1,0:T(8,128)S(1)}, f32[160,128]{1,0:T(8,128)S(1)}, u32[]{:S(2)}, u32[]{:S(2)}) collective-permute-start(f32[160,128]{1,0:T(8,128)S(1)} %get-tuple-element.21), channel_id=1, source_target_pairs={{0,4},{2,6},{4,8},{6,10},{8,12},{10,14},{12,16},{14,18},{16,20},{1... | collective-permute-start | bytes 245768 | tf_op jit(solution)/shard_map/ppermute | solution.py:499
  11.9 2.6 %collective-permute-done.3.corner = f32[2,16,256]{2,1,0:T(8,128)S(1)} collective-permute-done((f32[2,16,256]{2,1,0:T(8,128)}, f32[2,16,256]{2,1,0:T(8,128)S(1)}, u32[]{:S(2)}, u32[]{:S(2)}) %collective-permute-start.3) | collective-permute-done | bytes 32800 | tf_op jit(solution)/shard_map/ppermute | solution.py:502
  14.6 5.9 %first_step.3 = (f32[176,256]{1,0:T(8,128)S(1)}, f32[160,128]{1,0:T(8,128)S(1)}) custom-call(s32[1]{0:T(128)} %bitcast.place.refs_0_, f32[160,256]{1,0:T(8,128)S(1)} %get-tuple-element.27.own, f32[160,256]{1,0:T(8,128)S(1)} %collective-permute-done.6.near, f32[160,128]{1,0:T(8,128)S(1)} %collective-permute-done.7.far, ...), custom_call_target="tpu_custom_call" | custom-call | flops 8999999488 | bytes 29000000 | tf_op jit(solution)/shard_map/first_step/pallas_call | solution.py:430
  20.5 0.1 collective-permute-start.8
  20.5 0.1 collective-permute-start.9
  20.6 5.9 %first_step.2 = (f32[176,256]{1,0:T(8,128)S(1)}, f32[160,128]{1,0:T(8,128)S(1)}) custom-call(s32[1]{0:T(128)} %bitcast.place.refs_0_, f32[160,256]{1,0:T(8,128)S(1)} %get-tuple-element.20.own, f32[160,256]{1,0:T(8,128)S(1)} %collective-permute-done.1.near, f32[160,128]{1,0:T(8,128)S(1)} %collective-permute-done.2.far, ...), custom_call_target="tpu_custom_call" | custom-call | flops 8999999488 | bytes 29000000 | tf_op jit(solution)/shard_map/first_step/pallas_call | solution.py:430
  26.5 1.1 %collective-permute-start.4 = (f32[176,256]{1,0:T(8,128)S(1)}, f32[176,256]{1,0:T(8,128)S(1)}, u32[]{:S(2)}, u32[]{:S(2)}) collective-permute-start(f32[176,256]{1,0:T(8,128)S(1)} %get-tuple-element.23.own), channel_id=1, source_target_pairs={{0,2},{2,4},{4,6},{6,8},{8,10},{10,12},{12,14},{14,16},{16,18},{18... | collective-permute-start | bytes 540680 | tf_op jit(solution)/shard_map/ppermute | solution.py:498
  27.6 1.0 %collective-permute-start.5 = (f32[160,128]{1,0:T(8,128)S(1)}, f32[160,128]{1,0:T(8,128)S(1)}, u32[]{:S(2)}, u32[]{:S(2)}) collective-permute-start(f32[160,128]{1,0:T(8,128)S(1)} %get-tuple-element.24), channel_id=1, source_target_pairs={{0,4},{2,6},{4,8},{6,10},{8,12},{10,14},{12,16},{14,18},{16,20},{1... | collective-permute-start | bytes 245768 | tf_op jit(solution)/shard_map/ppermute | solution.py:499
  28.5 0.0 collective-permute-done.9.far
  28.5 0.5 %collective-permute-done.8.near = f32[176,256]{1,0:T(8,128)S(1)} collective-permute-done((f32[176,256]{1,0:T(8,128)S(1)}, f32[176,256]{1,0:T(8,128)S(1)}, u32[]{:S(2)}, u32[]{:S(2)}) %collective-permute-start.8) | collective-permute-done | bytes 180256 | tf_op jit(solution)/shard_map/ppermute | solution.py:498
  29.0 5.8 %last_step.2.rest_0_ = f32[160,256]{1,0:T(8,128)S(1)} custom-call(s32[1]{0:T(128)} %bitcast.place.refs_0_, f32[176,256]{1,0:T(8,128)S(1)} %get-tuple-element.29.own, f32[176,256]{1,0:T(8,128)S(1)} %collective-permute-done.8.near, f32[160,128]{1,0:T(8,128)S(1)} %collective-permute-done.9.far, f32[320,128]{1,0:T(8,128)S(1)} %get-tuple-element.25.spin, ...), custom_call_target="tpu_custom_call" | custom-call | flops 8999999488 | bytes 29000000 | tf_op jit(solution)/shard_map/last_step/pallas_call | solution.py:473
  34.8 0.9 %collective-permute-done.5.far = f32[160,128]{1,0:T(8,128)S(1)} collective-permute-done((f32[160,128]{1,0:T(8,128)S(1)}, f32[160,128]{1,0:T(8,128)S(1)}, u32[]{:S(2)}, u32[]{:S(2)}) %collective-permute-start.5) | collective-permute-done | bytes 81952 | tf_op jit(solution)/shard_map/ppermute | solution.py:499
  35.7 6.5 %last_step.3 = (f32[2,32,256]{2,1,0:T(8,128)}, f32[2,2,32,256]{3,2,1,0:T(8,128)}, f32[2,2,32,256]{3,2,1,0:T(8,128)}) custom-call(s32[1]{0:T(128)} %bitcast.place.refs_0_, f32[176,256]{1,0:T(8,128)S(1)} %get-tuple-element.23.own, f32[176,256]{1,0:T(8,128)S(1)} %collective-permute-done.4.near, f32[160,128]{1,0:T(8,128)S(1)} %collective-permute-done.5.far, ...), custom_call_target="tpu_custom_call" | custom-call | flops 8999999488 | bytes 29000000 | tf_op jit(solution)/shard_map/last_step/pallas_call | solution.py:473
  (13 shorter events, 0.0 us)
Async XLA Ops:
  0.6 1.8 %copy-start = (f32[2,2,32,256]{3,2,1,0:T(8,128)S(1)}, f32[2,2,32,256]{3,2,1,0:T(8,128)}, u32[]{:S(2)}) copy-start(f32[2,2,32,256]{3,2,1,0:T(8,128)} %refs_1_.1) | copy-start | bytes 393220
  0.6 1.8 %copy-start.1 = (f32[2,2,32,256]{3,2,1,0:T(8,128)S(1)}, f32[2,2,32,256]{3,2,1,0:T(8,128)}, u32[]{:S(2)}) copy-start(f32[2,2,32,256]{3,2,1,0:T(8,128)} %refs_2_.1) | copy-start | bytes 393220
  0.7 1.8 %copy-start.2 = (f32[2,32,256]{2,1,0:T(8,128)S(1)}, f32[2,32,256]{2,1,0:T(8,128)}, u32[]{:S(2)}) copy-start(f32[2,32,256]{2,1,0:T(8,128)} %refs_0_.1) | copy-start | bytes 196612
  2.5 7.3 %copy-start.4 = (s32[256]{0:T(256)S(1)}, s32[256]{0:T(256)}, u32[]{:S(2)}) copy-start(s32[256]{0:T(256)} %param.9) | copy-start | bytes 3076
  2.6 7.3 %copy-start.3 = (f32[256]{0:T(256)S(1)}, f32[256]{0:T(256)}, u32[]{:S(2)}) copy-start(f32[256]{0:T(256)} %param.8) | copy-start | bytes 3076
  2.6 12.0 %collective-permute-start.6 = (f32[160,256]{1,0:T(8,128)S(1)}, f32[160,256]{1,0:T(8,128)S(1)}, u32[]{:S(2)}, u32[]{:S(2)}) collective-permute-start(f32[160,256]{1,0:T(8,128)S(1)} %get-tuple-element.27.own), channel_id=1, source_target_pairs={{0,2},{2,4},{4,6},{6,8},{8,10},{10,12},{12,14},{14,16},{16,18},{18... | collective-permute-start | bytes 491528 | tf_op jit(solution)/shard_map/ppermute | solution.py:498
  3.1 11.5 %collective-permute-start.7 = (f32[160,128]{1,0:T(8,128)S(1)}, f32[160,128]{1,0:T(8,128)S(1)}, u32[]{:S(2)}, u32[]{:S(2)}) collective-permute-start(f32[160,128]{1,0:T(8,128)S(1)} %get-tuple-element.28), channel_id=1, source_target_pairs={{0,4},{2,6},{4,8},{6,10},{8,12},{10,14},{12,16},{14,18},{16,20},{1... | collective-permute-start | bytes 245768 | tf_op jit(solution)/shard_map/ppermute | solution.py:499
  5.7 4.2 %collective-permute-start = (f32[2,16,256]{2,1,0:T(8,128)}, f32[2,16,256]{2,1,0:T(8,128)S(1)}, u32[]{:S(2)}, u32[]{:S(2)}) collective-permute-start(f32[2,16,256]{2,1,0:T(8,128)} %edges.1.refs_3_), channel_id=1, source_target_pairs={{0,1},{1,0},{2,3},{3,2},{4,5},{5,4},{6,7},{7,6},{8,9},{9,8},{10,11... | collective-permute-start | bytes 98312 | tf_op jit(solution)/shard_map/ppermute | solution.py:503
  7.2 7.4 %collective-permute-start.3 = (f32[2,16,256]{2,1,0:T(8,128)}, f32[2,16,256]{2,1,0:T(8,128)S(1)}, u32[]{:S(2)}, u32[]{:S(2)}) collective-permute-start(f32[2,16,256]{2,1,0:T(8,128)} %edges.1.refs_3_), channel_id=1, source_target_pairs={{0,3},{1,2},{2,5},{3,4},{4,7},{5,6},{6,9},{7,8},{8,11},{9,10},{10,... | collective-permute-start | bytes 98312 | tf_op jit(solution)/shard_map/ppermute | solution.py:502
  10.2 10.4 %collective-permute-start.1 = (f32[160,256]{1,0:T(8,128)S(1)}, f32[160,256]{1,0:T(8,128)S(1)}, u32[]{:S(2)}, u32[]{:S(2)}) collective-permute-start(f32[160,256]{1,0:T(8,128)S(1)} %get-tuple-element.20.own), channel_id=1, source_target_pairs={{0,2},{2,4},{4,6},{6,8},{8,10},{10,12},{12,14},{14,16},{16,18},{18... | collective-permute-start | bytes 491528 | tf_op jit(solution)/shard_map/ppermute | solution.py:498
  10.7 9.9 %collective-permute-start.2 = (f32[160,128]{1,0:T(8,128)S(1)}, f32[160,128]{1,0:T(8,128)S(1)}, u32[]{:S(2)}, u32[]{:S(2)}) collective-permute-start(f32[160,128]{1,0:T(8,128)S(1)} %get-tuple-element.21), channel_id=1, source_target_pairs={{0,4},{2,6},{4,8},{6,10},{8,12},{10,14},{12,16},{14,18},{16,20},{1... | collective-permute-start | bytes 245768 | tf_op jit(solution)/shard_map/ppermute | solution.py:499
  20.5 8.5 %collective-permute-start.8 = (f32[176,256]{1,0:T(8,128)S(1)}, f32[176,256]{1,0:T(8,128)S(1)}, u32[]{:S(2)}, u32[]{:S(2)}) collective-permute-start(f32[176,256]{1,0:T(8,128)S(1)} %get-tuple-element.29.own), channel_id=1, source_target_pairs={{0,2},{2,4},{4,6},{6,8},{8,10},{10,12},{12,14},{14,16},{16,18},{18... | collective-permute-start | bytes 540680 | tf_op jit(solution)/shard_map/ppermute | solution.py:498
  20.5 8.0 %collective-permute-start.9 = (f32[160,128]{1,0:T(8,128)S(1)}, f32[160,128]{1,0:T(8,128)S(1)}, u32[]{:S(2)}, u32[]{:S(2)}) collective-permute-start(f32[160,128]{1,0:T(8,128)S(1)} %get-tuple-element.30), channel_id=1, source_target_pairs={{0,4},{2,6},{4,8},{6,10},{8,12},{10,14},{12,16},{14,18},{16,20},{1... | collective-permute-start | bytes 245768 | tf_op jit(solution)/shard_map/ppermute | solution.py:499
  26.5 9.1 %collective-permute-start.4 = (f32[176,256]{1,0:T(8,128)S(1)}, f32[176,256]{1,0:T(8,128)S(1)}, u32[]{:S(2)}, u32[]{:S(2)}) collective-permute-start(f32[176,256]{1,0:T(8,128)S(1)} %get-tuple-element.23.own), channel_id=1, source_target_pairs={{0,2},{2,4},{4,6},{6,8},{8,10},{10,12},{12,14},{14,16},{16,18},{18... | collective-permute-start | bytes 540680 | tf_op jit(solution)/shard_map/ppermute | solution.py:498
  27.6 8.1 %collective-permute-start.5 = (f32[160,128]{1,0:T(8,128)S(1)}, f32[160,128]{1,0:T(8,128)S(1)}, u32[]{:S(2)}, u32[]{:S(2)}) collective-permute-start(f32[160,128]{1,0:T(8,128)S(1)} %get-tuple-element.24), channel_id=1, source_target_pairs={{0,4},{2,6},{4,8},{6,10},{8,12},{10,14},{12,16},{14,18},{16,20},{1... | collective-permute-start | bytes 245768 | tf_op jit(solution)/shard_map/ppermute | solution.py:499

commit v20 on v18

--- a/solution.py
+++ b/solution.py
@@ -288,7 +288,18 @@
     for f in range(FIELDS):
         tops[f] = jnp.concatenate(far_rows(far, f * own_cells), axis=0)
 
-    def bring(f, _):
+    def bring(turn, _):
+        dealt = jnp.maximum(turn - 1, 0)
+        for j in range(SUB):
+            low, high = j, SUB + j
+            turn_low = (LANES - (2 * own_cells - REACH)) + blocks.bounds[low]
+            turn_high = (HALF - (2 * own_cells - REACH)) + blocks.bounds[high]
+            stages[0, dealt, pl.ds(j, DEALT, stride=SUB), :] = jnp.where(
+                front,
+                pltpu.roll(cells[dealt, blocks.rows_of(low), :], turn_low, 1),
+                pltpu.roll(cells[dealt, blocks.rows_of(high), :], turn_high, 1),
+            )
+        f = jnp.minimum(turn, FIELDS - 1)
         rows = pl.ds(pl.multiple_of(f * own_cells, SUB), own_cells)
         start = pl.multiple_of(f * own_cells, SUB)
         for part in range(parts):
@@ -308,19 +319,9 @@
             pltpu.roll(near_edge[:, columns], lax.rem(LANES + own_cells - lanes_at, LANES), 1),
             pltpu.roll(own_edge[:, columns], lax.rem(LANES + 2 * own_cells - lanes_at, LANES), 1),
         )
-
-        for j in range(SUB):
-            low, high = j, SUB + j
-            turn_low = (LANES - (2 * own_cells - REACH)) + blocks.bounds[low]
-            turn_high = (HALF - (2 * own_cells - REACH)) + blocks.bounds[high]
-            stages[0, f, pl.ds(j, DEALT, stride=SUB), :] = jnp.where(
-                front,
-                pltpu.roll(cells[f, blocks.rows_of(low), :], turn_low, 1),
-                pltpu.roll(cells[f, blocks.rows_of(high), :], turn_high, 1),
-            )
         return 0
 
-    lax.fori_loop(0, FIELDS, bring, 0)
+    lax.fori_loop(0, FIELDS + 1, bring, 0)
 
     edges = (
         (sublane == 0) & (lane < HALF) & (row == 0),

time: 42.2 us -> 41.8 us (level)
  Pallas kernels: 26 us -> 25.4 us
  transfers between devices with their start and end apart: 10 -> 10, of which waited for: 4 -> 5; matrix products, arithmetic and copies ran while one was open for 0% -> 0% of each run, Pallas kernels for 42% -> 42%
where the time goes in v20:
time: 41.8 us; the launch traced here: 41.6 us
  Pallas kernels  25.4 us (61%)
  starting transfers between devices  9.58 us (23%)
  waiting for transfers between devices  5.82 us (14%)
  between operations  0.75 us (2%)
    pallas_call x2, Pallas kernels, last_step(): pl.pallas_call(kernel, out_shape=out_shape, in_specs=[smem] + [vmem] * (5...  11.7 us
    pallas_call x2, Pallas kernels, first_step(): pl.pallas_call(kernel, out_shape=[f32(FIELDS * own_cells + EXTRA, radius)...  11.5 us
    ppermute x4, starting transfers between devices, body(): lax.ppermute(x, 'phi', [(p, (p + 2) % phi_count) for p in range(phi_count)])  4.83 us
    ppermute x1, waiting for transfers between devices, body(): send_corner = lambda x: lax.ppermute(x, ('phi', 'row'), diagonal)  2.65 us
    ppermute x4, starting transfers between devices, body(): lax.ppermute(x, 'phi', [(p, (p + 1) % phi_count) for p in range(phi_count)])  2.11 us
    pallas_call x1, Pallas kernels, body(): pl.pallas_call(edge_kernel, out_shape=f32(levels, EXTRA, 2 * LANES), in_s...  1.74 us
    ppermute x1, waiting for transfers between devices, body(): send_side = lambda x: lax.ppermute(x, 'row', [(0, 1), (1, 0)])  1.51 us
    ppermute x1, starting transfers between devices, body(): send_side = lambda x: lax.ppermute(x, 'row', [(0, 1), (1, 0)])  1.49 us
  transfers between devices with their start and end apart: 10, of which 5 were waited for; matrix products, arithmetic and copies ran while one was open for 0% of the time, Pallas kernels for 42%

profile of v20, /device:TPU:0, one launch (start us, length us, event | category | flops | bytes accessed | tf_op | source)
XLA Modules:
  0.0 41.6 jit_solution(1348679095917190389)
XLA Ops:
  0.7 1.7 %edges.1.refs_3_ = f32[2,16,256]{2,1,0:T(8,128)} custom-call(s32[1]{0:T(128)} %bitcast.place.refs_0_, f32[2,32,256]{2,1,0:T(8,128)} %refs_0_.1, f32[2,2,32,256]{3,2,1,0:T(8,128)} %refs_1_.1, f32[2,2,32,256]{3,2,1,0:T(8,128)} %refs_2_.1, f32[2,128]{1,0:T(2,128)} %bitcast.3, s32[2,128]{1,0:T(2,128)} %bitcast.5), custom_call_target="tpu_custom_call" | custom-call | tf_op jit(solution)/shard_map/edges/pallas_call | solution.py:517
  2.4 0.1 pack.1
  2.5 0.0 copy-start.4
  2.6 0.0 copy-start.3
  2.6 0.5 %collective-permute-start.6 = (f32[160,256]{1,0:T(8,128)S(1)}, f32[160,256]{1,0:T(8,128)S(1)}, u32[]{:S(2)}, u32[]{:S(2)}) collective-permute-start(f32[160,256]{1,0:T(8,128)S(1)} %get-tuple-element.27.own), channel_id=1, source_target_pairs={{0,2},{2,4},{4,6},{6,8},{8,10},{10,12},{12,14},{14,16},{16,18},{18... | collective-permute-start | bytes 491528 | tf_op jit(solution)/shard_map/ppermute | solution.py:507
  3.1 2.6 %collective-permute-start.7 = (f32[160,128]{1,0:T(8,128)S(1)}, f32[160,128]{1,0:T(8,128)S(1)}, u32[]{:S(2)}, u32[]{:S(2)}) collective-permute-start(f32[160,128]{1,0:T(8,128)S(1)} %get-tuple-element.28), channel_id=1, source_target_pairs={{0,4},{2,6},{4,8},{6,10},{8,12},{10,14},{12,16},{14,18},{16,20},{1... | collective-permute-start | bytes 245768 | tf_op jit(solution)/shard_map/ppermute | solution.py:508
  5.7 1.5 %collective-permute-start = (f32[2,16,256]{2,1,0:T(8,128)}, f32[2,16,256]{2,1,0:T(8,128)S(1)}, u32[]{:S(2)}, u32[]{:S(2)}) collective-permute-start(f32[2,16,256]{2,1,0:T(8,128)} %edges.1.refs_3_), channel_id=1, source_target_pairs={{0,1},{1,0},{2,3},{3,2},{4,5},{5,4},{6,7},{7,6},{8,9},{9,8},{10,11... | collective-permute-start | bytes 98312 | tf_op jit(solution)/shard_map/ppermute | solution.py:512
  7.2 1.1 %collective-permute-start.3 = (f32[2,16,256]{2,1,0:T(8,128)}, f32[2,16,256]{2,1,0:T(8,128)S(1)}, u32[]{:S(2)}, u32[]{:S(2)}) collective-permute-start(f32[2,16,256]{2,1,0:T(8,128)} %edges.1.refs_3_), channel_id=1, source_target_pairs={{0,3},{1,2},{2,5},{3,4},{4,7},{5,6},{6,9},{7,8},{8,11},{9,10},{10,... | collective-permute-start | bytes 98312 | tf_op jit(solution)/shard_map/ppermute | solution.py:511
  8.3 1.5 %collective-permute-done.refs_1_.side = f32[2,16,256]{2,1,0:T(8,128)S(1)} collective-permute-done((f32[2,16,256]{2,1,0:T(8,128)}, f32[2,16,256]{2,1,0:T(8,128)S(1)}, u32[]{:S(2)}, u32[]{:S(2)}) %collective-permute-start) | collective-permute-done | bytes 32800 | tf_op jit(solution)/shard_map/ppermute | solution.py:512
  9.8 0.4 tables.1
  10.2 0.5 %collective-permute-start.1 = (f32[160,256]{1,0:T(8,128)S(1)}, f32[160,256]{1,0:T(8,128)S(1)}, u32[]{:S(2)}, u32[]{:S(2)}) collective-permute-start(f32[160,256]{1,0:T(8,128)S(1)} %get-tuple-element.20.own), channel_id=1, source_target_pairs={{0,2},{2,4},{4,6},{6,8},{8,10},{10,12},{12,14},{14,16},{16,18},{18... | collective-permute-start | bytes 491528 | tf_op jit(solution)/shard_map/ppermute | solution.py:507
  10.7 1.2 %collective-permute-start.2 = (f32[160,128]{1,0:T(8,128)S(1)}, f32[160,128]{1,0:T(8,128)S(1)}, u32[]{:S(2)}, u32[]{:S(2)}) collective-permute-start(f32[160,128]{1,0:T(8,128)S(1)} %get-tuple-element.21), channel_id=1, source_target_pairs={{0,4},{2,6},{4,8},{6,10},{8,12},{10,14},{12,16},{14,18},{16,20},{1... | collective-permute-start | bytes 245768 | tf_op jit(solution)/shard_map/ppermute | solution.py:508
  11.9 2.6 %collective-permute-done.3.corner = f32[2,16,256]{2,1,0:T(8,128)S(1)} collective-permute-done((f32[2,16,256]{2,1,0:T(8,128)}, f32[2,16,256]{2,1,0:T(8,128)S(1)}, u32[]{:S(2)}, u32[]{:S(2)}) %collective-permute-start.3) | collective-permute-done | bytes 32800 | tf_op jit(solution)/shard_map/ppermute | solution.py:511
  14.6 5.8 %first_step.3 = (f32[176,256]{1,0:T(8,128)S(1)}, f32[160,128]{1,0:T(8,128)S(1)}) custom-call(s32[1]{0:T(128)} %bitcast.place.refs_0_, f32[160,256]{1,0:T(8,128)S(1)} %get-tuple-element.27.own, f32[160,256]{1,0:T(8,128)S(1)} %collective-permute-done.6.near, f32[160,128]{1,0:T(8,128)S(1)} %collective-permute-done.7.far, ...), custom_call_target="tpu_custom_call" | custom-call | flops 8999999488 | bytes 29000000 | tf_op jit(solution)/shard_map/first_step/pallas_call | solution.py:439
  20.3 0.1 collective-permute-start.8
  20.4 0.1 collective-permute-start.9
  20.5 5.8 %first_step.2 = (f32[176,256]{1,0:T(8,128)S(1)}, f32[160,128]{1,0:T(8,128)S(1)}) custom-call(s32[1]{0:T(128)} %bitcast.place.refs_0_, f32[160,256]{1,0:T(8,128)S(1)} %get-tuple-element.20.own, f32[160,256]{1,0:T(8,128)S(1)} %collective-permute-done.1.near, f32[160,128]{1,0:T(8,128)S(1)} %collective-permute-done.2.far, ...), custom_call_target="tpu_custom_call" | custom-call | flops 8999999488 | bytes 29000000 | tf_op jit(solution)/shard_map/first_step/pallas_call | solution.py:439
  26.2 1.1 %collective-permute-start.4 = (f32[176,256]{1,0:T(8,128)S(1)}, f32[176,256]{1,0:T(8,128)S(1)}, u32[]{:S(2)}, u32[]{:S(2)}) collective-permute-start(f32[176,256]{1,0:T(8,128)S(1)} %get-tuple-element.23.own), channel_id=1, source_target_pairs={{0,2},{2,4},{4,6},{6,8},{8,10},{10,12},{12,14},{14,16},{16,18},{18... | collective-permute-start | bytes 540680 | tf_op jit(solution)/shard_map/ppermute | solution.py:507
  27.3 1.0 %collective-permute-start.5 = (f32[160,128]{1,0:T(8,128)S(1)}, f32[160,128]{1,0:T(8,128)S(1)}, u32[]{:S(2)}, u32[]{:S(2)}) collective-permute-start(f32[160,128]{1,0:T(8,128)S(1)} %get-tuple-element.24), channel_id=1, source_target_pairs={{0,4},{2,6},{4,8},{6,10},{8,12},{10,14},{12,16},{14,18},{16,20},{1... | collective-permute-start | bytes 245768 | tf_op jit(solution)/shard_map/ppermute | solution.py:508
  28.3 0.1 collective-permute-done.9.far
  28.4 0.5 %collective-permute-done.8.near = f32[176,256]{1,0:T(8,128)S(1)} collective-permute-done((f32[176,256]{1,0:T(8,128)S(1)}, f32[176,256]{1,0:T(8,128)S(1)}, u32[]{:S(2)}, u32[]{:S(2)}) %collective-permute-start.8) | collective-permute-done | bytes 180256 | tf_op jit(solution)/shard_map/ppermute | solution.py:507
  28.9 5.5 %last_step.2.rest_0_ = f32[160,256]{1,0:T(8,128)S(1)} custom-call(s32[1]{0:T(128)} %bitcast.place.refs_0_, f32[176,256]{1,0:T(8,128)S(1)} %get-tuple-element.29.own, f32[176,256]{1,0:T(8,128)S(1)} %collective-permute-done.8.near, f32[160,128]{1,0:T(8,128)S(1)} %collective-permute-done.9.far, f32[320,128]{1,0:T(8,128)S(1)} %get-tuple-element.25.spin, ...), custom_call_target="tpu_custom_call" | custom-call | flops 8999999488 | bytes 29000000 | tf_op jit(solution)/shard_map/last_step/pallas_call | solution.py:482
  34.3 1.0 %collective-permute-done.5.far = f32[160,128]{1,0:T(8,128)S(1)} collective-permute-done((f32[160,128]{1,0:T(8,128)S(1)}, f32[160,128]{1,0:T(8,128)S(1)}, u32[]{:S(2)}, u32[]{:S(2)}) %collective-permute-start.5) | collective-permute-done | bytes 81952 | tf_op jit(solution)/shard_map/ppermute | solution.py:508
  35.4 6.2 %last_step.3 = (f32[2,32,256]{2,1,0:T(8,128)}, f32[2,2,32,256]{3,2,1,0:T(8,128)}, f32[2,2,32,256]{3,2,1,0:T(8,128)}) custom-call(s32[1]{0:T(128)} %bitcast.place.refs_0_, f32[176,256]{1,0:T(8,128)S(1)} %get-tuple-element.23.own, f32[176,256]{1,0:T(8,128)S(1)} %collective-permute-done.4.near, f32[160,128]{1,0:T(8,128)S(1)} %collective-permute-done.5.far, ...), custom_call_target="tpu_custom_call" | custom-call | flops 8999999488 | bytes 29000000 | tf_op jit(solution)/shard_map/last_step/pallas_call | solution.py:482
  (13 shorter events, 0.0 us)
Async XLA Ops:
  0.6 1.8 %copy-start = (f32[2,2,32,256]{3,2,1,0:T(8,128)S(1)}, f32[2,2,32,256]{3,2,1,0:T(8,128)}, u32[]{:S(2)}) copy-start(f32[2,2,32,256]{3,2,1,0:T(8,128)} %refs_1_.1) | copy-start | bytes 393220
  0.6 1.8 %copy-start.1 = (f32[2,2,32,256]{3,2,1,0:T(8,128)S(1)}, f32[2,2,32,256]{3,2,1,0:T(8,128)}, u32[]{:S(2)}) copy-start(f32[2,2,32,256]{3,2,1,0:T(8,128)} %refs_2_.1) | copy-start | bytes 393220
  0.7 1.8 %copy-start.2 = (f32[2,32,256]{2,1,0:T(8,128)S(1)}, f32[2,32,256]{2,1,0:T(8,128)}, u32[]{:S(2)}) copy-start(f32[2,32,256]{2,1,0:T(8,128)} %refs_0_.1) | copy-start | bytes 196612
  2.5 7.3 %copy-start.4 = (s32[256]{0:T(256)S(1)}, s32[256]{0:T(256)}, u32[]{:S(2)}) copy-start(s32[256]{0:T(256)} %param.9) | copy-start | bytes 3076
  2.6 7.3 %copy-start.3 = (f32[256]{0:T(256)S(1)}, f32[256]{0:T(256)}, u32[]{:S(2)}) copy-start(f32[256]{0:T(256)} %param.8) | copy-start | bytes 3076
  2.6 12.0 %collective-permute-start.6 = (f32[160,256]{1,0:T(8,128)S(1)}, f32[160,256]{1,0:T(8,128)S(1)}, u32[]{:S(2)}, u32[]{:S(2)}) collective-permute-start(f32[160,256]{1,0:T(8,128)S(1)} %get-tuple-element.27.own), channel_id=1, source_target_pairs={{0,2},{2,4},{4,6},{6,8},{8,10},{10,12},{12,14},{14,16},{16,18},{18... | collective-permute-start | bytes 491528 | tf_op jit(solution)/shard_map/ppermute | solution.py:507
  3.1 11.5 %collective-permute-start.7 = (f32[160,128]{1,0:T(8,128)S(1)}, f32[160,128]{1,0:T(8,128)S(1)}, u32[]{:S(2)}, u32[]{:S(2)}) collective-permute-start(f32[160,128]{1,0:T(8,128)S(1)} %get-tuple-element.28), channel_id=1, source_target_pairs={{0,4},{2,6},{4,8},{6,10},{8,12},{10,14},{12,16},{14,18},{16,20},{1... | collective-permute-start | bytes 245768 | tf_op jit(solution)/shard_map/ppermute | solution.py:508
  5.7 4.2 %collective-permute-start = (f32[2,16,256]{2,1,0:T(8,128)}, f32[2,16,256]{2,1,0:T(8,128)S(1)}, u32[]{:S(2)}, u32[]{:S(2)}) collective-permute-start(f32[2,16,256]{2,1,0:T(8,128)} %edges.1.refs_3_), channel_id=1, source_target_pairs={{0,1},{1,0},{2,3},{3,2},{4,5},{5,4},{6,7},{7,6},{8,9},{9,8},{10,11... | collective-permute-start | bytes 98312 | tf_op jit(solution)/shard_map/ppermute | solution.py:512
  7.2 7.4 %collective-permute-start.3 = (f32[2,16,256]{2,1,0:T(8,128)}, f32[2,16,256]{2,1,0:T(8,128)S(1)}, u32[]{:S(2)}, u32[]{:S(2)}) collective-permute-start(f32[2,16,256]{2,1,0:T(8,128)} %edges.1.refs_3_), channel_id=1, source_target_pairs={{0,3},{1,2},{2,5},{3,4},{4,7},{5,6},{6,9},{7,8},{8,11},{9,10},{10,... | collective-permute-start | bytes 98312 | tf_op jit(solution)/shard_map/ppermute | solution.py:511
  10.2 10.3 %collective-permute-start.1 = (f32[160,256]{1,0:T(8,128)S(1)}, f32[160,256]{1,0:T(8,128)S(1)}, u32[]{:S(2)}, u32[]{:S(2)}) collective-permute-start(f32[160,256]{1,0:T(8,128)S(1)} %get-tuple-element.20.own), channel_id=1, source_target_pairs={{0,2},{2,4},{4,6},{6,8},{8,10},{10,12},{12,14},{14,16},{16,18},{18... | collective-permute-start | bytes 491528 | tf_op jit(solution)/shard_map/ppermute | solution.py:507
  10.7 9.8 %collective-permute-start.2 = (f32[160,128]{1,0:T(8,128)S(1)}, f32[160,128]{1,0:T(8,128)S(1)}, u32[]{:S(2)}, u32[]{:S(2)}) collective-permute-start(f32[160,128]{1,0:T(8,128)S(1)} %get-tuple-element.21), channel_id=1, source_target_pairs={{0,4},{2,6},{4,8},{6,10},{8,12},{10,14},{12,16},{14,18},{16,20},{1... | collective-permute-start | bytes 245768 | tf_op jit(solution)/shard_map/ppermute | solution.py:508
  20.3 8.5 %collective-permute-start.8 = (f32[176,256]{1,0:T(8,128)S(1)}, f32[176,256]{1,0:T(8,128)S(1)}, u32[]{:S(2)}, u32[]{:S(2)}) collective-permute-start(f32[176,256]{1,0:T(8,128)S(1)} %get-tuple-element.29.own), channel_id=1, source_target_pairs={{0,2},{2,4},{4,6},{6,8},{8,10},{10,12},{12,14},{14,16},{16,18},{18... | collective-permute-start | bytes 540680 | tf_op jit(solution)/shard_map/ppermute | solution.py:507
  20.4 8.0 %collective-permute-start.9 = (f32[160,128]{1,0:T(8,128)S(1)}, f32[160,128]{1,0:T(8,128)S(1)}, u32[]{:S(2)}, u32[]{:S(2)}) collective-permute-start(f32[160,128]{1,0:T(8,128)S(1)} %get-tuple-element.30), channel_id=1, source_target_pairs={{0,4},{2,6},{4,8},{6,10},{8,12},{10,14},{12,16},{14,18},{16,20},{1... | collective-permute-start | bytes 245768 | tf_op jit(solution)/shard_map/ppermute | solution.py:508
  26.2 9.1 %collective-permute-start.4 = (f32[176,256]{1,0:T(8,128)S(1)}, f32[176,256]{1,0:T(8,128)S(1)}, u32[]{:S(2)}, u32[]{:S(2)}) collective-permute-start(f32[176,256]{1,0:T(8,128)S(1)} %get-tuple-element.23.own), channel_id=1, source_target_pairs={{0,2},{2,4},{4,6},{6,8},{8,10},{10,12},{12,14},{14,16},{16,18},{18... | collective-permute-start | bytes 540680 | tf_op jit(solution)/shard_map/ppermute | solution.py:507
  27.3 8.1 %collective-permute-start.5 = (f32[160,128]{1,0:T(8,128)S(1)}, f32[160,128]{1,0:T(8,128)S(1)}, u32[]{:S(2)}, u32[]{:S(2)}) collective-permute-start(f32[160,128]{1,0:T(8,128)S(1)} %get-tuple-element.24), channel_id=1, source_target_pairs={{0,4},{2,6},{4,8},{6,10},{8,12},{10,14},{12,16},{14,18},{16,20},{1... | collective-permute-start | bytes 245768 | tf_op jit(solution)/shard_map/ppermute | solution.py:508

commit v21 on v20

--- a/solution.py
+++ b/solution.py
@@ -384,13 +384,16 @@
 
 
 class ToBuffer:
-    def __init__(self, buffer):
-        self.buffer = buffer
+    def __init__(self, buffer, sent=None):
+        self.buffer, self.sent = buffer, sent
 
     def fields(self, columns, four, fifth):
+        part = columns.start // LANES
         split = four.shape[0]
-        self.buffer[0:split, columns] = four
-        self.buffer[split:, columns] = fifth[0 : self.buffer.shape[0] - split]
+        self.buffer[part, 0:split, :] = four
+        self.buffer[part, split:, :] = fifth[0 : self.buffer.shape[1] - split]
+        if self.sent is not None:
+            self.sent(part)
 
     def edge(self, first, second):
         pass
@@ -399,12 +402,13 @@
         pass
 
 
-def copies_out(level, buffer, outs, sent):
+def copies_out(level, part, buffer, outs, sent):
     density, momentum, magnetic = outs
     cells = density.shape[1]
-    targets = [density.at[level]] + [x.at[k, level] for x in (momentum, magnetic) for k in range(2)]
+    columns = pl.ds(part * LANES, LANES)
+    targets = [density.at[level, :, columns]] + [x.at[k, level, :, columns] for x in (momentum, magnetic) for k in range(2)]
     return [
-        pltpu.make_async_copy(buffer.at[pl.ds(f * cells, cells), :], x, sent.at[level * FIELDS + f])
+        pltpu.make_async_copy(buffer.at[part, pl.ds(f * cells, cells), :], x, sent.at[level, part, f])
         for f, x in enumerate(targets)
     ]
 
@@ -452,7 +456,8 @@
     n, radius, own_cells, total, moved = plan
     final = level == levels - 1
     tail = pl.ds(FIELDS * own_cells, EXTRA)
-    buffer = f32(FIELDS * own_cells, radius)
+    parts = radius // LANES
+    buffer = f32(parts, FIELDS * own_cells, LANES)
 
     def kernel(place, own, near, far, spin, pick, *rest):
         refs = (place, own, own.at[tail, :], near, near.at[tail, :], far, spin, pick)
@@ -462,20 +467,23 @@
         ready, outs, scratch = rest[: levels - 1], rest[levels - 1 : levels + 2], rest[levels + 2 :]
         last, sent = scratch[-2:]
         copies = []
+
+        def send(at, x, part):
+            started = copies_out(at, part, x, outs, sent)
+            for copy in started:
+                copy.start()
+            copies.extend(started)
+
         for k, x in enumerate(ready):
-            copies += copies_out(k, x, outs, sent)
+            for part in range(parts):
+                send(k, x, part)
+        step_kernel(plan, refs, ToBuffer(last, lambda part: send(level, last, part)), scratch[:-2])
         for copy in copies:
-            copy.start()
-        step_kernel(plan, refs, ToBuffer(last), scratch[:-2])
-        rest_of = copies_out(level, last, outs, sent)
-        for copy in rest_of:
-            copy.start()
-        for copy in copies + rest_of:
             copy.wait()
 
     if final:
         out_shape = [f32(levels, own_cells, radius), f32(2, levels, own_cells, radius), f32(2, levels, own_cells, radius)]
-        more = [pltpu.VMEM((FIELDS * own_cells, radius), jnp.float32), pltpu.SemaphoreType.DMA((levels * FIELDS,))]
+        more = [pltpu.VMEM(buffer.shape, jnp.float32), pltpu.SemaphoreType.DMA((levels, parts, FIELDS))]
     else:
         out_shape = buffer
         more = []

time: 41.8 us -> 41.8 us (level)
  no operation moved by 1% of the time
where the time goes in v21:
time: 41.8 us; the launch traced here: 41.7 us
  Pallas kernels  25.5 us (61%)
  starting transfers between devices  9.58 us (23%)
  waiting for transfers between devices  5.82 us (14%)
  between operations  0.75 us (2%)
    pallas_call x2, Pallas kernels, last_step(): pl.pallas_call(kernel, out_shape=out_shape, in_specs=[smem] + [vmem] * (5...  11.8 us
    pallas_call x2, Pallas kernels, first_step(): pl.pallas_call(kernel, out_shape=[f32(FIELDS * own_cells + EXTRA, radius)...  11.5 us
    ppermute x4, starting transfers between devices, body(): lax.ppermute(x, 'phi', [(p, (p + 2) % phi_count) for p in range(phi_count)])  4.83 us
    ppermute x1, waiting for transfers between devices, body(): send_corner = lambda x: lax.ppermute(x, ('phi', 'row'), diagonal)  2.65 us
    ppermute x4, starting transfers between devices, body(): lax.ppermute(x, 'phi', [(p, (p + 1) % phi_count) for p in range(phi_count)])  2.11 us
    pallas_call x1, Pallas kernels, body(): pl.pallas_call(edge_kernel, out_shape=f32(levels, EXTRA, 2 * LANES), in_s...  1.74 us
    ppermute x1, waiting for transfers between devices, body(): send_side = lambda x: lax.ppermute(x, 'row', [(0, 1), (1, 0)])  1.51 us
    ppermute x1, starting transfers between devices, body(): send_side = lambda x: lax.ppermute(x, 'row', [(0, 1), (1, 0)])  1.49 us
  transfers between devices with their start and end apart: 10, of which 5 were waited for; matrix products, arithmetic and copies ran while one was open for 0% of the time, Pallas kernels for 42%

profile of v21, /device:TPU:0, one launch (start us, length us, event | category | flops | bytes accessed | tf_op | source)
XLA Modules:
  0.0 41.7 jit_solution(16261444315792051596)
XLA Ops:
  0.7 1.7 %edges.1.refs_3_ = f32[2,16,256]{2,1,0:T(8,128)} custom-call(s32[1]{0:T(128)} %bitcast.place.refs_0_, f32[2,32,256]{2,1,0:T(8,128)} %refs_0_.1, f32[2,2,32,256]{3,2,1,0:T(8,128)} %refs_1_.1, f32[2,2,32,256]{3,2,1,0:T(8,128)} %refs_2_.1, f32[2,128]{1,0:T(2,128)} %bitcast.3, s32[2,128]{1,0:T(2,128)} %bitcast.5), custom_call_target="tpu_custom_call" | custom-call | tf_op jit(solution)/shard_map/edges/pallas_call | solution.py:525
  2.4 0.1 pack.1
  2.5 0.0 copy-start.4
  2.6 0.0 copy-start.3
  2.6 0.5 %collective-permute-start.6 = (f32[160,256]{1,0:T(8,128)S(1)}, f32[160,256]{1,0:T(8,128)S(1)}, u32[]{:S(2)}, u32[]{:S(2)}) collective-permute-start(f32[160,256]{1,0:T(8,128)S(1)} %get-tuple-element.27.own), channel_id=1, source_target_pairs={{0,2},{2,4},{4,6},{6,8},{8,10},{10,12},{12,14},{14,16},{16,18},{18... | collective-permute-start | bytes 491528 | tf_op jit(solution)/shard_map/ppermute | solution.py:515
  3.1 2.6 %collective-permute-start.7 = (f32[160,128]{1,0:T(8,128)S(1)}, f32[160,128]{1,0:T(8,128)S(1)}, u32[]{:S(2)}, u32[]{:S(2)}) collective-permute-start(f32[160,128]{1,0:T(8,128)S(1)} %get-tuple-element.28), channel_id=1, source_target_pairs={{0,4},{2,6},{4,8},{6,10},{8,12},{10,14},{12,16},{14,18},{16,20},{1... | collective-permute-start | bytes 245768 | tf_op jit(solution)/shard_map/ppermute | solution.py:516
  5.7 1.5 %collective-permute-start = (f32[2,16,256]{2,1,0:T(8,128)}, f32[2,16,256]{2,1,0:T(8,128)S(1)}, u32[]{:S(2)}, u32[]{:S(2)}) collective-permute-start(f32[2,16,256]{2,1,0:T(8,128)} %edges.1.refs_3_), channel_id=1, source_target_pairs={{0,1},{1,0},{2,3},{3,2},{4,5},{5,4},{6,7},{7,6},{8,9},{9,8},{10,11... | collective-permute-start | bytes 98312 | tf_op jit(solution)/shard_map/ppermute | solution.py:520
  7.2 1.1 %collective-permute-start.3 = (f32[2,16,256]{2,1,0:T(8,128)}, f32[2,16,256]{2,1,0:T(8,128)S(1)}, u32[]{:S(2)}, u32[]{:S(2)}) collective-permute-start(f32[2,16,256]{2,1,0:T(8,128)} %edges.1.refs_3_), channel_id=1, source_target_pairs={{0,3},{1,2},{2,5},{3,4},{4,7},{5,6},{6,9},{7,8},{8,11},{9,10},{10,... | collective-permute-start | bytes 98312 | tf_op jit(solution)/shard_map/ppermute | solution.py:519
  8.3 1.5 %collective-permute-done.refs_1_.side = f32[2,16,256]{2,1,0:T(8,128)S(1)} collective-permute-done((f32[2,16,256]{2,1,0:T(8,128)}, f32[2,16,256]{2,1,0:T(8,128)S(1)}, u32[]{:S(2)}, u32[]{:S(2)}) %collective-permute-start) | collective-permute-done | bytes 32800 | tf_op jit(solution)/shard_map/ppermute | solution.py:520
  9.8 0.4 tables.1
  10.2 0.5 %collective-permute-start.1 = (f32[160,256]{1,0:T(8,128)S(1)}, f32[160,256]{1,0:T(8,128)S(1)}, u32[]{:S(2)}, u32[]{:S(2)}) collective-permute-start(f32[160,256]{1,0:T(8,128)S(1)} %get-tuple-element.20.own), channel_id=1, source_target_pairs={{0,2},{2,4},{4,6},{6,8},{8,10},{10,12},{12,14},{14,16},{16,18},{18... | collective-permute-start | bytes 491528 | tf_op jit(solution)/shard_map/ppermute | solution.py:515
  10.7 1.2 %collective-permute-start.2 = (f32[160,128]{1,0:T(8,128)S(1)}, f32[160,128]{1,0:T(8,128)S(1)}, u32[]{:S(2)}, u32[]{:S(2)}) collective-permute-start(f32[160,128]{1,0:T(8,128)S(1)} %get-tuple-element.21), channel_id=1, source_target_pairs={{0,4},{2,6},{4,8},{6,10},{8,12},{10,14},{12,16},{14,18},{16,20},{1... | collective-permute-start | bytes 245768 | tf_op jit(solution)/shard_map/ppermute | solution.py:516
  11.9 2.6 %collective-permute-done.3.corner = f32[2,16,256]{2,1,0:T(8,128)S(1)} collective-permute-done((f32[2,16,256]{2,1,0:T(8,128)}, f32[2,16,256]{2,1,0:T(8,128)S(1)}, u32[]{:S(2)}, u32[]{:S(2)}) %collective-permute-start.3) | collective-permute-done | bytes 32800 | tf_op jit(solution)/shard_map/ppermute | solution.py:519
  14.6 5.8 %first_step.3 = (f32[176,256]{1,0:T(8,128)S(1)}, f32[160,128]{1,0:T(8,128)S(1)}) custom-call(s32[1]{0:T(128)} %bitcast.place.refs_0_, f32[160,256]{1,0:T(8,128)S(1)} %get-tuple-element.27.own, f32[160,256]{1,0:T(8,128)S(1)} %collective-permute-done.6.near, f32[160,128]{1,0:T(8,128)S(1)} %collective-permute-done.7.far, ...), custom_call_target="tpu_custom_call" | custom-call | flops 8999999488 | bytes 29000000 | tf_op jit(solution)/shard_map/first_step/pallas_call | solution.py:443
  20.3 0.1 collective-permute-start.8
  20.4 0.1 collective-permute-start.9
  20.5 5.8 %first_step.2 = (f32[176,256]{1,0:T(8,128)S(1)}, f32[160,128]{1,0:T(8,128)S(1)}) custom-call(s32[1]{0:T(128)} %bitcast.place.refs_0_, f32[160,256]{1,0:T(8,128)S(1)} %get-tuple-element.20.own, f32[160,256]{1,0:T(8,128)S(1)} %collective-permute-done.1.near, f32[160,128]{1,0:T(8,128)S(1)} %collective-permute-done.2.far, ...), custom_call_target="tpu_custom_call" | custom-call | flops 8999999488 | bytes 29000000 | tf_op jit(solution)/shard_map/first_step/pallas_call | solution.py:443
  26.2 1.1 %collective-permute-start.4 = (f32[176,256]{1,0:T(8,128)S(1)}, f32[176,256]{1,0:T(8,128)S(1)}, u32[]{:S(2)}, u32[]{:S(2)}) collective-permute-start(f32[176,256]{1,0:T(8,128)S(1)} %get-tuple-element.23.own), channel_id=1, source_target_pairs={{0,2},{2,4},{4,6},{6,8},{8,10},{10,12},{12,14},{14,16},{16,18},{18... | collective-permute-start | bytes 540680 | tf_op jit(solution)/shard_map/ppermute | solution.py:515
  27.3 1.0 %collective-permute-start.5 = (f32[160,128]{1,0:T(8,128)S(1)}, f32[160,128]{1,0:T(8,128)S(1)}, u32[]{:S(2)}, u32[]{:S(2)}) collective-permute-start(f32[160,128]{1,0:T(8,128)S(1)} %get-tuple-element.24), channel_id=1, source_target_pairs={{0,4},{2,6},{4,8},{6,10},{8,12},{10,14},{12,16},{14,18},{16,20},{1... | collective-permute-start | bytes 245768 | tf_op jit(solution)/shard_map/ppermute | solution.py:516
  28.3 0.1 collective-permute-done.9.far
  28.4 0.5 %collective-permute-done.8.near = f32[176,256]{1,0:T(8,128)S(1)} collective-permute-done((f32[176,256]{1,0:T(8,128)S(1)}, f32[176,256]{1,0:T(8,128)S(1)}, u32[]{:S(2)}, u32[]{:S(2)}) %collective-permute-start.8) | collective-permute-done | bytes 180256 | tf_op jit(solution)/shard_map/ppermute | solution.py:515
  28.9 5.5 %last_step.2.rest_0_ = f32[2,160,128]{2,1,0:T(8,128)S(1)} custom-call(s32[1]{0:T(128)} %bitcast.place.refs_0_, f32[176,256]{1,0:T(8,128)S(1)} %get-tuple-element.29.own, f32[176,256]{1,0:T(8,128)S(1)} %collective-permute-done.8.near, f32[160,128]{1,0:T(8,128)S(1)} %collective-permute-done.9.far, f32[320,128]{1,0:T(8,128)S(1)} %get-tuple-element.25.spin, ...), custom_call_target="tpu_custom_call" | custom-call | flops 8999999488 | bytes 29000000 | tf_op jit(solution)/shard_map/last_step/pallas_call | solution.py:490
  34.3 1.0 %collective-permute-done.5.far = f32[160,128]{1,0:T(8,128)S(1)} collective-permute-done((f32[160,128]{1,0:T(8,128)S(1)}, f32[160,128]{1,0:T(8,128)S(1)}, u32[]{:S(2)}, u32[]{:S(2)}) %collective-permute-start.5) | collective-permute-done | bytes 81952 | tf_op jit(solution)/shard_map/ppermute | solution.py:516
  35.4 6.3 %last_step.3 = (f32[2,32,256]{2,1,0:T(8,128)}, f32[2,2,32,256]{3,2,1,0:T(8,128)}, f32[2,2,32,256]{3,2,1,0:T(8,128)}) custom-call(s32[1]{0:T(128)} %bitcast.place.refs_0_, f32[176,256]{1,0:T(8,128)S(1)} %get-tuple-element.23.own, f32[176,256]{1,0:T(8,128)S(1)} %collective-permute-done.4.near, f32[160,128]{1,0:T(8,128)S(1)} %collective-permute-done.5.far, ...), custom_call_target="tpu_custom_call" | custom-call | flops 8999999488 | bytes 29000000 | tf_op jit(solution)/shard_map/last_step/pallas_call | solution.py:490
  (13 shorter events, 0.0 us)
Async XLA Ops:
  0.6 1.8 %copy-start = (f32[2,2,32,256]{3,2,1,0:T(8,128)S(1)}, f32[2,2,32,256]{3,2,1,0:T(8,128)}, u32[]{:S(2)}) copy-start(f32[2,2,32,256]{3,2,1,0:T(8,128)} %refs_1_.1) | copy-start | bytes 393220
  0.6 1.8 %copy-start.1 = (f32[2,2,32,256]{3,2,1,0:T(8,128)S(1)}, f32[2,2,32,256]{3,2,1,0:T(8,128)}, u32[]{:S(2)}) copy-start(f32[2,2,32,256]{3,2,1,0:T(8,128)} %refs_2_.1) | copy-start | bytes 393220
  0.7 1.8 %copy-start.2 = (f32[2,32,256]{2,1,0:T(8,128)S(1)}, f32[2,32,256]{2,1,0:T(8,128)}, u32[]{:S(2)}) copy-start(f32[2,32,256]{2,1,0:T(8,128)} %refs_0_.1) | copy-start | bytes 196612
  2.5 7.3 %copy-start.4 = (s32[256]{0:T(256)S(1)}, s32[256]{0:T(256)}, u32[]{:S(2)}) copy-start(s32[256]{0:T(256)} %param.9) | copy-start | bytes 3076
  2.6 7.3 %copy-start.3 = (f32[256]{0:T(256)S(1)}, f32[256]{0:T(256)}, u32[]{:S(2)}) copy-start(f32[256]{0:T(256)} %param.8) | copy-start | bytes 3076
  2.6 12.0 %collective-permute-start.6 = (f32[160,256]{1,0:T(8,128)S(1)}, f32[160,256]{1,0:T(8,128)S(1)}, u32[]{:S(2)}, u32[]{:S(2)}) collective-permute-start(f32[160,256]{1,0:T(8,128)S(1)} %get-tuple-element.27.own), channel_id=1, source_target_pairs={{0,2},{2,4},{4,6},{6,8},{8,10},{10,12},{12,14},{14,16},{16,18},{18... | collective-permute-start | bytes 491528 | tf_op jit(solution)/shard_map/ppermute | solution.py:515
  3.1 11.5 %collective-permute-start.7 = (f32[160,128]{1,0:T(8,128)S(1)}, f32[160,128]{1,0:T(8,128)S(1)}, u32[]{:S(2)}, u32[]{:S(2)}) collective-permute-start(f32[160,128]{1,0:T(8,128)S(1)} %get-tuple-element.28), channel_id=1, source_target_pairs={{0,4},{2,6},{4,8},{6,10},{8,12},{10,14},{12,16},{14,18},{16,20},{1... | collective-permute-start | bytes 245768 | tf_op jit(solution)/shard_map/ppermute | solution.py:516
  5.7 4.2 %collective-permute-start = (f32[2,16,256]{2,1,0:T(8,128)}, f32[2,16,256]{2,1,0:T(8,128)S(1)}, u32[]{:S(2)}, u32[]{:S(2)}) collective-permute-start(f32[2,16,256]{2,1,0:T(8,128)} %edges.1.refs_3_), channel_id=1, source_target_pairs={{0,1},{1,0},{2,3},{3,2},{4,5},{5,4},{6,7},{7,6},{8,9},{9,8},{10,11... | collective-permute-start | bytes 98312 | tf_op jit(solution)/shard_map/ppermute | solution.py:520
  7.2 7.4 %collective-permute-start.3 = (f32[2,16,256]{2,1,0:T(8,128)}, f32[2,16,256]{2,1,0:T(8,128)S(1)}, u32[]{:S(2)}, u32[]{:S(2)}) collective-permute-start(f32[2,16,256]{2,1,0:T(8,128)} %edges.1.refs_3_), channel_id=1, source_target_pairs={{0,3},{1,2},{2,5},{3,4},{4,7},{5,6},{6,9},{7,8},{8,11},{9,10},{10,... | collective-permute-start | bytes 98312 | tf_op jit(solution)/shard_map/ppermute | solution.py:519
  10.2 10.3 %collective-permute-start.1 = (f32[160,256]{1,0:T(8,128)S(1)}, f32[160,256]{1,0:T(8,128)S(1)}, u32[]{:S(2)}, u32[]{:S(2)}) collective-permute-start(f32[160,256]{1,0:T(8,128)S(1)} %get-tuple-element.20.own), channel_id=1, source_target_pairs={{0,2},{2,4},{4,6},{6,8},{8,10},{10,12},{12,14},{14,16},{16,18},{18... | collective-permute-start | bytes 491528 | tf_op jit(solution)/shard_map/ppermute | solution.py:515
  10.7 9.8 %collective-permute-start.2 = (f32[160,128]{1,0:T(8,128)S(1)}, f32[160,128]{1,0:T(8,128)S(1)}, u32[]{:S(2)}, u32[]{:S(2)}) collective-permute-start(f32[160,128]{1,0:T(8,128)S(1)} %get-tuple-element.21), channel_id=1, source_target_pairs={{0,4},{2,6},{4,8},{6,10},{8,12},{10,14},{12,16},{14,18},{16,20},{1... | collective-permute-start | bytes 245768 | tf_op jit(solution)/shard_map/ppermute | solution.py:516
  20.3 8.5 %collective-permute-start.8 = (f32[176,256]{1,0:T(8,128)S(1)}, f32[176,256]{1,0:T(8,128)S(1)}, u32[]{:S(2)}, u32[]{:S(2)}) collective-permute-start(f32[176,256]{1,0:T(8,128)S(1)} %get-tuple-element.29.own), channel_id=1, source_target_pairs={{0,2},{2,4},{4,6},{6,8},{8,10},{10,12},{12,14},{14,16},{16,18},{18... | collective-permute-start | bytes 540680 | tf_op jit(solution)/shard_map/ppermute | solution.py:515
  20.4 8.0 %collective-permute-start.9 = (f32[160,128]{1,0:T(8,128)S(1)}, f32[160,128]{1,0:T(8,128)S(1)}, u32[]{:S(2)}, u32[]{:S(2)}) collective-permute-start(f32[160,128]{1,0:T(8,128)S(1)} %get-tuple-element.30), channel_id=1, source_target_pairs={{0,4},{2,6},{4,8},{6,10},{8,12},{10,14},{12,16},{14,18},{16,20},{1... | collective-permute-start | bytes 245768 | tf_op jit(solution)/shard_map/ppermute | solution.py:516
  26.2 9.1 %collective-permute-start.4 = (f32[176,256]{1,0:T(8,128)S(1)}, f32[176,256]{1,0:T(8,128)S(1)}, u32[]{:S(2)}, u32[]{:S(2)}) collective-permute-start(f32[176,256]{1,0:T(8,128)S(1)} %get-tuple-element.23.own), channel_id=1, source_target_pairs={{0,2},{2,4},{4,6},{6,8},{8,10},{10,12},{12,14},{14,16},{16,18},{18... | collective-permute-start | bytes 540680 | tf_op jit(solution)/shard_map/ppermute | solution.py:515
  27.3 8.1 %collective-permute-start.5 = (f32[160,128]{1,0:T(8,128)S(1)}, f32[160,128]{1,0:T(8,128)S(1)}, u32[]{:S(2)}, u32[]{:S(2)}) collective-permute-start(f32[160,128]{1,0:T(8,128)S(1)} %get-tuple-element.24), channel_id=1, source_target_pairs={{0,4},{2,6},{4,8},{6,10},{8,12},{10,14},{12,16},{14,18},{16,20},{1... | collective-permute-start | bytes 245768 | tf_op jit(solution)/shard_map/ppermute | solution.py:516

commit v22 on v20

--- a/solution.py
+++ b/solution.py
@@ -555,7 +555,7 @@
     moved = []
     for own, far in zip(owns, fars):
         if moved:
-            own, far, _ = lax.optimization_barrier((own, far, tables[0]))
+            own, far, _ = lax.optimization_barrier((own, far, side))
         moved.append((send_near(own), send_far(far)))
     states = []
     for level in range(levels):

time: 41.8 us -> 41.8 us (level)
  no operation moved by 1% of the time
where the time goes in v22:
time: 41.8 us; the launch traced here: 41.6 us
  Pallas kernels  25.4 us (61%)
  starting transfers between devices  9.48 us (23%)
  waiting for transfers between devices  5.9 us (14%)
  between operations  0.77 us (2%)
    pallas_call x2, Pallas kernels, last_step(): pl.pallas_call(kernel, out_shape=out_shape, in_specs=[smem] + [vmem] * (5...  11.7 us
    pallas_call x2, Pallas kernels, first_step(): pl.pallas_call(kernel, out_shape=[f32(FIELDS * own_cells + EXTRA, radius)...  11.5 us
    ppermute x4, starting transfers between devices, body(): lax.ppermute(x, 'phi', [(p, (p + 2) % phi_count) for p in range(phi_count)])  4.78 us
    ppermute x1, waiting for transfers between devices, body(): send_corner = lambda x: lax.ppermute(x, ('phi', 'row'), diagonal)  2.7 us
    ppermute x4, starting transfers between devices, body(): lax.ppermute(x, 'phi', [(p, (p + 1) % phi_count) for p in range(phi_count)])  2.05 us
    pallas_call x1, Pallas kernels, body(): pl.pallas_call(edge_kernel, out_shape=f32(levels, EXTRA, 2 * LANES), in_s...  1.74 us
    ppermute x1, waiting for transfers between devices, body(): send_side = lambda x: lax.ppermute(x, 'row', [(0, 1), (1, 0)])  1.51 us
    ppermute x1, starting transfers between devices, body(): send_side = lambda x: lax.ppermute(x, 'row', [(0, 1), (1, 0)])  1.49 us
  transfers between devices with their start and end apart: 10, of which 5 were waited for; matrix products, arithmetic and copies ran while one was open for 0% of the time, Pallas kernels for 42%

profile of v22, /device:TPU:0, one launch (start us, length us, event | category | flops | bytes accessed | tf_op | source)
XLA Modules:
  0.0 41.6 jit_solution(18162248159371295164)
XLA Ops:
  0.7 1.7 %edges.1.refs_3_ = f32[2,16,256]{2,1,0:T(8,128)} custom-call(s32[1]{0:T(128)} %bitcast.place.refs_0_, f32[2,32,256]{2,1,0:T(8,128)} %refs_0_.1, f32[2,2,32,256]{3,2,1,0:T(8,128)} %refs_1_.1, f32[2,2,32,256]{3,2,1,0:T(8,128)} %refs_2_.1, f32[2,128]{1,0:T(2,128)} %bitcast.3, s32[2,128]{1,0:T(2,128)} %bitcast.5), custom_call_target="tpu_custom_call" | custom-call | tf_op jit(solution)/shard_map/edges/pallas_call | solution.py:517
  2.4 0.0 copy-start.4
  2.5 0.1 pack.1
  2.6 0.5 %collective-permute-start.6 = (f32[160,256]{1,0:T(8,128)S(1)}, f32[160,256]{1,0:T(8,128)S(1)}, u32[]{:S(2)}, u32[]{:S(2)}) collective-permute-start(f32[160,256]{1,0:T(8,128)S(1)} %get-tuple-element.27.own), channel_id=1, source_target_pairs={{0,2},{2,4},{4,6},{6,8},{8,10},{10,12},{12,14},{14,16},{16,18},{18... | collective-permute-start | bytes 491528 | tf_op jit(solution)/shard_map/ppermute | solution.py:507
  3.1 2.6 %collective-permute-start.7 = (f32[160,128]{1,0:T(8,128)S(1)}, f32[160,128]{1,0:T(8,128)S(1)}, u32[]{:S(2)}, u32[]{:S(2)}) collective-permute-start(f32[160,128]{1,0:T(8,128)S(1)} %get-tuple-element.28), channel_id=1, source_target_pairs={{0,4},{2,6},{4,8},{6,10},{8,12},{10,14},{12,16},{14,18},{16,20},{1... | collective-permute-start | bytes 245768 | tf_op jit(solution)/shard_map/ppermute | solution.py:508
  5.7 1.5 %collective-permute-start = (f32[2,16,256]{2,1,0:T(8,128)}, f32[2,16,256]{2,1,0:T(8,128)S(1)}, u32[]{:S(2)}, u32[]{:S(2)}) collective-permute-start(f32[2,16,256]{2,1,0:T(8,128)} %edges.1.refs_3_), channel_id=1, source_target_pairs={{0,1},{1,0},{2,3},{3,2},{4,5},{5,4},{6,7},{7,6},{8,9},{9,8},{10,11... | collective-permute-start | bytes 98312 | tf_op jit(solution)/shard_map/ppermute | solution.py:512
  7.1 1.1 %collective-permute-start.3 = (f32[2,16,256]{2,1,0:T(8,128)}, f32[2,16,256]{2,1,0:T(8,128)S(1)}, u32[]{:S(2)}, u32[]{:S(2)}) collective-permute-start(f32[2,16,256]{2,1,0:T(8,128)} %edges.1.refs_3_), channel_id=1, source_target_pairs={{0,3},{1,2},{2,5},{3,4},{4,7},{5,6},{6,9},{7,8},{8,11},{9,10},{10,... | collective-permute-start | bytes 98312 | tf_op jit(solution)/shard_map/ppermute | solution.py:511
  8.3 1.5 %collective-permute-done.refs_1_.side = f32[2,16,256]{2,1,0:T(8,128)S(1)} collective-permute-done((f32[2,16,256]{2,1,0:T(8,128)}, f32[2,16,256]{2,1,0:T(8,128)S(1)}, u32[]{:S(2)}, u32[]{:S(2)}) %collective-permute-start) | collective-permute-done | bytes 32800 | tf_op jit(solution)/shard_map/ppermute | solution.py:512
  9.8 0.4 %collective-permute-start.1 = (f32[160,256]{1,0:T(8,128)S(1)}, f32[160,256]{1,0:T(8,128)S(1)}, u32[]{:S(2)}, u32[]{:S(2)}) collective-permute-start(f32[160,256]{1,0:T(8,128)S(1)} %get-tuple-element.19.own), channel_id=1, source_target_pairs={{0,2},{2,4},{4,6},{6,8},{8,10},{10,12},{12,14},{14,16},{16,18},{18... | collective-permute-start | bytes 491528 | tf_op jit(solution)/shard_map/ppermute | solution.py:507
  10.2 1.2 %collective-permute-start.2 = (f32[160,128]{1,0:T(8,128)S(1)}, f32[160,128]{1,0:T(8,128)S(1)}, u32[]{:S(2)}, u32[]{:S(2)}) collective-permute-start(f32[160,128]{1,0:T(8,128)S(1)} %get-tuple-element.20), channel_id=1, source_target_pairs={{0,4},{2,6},{4,8},{6,10},{8,12},{10,14},{12,16},{14,18},{16,20},{1... | collective-permute-start | bytes 245768 | tf_op jit(solution)/shard_map/ppermute | solution.py:508
  11.5 0.4 tables.1
  11.8 2.7 %collective-permute-done.3.corner = f32[2,16,256]{2,1,0:T(8,128)S(1)} collective-permute-done((f32[2,16,256]{2,1,0:T(8,128)}, f32[2,16,256]{2,1,0:T(8,128)S(1)}, u32[]{:S(2)}, u32[]{:S(2)}) %collective-permute-start.3) | collective-permute-done | bytes 32800 | tf_op jit(solution)/shard_map/ppermute | solution.py:511
  14.5 0.0 collective-permute-done.7.far
  14.5 5.8 %first_step.3 = (f32[176,256]{1,0:T(8,128)S(1)}, f32[160,128]{1,0:T(8,128)S(1)}) custom-call(s32[1]{0:T(128)} %bitcast.place.refs_0_, f32[160,256]{1,0:T(8,128)S(1)} %get-tuple-element.27.own, f32[160,256]{1,0:T(8,128)S(1)} %collective-permute-done.6.near, f32[160,128]{1,0:T(8,128)S(1)} %collective-permute-done.7.far, ...), custom_call_target="tpu_custom_call" | custom-call | flops 8999999488 | bytes 29000000 | tf_op jit(solution)/shard_map/first_step/pallas_call | solution.py:439
  20.3 0.1 collective-permute-start.8
  20.4 0.1 collective-permute-start.9
  20.5 5.8 %first_step.2 = (f32[176,256]{1,0:T(8,128)S(1)}, f32[160,128]{1,0:T(8,128)S(1)}) custom-call(s32[1]{0:T(128)} %bitcast.place.refs_0_, f32[160,256]{1,0:T(8,128)S(1)} %get-tuple-element.19.own, f32[160,256]{1,0:T(8,128)S(1)} %collective-permute-done.1.near, f32[160,128]{1,0:T(8,128)S(1)} %collective-permute-done.2.far, ...), custom_call_target="tpu_custom_call" | custom-call | flops 8999999488 | bytes 29000000 | tf_op jit(solution)/shard_map/first_step/pallas_call | solution.py:439
  26.2 1.1 %collective-permute-start.4 = (f32[176,256]{1,0:T(8,128)S(1)}, f32[176,256]{1,0:T(8,128)S(1)}, u32[]{:S(2)}, u32[]{:S(2)}) collective-permute-start(f32[176,256]{1,0:T(8,128)S(1)} %get-tuple-element.23.own), channel_id=1, source_target_pairs={{0,2},{2,4},{4,6},{6,8},{8,10},{10,12},{12,14},{14,16},{16,18},{18... | collective-permute-start | bytes 540680 | tf_op jit(solution)/shard_map/ppermute | solution.py:507
  27.3 0.9 %collective-permute-start.5 = (f32[160,128]{1,0:T(8,128)S(1)}, f32[160,128]{1,0:T(8,128)S(1)}, u32[]{:S(2)}, u32[]{:S(2)}) collective-permute-start(f32[160,128]{1,0:T(8,128)S(1)} %get-tuple-element.24), channel_id=1, source_target_pairs={{0,4},{2,6},{4,8},{6,10},{8,12},{10,14},{12,16},{14,18},{16,20},{1... | collective-permute-start | bytes 245768 | tf_op jit(solution)/shard_map/ppermute | solution.py:508
  28.2 0.2 collective-permute-done.9.far
  28.4 0.5 %collective-permute-done.8.near = f32[176,256]{1,0:T(8,128)S(1)} collective-permute-done((f32[176,256]{1,0:T(8,128)S(1)}, f32[176,256]{1,0:T(8,128)S(1)}, u32[]{:S(2)}, u32[]{:S(2)}) %collective-permute-start.8) | collective-permute-done | bytes 180256 | tf_op jit(solution)/shard_map/ppermute | solution.py:507
  28.9 5.5 %last_step.2.rest_0_ = f32[160,256]{1,0:T(8,128)S(1)} custom-call(s32[1]{0:T(128)} %bitcast.place.refs_0_, f32[176,256]{1,0:T(8,128)S(1)} %get-tuple-element.29.own, f32[176,256]{1,0:T(8,128)S(1)} %collective-permute-done.8.near, f32[160,128]{1,0:T(8,128)S(1)} %collective-permute-done.9.far, f32[320,128]{1,0:T(8,128)S(1)} %get-tuple-element.25.spin, ...), custom_call_target="tpu_custom_call" | custom-call | flops 8999999488 | bytes 29000000 | tf_op jit(solution)/shard_map/last_step/pallas_call | solution.py:482
  34.3 1.0 %collective-permute-done.5.far = f32[160,128]{1,0:T(8,128)S(1)} collective-permute-done((f32[160,128]{1,0:T(8,128)S(1)}, f32[160,128]{1,0:T(8,128)S(1)}, u32[]{:S(2)}, u32[]{:S(2)}) %collective-permute-start.5) | collective-permute-done | bytes 81952 | tf_op jit(solution)/shard_map/ppermute | solution.py:508
  35.4 6.2 %last_step.3 = (f32[2,32,256]{2,1,0:T(8,128)}, f32[2,2,32,256]{3,2,1,0:T(8,128)}, f32[2,2,32,256]{3,2,1,0:T(8,128)}) custom-call(s32[1]{0:T(128)} %bitcast.place.refs_0_, f32[176,256]{1,0:T(8,128)S(1)} %get-tuple-element.23.own, f32[176,256]{1,0:T(8,128)S(1)} %collective-permute-done.4.near, f32[160,128]{1,0:T(8,128)S(1)} %collective-permute-done.5.far, ...), custom_call_target="tpu_custom_call" | custom-call | flops 8999999488 | bytes 29000000 | tf_op jit(solution)/shard_map/last_step/pallas_call | solution.py:482
  (13 shorter events, 0.0 us)
Async XLA Ops:
  0.6 1.8 %copy-start = (f32[2,2,32,256]{3,2,1,0:T(8,128)S(1)}, f32[2,2,32,256]{3,2,1,0:T(8,128)}, u32[]{:S(2)}) copy-start(f32[2,2,32,256]{3,2,1,0:T(8,128)} %refs_1_.1) | copy-start | bytes 393220
  0.6 1.8 %copy-start.1 = (f32[2,2,32,256]{3,2,1,0:T(8,128)S(1)}, f32[2,2,32,256]{3,2,1,0:T(8,128)}, u32[]{:S(2)}) copy-start(f32[2,2,32,256]{3,2,1,0:T(8,128)} %refs_2_.1) | copy-start | bytes 393220
  0.7 1.8 %copy-start.2 = (f32[2,32,256]{2,1,0:T(8,128)S(1)}, f32[2,32,256]{2,1,0:T(8,128)}, u32[]{:S(2)}) copy-start(f32[2,32,256]{2,1,0:T(8,128)} %refs_0_.1) | copy-start | bytes 196612
  2.4 9.0 %copy-start.4 = (s32[256]{0:T(256)S(1)}, s32[256]{0:T(256)}, u32[]{:S(2)}) copy-start(s32[256]{0:T(256)} %param.9) | copy-start | bytes 3076
  2.6 12.0 %collective-permute-start.6 = (f32[160,256]{1,0:T(8,128)S(1)}, f32[160,256]{1,0:T(8,128)S(1)}, u32[]{:S(2)}, u32[]{:S(2)}) collective-permute-start(f32[160,256]{1,0:T(8,128)S(1)} %get-tuple-element.27.own), channel_id=1, source_target_pairs={{0,2},{2,4},{4,6},{6,8},{8,10},{10,12},{12,14},{14,16},{16,18},{18... | collective-permute-start | bytes 491528 | tf_op jit(solution)/shard_map/ppermute | solution.py:507
  3.1 11.5 %collective-permute-start.7 = (f32[160,128]{1,0:T(8,128)S(1)}, f32[160,128]{1,0:T(8,128)S(1)}, u32[]{:S(2)}, u32[]{:S(2)}) collective-permute-start(f32[160,128]{1,0:T(8,128)S(1)} %get-tuple-element.28), channel_id=1, source_target_pairs={{0,4},{2,6},{4,8},{6,10},{8,12},{10,14},{12,16},{14,18},{16,20},{1... | collective-permute-start | bytes 245768 | tf_op jit(solution)/shard_map/ppermute | solution.py:508
  5.7 4.2 %collective-permute-start = (f32[2,16,256]{2,1,0:T(8,128)}, f32[2,16,256]{2,1,0:T(8,128)S(1)}, u32[]{:S(2)}, u32[]{:S(2)}) collective-permute-start(f32[2,16,256]{2,1,0:T(8,128)} %edges.1.refs_3_), channel_id=1, source_target_pairs={{0,1},{1,0},{2,3},{3,2},{4,5},{5,4},{6,7},{7,6},{8,9},{9,8},{10,11... | collective-permute-start | bytes 98312 | tf_op jit(solution)/shard_map/ppermute | solution.py:512
  7.1 7.4 %collective-permute-start.3 = (f32[2,16,256]{2,1,0:T(8,128)}, f32[2,16,256]{2,1,0:T(8,128)S(1)}, u32[]{:S(2)}, u32[]{:S(2)}) collective-permute-start(f32[2,16,256]{2,1,0:T(8,128)} %edges.1.refs_3_), channel_id=1, source_target_pairs={{0,3},{1,2},{2,5},{3,4},{4,7},{5,6},{6,9},{7,8},{8,11},{9,10},{10,... | collective-permute-start | bytes 98312 | tf_op jit(solution)/shard_map/ppermute | solution.py:511
  9.8 1.7 %copy-start.3 = (f32[256]{0:T(256)S(1)}, f32[256]{0:T(256)}, u32[]{:S(2)}) copy-start(f32[256]{0:T(256)} %param.8) | copy-start | bytes 3076
  9.8 10.7 %collective-permute-start.1 = (f32[160,256]{1,0:T(8,128)S(1)}, f32[160,256]{1,0:T(8,128)S(1)}, u32[]{:S(2)}, u32[]{:S(2)}) collective-permute-start(f32[160,256]{1,0:T(8,128)S(1)} %get-tuple-element.19.own), channel_id=1, source_target_pairs={{0,2},{2,4},{4,6},{6,8},{8,10},{10,12},{12,14},{14,16},{16,18},{18... | collective-permute-start | bytes 491528 | tf_op jit(solution)/shard_map/ppermute | solution.py:507
  10.2 10.2 %collective-permute-start.2 = (f32[160,128]{1,0:T(8,128)S(1)}, f32[160,128]{1,0:T(8,128)S(1)}, u32[]{:S(2)}, u32[]{:S(2)}) collective-permute-start(f32[160,128]{1,0:T(8,128)S(1)} %get-tuple-element.20), channel_id=1, source_target_pairs={{0,4},{2,6},{4,8},{6,10},{8,12},{10,14},{12,16},{14,18},{16,20},{1... | collective-permute-start | bytes 245768 | tf_op jit(solution)/shard_map/ppermute | solution.py:508
  20.3 8.5 %collective-permute-start.8 = (f32[176,256]{1,0:T(8,128)S(1)}, f32[176,256]{1,0:T(8,128)S(1)}, u32[]{:S(2)}, u32[]{:S(2)}) collective-permute-start(f32[176,256]{1,0:T(8,128)S(1)} %get-tuple-element.29.own), channel_id=1, source_target_pairs={{0,2},{2,4},{4,6},{6,8},{8,10},{10,12},{12,14},{14,16},{16,18},{18... | collective-permute-start | bytes 540680 | tf_op jit(solution)/shard_map/ppermute | solution.py:507
  20.4 8.0 %collective-permute-start.9 = (f32[160,128]{1,0:T(8,128)S(1)}, f32[160,128]{1,0:T(8,128)S(1)}, u32[]{:S(2)}, u32[]{:S(2)}) collective-permute-start(f32[160,128]{1,0:T(8,128)S(1)} %get-tuple-element.30), channel_id=1, source_target_pairs={{0,4},{2,6},{4,8},{6,10},{8,12},{10,14},{12,16},{14,18},{16,20},{1... | collective-permute-start | bytes 245768 | tf_op jit(solution)/shard_map/ppermute | solution.py:508
  26.2 9.1 %collective-permute-start.4 = (f32[176,256]{1,0:T(8,128)S(1)}, f32[176,256]{1,0:T(8,128)S(1)}, u32[]{:S(2)}, u32[]{:S(2)}) collective-permute-start(f32[176,256]{1,0:T(8,128)S(1)} %get-tuple-element.23.own), channel_id=1, source_target_pairs={{0,2},{2,4},{4,6},{6,8},{8,10},{10,12},{12,14},{14,16},{16,18},{18... | collective-permute-start | bytes 540680 | tf_op jit(solution)/shard_map/ppermute | solution.py:507
  27.3 8.1 %collective-permute-start.5 = (f32[160,128]{1,0:T(8,128)S(1)}, f32[160,128]{1,0:T(8,128)S(1)}, u32[]{:S(2)}, u32[]{:S(2)}) collective-permute-start(f32[160,128]{1,0:T(8,128)S(1)} %get-tuple-element.24), channel_id=1, source_target_pairs={{0,4},{2,6},{4,8},{6,10},{8,12},{10,14},{12,16},{14,18},{16,20},{1... | collective-permute-start | bytes 245768 | tf_op jit(solution)/shard_map/ppermute | solution.py:508
